TPU v7x, 32 devices: a whole 2x2x4 slice. The times are simulated.
32 devices in a mesh: grp: 4 (over y, x), box: 8 (over z, core).
Axes of the slice: x: 2, y: 2, z: 4, core: 2. Of those that a mesh axis runs over, the one named last changes fastest.
Arguments:
- source: float32 [128, 8, 16, 128], P('grp', 'box'), may hold values from -6 to 6
- alpha_coef: float32 [128, 8, 16, 128], P('grp', 'box'), may hold values from 0.02 to 0.2
- beta_coef: float32 [128, 8, 16, 128], P('grp', 'box'), may hold values from 0.5 to 5
Outputs:
- solution: float32 [128, 8, 16, 128], P('grp', 'box')
All inputs are finite; a program needn't handle non-finite values.
Results may differ from a plain program's by a relative error of at most 0.00002.
Values sent between devices are 32-bit elements; how exact they have to be, the bound alone decides.
No kernel may reach another device: no remote copies, remote signals or barrier semaphores. Data moves between devices by JAX's collectives and lax.ppermute only.
A program may use at most 128 MiB of HBM per device.

v0:
```python
import jax
import jax.numpy as jnp
import numpy as np
from jax import lax
from jax.sharding import PartitionSpec as P

SWEEPS = 2
COARSE_SWEEPS = 4


OMEGA = 0.7
SHIFTS = ((1, 0, 0), (-1, 0, 0), (0, 1, 0), (0, -1, 0), (0, 0, 1), (0, 0, -1))


def extended_2(cells, sides, width):
    for axis, dim in sides:
        count = lax.axis_size(axis)
        ends = count - 1
        head = lax.slice_in_dim(cells, 0, width, axis=dim)
        tail = lax.slice_in_dim(cells, cells.shape[dim] - width, cells.shape[dim], axis=dim)
        cells = jnp.concatenate(
            [
                lax.ppermute(tail, axis, [(i, (i + 1) % count) for i in range(ends)]),
                cells,
                lax.ppermute(head, axis, [((i + 1) % count, i) for i in range(ends)]),
            ],
            axis=dim,
        )
    return cells


def swapped(array, axis, apart):
    return lax.ppermute(array, axis, [(i, i ^ 1 << apart) for i in range(lax.axis_size(axis))])


def inner_view(padded, step_x, step_y, step_z):
    return padded[
        1 + step_x : padded.shape[0] - 1 + step_x,
        1 + step_y : padded.shape[1] - 1 + step_y,
        1 + step_z : padded.shape[2] - 1 + step_z,
    ]


def neighbours(field_pad, beta_pad):
    centre = inner_view(beta_pad, 0, 0, 0)
    diag_sum = jnp.zeros(centre.shape, jnp.float32)
    off_sum = jnp.zeros(centre.shape, jnp.float32)
    for shift in SHIFTS:
        face_coef = 0.5 * (centre + inner_view(beta_pad, shift[0], shift[1], shift[2]))
        diag_sum = diag_sum + face_coef
        off_sum = off_sum + face_coef * inner_view(field_pad, shift[0], shift[1], shift[2])
    return (diag_sum, off_sum)


def applied_region(extended, alpha_c, beta_ext, scale):
    diag_sum, off_sum = neighbours(extended, beta_ext)
    centre = extended[1:-1, 1:-1, 1:-1]
    return (alpha_c * centre + scale * (diag_sum * centre - off_sum), diag_sum, centre)


def relax(extended, source_c, alpha_c, beta_ext, scale):
    applied, diag_sum, centre = applied_region(extended, alpha_c, beta_ext, scale)
    return centre + OMEGA * (source_c - applied) / (alpha_c + scale * diag_sum)


def restrict(values):
    shaped = values.reshape(
        values.shape[0] // 2, 2, values.shape[1] // 2, 2, values.shape[2] // 2, 2
    )
    return jnp.sum(shaped, axis=(1, 3, 5)) * 0.125


def prolong(coarse):
    wide = jnp.broadcast_to(
        coarse[:, None, :, None, :, None],
        (coarse.shape[0], 2, coarse.shape[1], 2, coarse.shape[2], 2),
    )
    return wide.reshape(2 * coarse.shape[0], 2 * coarse.shape[1], 2 * coarse.shape[2])


def gray_position(device_code, bit_count):
    position = device_code
    for shift_bits in range(1, bit_count):
        position = position ^ device_code >> shift_bits
    return position


def body(source, alpha_coef, beta_coef):
    source = source[:, 0]
    alpha_coef = alpha_coef[:, 0]
    beta_coef = beta_coef[:, 0]
    group_index = lax.axis_index("grp")
    box_index = lax.axis_index("box")
    group_count = lax.axis_size("grp")
    block_count = lax.axis_size("box")
    bit_count = block_count.bit_length() - 1
    position = gray_position(box_index, bit_count)

    def rim(values, width):
        ext = extended_2(values, (("grp", 1),), width)
        rim_shape = ext.shape[:2] + (width,) + ext.shape[3:]
        below_rim = jnp.zeros(rim_shape, ext.dtype)
        above_rim = jnp.zeros(rim_shape, ext.dtype)
        for swap_bit in range(bit_count):
            partner_pos = gray_position(box_index ^ 1 << swap_bit, bit_count)
            partner_above = partner_pos == position + 1
            partner_below = partner_pos == position - 1
            outgoing = jnp.where(partner_above, ext[:, :, -width:], ext[:, :, :width])
            received = swapped(outgoing, "box", swap_bit)
            below_rim = jnp.where(partner_below, received, below_rim)
            above_rim = jnp.where(partner_above, received, above_rim)
        ext = jnp.concatenate((below_rim, ext, above_rim), 2)
        return jnp.pad(ext, ((0, 0), (0, 0), (0, 0), (width, width)))

    def prepare(source_c, alpha_c, beta_c):
        beta_rim = rim(beta_c[None], 1)[0]
        return (source_c, alpha_c, beta_rim, None, None)

    def smooth(field, context, scale):
        source_c, alpha_c, beta_rim, wide, valid = context
        for sweep in range(SWEEPS):
            extended = rim(field[None], 1)[0]
            field = relax(extended, source_c, alpha_c, beta_rim, scale)
        return field

    def residual(field, context, scale):
        source_c, alpha_c, beta_rim, wide, valid = context
        extended = rim(field[None], 1)[0]
        applied, diag_sum, centre = applied_region(extended, alpha_c, beta_rim, scale)
        return source_c - applied

    context0 = prepare(source, alpha_coef, beta_coef)
    field0 = smooth(jnp.zeros(source.shape, jnp.float32), context0, 1.0)
    source1 = restrict(residual(field0, context0, 1.0))
    alpha1 = restrict(alpha_coef)
    beta1 = restrict(beta_coef)
    context1 = prepare(source1, alpha1, beta1)
    field1 = smooth(jnp.zeros(source1.shape, jnp.float32), context1, 0.25)
    source2 = restrict(residual(field1, context1, 0.25))
    alpha2 = restrict(alpha1)
    beta2 = restrict(beta1)
    coarse_x = source2.shape[0]
    coarse_y = source2.shape[1]
    coarse_z = source2.shape[2]
    block_order = np.array(
        [slot_pos ^ slot_pos >> 1 for slot_pos in range(block_count)], dtype=np.int32
    )
    collected = lax.all_gather(jnp.stack((source2, alpha2, beta2))[None], "box", axis=0, tiled=True)
    collected = collected[block_order]
    gathered = jnp.transpose(collected, (1, 2, 0, 3, 4)).reshape(
        3, coarse_x, block_count * coarse_y, coarse_z
    )
    merged = gathered
    for level_bit in range(group_count.bit_length() - 1):
        partner = swapped(merged, "grp", level_bit)
        upper = group_index >> level_bit & 1 == 1
        merged = jnp.where(
            upper, jnp.concatenate((partner, merged), 1), jnp.concatenate((merged, partner), 1)
        )
    source_c = merged[0]
    alpha_c = merged[1]
    beta_ext = jnp.pad(merged[2], 1)
    field_c = jnp.zeros(source_c.shape, jnp.float32)
    for sweep in range(COARSE_SWEEPS):
        extended = jnp.pad(field_c, 1)
        field_c = relax(extended, source_c, alpha_c, beta_ext, 0.0625)
    field2 = lax.dynamic_slice(
        field_c,
        (group_index * coarse_x, position * coarse_y, jnp.int32(0)),
        (coarse_x, coarse_y, coarse_z),
    )
    field1 = smooth(field1 + prolong(field2), context1, 0.25)
    field0 = smooth(field0 + prolong(field1), context0, 1.0)
    return field0[:, None]


def solution(mesh):
    in_specs = (
        P("grp", "box", None, None),
        P("grp", "box", None, None),
        P("grp", "box", None, None),
    )
    out_specs = P("grp", "box", None, None)
    return jax.shard_map(body, mesh=mesh, in_specs=in_specs, out_specs=out_specs, check_vma=False)
```

profile of v0, /device:TPU:11, one launch (start us, length us, event | category | flops | bytes accessed | tf_op | source)
XLA Modules:
  0.0 325.2 jit_solution(4075721830554828643)
XLA Ops:
  2.2 4.0 %collective-permute-start = (f32[1,1,16,128]{3,2,1,0:T(8,128)S(1)}, f32[1,1,16,128]{3,2,1,0:T(8,128)S(1)}, u32[]{:S(2)}, u32[]{:S(2)}) collective-permute-start(f32[1,1,16,128]{3,2,1,0:T(8,128)S(1)} %broadcast.122), channel_id=1, source_target_pairs={{0,8},{8,16},{16,24},{1,9},{9,17},{17,25},{2,10},{10,18},{18,26},{... | collective-permute-start | bytes 24584 | tf_op jit(solution)/shard_map/ppermute | solution.py:23
  8.1 4.3 %collective-permute-start.15 = (f32[1,1,8,64]{3,2,1,0:T(8,128)S(1)}, f32[1,1,8,64]{3,2,1,0:T(8,128)S(1)}, u32[]{:S(2)}, u32[]{:S(2)}) collective-permute-start(f32[1,1,8,64]{3,2,1,0:T(8,128)S(1)} %broadcast.126), channel_id=1, source_target_pairs={{0,8},{8,16},{16,24},{1,9},{9,17},{17,25},{2,10},{10,18},{18,26},{... | collective-permute-start | bytes 6152 | tf_op jit(solution)/shard_map/ppermute | solution.py:23
  15.0 18.9 %reshape_squeeze.7 = f32[16,2,8,2,64,2]{5,4,3,2,1,0:T(8,128)} reshape(f32[32,1,16,128]{3,2,1,0:T(8,128)} %param.7) | data formatting | bytes 524288 | tf_op jit(solution)/shard_map/reshape;squeeze | solution.py:67
  33.9 7.0 %reduce_sum.56 = f32[16,8,64]{2,1,0:T(8,128)S(1)} reduce(f32[16,2,8,2,64,2]{5,4,3,2,1,0:T(8,128)} %reshape_squeeze.7, f32[]{:T(128)} %constant.22.clone.1), dimensions={1,3,5}, to_apply=%region_2.3 | reduce | flops 57344 | bytes 294916 | tf_op jit(solution)/shard_map/reduce_sum | solution.py:70
  41.6 18.1 %reshape_squeeze.6 = f32[16,2,8,2,64,2]{5,4,3,2,1,0:T(8,128)} reshape(f32[32,1,16,128]{3,2,1,0:T(8,128)S(1)} %copy-done) | data formatting | bytes 524288 | tf_op jit(solution)/shard_map/reshape;squeeze | solution.py:67
  59.7 7.0 %reduce_sum.55 = f32[16,8,64]{2,1,0:T(8,128)S(1)} reduce(f32[16,2,8,2,64,2]{5,4,3,2,1,0:T(8,128)} %reshape_squeeze.6, f32[]{:T(128)} %constant.22.clone.1), dimensions={1,3,5}, to_apply=%region_1.2 | reduce | flops 57344 | bytes 294916 | tf_op jit(solution)/shard_map/reduce_sum | solution.py:70
  68.7 4.3 %collective-permute-start.25 = (f32[1,1,8,64]{3,2,1,0:T(8,128)S(1)}, f32[1,1,8,64]{3,2,1,0:T(8,128)S(1)}, u32[]{:S(2)}, u32[]{:S(2)}) collective-permute-start(f32[1,1,8,64]{3,2,1,0:T(8,128)S(1)} %get-tuple-element.88), channel_id=1, source_target_pairs={{0,8},{8,16},{16,24},{1,9},{9,17},{17,25},{2,10},{10,18},{18,26},{... | collective-permute-start | bytes 6152 | tf_op jit(solution)/shard_map/ppermute | solution.py:23
  80.6 4.0 %collective-permute-start.4 = (f32[1,34,1,128]{3,2,1,0:T(1,128)S(1)}, f32[1,34,1,128]{3,2,1,0:T(1,128)S(1)}, u32[]{:S(2)}, u32[]{:S(2)}) collective-permute-start(f32[1,34,1,128]{3,2,1,0:T(1,128)S(1)} %get-tuple-element.53), channel_id=1, source_target_pairs={{0,1},{1,0},{2,3},{3,2},{4,5},{5,4},{6,7},{7,6},{8,9},{9,8},{10,11... | collective-permute-start | bytes 52232 | tf_op jit(solution)/shard_map/ppermute | solution.py:33
  99.1 4.3 %collective-permute-start.10 = (f32[1,1,16,128]{3,2,1,0:T(8,128)S(1)}, f32[1,1,16,128]{3,2,1,0:T(8,128)S(1)}, u32[]{:S(2)}, u32[]{:S(2)}) collective-permute-start(f32[1,1,16,128]{3,2,1,0:T(8,128)S(1)} %get-tuple-element.70), channel_id=1, source_target_pairs={{0,8},{8,16},{16,24},{1,9},{9,17},{17,25},{2,10},{10,18},{18,26},{... | collective-permute-start | bytes 24584 | tf_op jit(solution)/shard_map/ppermute | solution.py:23
  110.8 4.8 %collective-permute-start.20 = (f32[1,1,16,128]{3,2,1,0:T(8,128)S(1)}, f32[1,1,16,128]{3,2,1,0:T(8,128)S(1)}, u32[]{:S(2)}, u32[]{:S(2)}) collective-permute-start(f32[1,1,16,128]{3,2,1,0:T(8,128)S(1)} %get-tuple-element.68), channel_id=1, source_target_pairs={{0,8},{8,16},{16,24},{1,9},{9,17},{17,25},{2,10},{10,18},{18,26},{... | collective-permute-start | bytes 24584 | tf_op jit(solution)/shard_map/ppermute | solution.py:23
  124.0 18.1 %reshape.61 = f32[16,2,8,2,64,2]{5,4,3,2,1,0:T(8,128)} reshape(f32[32,16,128]{2,1,0:T(8,128)S(1)} %fusion.109) | data formatting | bytes 524288 | tf_op jit(solution)/shard_map/reshape | solution.py:67
  142.1 7.0 %reduce_sum.54 = f32[16,8,64]{2,1,0:T(8,128)S(1)} reduce(f32[16,2,8,2,64,2]{5,4,3,2,1,0:T(8,128)} %reshape.61, f32[]{:T(128)} %constant.22.clone.1), dimensions={1,3,5}, to_apply=%region_0.1 | reduce | flops 57344 | bytes 294916 | tf_op jit(solution)/shard_map/reduce_sum | solution.py:70
  152.1 4.8 %collective-permute-start.30 = (f32[1,1,8,64]{3,2,1,0:T(8,128)S(1)}, f32[1,1,8,64]{3,2,1,0:T(8,128)S(1)}, u32[]{:S(2)}, u32[]{:S(2)}) collective-permute-start(f32[1,1,8,64]{3,2,1,0:T(8,128)S(1)} %get-tuple-element.86), channel_id=1, source_target_pairs={{0,8},{8,16},{16,24},{1,9},{9,17},{17,25},{2,10},{10,18},{18,26},{... | collective-permute-start | bytes 6152 | tf_op jit(solution)/shard_map/ppermute | solution.py:23
  172.0 4.8 %collective-permute-start.35 = (f32[1,1,8,64]{3,2,1,0:T(8,128)S(1)}, f32[1,1,8,64]{3,2,1,0:T(8,128)S(1)}, u32[]{:S(2)}, u32[]{:S(2)}) collective-permute-start(f32[1,1,8,64]{3,2,1,0:T(8,128)S(1)} %get-tuple-element.82), channel_id=1, source_target_pairs={{0,8},{8,16},{16,24},{1,9},{9,17},{17,25},{2,10},{10,18},{18,26},{... | collective-permute-start | bytes 6152 | tf_op jit(solution)/shard_map/ppermute | solution.py:23
  192.9 14.2 %all-gather = f32[24,8,4,32]{3,1,2,0:T(8,128)S(1)} all-gather(f32[3,8,4,32]{3,1,2,0:T(8,128)S(1)} %copy.10), channel_id=2, replica_groups=mesh['grp'=4,'box'=8] {'box'}, dimensions={0}, use_global_device_ids=true | all-gather | bytes 110592 | tf_op jit(solution)/shard_map/all_gather | solution.py:148
  207.9 10.5 %collective-permute-done.40 = f32[3,8,32,32]{3,1,2,0:T(8,128)S(1)} collective-permute-done((f32[3,8,32,32]{3,1,2,0:T(8,128)S(1)}, f32[3,8,32,32]{3,1,2,0:T(8,128)S(1)}, u32[]{:S(2)}, u32[]{:S(2)}) %collective-permute-start.40) | collective-permute-done | bytes 98336 | tf_op jit(solution)/shard_map/ppermute | solution.py:33
  221.1 16.9 %collective-permute-done.41 = f32[3,16,32,32]{3,1,2,0:T(8,128)S(1)} collective-permute-done((f32[3,16,32,32]{3,1,2,0:T(8,128)S(1)}, f32[3,16,32,32]{3,1,2,0:T(8,128)S(1)}, u32[]{:S(2)}, u32[]{:S(2)}) %collective-permute-start.41) | collective-permute-done | bytes 196640 | tf_op jit(solution)/shard_map/ppermute | solution.py:33
  263.0 4.5 %collective-permute-start.47 = (f32[1,1,8,64]{3,2,1,0:T(8,128)S(1)}, f32[1,1,8,64]{3,2,1,0:T(8,128)S(1)}, u32[]{:S(2)}, u32[]{:S(2)}) collective-permute-start(f32[1,1,8,64]{3,2,1,0:T(8,128)S(1)} %get-tuple-element.76), channel_id=1, source_target_pairs={{0,8},{8,16},{16,24},{1,9},{9,17},{17,25},{2,10},{10,18},{18,26},{... | collective-permute-start | bytes 6152 | tf_op jit(solution)/shard_map/ppermute | solution.py:23
  270.4 4.0 %collective-permute-start.51 = (f32[1,18,1,64]{3,2,1,0:T(1,128)S(1)}, f32[1,18,1,64]{3,2,1,0:T(1,128)S(1)}, u32[]{:S(2)}, u32[]{:S(2)}) collective-permute-start(f32[1,18,1,64]{3,2,1,0:T(1,128)S(1)} %get-tuple-element.11), channel_id=1, source_target_pairs={{0,1},{1,0},{2,3},{3,2},{4,5},{5,4},{6,7},{7,6},{8,9},{9,8},{10,11... | collective-permute-start | bytes 13832 | tf_op jit(solution)/shard_map/ppermute | solution.py:33
  275.6 6.6 %broadcast_in_dim.59 = f32[16,2,8,2,64,2]{5,4,3,2,1,0:T(8,128)} broadcast(f32[16,8,64]{2,1,0:T(8,128)S(1)} %fusion.159), dimensions={0,2,4} | broadcast | bytes 294912 | tf_op jit(solution)/shard_map/broadcast_in_dim | solution.py:74
  282.2 12.7 %reshape.65 = f32[32,16,128]{2,1,0:T(8,128)S(1)} reshape(f32[16,2,8,2,64,2]{5,4,3,2,1,0:T(8,128)} %broadcast_in_dim.59) | data formatting | bytes 524288 | tf_op jit(solution)/shard_map/reshape | solution.py:78
  297.0 4.8 %collective-permute-start.52 = (f32[1,1,16,128]{3,2,1,0:T(8,128)S(1)}, f32[1,1,16,128]{3,2,1,0:T(8,128)S(1)}, u32[]{:S(2)}, u32[]{:S(2)}) collective-permute-start(f32[1,1,16,128]{3,2,1,0:T(8,128)S(1)} %get-tuple-element.66), channel_id=1, source_target_pairs={{0,8},{8,16},{16,24},{1,9},{9,17},{17,25},{2,10},{10,18},{18,26},{... | collective-permute-start | bytes 24584 | tf_op jit(solution)/shard_map/ppermute | solution.py:23
  311.2 4.8 %collective-permute-start.57 = (f32[1,1,16,128]{3,2,1,0:T(8,128)S(1)}, f32[1,1,16,128]{3,2,1,0:T(8,128)S(1)}, u32[]{:S(2)}, u32[]{:S(2)}) collective-permute-start(f32[1,1,16,128]{3,2,1,0:T(8,128)S(1)} %get-tuple-element.64), channel_id=1, source_target_pairs={{0,8},{8,16},{16,24},{1,9},{9,17},{17,25},{2,10},{10,18},{18,26},{... | collective-permute-start | bytes 24584 | tf_op jit(solution)/shard_map/ppermute | solution.py:23
  318.7 4.0 %collective-permute-start.61 = (f32[1,34,1,128]{3,2,1,0:T(1,128)S(1)}, f32[1,34,1,128]{3,2,1,0:T(1,128)S(1)}, u32[]{:S(2)}, u32[]{:S(2)}) collective-permute-start(f32[1,34,1,128]{3,2,1,0:T(1,128)S(1)} %get-tuple-element.5), channel_id=1, source_target_pairs={{0,1},{1,0},{2,3},{3,2},{4,5},{5,4},{6,7},{7,6},{8,9},{9,8},{10,11... | collective-permute-start | bytes 52232 | tf_op jit(solution)/shard_map/ppermute | solution.py:33
  (263 shorter events, 129.6 us)
Async XLA Ops:
  0.0 78.8 %collective-permute-start.1 = (f32[1,1,16,128]{3,2,1,0:T(8,128)S(1)}, f32[1,1,16,128]{3,2,1,0:T(8,128)S(1)}, u32[]{:S(2)}, u32[]{:S(2)}) collective-permute-start(f32[1,1,16,128]{3,2,1,0:T(8,128)S(1)} %broadcast.122), channel_id=1, source_target_pairs={{8,0},{16,8},{24,16},{9,1},{17,9},{25,17},{10,2},{18,10},{26,18},{... | collective-permute-start | bytes 24584 | tf_op jit(solution)/shard_map/ppermute | solution.py:25
  2.2 76.9 %collective-permute-start = (f32[1,1,16,128]{3,2,1,0:T(8,128)S(1)}, f32[1,1,16,128]{3,2,1,0:T(8,128)S(1)}, u32[]{:S(2)}, u32[]{:S(2)}) collective-permute-start(f32[1,1,16,128]{3,2,1,0:T(8,128)S(1)} %broadcast.122), channel_id=1, source_target_pairs={{0,8},{8,16},{16,24},{1,9},{9,17},{17,25},{2,10},{10,18},{18,26},{... | collective-permute-start | bytes 24584 | tf_op jit(solution)/shard_map/ppermute | solution.py:23
  6.2 60.5 %collective-permute-start.16 = (f32[1,1,8,64]{3,2,1,0:T(8,128)S(1)}, f32[1,1,8,64]{3,2,1,0:T(8,128)S(1)}, u32[]{:S(2)}, u32[]{:S(2)}) collective-permute-start(f32[1,1,8,64]{3,2,1,0:T(8,128)S(1)} %broadcast.126), channel_id=1, source_target_pairs={{8,0},{16,8},{24,16},{9,1},{17,9},{25,17},{10,2},{18,10},{26,18},{... | collective-permute-start | bytes 6152 | tf_op jit(solution)/shard_map/ppermute | solution.py:25
  8.1 60.5 %collective-permute-start.15 = (f32[1,1,8,64]{3,2,1,0:T(8,128)S(1)}, f32[1,1,8,64]{3,2,1,0:T(8,128)S(1)}, u32[]{:S(2)}, u32[]{:S(2)}) collective-permute-start(f32[1,1,8,64]{3,2,1,0:T(8,128)S(1)} %broadcast.126), channel_id=1, source_target_pairs={{0,8},{8,16},{16,24},{1,9},{9,17},{17,25},{2,10},{10,18},{18,26},{... | collective-permute-start | bytes 6152 | tf_op jit(solution)/shard_map/ppermute | solution.py:23
  13.1 66.2 %collective-permute-start.6 = (f32[1,1,16,128]{3,2,1,0:T(8,128)S(1)}, f32[1,1,16,128]{3,2,1,0:T(8,128)S(1)}, u32[]{:S(2)}, u32[]{:S(2)}) collective-permute-start(f32[1,1,16,128]{3,2,1,0:T(8,128)S(1)} %get-tuple-element.73), channel_id=1, source_target_pairs={{8,0},{16,8},{24,16},{9,1},{17,9},{25,17},{10,2},{18,10},{26,18},{... | collective-permute-start | bytes 24584 | tf_op jit(solution)/shard_map/ppermute | solution.py:25
  68.7 7.7 %collective-permute-start.25 = (f32[1,1,8,64]{3,2,1,0:T(8,128)S(1)}, f32[1,1,8,64]{3,2,1,0:T(8,128)S(1)}, u32[]{:S(2)}, u32[]{:S(2)}) collective-permute-start(f32[1,1,8,64]{3,2,1,0:T(8,128)S(1)} %get-tuple-element.88), channel_id=1, source_target_pairs={{0,8},{8,16},{16,24},{1,9},{9,17},{17,25},{2,10},{10,18},{18,26},{... | collective-permute-start | bytes 6152 | tf_op jit(solution)/shard_map/ppermute | solution.py:23
  73.0 7.6 %collective-permute-start.5 = (f32[1,1,16,128]{3,2,1,0:T(8,128)S(1)}, f32[1,1,16,128]{3,2,1,0:T(8,128)S(1)}, u32[]{:S(2)}, u32[]{:S(2)}) collective-permute-start(f32[1,1,16,128]{3,2,1,0:T(8,128)S(1)} %get-tuple-element.72), channel_id=1, source_target_pairs={{0,8},{8,16},{16,24},{1,9},{9,17},{17,25},{2,10},{10,18},{18,26},{... | collective-permute-start | bytes 24584 | tf_op jit(solution)/shard_map/ppermute | solution.py:23
  76.4 18.5 %collective-permute-start.17 = (f32[1,18,1,64]{3,2,1,0:T(1,128)S(1)}, f32[1,18,1,64]{3,2,1,0:T(1,128)S(1)}, u32[]{:S(2)}, u32[]{:S(2)}) collective-permute-start(f32[1,18,1,64]{3,2,1,0:T(1,128)S(1)} %get-tuple-element.75), channel_id=1, source_target_pairs={{0,4},{1,5},{2,6},{3,7},{4,0},{5,1},{6,2},{7,3},{8,12},{9,13},{10,... | collective-permute-start | bytes 13832 | tf_op jit(solution)/shard_map/ppermute | solution.py:33
  78.8 18.4 %collective-permute-start.18 = (f32[1,18,1,64]{3,2,1,0:T(1,128)S(1)}, f32[1,18,1,64]{3,2,1,0:T(1,128)S(1)}, u32[]{:S(2)}, u32[]{:S(2)}) collective-permute-start(f32[1,18,1,64]{3,2,1,0:T(1,128)S(1)} %broadcast_select_fusion.83), channel_id=1, source_target_pairs={{0,2},{1,3},{2,0},{3,1},{4,6},{5,7},{6,4},{7,5},{8,10},{9,11},{10,... | collective-permute-start | bytes 13832 | tf_op jit(solution)/shard_map/ppermute | solution.py:33
  79.3 7.8 %collective-permute-start.3 = (f32[1,34,1,128]{3,2,1,0:T(1,128)S(1)}, f32[1,34,1,128]{3,2,1,0:T(1,128)S(1)}, u32[]{:S(2)}, u32[]{:S(2)}) collective-permute-start(f32[1,34,1,128]{3,2,1,0:T(1,128)S(1)} %get-tuple-element.112), channel_id=1, source_target_pairs={{0,2},{1,3},{2,0},{3,1},{4,6},{5,7},{6,4},{7,5},{8,10},{9,11},{10,... | collective-permute-start | bytes 52232 | tf_op jit(solution)/shard_map/ppermute | solution.py:33
  80.6 6.6 %collective-permute-start.4 = (f32[1,34,1,128]{3,2,1,0:T(1,128)S(1)}, f32[1,34,1,128]{3,2,1,0:T(1,128)S(1)}, u32[]{:S(2)}, u32[]{:S(2)}) collective-permute-start(f32[1,34,1,128]{3,2,1,0:T(1,128)S(1)} %get-tuple-element.53), channel_id=1, source_target_pairs={{0,1},{1,0},{2,3},{3,2},{4,5},{5,4},{6,7},{7,6},{8,9},{9,8},{10,11... | collective-permute-start | bytes 52232 | tf_op jit(solution)/shard_map/ppermute | solution.py:33
  89.8 9.3 %collective-permute-start.19 = (f32[1,18,1,64]{3,2,1,0:T(1,128)S(1)}, f32[1,18,1,64]{3,2,1,0:T(1,128)S(1)}, u32[]{:S(2)}, u32[]{:S(2)}) collective-permute-start(f32[1,18,1,64]{3,2,1,0:T(1,128)S(1)} %get-tuple-element.74), channel_id=1, source_target_pairs={{0,1},{1,0},{2,3},{3,2},{4,5},{5,4},{6,7},{7,6},{8,9},{9,8},{10,11... | collective-permute-start | bytes 13832 | tf_op jit(solution)/shard_map/ppermute | solution.py:33
  92.0 13.0 %collective-permute-start.27 = (f32[1,18,1,64]{3,2,1,0:T(1,128)S(1)}, f32[1,18,1,64]{3,2,1,0:T(1,128)S(1)}, u32[]{:S(2)}, u32[]{:S(2)}) collective-permute-start(f32[1,18,1,64]{3,2,1,0:T(1,128)S(1)} %get-tuple-element.135), channel_id=1, source_target_pairs={{0,4},{1,5},{2,6},{3,7},{4,0},{5,1},{6,2},{7,3},{8,12},{9,13},{10,... | collective-permute-start | bytes 13832 | tf_op jit(solution)/shard_map/ppermute | solution.py:33
  92.3 14.5 %collective-permute-start.28 = (f32[1,18,1,64]{3,2,1,0:T(1,128)S(1)}, f32[1,18,1,64]{3,2,1,0:T(1,128)S(1)}, u32[]{:S(2)}, u32[]{:S(2)}) collective-permute-start(f32[1,18,1,64]{3,2,1,0:T(1,128)S(1)} %get-tuple-element.134), channel_id=1, source_target_pairs={{0,2},{1,3},{2,0},{3,1},{4,6},{5,7},{6,4},{7,5},{8,10},{9,11},{10,... | collective-permute-start | bytes 13832 | tf_op jit(solution)/shard_map/ppermute | solution.py:33
  94.9 11.9 %collective-permute-start.29 = (f32[1,18,1,64]{3,2,1,0:T(1,128)S(1)}, f32[1,18,1,64]{3,2,1,0:T(1,128)S(1)}, u32[]{:S(2)}, u32[]{:S(2)}) collective-permute-start(f32[1,18,1,64]{3,2,1,0:T(1,128)S(1)} %get-tuple-element.40), channel_id=1, source_target_pairs={{0,1},{1,0},{2,3},{3,2},{4,5},{5,4},{6,7},{7,6},{8,9},{9,8},{10,11... | collective-permute-start | bytes 13832 | tf_op jit(solution)/shard_map/ppermute | solution.py:33
  108.9 6.9 %collective-permute-start.21 = (f32[1,1,16,128]{3,2,1,0:T(8,128)S(1)}, f32[1,1,16,128]{3,2,1,0:T(8,128)S(1)}, u32[]{:S(2)}, u32[]{:S(2)}) collective-permute-start(f32[1,1,16,128]{3,2,1,0:T(8,128)S(1)} %get-tuple-element.69), channel_id=1, source_target_pairs={{8,0},{16,8},{24,16},{9,1},{17,9},{25,17},{10,2},{18,10},{26,18},{... | collective-permute-start | bytes 24584 | tf_op jit(solution)/shard_map/ppermute | solution.py:25
  150.2 6.7 %collective-permute-start.31 = (f32[1,1,8,64]{3,2,1,0:T(8,128)S(1)}, f32[1,1,8,64]{3,2,1,0:T(8,128)S(1)}, u32[]{:S(2)}, u32[]{:S(2)}) collective-permute-start(f32[1,1,8,64]{3,2,1,0:T(8,128)S(1)} %get-tuple-element.87), channel_id=1, source_target_pairs={{8,0},{16,8},{24,16},{9,1},{17,9},{25,17},{10,2},{18,10},{26,18},{... | collective-permute-start | bytes 6152 | tf_op jit(solution)/shard_map/ppermute | solution.py:25
  158.9 8.2 %collective-permute-start.32 = (f32[1,18,1,64]{3,2,1,0:T(1,128)}, f32[1,18,1,64]{3,2,1,0:T(1,128)}, u32[]{:S(2)}, u32[]{:S(2)}) collective-permute-start(f32[1,18,1,64]{3,2,1,0:T(1,128)} %get-tuple-element.133), channel_id=1, source_target_pairs={{0,4},{1,5},{2,6},{3,7},{4,0},{5,1},{6,2},{7,3},{8,12},{9,13},{10,... | collective-permute-start | bytes 13832 | tf_op jit(solution)/shard_map/ppermute | solution.py:33
  159.7 7.4 %collective-permute-start.33 = (f32[1,18,1,64]{3,2,1,0:T(1,128)}, f32[1,18,1,64]{3,2,1,0:T(1,128)}, u32[]{:S(2)}, u32[]{:S(2)}) collective-permute-start(f32[1,18,1,64]{3,2,1,0:T(1,128)} %get-tuple-element.132), channel_id=1, source_target_pairs={{0,2},{1,3},{2,0},{3,1},{4,6},{5,7},{6,4},{7,5},{8,10},{9,11},{10,... | collective-permute-start | bytes 13832 | tf_op jit(solution)/shard_map/ppermute | solution.py:33
  170.1 7.3 %collective-permute-start.36 = (f32[1,1,8,64]{3,2,1,0:T(8,128)S(1)}, f32[1,1,8,64]{3,2,1,0:T(8,128)S(1)}, u32[]{:S(2)}, u32[]{:S(2)}) collective-permute-start(f32[1,1,8,64]{3,2,1,0:T(8,128)S(1)} %get-tuple-element.83), channel_id=1, source_target_pairs={{8,0},{16,8},{24,16},{9,1},{17,9},{25,17},{10,2},{18,10},{26,18},{... | collective-permute-start | bytes 6152 | tf_op jit(solution)/shard_map/ppermute | solution.py:25
  207.8 10.6 %collective-permute-start.40 = (f32[3,8,32,32]{3,1,2,0:T(8,128)S(1)}, f32[3,8,32,32]{3,1,2,0:T(8,128)S(1)}, u32[]{:S(2)}, u32[]{:S(2)}) collective-permute-start(f32[3,8,32,32]{3,1,2,0:T(8,128)S(1)} %bitcast.131), channel_id=1, source_target_pairs={{0,8},{8,0},{16,24},{24,16},{1,9},{9,1},{17,25},{25,17},{2,10},{10... | collective-permute-start | bytes 294920 | tf_op jit(solution)/shard_map/ppermute | solution.py:33
  218.5 19.6 %collective-permute-start.41 = (f32[3,16,32,32]{3,1,2,0:T(8,128)S(1)}, f32[3,16,32,32]{3,1,2,0:T(8,128)S(1)}, u32[]{:S(2)}, u32[]{:S(2)}) collective-permute-start(f32[3,16,32,32]{3,1,2,0:T(8,128)S(1)} %maximum_select_fusion.1), channel_id=1, source_target_pairs={{0,16},{8,24},{16,0},{24,8},{1,17},{9,25},{17,1},{25,9},{2,18},{10... | collective-permute-start | bytes 589832 | tf_op jit(solution)/shard_map/ppermute | solution.py:33
  295.0 6.9 %collective-permute-start.53 = (f32[1,1,16,128]{3,2,1,0:T(8,128)S(1)}, f32[1,1,16,128]{3,2,1,0:T(8,128)S(1)}, u32[]{:S(2)}, u32[]{:S(2)}) collective-permute-start(f32[1,1,16,128]{3,2,1,0:T(8,128)S(1)} %get-tuple-element.67), channel_id=1, source_target_pairs={{8,0},{16,8},{24,16},{9,1},{17,9},{25,17},{10,2},{18,10},{26,18},{... | collective-permute-start | bytes 24584 | tf_op jit(solution)/shard_map/ppermute | solution.py:25
  309.3 6.8 %collective-permute-start.58 = (f32[1,1,16,128]{3,2,1,0:T(8,128)S(1)}, f32[1,1,16,128]{3,2,1,0:T(8,128)S(1)}, u32[]{:S(2)}, u32[]{:S(2)}) collective-permute-start(f32[1,1,16,128]{3,2,1,0:T(8,128)S(1)} %get-tuple-element.65), channel_id=1, source_target_pairs={{8,0},{16,8},{24,16},{9,1},{17,9},{25,17},{10,2},{18,10},{26,18},{... | collective-permute-start | bytes 24584 | tf_op jit(solution)/shard_map/ppermute | solution.py:25
  (65 other events, 714.8 us)
where the time goes:
time: 330 us; the launch traced here: 325 us
  starting transfers between devices  138 us (42%)
  local copies, waits for them, and re-layouts  87.7 us (27%)
  other arithmetic  46.3 us (14%)
  waiting for transfers between devices  37.8 us (11%)
  blocking collectives  14.2 us (4%)
    ppermute x38, starting transfers between devices, swapped(): lax.ppermute(array, axis, [(i, i ^ 1 << apart) for i in range(lax.axis_si...  61.7 us
    ppermute x12, starting transfers between devices, extended_2(): lax.ppermute(tail, axis, [(i, (i + 1) % count) for i in range(ends)])  52.4 us
    another operation x2, local copies, waits for them, and re-layouts, restrict(): values.reshape(values.shape[0] // 2, 2, values.shape[1] // 2, 2, values.s...  37 us
    ppermute x38, waiting for transfers between devices, swapped(): lax.ppermute(array, axis, [(i, i ^ 1 << apart) for i in range(lax.axis_si...  32.6 us
    ppermute x12, starting transfers between devices, extended_2(): lax.ppermute(head, axis, [((i + 1) % count, i) for i in range(ends)])  24 us
    reduce_sum x6, other arithmetic, restrict(): return jnp.sum(shaped, axis=(1, 3, 5)) * 0.125  22.4 us
    reshape x2, local copies, waits for them, and re-layouts, restrict(): values.reshape(values.shape[0] // 2, 2, values.shape[1] // 2, 2, values.s...  21.1 us
    reshape x2, local copies, waits for them, and re-layouts, prolong(): wide.reshape(2 * coarse.shape[0], 2 * coarse.shape[1], 2 * coarse.shape[2])  14.9 us
  transfers between devices with their start and end apart: 62, of which 16 were waited for; matrix products, arithmetic and copies ran while one was open for 18% of the time, Pallas kernels for 0%

commit v1 on v0

v1 whole, which is shorter than its diff:
```python
import functools

import jax
import jax.numpy as jnp
from jax import lax
from jax.experimental import pallas as pl
from jax.experimental.pallas import tpu as pltpu
from jax.sharding import PartitionSpec as P

OMEGA = 0.7
FRAME = 8
WIDE_F = 6
WIDE_B = 7
COARSE_X = 6
FINE_X = 3
LANES = 128
ANY = pl.BlockSpec(memory_space=pl.ANY)
VMEM = pl.BlockSpec(memory_space=pltpu.VMEM)
LIMIT = 56 * 1024 * 1024


def params():
    return pltpu.CompilerParams(vmem_limit_bytes=LIMIT)


def gray_position(code, bit_count):
    position = code
    for shift in range(1, bit_count):
        position = position ^ (code >> shift)
    return position


def box_parity():
    bit_count = lax.axis_size("box").bit_length() - 1
    return gray_position(lax.axis_index("box"), bit_count) & 1


def run_copies(pairs, sems):
    copies = [pltpu.make_async_copy(src, dst, sems.at[at]) for at, (src, dst) in enumerate(pairs)]
    for copy in copies:
        copy.start()
    return copies


def wait_copies(copies):
    for copy in copies:
        copy.wait()


def lane_ids(shape):
    return lax.broadcasted_iota(jnp.int32, shape, 1)


def y_next(row):
    return pltpu.roll(row, row.shape[0] - 1, 0)


def y_prev(row):
    return pltpu.roll(row, 1, 0)


def z_next(row, dist):
    return pltpu.roll(row, LANES - dist, 1)


def z_prev(row, dist):
    return pltpu.roll(row, dist, 1)


def coefficients(alpha, beta, beta_prev, beta_next, dist, scale):
    half = 0.5 * scale
    lane = lane_ids(beta.shape)
    inside = lane < LANES - dist
    up_z = jnp.where(inside, z_next(beta, dist), 0.0)
    down_z = jnp.where(lane >= dist, z_prev(beta, dist), 0.0)
    up_y = y_next(beta)
    face_x = half * (beta + beta_next)
    face_y = half * (beta + up_y)
    face_z = jnp.where(inside, half * (beta + up_z), 0.0)
    total = (beta_prev + beta_next) + (up_y + y_prev(beta)) + (up_z + down_z)
    diagonal = alpha + half * (6.0 * beta + total)
    inverse = jnp.where(alpha > 0.0, OMEGA / diagonal, 0.0)
    return face_x, face_y, face_z, diagonal, inverse


def off_sum(at, v, faces, dist):
    face_x, face_y, face_z = faces
    here = v[at]
    fy = face_y[at]
    fz = face_z[at]
    along_x = face_x[at] * v[at + 1] + face_x[at - 1] * v[at - 1]
    along_y = fy * y_next(here) + y_prev(fy * here)
    along_z = fz * z_next(here, dist) + z_prev(fz * here, dist)
    return here, along_x + along_y + along_z


def relaxed(at, v, f, inverse, faces, dist):
    here, off = off_sum(at, v, faces, dist)
    return (1.0 - OMEGA) * here + inverse[at] * (f[at] + off)


def rows_loop(low, high, step, fn):
    trips = (high - low) // step

    def trip(t, carry):
        base = low + t * step
        for k in range(step):
            fn(base + k)
        return carry

    lax.fori_loop(0, trips, trip, 0)
    for row in range(low + trips * step, high):
        fn(row)


def pair_sum_z(row, dist):
    lane = lane_ids(row.shape)
    first = (lane // dist) % 2 == 0
    return row + jnp.where(first, z_next(row, dist), z_prev(row, dist))


def strided_pair(ref, at, count):
    return ref[at, pl.ds(0, count, stride=2), :] + ref[at, pl.ds(1, count, stride=2), :]


def pack_x_kernel(f, a, b, up, down, sems):
    count = f.shape[0]
    pairs = []
    row = 0
    for ref, wide in ((f, WIDE_F), (a, WIDE_F), (b, WIDE_B)):
        pairs.append((ref.at[pl.ds(count - wide, wide)], up.at[pl.ds(row, wide)]))
        pairs.append((ref.at[pl.ds(0, wide)], down.at[pl.ds(row, wide)]))
        row += wide
    wait_copies(run_copies(pairs, sems))


def pack_y_kernel(f, a, b, low, high, to_even, to_odd, sems):
    count = f.shape[0]
    parity = box_parity()
    pairs = []
    for out, start in ((to_even, FRAME * (1 - parity)), (to_odd, FRAME * parity)):
        rows = pl.ds(pl.multiple_of(start, FRAME), FRAME)
        row = 0
        got = 0
        for ref, wide in ((f, WIDE_F), (a, WIDE_F), (b, WIDE_B)):
            pairs.append((low.at[pl.ds(got, wide), rows], out.at[pl.ds(row, wide)]))
            pairs.append((ref.at[:, rows], out.at[pl.ds(row + wide, count)]))
            pairs.append((high.at[pl.ds(got, wide), rows], out.at[pl.ds(row + wide + count, wide)]))
            row += count + 2 * wide
            got += wide
    wait_copies(run_copies(pairs, sems))


def down_kernel(
    f, a, b, low, high, from_even, from_odd,
    out_v, out_f, out_inv, out_fx, out_fy, out_fz,
    out_v1, out_f1, out_inv1, out_fx1, out_fy1, out_fz1,
    out_coarse, to_up, to_down,
    F, A, B, FX, FY, FZ, DG, IN, V, U,
    T, A1, B1, D1, W1, T1, T2, sems, out_sems,
):
    count = f.shape[0]
    depth = f.shape[1]
    parity = box_parity()
    own_y = pl.ds(FRAME, depth)
    even_y = pl.ds(pl.multiple_of((FRAME + depth) * (1 - parity), FRAME), FRAME)
    odd_y = pl.ds(pl.multiple_of((FRAME + depth) * parity, FRAME), FRAME)
    pairs = []
    row = 0
    got = 0
    for ref, wide, dst in ((f, WIDE_F, F), (a, WIDE_F, A), (b, WIDE_B, B)):
        span = count + 2 * wide
        pairs.append((ref, dst.at[pl.ds(FRAME, count), own_y]))
        pairs.append((low.at[pl.ds(got, wide)], dst.at[pl.ds(FRAME - wide, wide), own_y]))
        pairs.append((high.at[pl.ds(got, wide)], dst.at[pl.ds(FRAME + count, wide), own_y]))
        for src, rows in ((from_even, even_y), (from_odd, odd_y)):
            pairs.append((src.at[pl.ds(row, span)], dst.at[pl.ds(FRAME - wide, span), rows]))
        row += span
        got += wide
    wait_copies(run_copies(pairs, sems))

    faces = (FX, FY, FZ)
    end = count + 2 * FRAME

    FX[1] = 0.5 * (B[1] + B[2])

    def coef_row(i):
        fx, fy, fz, dg, inv = coefficients(A[i], B[i], B[i - 1], B[i + 1], 1, 1.0)
        FX[i] = fx
        FY[i] = fy
        FZ[i] = fz
        DG[i] = dg
        IN[i] = inv
        V[i] = inv * F[i]

    rows_loop(2, end - 2, 2, coef_row)

    kept = pl.ds(FRAME - 2, count + 4)
    outs = [(F, out_f), (IN, out_inv), (FX, out_fx), (FY, out_fy), (FZ, out_fz)]
    out_copies = run_copies([(src.at[kept], dst) for src, dst in outs], out_sems)

    def sweep_row(i):
        U[i] = relaxed(i, V, F, IN, faces, 1)

    rows_loop(3, end - 3, 2, sweep_row)
    last = pltpu.make_async_copy(U.at[kept], out_v, out_sems.at[5])
    last.start()
    out_copies.append(last)

    def residual(i):
        here, off = off_sum(i, U, faces, 1)
        return F[i] - DG[i] * here + off

    half_rows = (depth + 2 * FRAME) // 2

    def restrict_row(j):
        T[j] = residual(2 * j) + residual(2 * j + 1)

    rows_loop(2, end // 2 - 2, 1, restrict_row)

    def level1_source(j):
        out_f1[j] = 0.125 * pair_sum_z(strided_pair(T, j, half_rows), 1)

    rows_loop(2, end // 2 - 2, 2, level1_source)

    def level1_coef(j):
        for src, dst in ((A, A1), (B, B1)):
            both = strided_pair(src, 2 * j, half_rows) + strided_pair(src, 2 * j + 1, half_rows)
            dst[j] = 0.125 * pair_sum_z(both, 1)

    rows_loop(1, end // 2 - 1, 2, level1_coef)

    faces1 = (out_fx1, out_fy1, out_fz1)
    end1 = end // 2
    out_fx1[1] = 0.125 * (B1[1] + B1[2])

    def coef_row1(i):
        fx, fy, fz, dg, inv = coefficients(A1[i], B1[i], B1[i - 1], B1[i + 1], 2, 0.25)
        out_fx1[i] = fx
        out_fy1[i] = fy
        out_fz1[i] = fz
        D1[i] = dg
        out_inv1[i] = inv
        W1[i] = inv * out_f1[i]

    rows_loop(2, end1 - 2, 4, coef_row1)

    def sweep_row1(i):
        out_v1[i] = relaxed(i, W1, out_f1, out_inv1, faces1, 2)

    rows_loop(3, end1 - 3, 3, sweep_row1)

    def residual1(i):
        here, off = off_sum(i, out_v1, faces1, 2)
        return out_f1[i] - D1[i] * here + off

    first1 = FRAME // 2
    count1 = count // 2
    count2 = count // 4
    quarter_rows = half_rows // 2
    lane = lane_ids((1, LANES))

    def coarse_row(x):
        i = first1 + 2 * x
        T1[0, x] = residual1(i) + residual1(i + 1)
        T1[1, x] = A1[i] + A1[i + 1]
        T1[2, x] = B1[i] + B1[i + 1]

    rows_loop(0, count2, 1, coarse_row)
    own2 = FRAME // 4
    depth2 = depth // 4

    def coarse_pack(x):
        for k in range(3):
            both = T1[k, x, pl.ds(0, quarter_rows, stride=2), :] + T1[k, x, pl.ds(1, quarter_rows, stride=2), :]
            value = 0.125 * pair_sum_z(both, 2)
            packed = jnp.zeros((1, LANES), jnp.float32)
            for y in range(depth2):
                packed = packed + jnp.where(lane % depth2 == y, value[own2 + y:own2 + y + 1], 0.0)
            out_coarse[x, k:k + 1] = packed

    rows_loop(0, count2, 1, coarse_pack)

    own1 = slice(first1, first1 + depth // 2)
    for k in range(COARSE_X):
        to_up[k, 0:3] = out_coarse[count2 - COARSE_X + k, 0:3]
        to_down[k, 0:3] = out_coarse[k, 0:3]
    for k in range(FINE_X):
        to_up[COARSE_X + k] = out_v1[first1 + count1 - FINE_X + k, own1]
        to_down[COARSE_X + k] = out_v1[first1 + k, own1]
    wait_copies(out_copies)


def pack_coarse_kernel(coarse, v1, low, high, to_even, to_odd):
    parity = box_parity()
    count2 = coarse.shape[0]
    first1 = FRAME // 2
    depth1 = 8
    count1 = 2 * count2
    for out, top in ((to_even, parity == 0), (to_odd, parity == 1)):
        for k in range(COARSE_X):
            out[k, 0:3] = low[k, 0:3]
            out[COARSE_X + count2 + k, 0:3] = high[k, 0:3]
        for k in range(count2):
            out[COARSE_X + k, 0:3] = coarse[k, 0:3]

        def facing(tile):
            return jnp.where(top, tile[depth1 - FINE_X:], tile[:FINE_X])

        for k in range(FINE_X):
            out[k, 3:3 + FINE_X] = facing(low[COARSE_X + k])
            out[FINE_X + count1 + k, 3:3 + FINE_X] = facing(high[COARSE_X + k])
        for k in range(count1):
            out[FINE_X + k, 3:3 + FINE_X] = facing(v1[first1 + k, first1:first1 + depth1])


def up_kernel(
    own, near_even, near_odd, far_even, far_odd, low, high,
    in_v, in_f, in_inv, in_fx, in_fy, in_fz,
    in_v1, in_f1, in_inv1, in_fx1, in_fy1, in_fz1,
    out,
    V, F, IN, FX, FY, FZ, U,
    V1, F1, IN1, FX1, FY1, FZ1, U1,
    R, S2, A2, B2, FX2, FY2, FZ2, IN2, V2, U2, PT, P0,
    sems, state_sems,
):
    parity = box_parity()
    below = 1 + 2 * (1 - parity)
    copies = run_copies(
        [
            (own, R.at[2]),
            (near_even, R.at[below]),
            (near_odd, R.at[4 - below]),
            (far_even, R.at[4 * (1 - parity)]),
            (far_odd, R.at[4 * parity]),
        ],
        sems,
    )
    states = run_copies(
        [
            (in_v1, V1), (in_f1, F1), (in_inv1, IN1), (in_fx1, FX1), (in_fy1, FY1), (in_fz1, FZ1),
            (in_v, V), (in_f, F), (in_inv, IN), (in_fx, FX), (in_fy, FY), (in_fz, FZ),
        ],
        state_sems,
    )
    wait_copies(copies)

    rows2 = B2.shape[1]
    span2 = B2.shape[0]
    sub = lax.broadcasted_iota(jnp.int32, (rows2, LANES), 0)
    lane = lane_ids((rows2, LANES))
    block = (sub + 2) // 4
    mine = lane % 4 == (sub + 2) % 4
    last_of_four = lane % 4 == 3

    def unpack_row(x):
        for k, dst in enumerate((S2, A2, B2)):
            packed = jnp.broadcast_to(R[0, x, k:k + 1], (rows2, LANES))
            for slot in range(1, 5):
                packed = jnp.where(block == slot, jnp.broadcast_to(R[slot, x, k:k + 1], (rows2, LANES)), packed)
            t = jnp.where(mine, packed, 0.0)
            t = t + z_prev(t, 1)
            t = t + z_prev(t, 2)
            t = jnp.where(last_of_four, t, 0.0)
            t = t + z_next(t, 1)
            dst[x] = t + z_next(t, 2)

    rows_loop(0, span2, 2, unpack_row)
    FX2[0] = 0.5 * 0.0625 * (B2[0] + B2[1])

    def coef_row2(i):
        fx, fy, fz, dg, inv = coefficients(A2[i], B2[i], B2[i - 1], B2[i + 1], 4, 0.0625)
        FX2[i] = fx
        FY2[i] = fy
        FZ2[i] = fz
        IN2[i] = inv
        V2[i] = inv * S2[i]

    rows_loop(1, span2 - 1, 2, coef_row2)
    faces2 = (FX2, FY2, FZ2)
    src, dst = V2, U2
    for sweep in range(1, 4):

        def sweep_row2(i, src=src, dst=dst):
            dst[i] = relaxed(i, src, S2, IN2, faces2, 4)

        rows_loop(1 + sweep, span2 - 1 - sweep, 2, sweep_row2)
        src, dst = dst, src
    coarse = src

    first1 = FRAME // 2
    depth1 = 8
    span1 = V1.shape[0]
    own_rows = pl.ds(first1, depth1)
    wait_copies(states[:6])
    for k in range(FINE_X):
        V1[first1 - FINE_X + k, own_rows] = low[COARSE_X + k]
        V1[span1 - first1 + k, own_rows] = high[COARSE_X + k]

    def add_coarse(x):
        half = coarse[x + COARSE_X - first1 // 2, first1:first1 + depth1]
        PT[x, pl.ds(0, depth1, stride=2), :] = half
        PT[x, pl.ds(1, depth1, stride=2), :] = half

    rows_loop(0, span1 // 2, 2, add_coarse)

    def rim_row(x):
        i = x + first1 - FINE_X
        V1[i, first1 - FINE_X:first1] = R[1, x, 3:3 + FINE_X]
        V1[i, first1 + depth1:first1 + depth1 + FINE_X] = R[3, x, 3:3 + FINE_X]

    rows_loop(0, span1 - 2 * (first1 - FINE_X), 2, rim_row)

    def corrected_row(x):
        add = PT[x]
        V1[2 * x] = V1[2 * x] + add
        V1[2 * x + 1] = V1[2 * x + 1] + add

    rows_loop(0, span1 // 2, 2, corrected_row)
    faces1 = (FX1, FY1, FZ1)

    def sweep_a1(i):
        U1[i] = relaxed(i, V1, F1, IN1, faces1, 2)

    rows_loop(2, span1 - 2, 4, sweep_a1)

    def sweep_b1(i):
        V1[i] = relaxed(i, U1, F1, IN1, faces1, 2)

    rows_loop(3, span1 - 3, 3, sweep_b1)

    span = V.shape[0]
    rows1 = V1.shape[1]
    wait_copies(states[6:])

    def widen(x):
        row = V1[x + first1 - 1]
        P0[x, pl.ds(0, rows1, stride=2), :] = row
        P0[x, pl.ds(1, rows1, stride=2), :] = row

    rows_loop(0, span // 2, 2, widen)

    def corrected0(x):
        add = P0[x]
        V[2 * x] = V[2 * x] + add
        V[2 * x + 1] = V[2 * x + 1] + add

    rows_loop(0, span // 2, 2, corrected0)
    faces = (FX, FY, FZ)

    def sweep_a(i):
        U[i] = relaxed(i, V, F, IN, faces, 1)

    rows_loop(1, span - 1, 2, sweep_a)
    depth = out.shape[1]

    def sweep_b(i):
        out[i - 2] = relaxed(i, U, F, IN, faces, 1)[FRAME:FRAME + depth]

    rows_loop(2, span - 2, 2, sweep_b)


def body(source, alpha, beta):
    f = source[:, 0]
    a = alpha[:, 0]
    b = beta[:, 0]
    count, depth, lanes = f.shape
    groups = lax.axis_size("grp")
    blocks = lax.axis_size("box")
    code = [p ^ (p >> 1) for p in range(blocks)]
    up_perm = [(i, i + 1) for i in range(groups - 1)]
    down_perm = [(i + 1, i) for i in range(groups - 1)]
    even_perm = [(code[p], code[p ^ 1]) for p in range(blocks)]
    odd_perm = [(code[p], code[((p - 1) ^ 1) + 1]) for p in range(1, blocks - 1)]

    def arr(*shape):
        return jax.ShapeDtypeStruct(shape, jnp.float32)

    def vm(*shape):
        return pltpu.VMEM(shape, jnp.float32)

    dma = pltpu.SemaphoreType.DMA
    x_rows = 2 * WIDE_F + WIDE_B
    up, down = pl.pallas_call(
        pack_x_kernel,
        out_shape=[arr(x_rows, depth, lanes)] * 2,
        in_specs=[ANY] * 3,
        out_specs=[ANY] * 2,
        scratch_shapes=[dma((6,))],
        compiler_params=params(),
    )(f, a, b)
    low = lax.ppermute(up, "grp", up_perm)
    high = lax.ppermute(down, "grp", down_perm)

    y_rows = 3 * count + 2 * x_rows
    to_even, to_odd = pl.pallas_call(
        pack_y_kernel,
        out_shape=[arr(y_rows, FRAME, lanes)] * 2,
        in_specs=[ANY] * 5,
        out_specs=[ANY] * 2,
        scratch_shapes=[dma((18,))],
        compiler_params=params(),
    )(f, a, b, low, high)
    from_even = lax.ppermute(to_even, "box", even_perm)
    from_odd = lax.ppermute(to_odd, "box", odd_perm)

    framed = (count + 2 * FRAME, depth + 2 * FRAME, lanes)
    framed1 = (framed[0] // 2, framed[1] // 2, lanes)
    kept = (count + 4, framed[1], lanes)
    count2 = count // 4
    x2_tiles = COARSE_X + FINE_X
    results = pl.pallas_call(
        down_kernel,
        out_shape=[arr(*kept)] * 6 + [arr(*framed1)] * 6
        + [arr(count2, 8, lanes)] + [arr(x2_tiles, 8, lanes)] * 2,
        in_specs=[ANY] * 7,
        out_specs=[ANY] * 6 + [VMEM] * 9,
        scratch_shapes=[vm(*framed)] * 10
        + [vm(framed1[0], framed[1], lanes)] + [vm(*framed1)] * 4
        + [vm(3, count2, framed1[1], lanes), vm(8, 128), dma((15,)), dma((6,))],
        compiler_params=params(),
    )(f, a, b, low, high, from_even, from_odd)
    state0 = results[:6]
    state1 = results[6:12]
    coarse, to_up, to_down = results[12:]

    low2 = lax.ppermute(to_up, "grp", up_perm)
    high2 = lax.ppermute(to_down, "grp", down_perm)
    span = framed1[0] - 2 * (FRAME // 2 - FINE_X)
    even2, odd2 = pl.pallas_call(
        pack_coarse_kernel,
        out_shape=[arr(span, 8, lanes)] * 2,
        in_specs=[VMEM] * 4,
        out_specs=[VMEM] * 2,
        compiler_params=params(),
    )(coarse, state1[0], low2, high2)
    near_even = lax.ppermute(even2, "box", even_perm)
    near_odd = lax.ppermute(odd2, "box", odd_perm)
    far_odd = lax.ppermute(near_even, "box", odd_perm)
    far_even = lax.ppermute(near_odd, "box", even_perm)

    framed2 = (count2 + 2 * COARSE_X, depth // 4 + 2 * COARSE_X, lanes)
    out = pl.pallas_call(
        up_kernel,
        out_shape=arr(count, depth, lanes),
        in_specs=[ANY] * 5 + [VMEM] * 2 + [ANY] * 12,
        out_specs=VMEM,
        scratch_shapes=[vm(*kept)] * 7 + [vm(*framed1)] * 7
        + [vm(5, span, 8, lanes)] + [vm(*framed2)] * 9
        + [vm(framed1[0] // 2, framed1[1], lanes), vm(kept[0] // 2, kept[1], lanes)]
        + [dma((5,)), dma((12,))],
        compiler_params=params(),
    )(even2, near_even, near_odd, far_even, far_odd, low2, high2, *state0, *state1)
    return out[:, None]


def solution(mesh):
    spec = P("grp", "box", None, None)
    return jax.shard_map(body, mesh=mesh, in_specs=(spec,) * 3, out_specs=spec, check_vma=False)
```

time: 330 us -> 131 us (0.40)
  starting transfers between devices: 138 us -> 32.4 us
  local copies, waits for them, and re-layouts: 87.7 us -> 2.7 us
  Pallas kernels: 0 us -> 73.1 us
  other arithmetic: 46.3 us -> 0 us
  waiting for transfers between devices: 37.8 us -> 20.3 us
  blocking collectives: 14.2 us -> 0 us
    ppermute x62 -> x10, starting transfers between devices: 138 us -> 32.4 us  [the longest x1 8.78 us: body(): near_even = lax.ppermute(even2, 'box', even_perm)]
    pallas_call x0 -> x5, Pallas kernels: none -> 73.1 us  [the longest x1 34.5 us: body(): pl.pallas_call(pack_y_kernel, out_shape=[arr(y_rows, FRAME, lanes)] * 2,...]
    another operation x7 -> x0, local copies, waits for them, and re-layouts: 37 us -> none  [the longest x2 37 us: restrict(): values.reshape(values.shape[0] // 2, 2, values.shape[1] // 2, 2, values.s...]
    reshape x4 -> x0, local copies, waits for them, and re-layouts: 36.1 us -> none  [the longest x2 21.1 us: restrict(): values.reshape(values.shape[0] // 2, 2, values.shape[1] // 2, 2, values.s...]
    reduce_sum x6 -> x0, other arithmetic: 22.4 us -> none  [restrict(): return jnp.sum(shaped, axis=(1, 3, 5)) * 0.125]
    ppermute x62 -> x10, waiting for transfers between devices: 37.8 us -> 20.3 us  [the longest x1 8.59 us: body(): from_odd = lax.ppermute(to_odd, 'box', odd_perm)]
    all_gather x1 -> x0, blocking collectives: 14.2 us -> none  [body(): lax.all_gather(jnp.stack((source2, alpha2, beta2))[None], 'box', axis=0,...]
    broadcast_in_dim x3 -> x0, local copies, waits for them, and re-layouts: 6.93 us -> none  [the longest x2 6.88 us: prolong(): jnp.broadcast_to(coarse[:, None, :, None, :, None], (coarse.shape[0], 2,...]
  transfers between devices with their start and end apart: 62 -> 10, of which waited for: 16 -> 5; matrix products, arithmetic and copies ran while one was open for 18% -> 0% of each run, Pallas kernels for 0% -> 0%
where the time goes in v1:
time: 131 us; the launch traced here: 129 us
  Pallas kernels  73.1 us (56%)
  starting transfers between devices  32.4 us (25%)
  waiting for transfers between devices  20.3 us (15%)
  local copies, waits for them, and re-layouts  2.7 us (2%)
    pallas_call x1, Pallas kernels, body(): pl.pallas_call(pack_y_kernel, out_shape=[arr(y_rows, FRAME, lanes)] * 2,...  34.5 us
    pallas_call x1, Pallas kernels, body(): pl.pallas_call(up_kernel, out_shape=arr(count, depth, lanes), in_specs=[A...  13.6 us
    pallas_call x1, Pallas kernels, body(): pl.pallas_call(down_kernel, out_shape=[arr(*kept)] * 6 + [arr(*framed1)]...  12.8 us
    pallas_call x1, Pallas kernels, body(): pl.pallas_call(pack_x_kernel, out_shape=[arr(x_rows, depth, lanes)] * 2,...  10.6 us
    ppermute x1, starting transfers between devices, body(): near_even = lax.ppermute(even2, 'box', even_perm)  8.78 us
    ppermute x1, waiting for transfers between devices, body(): from_odd = lax.ppermute(to_odd, 'box', odd_perm)  8.59 us
    ppermute x1, starting transfers between devices, body(): far_even = lax.ppermute(near_odd, 'box', even_perm)  5.54 us
    ppermute x1, waiting for transfers between devices, body(): high = lax.ppermute(down, 'grp', down_perm)  4.23 us
  transfers between devices with their start and end apart: 10, of which 5 were waited for; matrix products, arithmetic and copies ran while one was open for 0% of the time, Pallas kernels for 0%

profile of v1, /device:TPU:11, one launch (start us, length us, event | category | flops | bytes accessed | tf_op | source)
XLA Modules:
  0.0 128.7 jit_solution(9571355589874125306)
XLA Ops:
  0.0 10.6 %shard_map.37 = (f32[19,16,128]{2,1,0:T(8,128)}, f32[19,16,128]{2,1,0:T(8,128)}) custom-call(f32[32,16,128]{2,1,0:T(8,128)} %bitcast.6, f32[32,16,128]{2,1,0:T(8,128)} %bitcast.9, f32[32,16,128]{2,1,0:T(8,128)} %bitcast.12), custom_call_target="tpu_custom_call" | custom-call | tf_op jit(solution)/shard_map/pallas_call | solution.py:484
  10.6 3.1 %collective-permute-start = (f32[19,16,128]{2,1,0:T(8,128)}, f32[19,16,128]{2,1,0:T(8,128)S(1)}, u32[]{:S(2)}, u32[]{:S(2)}) collective-permute-start(f32[19,16,128]{2,1,0:T(8,128)} %get-tuple-element.26), channel_id=1, source_target_pairs={{0,8},{8,16},{16,24},{1,9},{9,17},{17,25},{2,10},{10,18},{18,26},{... | collective-permute-start | bytes 466952 | tf_op jit(solution)/shard_map/ppermute | solution.py:492
  13.7 2.2 %collective-permute-start.1 = (f32[19,16,128]{2,1,0:T(8,128)}, f32[19,16,128]{2,1,0:T(8,128)S(1)}, u32[]{:S(2)}, u32[]{:S(2)}) collective-permute-start(f32[19,16,128]{2,1,0:T(8,128)} %get-tuple-element.27), channel_id=1, source_target_pairs={{8,0},{16,8},{24,16},{9,1},{17,9},{25,17},{10,2},{18,10},{26,18},{... | collective-permute-start | bytes 466952 | tf_op jit(solution)/shard_map/ppermute | solution.py:493
  15.9 1.7 %collective-permute-done.low = f32[19,16,128]{2,1,0:T(8,128)S(1)} collective-permute-done((f32[19,16,128]{2,1,0:T(8,128)}, f32[19,16,128]{2,1,0:T(8,128)S(1)}, u32[]{:S(2)}, u32[]{:S(2)}) %collective-permute-start) | collective-permute-done | bytes 155680 | tf_op jit(solution)/shard_map/ppermute | solution.py:492
  17.6 4.2 %collective-permute-done.1.high = f32[19,16,128]{2,1,0:T(8,128)S(1)} collective-permute-done((f32[19,16,128]{2,1,0:T(8,128)}, f32[19,16,128]{2,1,0:T(8,128)S(1)}, u32[]{:S(2)}, u32[]{:S(2)}) %collective-permute-start.1) | collective-permute-done | bytes 155680 | tf_op jit(solution)/shard_map/ppermute | solution.py:493
  21.8 0.7 copy-done.1
  22.5 34.5 %shard_map.38 = (f32[134,8,128]{2,1,0:T(8,128)}, f32[134,8,128]{2,1,0:T(8,128)}) custom-call(f32[32,16,128]{2,1,0:T(8,128)} %bitcast.7, f32[32,16,128]{2,1,0:T(8,128)} %bitcast.10, f32[32,16,128]{2,1,0:T(8,128)} %bitcast.13, f32[19,16,128]{2,1,0:T(8,128)} %copy-done, f32[19,16,128]{2,1,0:T(8,128)} %copy-done.1), custom_call_target="tpu_custom_call" | custom-call | tf_op jit(solution)/shard_map/pallas_call | solution.py:496
  57.0 1.7 %collective-permute-start.2 = (f32[134,8,128]{2,1,0:T(8,128)}, f32[134,8,128]{2,1,0:T(8,128)S(1)}, u32[]{:S(2)}, u32[]{:S(2)}) collective-permute-start(f32[134,8,128]{2,1,0:T(8,128)} %get-tuple-element.28), channel_id=1, source_target_pairs={{0,1},{1,0},{3,2},{2,3},{6,7},{7,6},{5,4},{4,5},{8,9},{9,8},{11,10... | collective-permute-start | bytes 1646600 | tf_op jit(solution)/shard_map/ppermute | solution.py:504
  58.7 2.1 %collective-permute-start.3 = (f32[134,8,128]{2,1,0:T(8,128)}, f32[134,8,128]{2,1,0:T(8,128)S(1)}, u32[]{:S(2)}, u32[]{:S(2)}) collective-permute-start(f32[134,8,128]{2,1,0:T(8,128)} %get-tuple-element.29), channel_id=1, source_target_pairs={{1,3},{3,1},{2,6},{6,2},{7,5},{5,7},{9,11},{11,9},{10,14},{14,10},... | collective-permute-start | bytes 1646600 | tf_op jit(solution)/shard_map/ppermute | solution.py:505
  60.8 8.6 %collective-permute-done.3.from_odd = f32[134,8,128]{2,1,0:T(8,128)S(1)} collective-permute-done((f32[134,8,128]{2,1,0:T(8,128)}, f32[134,8,128]{2,1,0:T(8,128)S(1)}, u32[]{:S(2)}, u32[]{:S(2)}) %collective-permute-start.3) | collective-permute-done | bytes 548896 | tf_op jit(solution)/shard_map/ppermute | solution.py:505
  69.4 0.8 copy-done.3
  70.2 12.8 %shard_map.39 = (f32[36,32,128]{2,1,0:T(8,128)}, f32[36,32,128]{2,1,0:T(8,128)}, f32[36,32,128]{2,1,0:T(8,128)}, f32[36,32,128]{2,1,0:T(8,128)}, f32[36,32,128]{...) custom-call(f32[32,16,128]{2,1,0:T(8,128)} %bitcast.8, ...), custom_call_target="tpu_custom_call" | custom-call | tf_op jit(solution)/shard_map/pallas_call | solution.py:512
  83.0 2.0 %collective-permute-start.4 = (f32[9,8,128]{2,1,0:T(8,128)}, f32[9,8,128]{2,1,0:T(8,128)S(1)}, u32[]{:S(2)}, u32[]{:S(2)}) collective-permute-start(f32[9,8,128]{2,1,0:T(8,128)} %get-tuple-element.32), channel_id=1, source_target_pairs={{0,8},{8,16},{16,24},{1,9},{9,17},{17,25},{2,10},{10,18},{18,26},{... | collective-permute-start | bytes 110600 | tf_op jit(solution)/shard_map/ppermute | solution.py:527
  84.9 3.3 %collective-permute-start.5 = (f32[9,8,128]{2,1,0:T(8,128)}, f32[9,8,128]{2,1,0:T(8,128)S(1)}, u32[]{:S(2)}, u32[]{:S(2)}) collective-permute-start(f32[9,8,128]{2,1,0:T(8,128)} %get-tuple-element.33), channel_id=1, source_target_pairs={{8,0},{16,8},{24,16},{9,1},{17,9},{25,17},{10,2},{18,10},{26,18},{... | collective-permute-start | bytes 110600 | tf_op jit(solution)/shard_map/ppermute | solution.py:528
  88.3 2.5 %collective-permute-done.5.high = f32[9,8,128]{2,1,0:T(8,128)S(1)} collective-permute-done((f32[9,8,128]{2,1,0:T(8,128)}, f32[9,8,128]{2,1,0:T(8,128)S(1)}, u32[]{:S(2)}, u32[]{:S(2)}) %collective-permute-start.5) | collective-permute-done | bytes 36896 | tf_op jit(solution)/shard_map/ppermute | solution.py:528
  90.7 0.6 copy-done.5
  91.3 1.6 %shard_map.40 = (f32[22,8,128]{2,1,0:T(8,128)}, f32[22,8,128]{2,1,0:T(8,128)}) custom-call(f32[8,8,128]{2,1,0:T(8,128)} %get-tuple-element.30.coarse, f32[24,16,128]{2,1,0:T(8,128)} %get-tuple-element.31.v1.in_v1, f32[9,8,128]{2,1,0:T(8,128)} %copy-done.4, f32[9,8,128]{2,1,0:T(8,128)} %copy-done.5), custom_call_target="tpu_custom_call" | custom-call | tf_op jit(solution)/shard_map/pallas_call | solution.py:530
  92.9 1.9 %collective-permute-start.7 = (f32[22,8,128]{2,1,0:T(8,128)}, f32[22,8,128]{2,1,0:T(8,128)S(1)}, u32[]{:S(2)}, u32[]{:S(2)}) collective-permute-start(f32[22,8,128]{2,1,0:T(8,128)} %get-tuple-element.35), channel_id=1, source_target_pairs={{1,3},{3,1},{2,6},{6,2},{7,5},{5,7},{9,11},{11,9},{10,14},{14,10},... | collective-permute-start | bytes 270344 | tf_op jit(solution)/shard_map/ppermute | solution.py:538
  94.9 8.8 %collective-permute-start.6 = (f32[22,8,128]{2,1,0:T(8,128)}, f32[22,8,128]{2,1,0:T(8,128)S(1)}, u32[]{:S(2)}, u32[]{:S(2)}) collective-permute-start(f32[22,8,128]{2,1,0:T(8,128)} %get-tuple-element.34.own), channel_id=1, source_target_pairs={{0,1},{1,0},{3,2},{2,3},{6,7},{7,6},{5,4},{4,5},{8,9},{9,8},{11,10... | collective-permute-start | bytes 270344 | tf_op jit(solution)/shard_map/ppermute | solution.py:537
  103.7 5.5 %collective-permute-start.8 = (f32[22,8,128]{2,1,0:T(8,128)S(1)}, f32[22,8,128]{2,1,0:T(8,128)S(1)}, u32[]{:S(2)}, u32[]{:S(2)}) collective-permute-start(f32[22,8,128]{2,1,0:T(8,128)S(1)} %collective-permute-done.7.near_odd), channel_id=1, source_target_pairs={{0,1},{1,0},{3,2},{2,3},{6,7},{7,6},{5,4},{4,5},{8,9},{9,8},{11,10... | collective-permute-start | bytes 270344 | tf_op jit(solution)/shard_map/ppermute | solution.py:540
  109.2 1.9 %collective-permute-start.9 = (f32[22,8,128]{2,1,0:T(8,128)S(1)}, f32[22,8,128]{2,1,0:T(8,128)S(1)}, u32[]{:S(2)}, u32[]{:S(2)}) collective-permute-start(f32[22,8,128]{2,1,0:T(8,128)S(1)} %collective-permute-done.6.near_even), channel_id=1, source_target_pairs={{1,3},{3,1},{2,6},{6,2},{7,5},{5,7},{9,11},{11,9},{10,14},{14,10},... | collective-permute-start | bytes 270344 | tf_op jit(solution)/shard_map/ppermute | solution.py:539
  111.1 3.3 %collective-permute-done.9.far_odd = f32[22,8,128]{2,1,0:T(8,128)S(1)} collective-permute-done((f32[22,8,128]{2,1,0:T(8,128)S(1)}, f32[22,8,128]{2,1,0:T(8,128)S(1)}, u32[]{:S(2)}, u32[]{:S(2)}) %collective-permute-start.9) | collective-permute-done | bytes 90144 | tf_op jit(solution)/shard_map/ppermute | solution.py:539
  114.5 0.6 copy-done.9
  115.1 13.6 %shard_map.41 = f32[32,16,128]{2,1,0:T(8,128)} custom-call(f32[22,8,128]{2,1,0:T(8,128)} %get-tuple-element.34.own, f32[22,8,128]{2,1,0:T(8,128)} %copy-done.7, f32[22,8,128]{2,1,0:T(8,128)} %copy-done.6, f32[22,8,128]{2,1,0:T(8,128)} %copy-done.8, f32[22,8,128]{2,1,0:T(8,128)} %copy-done.9, f32[9,8,128]{2,1,0:T(8,128)} %copy-done.4, ...), custom_call_target="tpu_custom_call" | custom-call | tf_op jit(solution)/shard_map/pallas_call | solution.py:543
  (21 shorter events, 0.0 us)
Async XLA Ops:
  10.6 7.0 %collective-permute-start = (f32[19,16,128]{2,1,0:T(8,128)}, f32[19,16,128]{2,1,0:T(8,128)S(1)}, u32[]{:S(2)}, u32[]{:S(2)}) collective-permute-start(f32[19,16,128]{2,1,0:T(8,128)} %get-tuple-element.26), channel_id=1, source_target_pairs={{0,8},{8,16},{16,24},{1,9},{9,17},{17,25},{2,10},{10,18},{18,26},{... | collective-permute-start | bytes 466952 | tf_op jit(solution)/shard_map/ppermute | solution.py:492
  13.7 8.1 %collective-permute-start.1 = (f32[19,16,128]{2,1,0:T(8,128)}, f32[19,16,128]{2,1,0:T(8,128)S(1)}, u32[]{:S(2)}, u32[]{:S(2)}) collective-permute-start(f32[19,16,128]{2,1,0:T(8,128)} %get-tuple-element.27), channel_id=1, source_target_pairs={{8,0},{16,8},{24,16},{9,1},{17,9},{25,17},{10,2},{18,10},{26,18},{... | collective-permute-start | bytes 466952 | tf_op jit(solution)/shard_map/ppermute | solution.py:493
  17.6 4.2 %copy-start = (f32[19,16,128]{2,1,0:T(8,128)}, f32[19,16,128]{2,1,0:T(8,128)S(1)}, u32[]{:S(2)}) copy-start(f32[19,16,128]{2,1,0:T(8,128)S(1)} %collective-permute-done.low) | copy-start | bytes 466948
  21.8 0.7 copy-start.1
  57.0 3.7 %collective-permute-start.2 = (f32[134,8,128]{2,1,0:T(8,128)}, f32[134,8,128]{2,1,0:T(8,128)S(1)}, u32[]{:S(2)}, u32[]{:S(2)}) collective-permute-start(f32[134,8,128]{2,1,0:T(8,128)} %get-tuple-element.28), channel_id=1, source_target_pairs={{0,1},{1,0},{3,2},{2,3},{6,7},{7,6},{5,4},{4,5},{8,9},{9,8},{11,10... | collective-permute-start | bytes 1646600 | tf_op jit(solution)/shard_map/ppermute | solution.py:504
  58.7 10.7 %collective-permute-start.3 = (f32[134,8,128]{2,1,0:T(8,128)}, f32[134,8,128]{2,1,0:T(8,128)S(1)}, u32[]{:S(2)}, u32[]{:S(2)}) collective-permute-start(f32[134,8,128]{2,1,0:T(8,128)} %get-tuple-element.29), channel_id=1, source_target_pairs={{1,3},{3,1},{2,6},{6,2},{7,5},{5,7},{9,11},{11,9},{10,14},{14,10},... | collective-permute-start | bytes 1646600 | tf_op jit(solution)/shard_map/ppermute | solution.py:505
  60.8 8.6 %copy-start.2 = (f32[134,8,128]{2,1,0:T(8,128)}, f32[134,8,128]{2,1,0:T(8,128)S(1)}, u32[]{:S(2)}) copy-start(f32[134,8,128]{2,1,0:T(8,128)S(1)} %collective-permute-done.2.from_even) | copy-start | bytes 1646596
  69.4 0.8 copy-start.3
  83.0 5.3 %collective-permute-start.4 = (f32[9,8,128]{2,1,0:T(8,128)}, f32[9,8,128]{2,1,0:T(8,128)S(1)}, u32[]{:S(2)}, u32[]{:S(2)}) collective-permute-start(f32[9,8,128]{2,1,0:T(8,128)} %get-tuple-element.32), channel_id=1, source_target_pairs={{0,8},{8,16},{16,24},{1,9},{9,17},{17,25},{2,10},{10,18},{18,26},{... | collective-permute-start | bytes 110600 | tf_op jit(solution)/shard_map/ppermute | solution.py:527
  84.9 5.8 %collective-permute-start.5 = (f32[9,8,128]{2,1,0:T(8,128)}, f32[9,8,128]{2,1,0:T(8,128)S(1)}, u32[]{:S(2)}, u32[]{:S(2)}) collective-permute-start(f32[9,8,128]{2,1,0:T(8,128)} %get-tuple-element.33), channel_id=1, source_target_pairs={{8,0},{16,8},{24,16},{9,1},{17,9},{25,17},{10,2},{18,10},{26,18},{... | collective-permute-start | bytes 110600 | tf_op jit(solution)/shard_map/ppermute | solution.py:528
  88.3 2.5 %copy-start.4 = (f32[9,8,128]{2,1,0:T(8,128)}, f32[9,8,128]{2,1,0:T(8,128)S(1)}, u32[]{:S(2)}) copy-start(f32[9,8,128]{2,1,0:T(8,128)S(1)} %collective-permute-done.4.low) | copy-start | bytes 110596
  90.7 0.6 copy-start.5
  92.9 10.7 %collective-permute-start.7 = (f32[22,8,128]{2,1,0:T(8,128)}, f32[22,8,128]{2,1,0:T(8,128)S(1)}, u32[]{:S(2)}, u32[]{:S(2)}) collective-permute-start(f32[22,8,128]{2,1,0:T(8,128)} %get-tuple-element.35), channel_id=1, source_target_pairs={{1,3},{3,1},{2,6},{6,2},{7,5},{5,7},{9,11},{11,9},{10,14},{14,10},... | collective-permute-start | bytes 270344 | tf_op jit(solution)/shard_map/ppermute | solution.py:538
  94.9 14.3 %collective-permute-start.6 = (f32[22,8,128]{2,1,0:T(8,128)}, f32[22,8,128]{2,1,0:T(8,128)S(1)}, u32[]{:S(2)}, u32[]{:S(2)}) collective-permute-start(f32[22,8,128]{2,1,0:T(8,128)} %get-tuple-element.34.own), channel_id=1, source_target_pairs={{0,1},{1,0},{3,2},{2,3},{6,7},{7,6},{5,4},{4,5},{8,9},{9,8},{11,10... | collective-permute-start | bytes 270344 | tf_op jit(solution)/shard_map/ppermute | solution.py:537
  103.7 10.8 %copy-start.6 = (f32[22,8,128]{2,1,0:T(8,128)}, f32[22,8,128]{2,1,0:T(8,128)S(1)}, u32[]{:S(2)}) copy-start(f32[22,8,128]{2,1,0:T(8,128)S(1)} %collective-permute-done.7.near_odd) | copy-start | bytes 270340
  103.7 7.5 %collective-permute-start.8 = (f32[22,8,128]{2,1,0:T(8,128)S(1)}, f32[22,8,128]{2,1,0:T(8,128)S(1)}, u32[]{:S(2)}, u32[]{:S(2)}) collective-permute-start(f32[22,8,128]{2,1,0:T(8,128)S(1)} %collective-permute-done.7.near_odd), channel_id=1, source_target_pairs={{0,1},{1,0},{3,2},{2,3},{6,7},{7,6},{5,4},{4,5},{8,9},{9,8},{11,10... | collective-permute-start | bytes 270344 | tf_op jit(solution)/shard_map/ppermute | solution.py:540
  109.2 5.3 %copy-start.7 = (f32[22,8,128]{2,1,0:T(8,128)}, f32[22,8,128]{2,1,0:T(8,128)S(1)}, u32[]{:S(2)}) copy-start(f32[22,8,128]{2,1,0:T(8,128)S(1)} %collective-permute-done.6.near_even) | copy-start | bytes 270340
  109.2 5.3 %collective-permute-start.9 = (f32[22,8,128]{2,1,0:T(8,128)S(1)}, f32[22,8,128]{2,1,0:T(8,128)S(1)}, u32[]{:S(2)}, u32[]{:S(2)}) collective-permute-start(f32[22,8,128]{2,1,0:T(8,128)S(1)} %collective-permute-done.6.near_even), channel_id=1, source_target_pairs={{1,3},{3,1},{2,6},{6,2},{7,5},{5,7},{9,11},{11,9},{10,14},{14,10},... | collective-permute-start | bytes 270344 | tf_op jit(solution)/shard_map/ppermute | solution.py:539
  111.1 3.3 %copy-start.8 = (f32[22,8,128]{2,1,0:T(8,128)}, f32[22,8,128]{2,1,0:T(8,128)S(1)}, u32[]{:S(2)}) copy-start(f32[22,8,128]{2,1,0:T(8,128)S(1)} %collective-permute-done.8.far_even) | copy-start | bytes 270340
  114.5 0.6 copy-start.9

commit v2 on v1

--- a/solution.py
+++ b/solution.py
@@ -16,7 +16,7 @@
 LANES = 128
 ANY = pl.BlockSpec(memory_space=pl.ANY)
 VMEM = pl.BlockSpec(memory_space=pltpu.VMEM)
-LIMIT = 56 * 1024 * 1024
+LIMIT = 16 * 1024 * 1024
 
 
 def params():
@@ -102,15 +102,20 @@
 def rows_loop(low, high, step, fn):
     trips = (high - low) // step
 
+    def run(rows):
+        stores = [item for row in rows for item in fn(row)]
+        for ref, at, value in stores:
+            ref[at] = value
+
     def trip(t, carry):
         base = low + t * step
-        for k in range(step):
-            fn(base + k)
+        run([base + k for k in range(step)])
         return carry
 
     lax.fori_loop(0, trips, trip, 0)
-    for row in range(low + trips * step, high):
-        fn(row)
+    rest = list(range(low + trips * step, high))
+    if rest:
+        run(rest)
 
 
 def pair_sum_z(row, dist):
@@ -186,23 +191,18 @@
 
     def coef_row(i):
         fx, fy, fz, dg, inv = coefficients(A[i], B[i], B[i - 1], B[i + 1], 1, 1.0)
-        FX[i] = fx
-        FY[i] = fy
-        FZ[i] = fz
-        DG[i] = dg
-        IN[i] = inv
-        V[i] = inv * F[i]
-
-    rows_loop(2, end - 2, 2, coef_row)
+        return [(FX, i, fx), (FY, i, fy), (FZ, i, fz), (DG, i, dg), (IN, i, inv), (V, i, inv * F[i])]
+
+    rows_loop(2, end - 2, 11, coef_row)
 
     kept = pl.ds(FRAME - 2, count + 4)
     outs = [(F, out_f), (IN, out_inv), (FX, out_fx), (FY, out_fy), (FZ, out_fz)]
     out_copies = run_copies([(src.at[kept], dst) for src, dst in outs], out_sems)
 
     def sweep_row(i):
-        U[i] = relaxed(i, V, F, IN, faces, 1)
-
-    rows_loop(3, end - 3, 2, sweep_row)
+        return [(U, i, relaxed(i, V, F, IN, faces, 1))]
+
+    rows_loop(3, end - 3, 14, sweep_row)
     last = pltpu.make_async_copy(U.at[kept], out_v, out_sems.at[5])
     last.start()
     out_copies.append(last)
@@ -214,21 +214,23 @@
     half_rows = (depth + 2 * FRAME) // 2
 
     def restrict_row(j):
-        T[j] = residual(2 * j) + residual(2 * j + 1)
-
-    rows_loop(2, end // 2 - 2, 1, restrict_row)
+        return [(T, j, residual(2 * j) + residual(2 * j + 1))]
+
+    rows_loop(2, end // 2 - 2, 5, restrict_row)
 
     def level1_source(j):
-        out_f1[j] = 0.125 * pair_sum_z(strided_pair(T, j, half_rows), 1)
-
-    rows_loop(2, end // 2 - 2, 2, level1_source)
+        return [(out_f1, j, 0.125 * pair_sum_z(strided_pair(T, j, half_rows), 1))]
+
+    rows_loop(2, end // 2 - 2, 10, level1_source)
 
     def level1_coef(j):
+        stores = []
         for src, dst in ((A, A1), (B, B1)):
             both = strided_pair(src, 2 * j, half_rows) + strided_pair(src, 2 * j + 1, half_rows)
-            dst[j] = 0.125 * pair_sum_z(both, 1)
-
-    rows_loop(1, end // 2 - 1, 2, level1_coef)
+            stores.append((dst, j, 0.125 * pair_sum_z(both, 1)))
+        return stores
+
+    rows_loop(1, end // 2 - 1, 11, level1_coef)
 
     faces1 = (out_fx1, out_fy1, out_fz1)
     end1 = end // 2
@@ -236,19 +238,17 @@
 
     def coef_row1(i):
         fx, fy, fz, dg, inv = coefficients(A1[i], B1[i], B1[i - 1], B1[i + 1], 2, 0.25)
-        out_fx1[i] = fx
-        out_fy1[i] = fy
-        out_fz1[i] = fz
-        D1[i] = dg
-        out_inv1[i] = inv
-        W1[i] = inv * out_f1[i]
-
-    rows_loop(2, end1 - 2, 4, coef_row1)
+        return [
+            (out_fx1, i, fx), (out_fy1, i, fy), (out_fz1, i, fz),
+            (D1, i, dg), (out_inv1, i, inv), (W1, i, inv * out_f1[i]),
+        ]
+
+    rows_loop(2, end1 - 2, 10, coef_row1)
 
     def sweep_row1(i):
-        out_v1[i] = relaxed(i, W1, out_f1, out_inv1, faces1, 2)
-
-    rows_loop(3, end1 - 3, 3, sweep_row1)
+        return [(out_v1, i, relaxed(i, W1, out_f1, out_inv1, faces1, 2))]
+
+    rows_loop(3, end1 - 3, 18, sweep_row1)
 
     def residual1(i):
         here, off = off_sum(i, out_v1, faces1, 2)
@@ -262,24 +262,28 @@
 
     def coarse_row(x):
         i = first1 + 2 * x
-        T1[0, x] = residual1(i) + residual1(i + 1)
-        T1[1, x] = A1[i] + A1[i + 1]
-        T1[2, x] = B1[i] + B1[i + 1]
-
-    rows_loop(0, count2, 1, coarse_row)
+        return [
+            (T1, (0, x), residual1(i) + residual1(i + 1)),
+            (T1, (1, x), A1[i] + A1[i + 1]),
+            (T1, (2, x), B1[i] + B1[i + 1]),
+        ]
+
+    rows_loop(0, count2, 8, coarse_row)
     own2 = FRAME // 4
     depth2 = depth // 4
 
     def coarse_pack(x):
+        stores = []
         for k in range(3):
             both = T1[k, x, pl.ds(0, quarter_rows, stride=2), :] + T1[k, x, pl.ds(1, quarter_rows, stride=2), :]
             value = 0.125 * pair_sum_z(both, 2)
             packed = jnp.zeros((1, LANES), jnp.float32)
             for y in range(depth2):
                 packed = packed + jnp.where(lane % depth2 == y, value[own2 + y:own2 + y + 1], 0.0)
-            out_coarse[x, k:k + 1] = packed
-
-    rows_loop(0, count2, 1, coarse_pack)
+            stores.append((out_coarse, (x, slice(k, k + 1)), packed))
+        return stores
+
+    rows_loop(0, count2, 8, coarse_pack)
 
     own1 = slice(first1, first1 + depth // 2)
     for k in range(COARSE_X):
@@ -316,13 +320,12 @@
 
 def up_kernel(
     own, near_even, near_odd, far_even, far_odd, low, high,
-    in_v, in_f, in_inv, in_fx, in_fy, in_fz,
-    in_v1, in_f1, in_inv1, in_fx1, in_fy1, in_fz1,
+    in_v, F, IN, FX, FY, FZ,
+    in_v1, F1, IN1, FX1, FY1, FZ1,
     out,
-    V, F, IN, FX, FY, FZ, U,
-    V1, F1, IN1, FX1, FY1, FZ1, U1,
+    V, U, V1, U1,
     R, S2, A2, B2, FX2, FY2, FZ2, IN2, V2, U2, PT, P0,
-    sems, state_sems,
+    sems,
 ):
     parity = box_parity()
     below = 1 + 2 * (1 - parity)
@@ -336,13 +339,6 @@
         ],
         sems,
     )
-    states = run_copies(
-        [
-            (in_v1, V1), (in_f1, F1), (in_inv1, IN1), (in_fx1, FX1), (in_fy1, FY1), (in_fz1, FZ1),
-            (in_v, V), (in_f, F), (in_inv, IN), (in_fx, FX), (in_fy, FY), (in_fz, FZ),
-        ],
-        state_sems,
-    )
     wait_copies(copies)
 
     rows2 = B2.shape[1]
@@ -354,6 +350,7 @@
     last_of_four = lane % 4 == 3
 
     def unpack_row(x):
+        stores = []
         for k, dst in enumerate((S2, A2, B2)):
             packed = jnp.broadcast_to(R[0, x, k:k + 1], (rows2, LANES))
             for slot in range(1, 5):
@@ -363,28 +360,25 @@
             t = t + z_prev(t, 2)
             t = jnp.where(last_of_four, t, 0.0)
             t = t + z_next(t, 1)
-            dst[x] = t + z_next(t, 2)
-
-    rows_loop(0, span2, 2, unpack_row)
+            stores.append((dst, x, t + z_next(t, 2)))
+        return stores
+
+    rows_loop(0, span2, 5, unpack_row)
     FX2[0] = 0.5 * 0.0625 * (B2[0] + B2[1])
 
     def coef_row2(i):
         fx, fy, fz, dg, inv = coefficients(A2[i], B2[i], B2[i - 1], B2[i + 1], 4, 0.0625)
-        FX2[i] = fx
-        FY2[i] = fy
-        FZ2[i] = fz
-        IN2[i] = inv
-        V2[i] = inv * S2[i]
-
-    rows_loop(1, span2 - 1, 2, coef_row2)
+        return [(FX2, i, fx), (FY2, i, fy), (FZ2, i, fz), (IN2, i, inv), (V2, i, inv * S2[i])]
+
+    rows_loop(1, span2 - 1, 9, coef_row2)
     faces2 = (FX2, FY2, FZ2)
     src, dst = V2, U2
     for sweep in range(1, 4):
 
         def sweep_row2(i, src=src, dst=dst):
-            dst[i] = relaxed(i, src, S2, IN2, faces2, 4)
-
-        rows_loop(1 + sweep, span2 - 1 - sweep, 2, sweep_row2)
+            return [(dst, i, relaxed(i, src, S2, IN2, faces2, 4))]
+
+        rows_loop(1 + sweep, span2 - 1 - sweep, 9 - sweep, sweep_row2)
         src, dst = dst, src
     coarse = src
 
@@ -392,72 +386,74 @@
     depth1 = 8
     span1 = V1.shape[0]
     own_rows = pl.ds(first1, depth1)
-    wait_copies(states[:6])
+
+    def own_row(x):
+        i = first1 + x
+        return [(V1, (i, own_rows), in_v1[i, own_rows])]
+
+    rows_loop(0, span1 - 2 * first1, 16, own_row)
     for k in range(FINE_X):
         V1[first1 - FINE_X + k, own_rows] = low[COARSE_X + k]
         V1[span1 - first1 + k, own_rows] = high[COARSE_X + k]
 
     def add_coarse(x):
         half = coarse[x + COARSE_X - first1 // 2, first1:first1 + depth1]
-        PT[x, pl.ds(0, depth1, stride=2), :] = half
-        PT[x, pl.ds(1, depth1, stride=2), :] = half
-
-    rows_loop(0, span1 // 2, 2, add_coarse)
+        return [(PT, (x, pl.ds(k, depth1, stride=2)), half) for k in range(2)]
+
+    rows_loop(0, span1 // 2, 12, add_coarse)
 
     def rim_row(x):
         i = x + first1 - FINE_X
-        V1[i, first1 - FINE_X:first1] = R[1, x, 3:3 + FINE_X]
-        V1[i, first1 + depth1:first1 + depth1 + FINE_X] = R[3, x, 3:3 + FINE_X]
-
-    rows_loop(0, span1 - 2 * (first1 - FINE_X), 2, rim_row)
+        return [
+            (V1, (i, slice(first1 - FINE_X, first1)), R[1, x, 3:3 + FINE_X]),
+            (V1, (i, slice(first1 + depth1, first1 + depth1 + FINE_X)), R[3, x, 3:3 + FINE_X]),
+        ]
+
+    rows_loop(0, span1 - 2 * (first1 - FINE_X), 22, rim_row)
 
     def corrected_row(x):
         add = PT[x]
-        V1[2 * x] = V1[2 * x] + add
-        V1[2 * x + 1] = V1[2 * x + 1] + add
-
-    rows_loop(0, span1 // 2, 2, corrected_row)
+        return [(V1, 2 * x + k, V1[2 * x + k] + add) for k in range(2)]
+
+    rows_loop(0, span1 // 2, 12, corrected_row)
     faces1 = (FX1, FY1, FZ1)
 
     def sweep_a1(i):
-        U1[i] = relaxed(i, V1, F1, IN1, faces1, 2)
-
-    rows_loop(2, span1 - 2, 4, sweep_a1)
+        return [(U1, i, relaxed(i, V1, F1, IN1, faces1, 2))]
+
+    rows_loop(2, span1 - 2, 10, sweep_a1)
 
     def sweep_b1(i):
-        V1[i] = relaxed(i, U1, F1, IN1, faces1, 2)
-
-    rows_loop(3, span1 - 3, 3, sweep_b1)
+        return [(V1, i, relaxed(i, U1, F1, IN1, faces1, 2))]
+
+    rows_loop(3, span1 - 3, 18, sweep_b1)
 
     span = V.shape[0]
     rows1 = V1.shape[1]
-    wait_copies(states[6:])
 
     def widen(x):
         row = V1[x + first1 - 1]
-        P0[x, pl.ds(0, rows1, stride=2), :] = row
-        P0[x, pl.ds(1, rows1, stride=2), :] = row
-
-    rows_loop(0, span // 2, 2, widen)
+        return [(P0, (x, pl.ds(k, rows1, stride=2)), row) for k in range(2)]
+
+    rows_loop(0, span // 2, 18, widen)
 
     def corrected0(x):
         add = P0[x]
-        V[2 * x] = V[2 * x] + add
-        V[2 * x + 1] = V[2 * x + 1] + add
-
-    rows_loop(0, span // 2, 2, corrected0)
+        return [(V, 2 * x + k, in_v[2 * x + k] + add) for k in range(2)]
+
+    rows_loop(0, span // 2, 9, corrected0)
     faces = (FX, FY, FZ)
 
     def sweep_a(i):
-        U[i] = relaxed(i, V, F, IN, faces, 1)
-
-    rows_loop(1, span - 1, 2, sweep_a)
+        return [(U, i, relaxed(i, V, F, IN, faces, 1))]
+
+    rows_loop(1, span - 1, 17, sweep_a)
     depth = out.shape[1]
 
     def sweep_b(i):
-        out[i - 2] = relaxed(i, U, F, IN, faces, 1)[FRAME:FRAME + depth]
-
-    rows_loop(2, span - 2, 2, sweep_b)
+        return [(out, i - 2, relaxed(i, U, F, IN, faces, 1)[FRAME:FRAME + depth])]
+
+    rows_loop(2, span - 2, 16, sweep_b)
 
 
 def body(source, alpha, beta):
@@ -485,7 +481,7 @@
         pack_x_kernel,
         out_shape=[arr(x_rows, depth, lanes)] * 2,
         in_specs=[ANY] * 3,
-        out_specs=[ANY] * 2,
+        out_specs=[VMEM] * 2,
         scratch_shapes=[dma((6,))],
         compiler_params=params(),
     )(f, a, b)
@@ -497,7 +493,7 @@
         pack_y_kernel,
         out_shape=[arr(y_rows, FRAME, lanes)] * 2,
         in_specs=[ANY] * 5,
-        out_specs=[ANY] * 2,
+        out_specs=[VMEM] * 2,
         scratch_shapes=[dma((18,))],
         compiler_params=params(),
     )(f, a, b, low, high)
@@ -543,12 +539,12 @@
     out = pl.pallas_call(
         up_kernel,
         out_shape=arr(count, depth, lanes),
-        in_specs=[ANY] * 5 + [VMEM] * 2 + [ANY] * 12,
+        in_specs=[ANY] * 5 + [VMEM] * 14,
         out_specs=VMEM,
-        scratch_shapes=[vm(*kept)] * 7 + [vm(*framed1)] * 7
+        scratch_shapes=[vm(*kept)] * 2 + [vm(*framed1)] * 2
         + [vm(5, span, 8, lanes)] + [vm(*framed2)] * 9
         + [vm(framed1[0] // 2, framed1[1], lanes), vm(kept[0] // 2, kept[1], lanes)]
-        + [dma((5,)), dma((12,))],
+        + [dma((5,))],
         compiler_params=params(),
     )(even2, near_even, near_odd, far_even, far_odd, low2, high2, *state0, *state1)
     return out[:, None]

time: 131 us -> 66.8 us (0.51)
  the two profiles are of different devices: /device:TPU:11 before, /device:TPU:8 now
where the time goes in v2:
time: 66.8 us; the launch traced here: 66.4 us
  waiting for transfers between devices  35.7 us (53%)
  starting transfers between devices  17.9 us (27%)
  Pallas kernels  9.88 us (15%)
  local copies, waits for them, and re-layouts  2.85 us (4%)
    ppermute x1, waiting for transfers between devices, body(): from_odd = lax.ppermute(to_odd, 'box', odd_perm)  13.2 us
    ppermute x1, waiting for transfers between devices, body(): far_odd = lax.ppermute(near_even, 'box', odd_perm)  5.38 us
    ppermute x1, waiting for transfers between devices, body(): near_odd = lax.ppermute(odd2, 'box', odd_perm)  5.31 us
    ppermute x1, waiting for transfers between devices, body(): high = lax.ppermute(down, 'grp', down_perm)  5.28 us
    pallas_call x1, Pallas kernels, body(): pl.pallas_call(up_kernel, out_shape=arr(count, depth, lanes), in_specs=[A...  4.73 us
    ppermute x1, starting transfers between devices, body(): from_odd = lax.ppermute(to_odd, 'box', odd_perm)  4.5 us
    pallas_call x1, Pallas kernels, body(): pl.pallas_call(down_kernel, out_shape=[arr(*kept)] * 6 + [arr(*framed1)]...  4.38 us
    ppermute x1, waiting for transfers between devices, body(): high2 = lax.ppermute(to_down, 'grp', down_perm)  4.24 us
  transfers between devices with their start and end apart: 10, of which 7 were waited for; matrix products, arithmetic and copies ran while one was open for 0% of the time, Pallas kernels for 0%

profile of v2, /device:TPU:8, one launch (start us, length us, event | category | flops | bytes accessed | tf_op | source)
XLA Modules:
  0.0 66.4 jit_solution(8209341952534958784)
XLA Ops:
  0.0 0.9 %copy-done = f32[32,1,16,128]{3,2,1,0:T(8,128)S(1)} copy-done((f32[32,1,16,128]{3,2,1,0:T(8,128)S(1)}, f32[32,1,16,128]{3,2,1,0:T(8,128)}, u32[]{:S(2)}) %copy-start) | copy-done | bytes 262168
  1.0 0.9 %copy-done.1 = f32[32,1,16,128]{3,2,1,0:T(8,128)S(1)} copy-done((f32[32,1,16,128]{3,2,1,0:T(8,128)S(1)}, f32[32,1,16,128]{3,2,1,0:T(8,128)}, u32[]{:S(2)}) %copy-start.1) | copy-done | bytes 262168
  1.9 0.9 %copy-done.2 = f32[32,1,16,128]{3,2,1,0:T(8,128)S(1)} copy-done((f32[32,1,16,128]{3,2,1,0:T(8,128)S(1)}, f32[32,1,16,128]{3,2,1,0:T(8,128)}, u32[]{:S(2)}) %copy-start.2) | copy-done | bytes 262168
  2.9 0.4 shard_map.37
  3.3 3.4 %collective-permute-start = (f32[19,16,128]{2,1,0:T(8,128)S(1)}, f32[19,16,128]{2,1,0:T(8,128)S(1)}, u32[]{:S(2)}, u32[]{:S(2)}) collective-permute-start(f32[19,16,128]{2,1,0:T(8,128)S(1)} %get-tuple-element.26), channel_id=1, source_target_pairs={{0,8},{8,16},{16,24},{1,9},{9,17},{17,25},{2,10},{10,18},{18,26},{... | collective-permute-start | bytes 466952 | tf_op jit(solution)/shard_map/ppermute | solution.py:488
  6.7 1.3 %collective-permute-start.1 = (f32[19,16,128]{2,1,0:T(8,128)S(1)}, f32[19,16,128]{2,1,0:T(8,128)S(1)}, u32[]{:S(2)}, u32[]{:S(2)}) collective-permute-start(f32[19,16,128]{2,1,0:T(8,128)S(1)} %get-tuple-element.27), channel_id=1, source_target_pairs={{8,0},{16,8},{24,16},{9,1},{17,9},{25,17},{10,2},{18,10},{26,18},{... | collective-permute-start | bytes 466952 | tf_op jit(solution)/shard_map/ppermute | solution.py:489
  8.0 2.0 %collective-permute-done.low = f32[19,16,128]{2,1,0:T(8,128)S(1)} collective-permute-done((f32[19,16,128]{2,1,0:T(8,128)S(1)}, f32[19,16,128]{2,1,0:T(8,128)S(1)}, u32[]{:S(2)}, u32[]{:S(2)}) %collective-permute-start) | collective-permute-done | bytes 155680 | tf_op jit(solution)/shard_map/ppermute | solution.py:488
  10.0 5.3 %collective-permute-done.1.high = f32[19,16,128]{2,1,0:T(8,128)S(1)} collective-permute-done((f32[19,16,128]{2,1,0:T(8,128)S(1)}, f32[19,16,128]{2,1,0:T(8,128)S(1)}, u32[]{:S(2)}, u32[]{:S(2)}) %collective-permute-start.1) | collective-permute-done | bytes 155680 | tf_op jit(solution)/shard_map/ppermute | solution.py:489
  15.2 0.3 shard_map.38
  15.6 0.1 collective-permute-start.2
  15.6 4.5 %collective-permute-start.3 = (f32[134,8,128]{2,1,0:T(8,128)S(1)}, f32[134,8,128]{2,1,0:T(8,128)S(1)}, u32[]{:S(2)}, u32[]{:S(2)}) collective-permute-start(f32[134,8,128]{2,1,0:T(8,128)S(1)} %get-tuple-element.29), channel_id=1, source_target_pairs={{1,3},{3,1},{2,6},{6,2},{7,5},{5,7},{9,11},{11,9},{10,14},{14,10},... | collective-permute-start | bytes 1646600 | tf_op jit(solution)/shard_map/ppermute | solution.py:501
  20.1 0.0 collective-permute-done.2.from_even
  20.2 13.2 %collective-permute-done.3.from_odd = f32[134,8,128]{2,1,0:T(8,128)S(1)} collective-permute-done((f32[134,8,128]{2,1,0:T(8,128)S(1)}, f32[134,8,128]{2,1,0:T(8,128)S(1)}, u32[]{:S(2)}, u32[]{:S(2)}) %collective-permute-start.3) | collective-permute-done | bytes 548896 | tf_op jit(solution)/shard_map/ppermute | solution.py:501
  33.4 4.4 %shard_map.39 = (f32[36,32,128]{2,1,0:T(8,128)S(1)}, f32[36,32,128]{2,1,0:T(8,128)S(1)}, f32[36,32,128]{2,1,0:T(8,128)S(1)}, f32[36,32,128]{2,1,0:T(8,128)S(1)},...) custom-call(f32[32,16,128]{2,1,0:T(8,128)S(1)} %bitcast.8, ...), custom_call_target="tpu_custom_call" | custom-call | tf_op jit(solution)/shard_map/pallas_call | solution.py:508
  37.8 3.4 %collective-permute-start.4 = (f32[9,8,128]{2,1,0:T(8,128)S(1)}, f32[9,8,128]{2,1,0:T(8,128)S(1)}, u32[]{:S(2)}, u32[]{:S(2)}) collective-permute-start(f32[9,8,128]{2,1,0:T(8,128)S(1)} %get-tuple-element.32), channel_id=1, source_target_pairs={{0,8},{8,16},{16,24},{1,9},{9,17},{17,25},{2,10},{10,18},{18,26},{... | collective-permute-start | bytes 110600 | tf_op jit(solution)/shard_map/ppermute | solution.py:523
  41.2 1.3 %collective-permute-start.5 = (f32[9,8,128]{2,1,0:T(8,128)S(1)}, f32[9,8,128]{2,1,0:T(8,128)S(1)}, u32[]{:S(2)}, u32[]{:S(2)}) collective-permute-start(f32[9,8,128]{2,1,0:T(8,128)S(1)} %get-tuple-element.33), channel_id=1, source_target_pairs={{8,0},{16,8},{24,16},{9,1},{17,9},{25,17},{10,2},{18,10},{26,18},{... | collective-permute-start | bytes 110600 | tf_op jit(solution)/shard_map/ppermute | solution.py:524
  42.5 0.3 collective-permute-done.4.low
  42.8 4.2 %collective-permute-done.5.high = f32[9,8,128]{2,1,0:T(8,128)S(1)} collective-permute-done((f32[9,8,128]{2,1,0:T(8,128)S(1)}, f32[9,8,128]{2,1,0:T(8,128)S(1)}, u32[]{:S(2)}, u32[]{:S(2)}) %collective-permute-start.5) | collective-permute-done | bytes 36896 | tf_op jit(solution)/shard_map/ppermute | solution.py:524
  47.1 1.9 %collective-permute-start.7 = (f32[22,8,128]{2,1,0:T(8,128)S(1)}, f32[22,8,128]{2,1,0:T(8,128)S(1)}, u32[]{:S(2)}, u32[]{:S(2)}) collective-permute-start(f32[22,8,128]{2,1,0:T(8,128)S(1)} %get-tuple-element.35), channel_id=1, source_target_pairs={{1,3},{3,1},{2,6},{6,2},{7,5},{5,7},{9,11},{11,9},{10,14},{14,10},... | collective-permute-start | bytes 270344 | tf_op jit(solution)/shard_map/ppermute | solution.py:534
  49.0 0.1 collective-permute-start.6
  49.1 5.3 %collective-permute-done.7.near_odd = f32[22,8,128]{2,1,0:T(8,128)S(1)} collective-permute-done((f32[22,8,128]{2,1,0:T(8,128)S(1)}, f32[22,8,128]{2,1,0:T(8,128)S(1)}, u32[]{:S(2)}, u32[]{:S(2)}) %collective-permute-start.7) | collective-permute-done | bytes 90144 | tf_op jit(solution)/shard_map/ppermute | solution.py:534
  54.4 1.9 %collective-permute-start.9 = (f32[22,8,128]{2,1,0:T(8,128)S(1)}, f32[22,8,128]{2,1,0:T(8,128)S(1)}, u32[]{:S(2)}, u32[]{:S(2)}) collective-permute-start(f32[22,8,128]{2,1,0:T(8,128)S(1)} %collective-permute-done.6.near_even), channel_id=1, source_target_pairs={{1,3},{3,1},{2,6},{6,2},{7,5},{5,7},{9,11},{11,9},{10,14},{14,10},... | collective-permute-start | bytes 270344 | tf_op jit(solution)/shard_map/ppermute | solution.py:535
  56.3 5.4 %collective-permute-done.9.far_odd = f32[22,8,128]{2,1,0:T(8,128)S(1)} collective-permute-done((f32[22,8,128]{2,1,0:T(8,128)S(1)}, f32[22,8,128]{2,1,0:T(8,128)S(1)}, u32[]{:S(2)}, u32[]{:S(2)}) %collective-permute-start.9) | collective-permute-done | bytes 90144 | tf_op jit(solution)/shard_map/ppermute | solution.py:535
  61.7 4.7 %shard_map.41 = f32[32,16,128]{2,1,0:T(8,128)} custom-call(f32[22,8,128]{2,1,0:T(8,128)S(1)} %get-tuple-element.34.own, f32[22,8,128]{2,1,0:T(8,128)S(1)} %collective-permute-done.6.near_even, f32[22,8,128]{2,1,0:T(8,128)S(1)} %collective-permute-done.7.near_odd, f32[22,8,128]{2,1,0:T(8,128)S(1)} %collective-permute-done.8.far_even, ...), custom_call_target="tpu_custom_call" | custom-call | tf_op jit(solution)/shard_map/pallas_call | solution.py:539
  (7 shorter events, 0.0 us)
Async XLA Ops:
  0.0 0.9 %copy-start = (f32[32,1,16,128]{3,2,1,0:T(8,128)S(1)}, f32[32,1,16,128]{3,2,1,0:T(8,128)}, u32[]{:S(2)}) copy-start(f32[32,1,16,128]{3,2,1,0:T(8,128)} %param.3) | copy-start | bytes 786436
  1.0 0.9 %copy-start.1 = (f32[32,1,16,128]{3,2,1,0:T(8,128)S(1)}, f32[32,1,16,128]{3,2,1,0:T(8,128)}, u32[]{:S(2)}) copy-start(f32[32,1,16,128]{3,2,1,0:T(8,128)} %param.4) | copy-start | bytes 786436
  1.9 0.9 %copy-start.2 = (f32[32,1,16,128]{3,2,1,0:T(8,128)S(1)}, f32[32,1,16,128]{3,2,1,0:T(8,128)}, u32[]{:S(2)}) copy-start(f32[32,1,16,128]{3,2,1,0:T(8,128)} %param.5) | copy-start | bytes 786436
  3.3 6.7 %collective-permute-start = (f32[19,16,128]{2,1,0:T(8,128)S(1)}, f32[19,16,128]{2,1,0:T(8,128)S(1)}, u32[]{:S(2)}, u32[]{:S(2)}) collective-permute-start(f32[19,16,128]{2,1,0:T(8,128)S(1)} %get-tuple-element.26), channel_id=1, source_target_pairs={{0,8},{8,16},{16,24},{1,9},{9,17},{17,25},{2,10},{10,18},{18,26},{... | collective-permute-start | bytes 466952 | tf_op jit(solution)/shard_map/ppermute | solution.py:488
  6.7 8.5 %collective-permute-start.1 = (f32[19,16,128]{2,1,0:T(8,128)S(1)}, f32[19,16,128]{2,1,0:T(8,128)S(1)}, u32[]{:S(2)}, u32[]{:S(2)}) collective-permute-start(f32[19,16,128]{2,1,0:T(8,128)S(1)} %get-tuple-element.27), channel_id=1, source_target_pairs={{8,0},{16,8},{24,16},{9,1},{17,9},{25,17},{10,2},{18,10},{26,18},{... | collective-permute-start | bytes 466952 | tf_op jit(solution)/shard_map/ppermute | solution.py:489
  15.6 4.6 %collective-permute-start.2 = (f32[134,8,128]{2,1,0:T(8,128)S(1)}, f32[134,8,128]{2,1,0:T(8,128)S(1)}, u32[]{:S(2)}, u32[]{:S(2)}) collective-permute-start(f32[134,8,128]{2,1,0:T(8,128)S(1)} %get-tuple-element.28), channel_id=1, source_target_pairs={{0,1},{1,0},{3,2},{2,3},{6,7},{7,6},{5,4},{4,5},{8,9},{9,8},{11,10... | collective-permute-start | bytes 1646600 | tf_op jit(solution)/shard_map/ppermute | solution.py:500
  15.6 17.7 %collective-permute-start.3 = (f32[134,8,128]{2,1,0:T(8,128)S(1)}, f32[134,8,128]{2,1,0:T(8,128)S(1)}, u32[]{:S(2)}, u32[]{:S(2)}) collective-permute-start(f32[134,8,128]{2,1,0:T(8,128)S(1)} %get-tuple-element.29), channel_id=1, source_target_pairs={{1,3},{3,1},{2,6},{6,2},{7,5},{5,7},{9,11},{11,9},{10,14},{14,10},... | collective-permute-start | bytes 1646600 | tf_op jit(solution)/shard_map/ppermute | solution.py:501
  37.8 5.0 %collective-permute-start.4 = (f32[9,8,128]{2,1,0:T(8,128)S(1)}, f32[9,8,128]{2,1,0:T(8,128)S(1)}, u32[]{:S(2)}, u32[]{:S(2)}) collective-permute-start(f32[9,8,128]{2,1,0:T(8,128)S(1)} %get-tuple-element.32), channel_id=1, source_target_pairs={{0,8},{8,16},{16,24},{1,9},{9,17},{17,25},{2,10},{10,18},{18,26},{... | collective-permute-start | bytes 110600 | tf_op jit(solution)/shard_map/ppermute | solution.py:523
  41.2 5.9 %collective-permute-start.5 = (f32[9,8,128]{2,1,0:T(8,128)S(1)}, f32[9,8,128]{2,1,0:T(8,128)S(1)}, u32[]{:S(2)}, u32[]{:S(2)}) collective-permute-start(f32[9,8,128]{2,1,0:T(8,128)S(1)} %get-tuple-element.33), channel_id=1, source_target_pairs={{8,0},{16,8},{24,16},{9,1},{17,9},{25,17},{10,2},{18,10},{26,18},{... | collective-permute-start | bytes 110600 | tf_op jit(solution)/shard_map/ppermute | solution.py:524
  47.1 7.3 %collective-permute-start.7 = (f32[22,8,128]{2,1,0:T(8,128)S(1)}, f32[22,8,128]{2,1,0:T(8,128)S(1)}, u32[]{:S(2)}, u32[]{:S(2)}) collective-permute-start(f32[22,8,128]{2,1,0:T(8,128)S(1)} %get-tuple-element.35), channel_id=1, source_target_pairs={{1,3},{3,1},{2,6},{6,2},{7,5},{5,7},{9,11},{11,9},{10,14},{14,10},... | collective-permute-start | bytes 270344 | tf_op jit(solution)/shard_map/ppermute | solution.py:534
  49.0 5.4 %collective-permute-start.6 = (f32[22,8,128]{2,1,0:T(8,128)S(1)}, f32[22,8,128]{2,1,0:T(8,128)S(1)}, u32[]{:S(2)}, u32[]{:S(2)}) collective-permute-start(f32[22,8,128]{2,1,0:T(8,128)S(1)} %get-tuple-element.34.own), channel_id=1, source_target_pairs={{0,1},{1,0},{3,2},{2,3},{6,7},{7,6},{5,4},{4,5},{8,9},{9,8},{11,10... | collective-permute-start | bytes 270344 | tf_op jit(solution)/shard_map/ppermute | solution.py:533
  54.4 1.9 %collective-permute-start.8 = (f32[22,8,128]{2,1,0:T(8,128)S(1)}, f32[22,8,128]{2,1,0:T(8,128)S(1)}, u32[]{:S(2)}, u32[]{:S(2)}) collective-permute-start(f32[22,8,128]{2,1,0:T(8,128)S(1)} %collective-permute-done.7.near_odd), channel_id=1, source_target_pairs={{0,1},{1,0},{3,2},{2,3},{6,7},{7,6},{5,4},{4,5},{8,9},{9,8},{11,10... | collective-permute-start | bytes 270344 | tf_op jit(solution)/shard_map/ppermute | solution.py:536
  54.4 7.3 %collective-permute-start.9 = (f32[22,8,128]{2,1,0:T(8,128)S(1)}, f32[22,8,128]{2,1,0:T(8,128)S(1)}, u32[]{:S(2)}, u32[]{:S(2)}) collective-permute-start(f32[22,8,128]{2,1,0:T(8,128)S(1)} %collective-permute-done.6.near_even), channel_id=1, source_target_pairs={{1,3},{3,1},{2,6},{6,2},{7,5},{5,7},{9,11},{11,9},{10,14},{14,10},... | collective-permute-start | bytes 270344 | tf_op jit(solution)/shard_map/ppermute | solution.py:535

commit v3 on v2

--- a/solution.py
+++ b/solution.py
@@ -1,5 +1,3 @@
-import functools
-
 import jax
 import jax.numpy as jnp
 from jax import lax
@@ -15,6 +13,7 @@
 FINE_X = 3
 LANES = 128
 ANY = pl.BlockSpec(memory_space=pl.ANY)
+HBM = pl.BlockSpec(memory_space=pltpu.HBM)
 VMEM = pl.BlockSpec(memory_space=pltpu.VMEM)
 LIMIT = 16 * 1024 * 1024
 
@@ -30,9 +29,9 @@
     return position
 
 
-def box_parity():
+def box_position():
     bit_count = lax.axis_size("box").bit_length() - 1
-    return gray_position(lax.axis_index("box"), bit_count) & 1
+    return gray_position(lax.axis_index("box"), bit_count)
 
 
 def run_copies(pairs, sems):
@@ -128,36 +127,34 @@
     return ref[at, pl.ds(0, count, stride=2), :] + ref[at, pl.ds(1, count, stride=2), :]
 
 
-def pack_x_kernel(f, a, b, up, down, sems):
-    count = f.shape[0]
+def zero(ref, *at):
+    ref[at] = jnp.zeros_like(ref[at])
+
+
+def pack_faces_kernel(f, a, b, x_up, x_down, y_up, y_down, sems):
+    count, depth = f.shape[:2]
     pairs = []
     row = 0
-    for ref, wide in ((f, WIDE_F), (a, WIDE_F), (b, WIDE_B)):
-        pairs.append((ref.at[pl.ds(count - wide, wide)], up.at[pl.ds(row, wide)]))
-        pairs.append((ref.at[pl.ds(0, wide)], down.at[pl.ds(row, wide)]))
+    for k, (ref, wide) in enumerate(((f, WIDE_F), (a, WIDE_F), (b, WIDE_B))):
+        pairs.append((ref.at[pl.ds(count - wide, wide)], x_up.at[pl.ds(row, wide)]))
+        pairs.append((ref.at[pl.ds(0, wide)], x_down.at[pl.ds(row, wide)]))
+        pairs.append((ref.at[:, pl.ds(depth - FRAME, FRAME)], y_up.at[pl.ds(k * count, count)]))
+        pairs.append((ref.at[:, pl.ds(0, FRAME)], y_down.at[pl.ds(k * count, count)]))
         row += wide
     wait_copies(run_copies(pairs, sems))
 
 
-def pack_y_kernel(f, a, b, low, high, to_even, to_odd, sems):
-    count = f.shape[0]
-    parity = box_parity()
+def pack_corners_kernel(low, high, up, down, sems):
+    rows, depth = low.shape[:2]
     pairs = []
-    for out, start in ((to_even, FRAME * (1 - parity)), (to_odd, FRAME * parity)):
-        rows = pl.ds(pl.multiple_of(start, FRAME), FRAME)
-        row = 0
-        got = 0
-        for ref, wide in ((f, WIDE_F), (a, WIDE_F), (b, WIDE_B)):
-            pairs.append((low.at[pl.ds(got, wide), rows], out.at[pl.ds(row, wide)]))
-            pairs.append((ref.at[:, rows], out.at[pl.ds(row + wide, count)]))
-            pairs.append((high.at[pl.ds(got, wide), rows], out.at[pl.ds(row + wide + count, wide)]))
-            row += count + 2 * wide
-            got += wide
+    for k, ref in enumerate((low, high)):
+        pairs.append((ref.at[:, pl.ds(depth - FRAME, FRAME)], up.at[pl.ds(k * rows, rows)]))
+        pairs.append((ref.at[:, pl.ds(0, FRAME)], down.at[pl.ds(k * rows, rows)]))
     wait_copies(run_copies(pairs, sems))
 
 
 def down_kernel(
-    f, a, b, low, high, from_even, from_odd,
+    f, a, b, low, high, y_low, y_high, c_low, c_high,
     out_v, out_f, out_inv, out_fx, out_fy, out_fz,
     out_v1, out_f1, out_inv1, out_fx1, out_fy1, out_fz1,
     out_coarse, to_up, to_down,
@@ -166,23 +163,46 @@
 ):
     count = f.shape[0]
     depth = f.shape[1]
-    parity = box_parity()
     own_y = pl.ds(FRAME, depth)
-    even_y = pl.ds(pl.multiple_of((FRAME + depth) * (1 - parity), FRAME), FRAME)
-    odd_y = pl.ds(pl.multiple_of((FRAME + depth) * parity, FRAME), FRAME)
+    low_y = pl.ds(0, FRAME)
+    high_y = pl.ds(FRAME + depth, FRAME)
+    own_x = pl.ds(FRAME, count)
+    x_rows = low.shape[0]
     pairs = []
-    row = 0
     got = 0
-    for ref, wide, dst in ((f, WIDE_F, F), (a, WIDE_F, A), (b, WIDE_B, B)):
-        span = count + 2 * wide
-        pairs.append((ref, dst.at[pl.ds(FRAME, count), own_y]))
-        pairs.append((low.at[pl.ds(got, wide)], dst.at[pl.ds(FRAME - wide, wide), own_y]))
-        pairs.append((high.at[pl.ds(got, wide)], dst.at[pl.ds(FRAME + count, wide), own_y]))
-        for src, rows in ((from_even, even_y), (from_odd, odd_y)):
-            pairs.append((src.at[pl.ds(row, span)], dst.at[pl.ds(FRAME - wide, span), rows]))
-        row += span
+    for k, (ref, wide, dst) in enumerate(((f, WIDE_F, F), (a, WIDE_F, A), (b, WIDE_B, B))):
+        layers = pl.ds(got, wide)
+        layers_too = pl.ds(x_rows + got, wide)
+        low_x = pl.ds(FRAME - wide, wide)
+        high_x = pl.ds(FRAME + count, wide)
+        block = pl.ds(k * count, count)
+        pairs += [
+            (ref, dst.at[own_x, own_y]),
+            (low.at[layers], dst.at[low_x, own_y]),
+            (high.at[layers], dst.at[high_x, own_y]),
+            (y_low.at[block], dst.at[own_x, low_y]),
+            (y_high.at[block], dst.at[own_x, high_y]),
+            (c_low.at[layers], dst.at[low_x, low_y]),
+            (c_low.at[layers_too], dst.at[high_x, low_y]),
+            (c_high.at[layers], dst.at[low_x, high_y]),
+            (c_high.at[layers_too], dst.at[high_x, high_y]),
+        ]
         got += wide
     wait_copies(run_copies(pairs, sems))
+
+    group = lax.axis_index("grp")
+    position = box_position()
+    for edge, x, y in (
+        (group == 0, slice(0, FRAME), slice(None)),
+        (group == lax.axis_size("grp") - 1, slice(FRAME + count, None), slice(None)),
+        (position == 0, slice(None), slice(0, FRAME)),
+        (position == lax.axis_size("box") - 1, slice(None), slice(FRAME + depth, None)),
+    ):
+
+        @pl.when(edge)
+        def _(x=x, y=y):
+            for ref in (F, A, B):
+                zero(ref, x, y)
 
     faces = (FX, FY, FZ)
     end = count + 2 * FRAME
@@ -295,31 +315,26 @@
     wait_copies(out_copies)
 
 
-def pack_coarse_kernel(coarse, v1, low, high, to_even, to_odd):
-    parity = box_parity()
+def pack_coarse_kernel(coarse, v1, low, high, up, down):
     count2 = coarse.shape[0]
     first1 = FRAME // 2
     depth1 = 8
     count1 = 2 * count2
-    for out, top in ((to_even, parity == 0), (to_odd, parity == 1)):
+    for out, face in ((up, slice(depth1 - FINE_X, depth1)), (down, slice(0, FINE_X))):
         for k in range(COARSE_X):
             out[k, 0:3] = low[k, 0:3]
             out[COARSE_X + count2 + k, 0:3] = high[k, 0:3]
         for k in range(count2):
             out[COARSE_X + k, 0:3] = coarse[k, 0:3]
-
-        def facing(tile):
-            return jnp.where(top, tile[depth1 - FINE_X:], tile[:FINE_X])
-
         for k in range(FINE_X):
-            out[k, 3:3 + FINE_X] = facing(low[COARSE_X + k])
-            out[FINE_X + count1 + k, 3:3 + FINE_X] = facing(high[COARSE_X + k])
+            out[k, 3:3 + FINE_X] = low[COARSE_X + k, face]
+            out[FINE_X + count1 + k, 3:3 + FINE_X] = high[COARSE_X + k, face]
         for k in range(count1):
-            out[FINE_X + k, 3:3 + FINE_X] = facing(v1[first1 + k, first1:first1 + depth1])
+            out[FINE_X + k, 3:3 + FINE_X] = v1[first1 + k, slice(first1 + face.start, first1 + face.stop)]
 
 
 def up_kernel(
-    own, near_even, near_odd, far_even, far_odd, low, high,
+    far_low, near_low, own, near_high, far_high, low, high,
     in_v, F, IN, FX, FY, FZ,
     in_v1, F1, IN1, FX1, FY1, FZ1,
     out,
@@ -327,19 +342,26 @@
     R, S2, A2, B2, FX2, FY2, FZ2, IN2, V2, U2, PT, P0,
     sems,
 ):
-    parity = box_parity()
-    below = 1 + 2 * (1 - parity)
-    copies = run_copies(
-        [
-            (own, R.at[2]),
-            (near_even, R.at[below]),
-            (near_odd, R.at[4 - below]),
-            (far_even, R.at[4 * (1 - parity)]),
-            (far_odd, R.at[4 * parity]),
-        ],
-        sems,
-    )
-    wait_copies(copies)
+    sources = (far_low, near_low, own, near_high, far_high)
+    wait_copies(run_copies([(src, R.at[slot]) for slot, src in enumerate(sources)], sems))
+    group = lax.axis_index("grp")
+    position = box_position()
+    groups = lax.axis_size("grp")
+    blocks = lax.axis_size("box")
+    for edge, at in (
+        (position < 2, (0,)),
+        (position < 1, (1,)),
+        (position >= blocks - 1, (3,)),
+        (position >= blocks - 2, (4,)),
+        (group == 0, (slice(None), slice(0, FINE_X))),
+        (group == 0, (slice(None), slice(FINE_X, COARSE_X), slice(0, 3))),
+        (group == groups - 1, (slice(None), slice(R.shape[1] - FINE_X, None))),
+        (group == groups - 1, (slice(None), slice(B2.shape[0] - COARSE_X, R.shape[1] - FINE_X), slice(0, 3))),
+    ):
+
+        @pl.when(edge)
+        def _(at=at):
+            zero(R, *at)
 
     rows2 = B2.shape[1]
     span2 = B2.shape[0]
@@ -393,8 +415,8 @@
 
     rows_loop(0, span1 - 2 * first1, 16, own_row)
     for k in range(FINE_X):
-        V1[first1 - FINE_X + k, own_rows] = low[COARSE_X + k]
-        V1[span1 - first1 + k, own_rows] = high[COARSE_X + k]
+        V1[first1 - FINE_X + k, own_rows] = jnp.where(group > 0, low[COARSE_X + k], 0.0)
+        V1[span1 - first1 + k, own_rows] = jnp.where(group < groups - 1, high[COARSE_X + k], 0.0)
 
     def add_coarse(x):
         half = coarse[x + COARSE_X - first1 // 2, first1:first1 + depth1]
@@ -464,10 +486,12 @@
     groups = lax.axis_size("grp")
     blocks = lax.axis_size("box")
     code = [p ^ (p >> 1) for p in range(blocks)]
-    up_perm = [(i, i + 1) for i in range(groups - 1)]
-    down_perm = [(i + 1, i) for i in range(groups - 1)]
-    even_perm = [(code[p], code[p ^ 1]) for p in range(blocks)]
-    odd_perm = [(code[p], code[((p - 1) ^ 1) + 1]) for p in range(1, blocks - 1)]
+
+    def along_x(array, by):
+        return lax.ppermute(array, "grp", [(i, (i + by) % groups) for i in range(groups)])
+
+    def along_y(array, by):
+        return lax.ppermute(array, "box", [(code[p], code[(p + by) % blocks]) for p in range(blocks)])
 
     def arr(*shape):
         return jax.ShapeDtypeStruct(shape, jnp.float32)
@@ -477,28 +501,30 @@
 
     dma = pltpu.SemaphoreType.DMA
     x_rows = 2 * WIDE_F + WIDE_B
-    up, down = pl.pallas_call(
-        pack_x_kernel,
-        out_shape=[arr(x_rows, depth, lanes)] * 2,
-        in_specs=[ANY] * 3,
-        out_specs=[VMEM] * 2,
-        scratch_shapes=[dma((6,))],
+    faces_out = [arr(x_rows, depth, lanes)] * 2 + [arr(3 * count, FRAME, lanes)] * 2
+    x_up, x_down, y_up, y_down = pl.pallas_call(
+        pack_faces_kernel,
+        out_shape=faces_out,
+        in_specs=[HBM] * 3,
+        out_specs=[VMEM] * 4,
+        scratch_shapes=[dma((12,))],
         compiler_params=params(),
     )(f, a, b)
-    low = lax.ppermute(up, "grp", up_perm)
-    high = lax.ppermute(down, "grp", down_perm)
-
-    y_rows = 3 * count + 2 * x_rows
-    to_even, to_odd = pl.pallas_call(
-        pack_y_kernel,
-        out_shape=[arr(y_rows, FRAME, lanes)] * 2,
-        in_specs=[ANY] * 5,
+    low = along_x(x_up, 1)
+    high = along_x(x_down, -1)
+    y_low = along_y(y_up, 1)
+    y_high = along_y(y_down, -1)
+
+    c_up, c_down = pl.pallas_call(
+        pack_corners_kernel,
+        out_shape=[arr(2 * x_rows, FRAME, lanes)] * 2,
+        in_specs=[ANY] * 2,
         out_specs=[VMEM] * 2,
-        scratch_shapes=[dma((18,))],
+        scratch_shapes=[dma((4,))],
         compiler_params=params(),
-    )(f, a, b, low, high)
-    from_even = lax.ppermute(to_even, "box", even_perm)
-    from_odd = lax.ppermute(to_odd, "box", odd_perm)
+    )(low, high)
+    c_low = along_y(c_up, 1)
+    c_high = along_y(c_down, -1)
 
     framed = (count + 2 * FRAME, depth + 2 * FRAME, lanes)
     framed1 = (framed[0] // 2, framed[1] // 2, lanes)
@@ -509,31 +535,31 @@
         down_kernel,
         out_shape=[arr(*kept)] * 6 + [arr(*framed1)] * 6
         + [arr(count2, 8, lanes)] + [arr(x2_tiles, 8, lanes)] * 2,
-        in_specs=[ANY] * 7,
+        in_specs=[ANY] * 9,
         out_specs=[ANY] * 6 + [VMEM] * 9,
         scratch_shapes=[vm(*framed)] * 10
         + [vm(framed1[0], framed[1], lanes)] + [vm(*framed1)] * 4
-        + [vm(3, count2, framed1[1], lanes), vm(8, 128), dma((15,)), dma((6,))],
+        + [vm(3, count2, framed1[1], lanes), vm(8, 128), dma((27,)), dma((6,))],
         compiler_params=params(),
-    )(f, a, b, low, high, from_even, from_odd)
+    )(f, a, b, low, high, y_low, y_high, c_low, c_high)
     state0 = results[:6]
     state1 = results[6:12]
     coarse, to_up, to_down = results[12:]
 
-    low2 = lax.ppermute(to_up, "grp", up_perm)
-    high2 = lax.ppermute(to_down, "grp", down_perm)
+    low2 = along_x(to_up, 1)
+    high2 = along_x(to_down, -1)
     span = framed1[0] - 2 * (FRAME // 2 - FINE_X)
-    even2, odd2 = pl.pallas_call(
+    up2, down2 = pl.pallas_call(
         pack_coarse_kernel,
         out_shape=[arr(span, 8, lanes)] * 2,
         in_specs=[VMEM] * 4,
         out_specs=[VMEM] * 2,
         compiler_params=params(),
     )(coarse, state1[0], low2, high2)
-    near_even = lax.ppermute(even2, "box", even_perm)
-    near_odd = lax.ppermute(odd2, "box", odd_perm)
-    far_odd = lax.ppermute(near_even, "box", odd_perm)
-    far_even = lax.ppermute(near_odd, "box", even_perm)
+    near_low = along_y(up2, 1)
+    near_high = along_y(down2, -1)
+    far_low = along_y(up2, 2)
+    far_high = along_y(down2, -2)
 
     framed2 = (count2 + 2 * COARSE_X, depth // 4 + 2 * COARSE_X, lanes)
     out = pl.pallas_call(
@@ -546,7 +572,7 @@
         + [vm(framed1[0] // 2, framed1[1], lanes), vm(kept[0] // 2, kept[1], lanes)]
         + [dma((5,))],
         compiler_params=params(),
-    )(even2, near_even, near_odd, far_even, far_odd, low2, high2, *state0, *state1)
+    )(far_low, near_low, up2, near_high, far_high, low2, high2, *state0, *state1)
     return out[:, None]
 
 

time: 66.8 us -> 49.2 us (0.74)
  the two profiles are of different devices: /device:TPU:8 before, /device:TPU:1 now
where the time goes in v3:
time: 49.2 us; the launch traced here: 49 us
  starting transfers between devices  18.3 us (37%)
  waiting for transfers between devices  17.8 us (36%)
  Pallas kernels  10.1 us (21%)
  local copies, waits for them, and re-layouts  2.86 us (6%)
    ppermute x8, starting transfers between devices, along_y(): lax.ppermute(array, 'box', [(code[p], code[(p + by) % blocks]) for p in r...  13.5 us
    ppermute x8, waiting for transfers between devices, along_y(): lax.ppermute(array, 'box', [(code[p], code[(p + by) % blocks]) for p in r...  10.9 us
    ppermute x4, waiting for transfers between devices, along_x(): lax.ppermute(array, 'grp', [(i, (i + by) % groups) for i in range(groups)])  6.89 us
    pallas_call x1, Pallas kernels, body(): pl.pallas_call(up_kernel, out_shape=arr(count, depth, lanes), in_specs=[A...  4.84 us
    ppermute x4, starting transfers between devices, along_x(): lax.ppermute(array, 'grp', [(i, (i + by) % groups) for i in range(groups)])  4.78 us
    pallas_call x1, Pallas kernels, body(): pl.pallas_call(down_kernel, out_shape=[arr(*kept)] * 6 + [arr(*framed1)]...  4.57 us
    unnamed x12, local copies, waits for them, and re-layouts  2.86 us
  transfers between devices with their start and end apart: 12, of which 9 were waited for; matrix products, arithmetic and copies ran while one was open for 0% of the time, Pallas kernels for 0%

profile of v3, /device:TPU:1, one launch (start us, length us, event | category | flops | bytes accessed | tf_op | source)
XLA Modules:
  0.0 49.0 jit_solution(11360097371482814978)
XLA Ops:
  0.0 0.9 %copy-done = f32[32,1,16,128]{3,2,1,0:T(8,128)S(1)} copy-done((f32[32,1,16,128]{3,2,1,0:T(8,128)S(1)}, f32[32,1,16,128]{3,2,1,0:T(8,128)}, u32[]{:S(2)}) %copy-start) | copy-done | bytes 262168
  1.0 0.9 %copy-done.2 = f32[32,1,16,128]{3,2,1,0:T(8,128)S(1)} copy-done((f32[32,1,16,128]{3,2,1,0:T(8,128)S(1)}, f32[32,1,16,128]{3,2,1,0:T(8,128)}, u32[]{:S(2)}) %copy-start.2) | copy-done | bytes 262168
  1.9 0.9 %copy-done.4 = f32[32,1,16,128]{3,2,1,0:T(8,128)S(1)} copy-done((f32[32,1,16,128]{3,2,1,0:T(8,128)S(1)}, f32[32,1,16,128]{3,2,1,0:T(8,128)}, u32[]{:S(2)}) %copy-start.4) | copy-done | bytes 262168
  2.9 0.6 %shard_map.37 = (f32[19,16,128]{2,1,0:T(8,128)S(1)}, f32[19,16,128]{2,1,0:T(8,128)S(1)}, f32[96,8,128]{2,1,0:T(8,128)S(1)}, f32[96,8,128]{2,1,0:T(8,128)S(1)}) custom-call(f32[32,16,128]{2,1,0:T(8,128)S(1)} %bitcast.6, f32[32,16,128]{2,1,0:T(8,128)S(1)} %bitcast.8, f32[32,16,128]{2,1,0:T(8,128)S(1)} %bitcast.10), custom_call_target="tpu_custom_call" | custom-call | tf_op jit(solution)/shard_map/pallas_call | solution.py:505
  3.4 2.2 %collective-permute-start.2 = (f32[96,8,128]{2,1,0:T(8,128)S(1)}, f32[96,8,128]{2,1,0:T(8,128)S(1)}, u32[]{:S(2)}, u32[]{:S(2)}) collective-permute-start(f32[96,8,128]{2,1,0:T(8,128)S(1)} %get-tuple-element.30), channel_id=1, source_target_pairs={{0,1},{1,3},{3,2},{2,6},{6,7},{7,5},{5,4},{4,0},{8,9},{9,11},{11,1... | collective-permute-start | bytes 1179656 | tf_op jit(solution)/shard_map/ppermute | solution.py:494
  5.6 1.2 %collective-permute-start = (f32[19,16,128]{2,1,0:T(8,128)S(1)}, f32[19,16,128]{2,1,0:T(8,128)S(1)}, u32[]{:S(2)}, u32[]{:S(2)}) collective-permute-start(f32[19,16,128]{2,1,0:T(8,128)S(1)} %get-tuple-element.28), channel_id=1, source_target_pairs={{0,8},{8,16},{16,24},{24,0},{1,9},{9,17},{17,25},{25,1},{2,10},{10... | collective-permute-start | bytes 466952 | tf_op jit(solution)/shard_map/ppermute | solution.py:491
  6.8 1.2 %collective-permute-start.1 = (f32[19,16,128]{2,1,0:T(8,128)S(1)}, f32[19,16,128]{2,1,0:T(8,128)S(1)}, u32[]{:S(2)}, u32[]{:S(2)}) collective-permute-start(f32[19,16,128]{2,1,0:T(8,128)S(1)} %get-tuple-element.29), channel_id=1, source_target_pairs={{0,24},{8,0},{16,8},{24,16},{1,25},{9,1},{17,9},{25,17},{2,26},{10... | collective-permute-start | bytes 466952 | tf_op jit(solution)/shard_map/ppermute | solution.py:491
  8.0 2.9 %collective-permute-done.low = f32[19,16,128]{2,1,0:T(8,128)S(1)} collective-permute-done((f32[19,16,128]{2,1,0:T(8,128)S(1)}, f32[19,16,128]{2,1,0:T(8,128)S(1)}, u32[]{:S(2)}, u32[]{:S(2)}) %collective-permute-start) | collective-permute-done | bytes 155680 | tf_op jit(solution)/shard_map/ppermute | solution.py:491
  10.9 2.2 %collective-permute-done.1.high = f32[19,16,128]{2,1,0:T(8,128)S(1)} collective-permute-done((f32[19,16,128]{2,1,0:T(8,128)S(1)}, f32[19,16,128]{2,1,0:T(8,128)S(1)}, u32[]{:S(2)}, u32[]{:S(2)}) %collective-permute-start.1) | collective-permute-done | bytes 155680 | tf_op jit(solution)/shard_map/ppermute | solution.py:491
  13.2 2.0 %collective-permute-start.4 = (f32[38,8,128]{2,1,0:T(8,128)S(1)}, f32[38,8,128]{2,1,0:T(8,128)S(1)}, u32[]{:S(2)}, u32[]{:S(2)}) collective-permute-start(f32[38,8,128]{2,1,0:T(8,128)S(1)} %get-tuple-element.32), channel_id=1, source_target_pairs={{0,1},{1,3},{3,2},{2,6},{6,7},{7,5},{5,4},{4,0},{8,9},{9,11},{11,1... | collective-permute-start | bytes 466952 | tf_op jit(solution)/shard_map/ppermute | solution.py:494
  15.2 1.3 %collective-permute-start.5 = (f32[38,8,128]{2,1,0:T(8,128)S(1)}, f32[38,8,128]{2,1,0:T(8,128)S(1)}, u32[]{:S(2)}, u32[]{:S(2)}) collective-permute-start(f32[38,8,128]{2,1,0:T(8,128)S(1)} %get-tuple-element.33), channel_id=1, source_target_pairs={{0,4},{1,0},{3,1},{2,3},{6,2},{7,6},{5,7},{4,5},{8,12},{9,8},{11,9... | collective-permute-start | bytes 466952 | tf_op jit(solution)/shard_map/ppermute | solution.py:494
  16.6 0.8 %collective-permute-done.4.c_low = f32[38,8,128]{2,1,0:T(8,128)S(1)} collective-permute-done((f32[38,8,128]{2,1,0:T(8,128)S(1)}, f32[38,8,128]{2,1,0:T(8,128)S(1)}, u32[]{:S(2)}, u32[]{:S(2)}) %collective-permute-start.4) | collective-permute-done | bytes 155680 | tf_op jit(solution)/shard_map/ppermute | solution.py:494
  17.4 4.9 %collective-permute-done.5.c_high = f32[38,8,128]{2,1,0:T(8,128)S(1)} collective-permute-done((f32[38,8,128]{2,1,0:T(8,128)S(1)}, f32[38,8,128]{2,1,0:T(8,128)S(1)}, u32[]{:S(2)}, u32[]{:S(2)}) %collective-permute-start.5) | collective-permute-done | bytes 155680 | tf_op jit(solution)/shard_map/ppermute | solution.py:494
  22.3 4.6 %shard_map.39 = (f32[36,32,128]{2,1,0:T(8,128)S(1)}, f32[36,32,128]{2,1,0:T(8,128)S(1)}, f32[36,32,128]{2,1,0:T(8,128)S(1)}, f32[36,32,128]{2,1,0:T(8,128)S(1)},...) custom-call(f32[32,16,128]{2,1,0:T(8,128)S(1)} %bitcast.7, ...), custom_call_target="tpu_custom_call" | custom-call | tf_op jit(solution)/shard_map/pallas_call | solution.py:534
  26.9 1.2 %collective-permute-start.6 = (f32[9,8,128]{2,1,0:T(8,128)S(1)}, f32[9,8,128]{2,1,0:T(8,128)S(1)}, u32[]{:S(2)}, u32[]{:S(2)}) collective-permute-start(f32[9,8,128]{2,1,0:T(8,128)S(1)} %get-tuple-element.36), channel_id=1, source_target_pairs={{0,8},{8,16},{16,24},{24,0},{1,9},{9,17},{17,25},{25,1},{2,10},{10... | collective-permute-start | bytes 110600 | tf_op jit(solution)/shard_map/ppermute | solution.py:491
  28.1 1.2 %collective-permute-start.7 = (f32[9,8,128]{2,1,0:T(8,128)S(1)}, f32[9,8,128]{2,1,0:T(8,128)S(1)}, u32[]{:S(2)}, u32[]{:S(2)}) collective-permute-start(f32[9,8,128]{2,1,0:T(8,128)S(1)} %get-tuple-element.37), channel_id=1, source_target_pairs={{0,24},{8,0},{16,8},{24,16},{1,25},{9,1},{17,9},{25,17},{2,26},{10... | collective-permute-start | bytes 110600 | tf_op jit(solution)/shard_map/ppermute | solution.py:491
  29.3 1.3 %collective-permute-done.6.low = f32[9,8,128]{2,1,0:T(8,128)S(1)} collective-permute-done((f32[9,8,128]{2,1,0:T(8,128)S(1)}, f32[9,8,128]{2,1,0:T(8,128)S(1)}, u32[]{:S(2)}, u32[]{:S(2)}) %collective-permute-start.6) | collective-permute-done | bytes 36896 | tf_op jit(solution)/shard_map/ppermute | solution.py:491
  30.7 0.4 collective-permute-done.7.high
  31.1 4.4 %collective-permute-start.11 = (f32[22,8,128]{2,1,0:T(8,128)S(1)}, f32[22,8,128]{2,1,0:T(8,128)S(1)}, u32[]{:S(2)}, u32[]{:S(2)}) collective-permute-start(f32[22,8,128]{2,1,0:T(8,128)S(1)} %get-tuple-element.39), channel_id=1, source_target_pairs={{0,5},{1,4},{3,0},{2,1},{6,3},{7,2},{5,6},{4,7},{8,13},{9,12},{11,... | collective-permute-start | bytes 270344 | tf_op jit(solution)/shard_map/ppermute | solution.py:494
  35.5 1.5 %collective-permute-start.9 = (f32[22,8,128]{2,1,0:T(8,128)S(1)}, f32[22,8,128]{2,1,0:T(8,128)S(1)}, u32[]{:S(2)}, u32[]{:S(2)}) collective-permute-start(f32[22,8,128]{2,1,0:T(8,128)S(1)} %get-tuple-element.38.own), channel_id=1, source_target_pairs={{0,1},{1,3},{3,2},{2,6},{6,7},{7,5},{5,4},{4,0},{8,9},{9,11},{11,1... | collective-permute-start | bytes 270344 | tf_op jit(solution)/shard_map/ppermute | solution.py:494
  37.0 2.1 %collective-permute-start.8 = (f32[22,8,128]{2,1,0:T(8,128)S(1)}, f32[22,8,128]{2,1,0:T(8,128)S(1)}, u32[]{:S(2)}, u32[]{:S(2)}) collective-permute-start(f32[22,8,128]{2,1,0:T(8,128)S(1)} %get-tuple-element.38.own), channel_id=1, source_target_pairs={{0,3},{1,2},{3,6},{2,7},{6,5},{7,4},{5,0},{4,1},{8,11},{9,10},{11,... | collective-permute-start | bytes 270344 | tf_op jit(solution)/shard_map/ppermute | solution.py:494
  39.2 0.2 collective-permute-done.9.near_low
  39.4 4.8 %collective-permute-done.8.far_low = f32[22,8,128]{2,1,0:T(8,128)S(1)} collective-permute-done((f32[22,8,128]{2,1,0:T(8,128)S(1)}, f32[22,8,128]{2,1,0:T(8,128)S(1)}, u32[]{:S(2)}, u32[]{:S(2)}) %collective-permute-start.8) | collective-permute-done | bytes 90144 | tf_op jit(solution)/shard_map/ppermute | solution.py:494
  44.2 4.8 %shard_map.41 = f32[32,16,128]{2,1,0:T(8,128)} custom-call(f32[22,8,128]{2,1,0:T(8,128)S(1)} %collective-permute-done.8.far_low, f32[22,8,128]{2,1,0:T(8,128)S(1)} %collective-permute-done.9.near_low, f32[22,8,128]{2,1,0:T(8,128)S(1)} %get-tuple-element.38.own, f32[22,8,128]{2,1,0:T(8,128)S(1)} %collective-permute-done.10.near_high, ...), custom_call_target="tpu_custom_call" | custom-call | tf_op jit(solution)/shard_map/pallas_call | solution.py:565
  (17 shorter events, 0.3 us)
Async XLA Ops:
  0.0 0.9 %copy-start = (f32[32,1,16,128]{3,2,1,0:T(8,128)S(1)}, f32[32,1,16,128]{3,2,1,0:T(8,128)}, u32[]{:S(2)}) copy-start(f32[32,1,16,128]{3,2,1,0:T(8,128)} %param.3) | copy-start | bytes 786436
  1.0 0.9 %copy-start.2 = (f32[32,1,16,128]{3,2,1,0:T(8,128)S(1)}, f32[32,1,16,128]{3,2,1,0:T(8,128)}, u32[]{:S(2)}) copy-start(f32[32,1,16,128]{3,2,1,0:T(8,128)} %param.4) | copy-start | bytes 786436
  1.9 0.9 %copy-start.4 = (f32[32,1,16,128]{3,2,1,0:T(8,128)S(1)}, f32[32,1,16,128]{3,2,1,0:T(8,128)}, u32[]{:S(2)}) copy-start(f32[32,1,16,128]{3,2,1,0:T(8,128)} %param.5) | copy-start | bytes 786436
  2.9 19.4 %copy-start.3 = (f32[32,1,16,128]{3,2,1,0:T(8,128)S(1)}, f32[32,1,16,128]{3,2,1,0:T(8,128)}, u32[]{:S(2)}) copy-start(f32[32,1,16,128]{3,2,1,0:T(8,128)} %param.4) | copy-start | bytes 786436
  2.9 19.4 %copy-start.5 = (f32[32,1,16,128]{3,2,1,0:T(8,128)S(1)}, f32[32,1,16,128]{3,2,1,0:T(8,128)}, u32[]{:S(2)}) copy-start(f32[32,1,16,128]{3,2,1,0:T(8,128)} %param.5) | copy-start | bytes 786436
  3.4 18.9 %copy-start.1 = (f32[32,1,16,128]{3,2,1,0:T(8,128)S(1)}, f32[32,1,16,128]{3,2,1,0:T(8,128)}, u32[]{:S(2)}) copy-start(f32[32,1,16,128]{3,2,1,0:T(8,128)} %param.3) | copy-start | bytes 786436
  3.4 18.8 %collective-permute-start.2 = (f32[96,8,128]{2,1,0:T(8,128)S(1)}, f32[96,8,128]{2,1,0:T(8,128)S(1)}, u32[]{:S(2)}, u32[]{:S(2)}) collective-permute-start(f32[96,8,128]{2,1,0:T(8,128)S(1)} %get-tuple-element.30), channel_id=1, source_target_pairs={{0,1},{1,3},{3,2},{2,6},{6,7},{7,5},{5,4},{4,0},{8,9},{9,11},{11,1... | collective-permute-start | bytes 1179656 | tf_op jit(solution)/shard_map/ppermute | solution.py:494
  5.6 16.7 %collective-permute-start.3 = (f32[96,8,128]{2,1,0:T(8,128)S(1)}, f32[96,8,128]{2,1,0:T(8,128)S(1)}, u32[]{:S(2)}, u32[]{:S(2)}) collective-permute-start(f32[96,8,128]{2,1,0:T(8,128)S(1)} %get-tuple-element.31), channel_id=1, source_target_pairs={{0,4},{1,0},{3,1},{2,3},{6,2},{7,6},{5,7},{4,5},{8,12},{9,8},{11,9... | collective-permute-start | bytes 1179656 | tf_op jit(solution)/shard_map/ppermute | solution.py:494
  5.6 5.3 %collective-permute-start = (f32[19,16,128]{2,1,0:T(8,128)S(1)}, f32[19,16,128]{2,1,0:T(8,128)S(1)}, u32[]{:S(2)}, u32[]{:S(2)}) collective-permute-start(f32[19,16,128]{2,1,0:T(8,128)S(1)} %get-tuple-element.28), channel_id=1, source_target_pairs={{0,8},{8,16},{16,24},{24,0},{1,9},{9,17},{17,25},{25,1},{2,10},{10... | collective-permute-start | bytes 466952 | tf_op jit(solution)/shard_map/ppermute | solution.py:491
  6.8 6.3 %collective-permute-start.1 = (f32[19,16,128]{2,1,0:T(8,128)S(1)}, f32[19,16,128]{2,1,0:T(8,128)S(1)}, u32[]{:S(2)}, u32[]{:S(2)}) collective-permute-start(f32[19,16,128]{2,1,0:T(8,128)S(1)} %get-tuple-element.29), channel_id=1, source_target_pairs={{0,24},{8,0},{16,8},{24,16},{1,25},{9,1},{17,9},{25,17},{2,26},{10... | collective-permute-start | bytes 466952 | tf_op jit(solution)/shard_map/ppermute | solution.py:491
  13.2 4.2 %collective-permute-start.4 = (f32[38,8,128]{2,1,0:T(8,128)S(1)}, f32[38,8,128]{2,1,0:T(8,128)S(1)}, u32[]{:S(2)}, u32[]{:S(2)}) collective-permute-start(f32[38,8,128]{2,1,0:T(8,128)S(1)} %get-tuple-element.32), channel_id=1, source_target_pairs={{0,1},{1,3},{3,2},{2,6},{6,7},{7,5},{5,4},{4,0},{8,9},{9,11},{11,1... | collective-permute-start | bytes 466952 | tf_op jit(solution)/shard_map/ppermute | solution.py:494
  15.2 7.0 %collective-permute-start.5 = (f32[38,8,128]{2,1,0:T(8,128)S(1)}, f32[38,8,128]{2,1,0:T(8,128)S(1)}, u32[]{:S(2)}, u32[]{:S(2)}) collective-permute-start(f32[38,8,128]{2,1,0:T(8,128)S(1)} %get-tuple-element.33), channel_id=1, source_target_pairs={{0,4},{1,0},{3,1},{2,3},{6,2},{7,6},{5,7},{4,5},{8,12},{9,8},{11,9... | collective-permute-start | bytes 466952 | tf_op jit(solution)/shard_map/ppermute | solution.py:494
  26.9 3.8 %collective-permute-start.6 = (f32[9,8,128]{2,1,0:T(8,128)S(1)}, f32[9,8,128]{2,1,0:T(8,128)S(1)}, u32[]{:S(2)}, u32[]{:S(2)}) collective-permute-start(f32[9,8,128]{2,1,0:T(8,128)S(1)} %get-tuple-element.36), channel_id=1, source_target_pairs={{0,8},{8,16},{16,24},{24,0},{1,9},{9,17},{17,25},{25,1},{2,10},{10... | collective-permute-start | bytes 110600 | tf_op jit(solution)/shard_map/ppermute | solution.py:491
  28.1 2.9 %collective-permute-start.7 = (f32[9,8,128]{2,1,0:T(8,128)S(1)}, f32[9,8,128]{2,1,0:T(8,128)S(1)}, u32[]{:S(2)}, u32[]{:S(2)}) collective-permute-start(f32[9,8,128]{2,1,0:T(8,128)S(1)} %get-tuple-element.37), channel_id=1, source_target_pairs={{0,24},{8,0},{16,8},{24,16},{1,25},{9,1},{17,9},{25,17},{2,26},{10... | collective-permute-start | bytes 110600 | tf_op jit(solution)/shard_map/ppermute | solution.py:491
  31.1 7.9 %collective-permute-start.11 = (f32[22,8,128]{2,1,0:T(8,128)S(1)}, f32[22,8,128]{2,1,0:T(8,128)S(1)}, u32[]{:S(2)}, u32[]{:S(2)}) collective-permute-start(f32[22,8,128]{2,1,0:T(8,128)S(1)} %get-tuple-element.39), channel_id=1, source_target_pairs={{0,5},{1,4},{3,0},{2,1},{6,3},{7,2},{5,6},{4,7},{8,13},{9,12},{11,... | collective-permute-start | bytes 270344 | tf_op jit(solution)/shard_map/ppermute | solution.py:494
  35.5 3.7 %collective-permute-start.10 = (f32[22,8,128]{2,1,0:T(8,128)S(1)}, f32[22,8,128]{2,1,0:T(8,128)S(1)}, u32[]{:S(2)}, u32[]{:S(2)}) collective-permute-start(f32[22,8,128]{2,1,0:T(8,128)S(1)} %get-tuple-element.39), channel_id=1, source_target_pairs={{0,4},{1,0},{3,1},{2,3},{6,2},{7,6},{5,7},{4,5},{8,12},{9,8},{11,9... | collective-permute-start | bytes 270344 | tf_op jit(solution)/shard_map/ppermute | solution.py:494
  35.5 3.9 %collective-permute-start.9 = (f32[22,8,128]{2,1,0:T(8,128)S(1)}, f32[22,8,128]{2,1,0:T(8,128)S(1)}, u32[]{:S(2)}, u32[]{:S(2)}) collective-permute-start(f32[22,8,128]{2,1,0:T(8,128)S(1)} %get-tuple-element.38.own), channel_id=1, source_target_pairs={{0,1},{1,3},{3,2},{2,6},{6,7},{7,5},{5,4},{4,0},{8,9},{9,11},{11,1... | collective-permute-start | bytes 270344 | tf_op jit(solution)/shard_map/ppermute | solution.py:494
  37.0 7.2 %collective-permute-start.8 = (f32[22,8,128]{2,1,0:T(8,128)S(1)}, f32[22,8,128]{2,1,0:T(8,128)S(1)}, u32[]{:S(2)}, u32[]{:S(2)}) collective-permute-start(f32[22,8,128]{2,1,0:T(8,128)S(1)} %get-tuple-element.38.own), channel_id=1, source_target_pairs={{0,3},{1,2},{3,6},{2,7},{6,5},{7,4},{5,0},{4,1},{8,11},{9,10},{11,... | collective-permute-start | bytes 270344 | tf_op jit(solution)/shard_map/ppermute | solution.py:494

commit v4 on v3

--- a/solution.py
+++ b/solution.py
@@ -155,11 +155,10 @@
 
 def down_kernel(
     f, a, b, low, high, y_low, y_high, c_low, c_high,
-    out_v, out_f, out_inv, out_fx, out_fy, out_fz,
+    U, F, IN, FX, FY, FZ,
     out_v1, out_f1, out_inv1, out_fx1, out_fy1, out_fz1,
     out_coarse, to_up, to_down,
-    F, A, B, FX, FY, FZ, DG, IN, V, U,
-    T, A1, B1, D1, W1, T1, T2, sems, out_sems,
+    A, B, DG, V, T, A1, B1, D1, W1, T1, sems,
 ):
     count = f.shape[0]
     depth = f.shape[1]
@@ -215,18 +214,10 @@
 
     rows_loop(2, end - 2, 11, coef_row)
 
-    kept = pl.ds(FRAME - 2, count + 4)
-    outs = [(F, out_f), (IN, out_inv), (FX, out_fx), (FY, out_fy), (FZ, out_fz)]
-    out_copies = run_copies([(src.at[kept], dst) for src, dst in outs], out_sems)
-
     def sweep_row(i):
         return [(U, i, relaxed(i, V, F, IN, faces, 1))]
 
     rows_loop(3, end - 3, 14, sweep_row)
-    last = pltpu.make_async_copy(U.at[kept], out_v, out_sems.at[5])
-    last.start()
-    out_copies.append(last)
-
     def residual(i):
         here, off = off_sum(i, U, faces, 1)
         return F[i] - DG[i] * here + off
@@ -300,37 +291,47 @@
             packed = jnp.zeros((1, LANES), jnp.float32)
             for y in range(depth2):
                 packed = packed + jnp.where(lane % depth2 == y, value[own2 + y:own2 + y + 1], 0.0)
-            stores.append((out_coarse, (x, slice(k, k + 1)), packed))
+            stores.append((out_coarse, pl.ds(k * count2 + x, 1), packed))
         return stores
 
     rows_loop(0, count2, 8, coarse_pack)
 
     own1 = slice(first1, first1 + depth // 2)
-    for k in range(COARSE_X):
-        to_up[k, 0:3] = out_coarse[count2 - COARSE_X + k, 0:3]
-        to_down[k, 0:3] = out_coarse[k, 0:3]
+    for k in range(3):
+        rows = slice(k * COARSE_X, (k + 1) * COARSE_X)
+        to_up[rows] = out_coarse[(k + 1) * count2 - COARSE_X:(k + 1) * count2]
+        to_down[rows] = out_coarse[k * count2:k * count2 + COARSE_X]
     for k in range(FINE_X):
-        to_up[COARSE_X + k] = out_v1[first1 + count1 - FINE_X + k, own1]
-        to_down[COARSE_X + k] = out_v1[first1 + k, own1]
-    wait_copies(out_copies)
-
-
-def pack_coarse_kernel(coarse, v1, low, high, up, down):
-    count2 = coarse.shape[0]
+        rows = slice(3 * COARSE_X + k * depth // 2, 3 * COARSE_X + (k + 1) * depth // 2)
+        to_up[rows] = out_v1[first1 + count1 - FINE_X + k, own1]
+        to_down[rows] = out_v1[first1 + k, own1]
+
+
+def pack_coarse_kernel(coarse, v1, low, high, far, near_up, near_down):
+    count2 = coarse.shape[0] // 3
+    span2 = count2 + 2 * COARSE_X
     first1 = FRAME // 2
-    depth1 = 8
+    depth1 = v1.shape[1] - FRAME
     count1 = 2 * count2
-    for out, face in ((up, slice(depth1 - FINE_X, depth1)), (down, slice(0, FINE_X))):
-        for k in range(COARSE_X):
-            out[k, 0:3] = low[k, 0:3]
-            out[COARSE_X + count2 + k, 0:3] = high[k, 0:3]
-        for k in range(count2):
-            out[COARSE_X + k, 0:3] = coarse[k, 0:3]
+    for k in range(3):
+        row = k * span2
+        part = slice(k * COARSE_X, (k + 1) * COARSE_X)
+        far[row:row + COARSE_X] = low[part]
+        far[row + COARSE_X:row + COARSE_X + count2] = coarse[k * count2:(k + 1) * count2]
+        far[row + COARSE_X + count2:row + span2] = high[part]
+    rows = far.shape[0]
+    for out, face in ((near_up, depth1 - FINE_X), (near_down, 0)):
+        out[0:rows] = far[...]
+        row = rows
         for k in range(FINE_X):
-            out[k, 3:3 + FINE_X] = low[COARSE_X + k, face]
-            out[FINE_X + count1 + k, 3:3 + FINE_X] = high[COARSE_X + k, face]
+            start = 3 * COARSE_X + k * depth1 + face
+            out[row:row + FINE_X] = low[start:start + FINE_X]
+            last = row + FINE_X * (FINE_X + count1)
+            out[last:last + FINE_X] = high[start:start + FINE_X]
+            row += FINE_X
         for k in range(count1):
-            out[FINE_X + k, 3:3 + FINE_X] = v1[first1 + k, slice(first1 + face.start, first1 + face.stop)]
+            out[row:row + FINE_X] = v1[first1 + k, first1 + face:first1 + face + FINE_X]
+            row += FINE_X
 
 
 def up_kernel(
@@ -339,44 +340,32 @@
     in_v1, F1, IN1, FX1, FY1, FZ1,
     out,
     V, U, V1, U1,
-    R, S2, A2, B2, FX2, FY2, FZ2, IN2, V2, U2, PT, P0,
-    sems,
+    S2, A2, B2, FX2, FY2, FZ2, IN2, V2, U2, PT, P0,
 ):
     sources = (far_low, near_low, own, near_high, far_high)
-    wait_copies(run_copies([(src, R.at[slot]) for slot, src in enumerate(sources)], sems))
     group = lax.axis_index("grp")
     position = box_position()
-    groups = lax.axis_size("grp")
-    blocks = lax.axis_size("box")
-    for edge, at in (
-        (position < 2, (0,)),
-        (position < 1, (1,)),
-        (position >= blocks - 1, (3,)),
-        (position >= blocks - 2, (4,)),
-        (group == 0, (slice(None), slice(0, FINE_X))),
-        (group == 0, (slice(None), slice(FINE_X, COARSE_X), slice(0, 3))),
-        (group == groups - 1, (slice(None), slice(R.shape[1] - FINE_X, None))),
-        (group == groups - 1, (slice(None), slice(B2.shape[0] - COARSE_X, R.shape[1] - FINE_X), slice(0, 3))),
-    ):
-
-        @pl.when(edge)
-        def _(at=at):
-            zero(R, *at)
+    last_group = lax.axis_size("grp") - 1
+    last_block = lax.axis_size("box") - 1
+    depth = out.shape[1]
 
     rows2 = B2.shape[1]
     span2 = B2.shape[0]
     sub = lax.broadcasted_iota(jnp.int32, (rows2, LANES), 0)
     lane = lane_ids((rows2, LANES))
     block = (sub + 2) // 4
-    mine = lane % 4 == (sub + 2) % 4
+    cell = position * (depth // 4) + sub - COARSE_X
+    inside = (cell >= 0) & (cell < (last_block + 1) * (depth // 4))
+    mine = (lane % 4 == (sub + 2) % 4) & inside
     last_of_four = lane % 4 == 3
 
     def unpack_row(x):
         stores = []
         for k, dst in enumerate((S2, A2, B2)):
-            packed = jnp.broadcast_to(R[0, x, k:k + 1], (rows2, LANES))
+            row = pl.ds(k * span2 + x, 1)
+            packed = jnp.broadcast_to(sources[0][row], (rows2, LANES))
             for slot in range(1, 5):
-                packed = jnp.where(block == slot, jnp.broadcast_to(R[slot, x, k:k + 1], (rows2, LANES)), packed)
+                packed = jnp.where(block == slot, jnp.broadcast_to(sources[slot][row], (rows2, LANES)), packed)
             t = jnp.where(mine, packed, 0.0)
             t = t + z_prev(t, 1)
             t = t + z_prev(t, 2)
@@ -386,6 +375,13 @@
         return stores
 
     rows_loop(0, span2, 5, unpack_row)
+    for edge, rows in ((group == 0, slice(0, COARSE_X)), (group == last_group, slice(span2 - COARSE_X, span2))):
+
+        @pl.when(edge)
+        def _(rows=rows):
+            zero(A2, rows)
+            zero(B2, rows)
+
     FX2[0] = 0.5 * 0.0625 * (B2[0] + B2[1])
 
     def coef_row2(i):
@@ -405,7 +401,7 @@
     coarse = src
 
     first1 = FRAME // 2
-    depth1 = 8
+    depth1 = depth // 2
     span1 = V1.shape[0]
     own_rows = pl.ds(first1, depth1)
 
@@ -415,8 +411,9 @@
 
     rows_loop(0, span1 - 2 * first1, 16, own_row)
     for k in range(FINE_X):
-        V1[first1 - FINE_X + k, own_rows] = jnp.where(group > 0, low[COARSE_X + k], 0.0)
-        V1[span1 - first1 + k, own_rows] = jnp.where(group < groups - 1, high[COARSE_X + k], 0.0)
+        tile = pl.ds(3 * COARSE_X + k * depth1, depth1)
+        V1[first1 - FINE_X + k, own_rows] = low[tile]
+        V1[span1 - first1 + k, own_rows] = high[tile]
 
     def add_coarse(x):
         half = coarse[x + COARSE_X - first1 // 2, first1:first1 + depth1]
@@ -424,14 +421,26 @@
 
     rows_loop(0, span1 // 2, 12, add_coarse)
 
+    rim = far_low.shape[0]
+
     def rim_row(x):
         i = x + first1 - FINE_X
+        part = pl.ds(rim + FINE_X * x, FINE_X)
         return [
-            (V1, (i, slice(first1 - FINE_X, first1)), R[1, x, 3:3 + FINE_X]),
-            (V1, (i, slice(first1 + depth1, first1 + depth1 + FINE_X)), R[3, x, 3:3 + FINE_X]),
+            (V1, (i, slice(first1 - FINE_X, first1)), jnp.where(position > 0, near_low[part], 0.0)),
+            (
+                V1,
+                (i, slice(first1 + depth1, first1 + depth1 + FINE_X)),
+                jnp.where(position < last_block, near_high[part], 0.0),
+            ),
         ]
 
     rows_loop(0, span1 - 2 * (first1 - FINE_X), 22, rim_row)
+    for edge, rows in ((group == 0, slice(0, first1)), (group == last_group, slice(span1 - first1, span1))):
+
+        @pl.when(edge)
+        def _(rows=rows):
+            zero(V1, rows)
 
     def corrected_row(x):
         add = PT[x]
@@ -452,30 +461,39 @@
 
     span = V.shape[0]
     rows1 = V1.shape[1]
+    start = FRAME - 2
 
     def widen(x):
-        row = V1[x + first1 - 1]
+        row = V1[x + start // 2]
         return [(P0, (x, pl.ds(k, rows1, stride=2)), row) for k in range(2)]
 
-    rows_loop(0, span // 2, 18, widen)
+    rows_loop(0, (span - 2 * start) // 2, 18, widen)
 
     def corrected0(x):
         add = P0[x]
-        return [(V, 2 * x + k, in_v[2 * x + k] + add) for k in range(2)]
-
-    rows_loop(0, span // 2, 9, corrected0)
+        i = start + 2 * x
+        return [(V, i + k, in_v[i + k] + add) for k in range(2)]
+
+    rows_loop(0, (span - 2 * start) // 2, 9, corrected0)
     faces = (FX, FY, FZ)
 
     def sweep_a(i):
         return [(U, i, relaxed(i, V, F, IN, faces, 1))]
 
-    rows_loop(1, span - 1, 17, sweep_a)
-    depth = out.shape[1]
+    rows_loop(start + 1, span - start - 1, 17, sweep_a)
 
     def sweep_b(i):
-        return [(out, i - 2, relaxed(i, U, F, IN, faces, 1)[FRAME:FRAME + depth])]
-
-    rows_loop(2, span - 2, 16, sweep_b)
+        rows = pl.ds(FRAME, depth)
+        here = U[i, rows]
+        fz = FZ[i, rows]
+        along_x = FX[i, rows] * U[i + 1, rows] + FX[i - 1, rows] * U[i - 1, rows]
+        before = pl.ds(FRAME - 1, depth)
+        along_y = FY[i, rows] * U[i, pl.ds(FRAME + 1, depth)] + FY[i, before] * U[i, before]
+        along_z = fz * z_next(here, 1) + z_prev(fz * here, 1)
+        off = along_x + along_y + along_z
+        return [(out, i - FRAME, (1.0 - OMEGA) * here + IN[i, rows] * (F[i, rows] + off))]
+
+    rows_loop(FRAME, span - FRAME, 16, sweep_b)
 
 
 def body(source, alpha, beta):
@@ -509,7 +527,7 @@
         out_specs=[VMEM] * 4,
         scratch_shapes=[dma((12,))],
         compiler_params=params(),
-    )(f, a, b)
+    )(*[pltpu.with_memory_space_constraint(t, pltpu.HBM) for t in (f, a, b)])
     low = along_x(x_up, 1)
     high = along_x(x_down, -1)
     y_low = along_y(y_up, 1)
@@ -528,18 +546,18 @@
 
     framed = (count + 2 * FRAME, depth + 2 * FRAME, lanes)
     framed1 = (framed[0] // 2, framed[1] // 2, lanes)
-    kept = (count + 4, framed[1], lanes)
     count2 = count // 4
-    x2_tiles = COARSE_X + FINE_X
+    x2_rows = 3 * COARSE_X + FINE_X * depth // 2
+    x2_rows += -x2_rows % 8
     results = pl.pallas_call(
         down_kernel,
-        out_shape=[arr(*kept)] * 6 + [arr(*framed1)] * 6
-        + [arr(count2, 8, lanes)] + [arr(x2_tiles, 8, lanes)] * 2,
+        out_shape=[arr(*framed)] * 6 + [arr(*framed1)] * 6
+        + [arr(3 * count2, lanes)] + [arr(x2_rows, lanes)] * 2,
         in_specs=[ANY] * 9,
-        out_specs=[ANY] * 6 + [VMEM] * 9,
-        scratch_shapes=[vm(*framed)] * 10
+        out_specs=[VMEM] * 15,
+        scratch_shapes=[vm(*framed)] * 4
         + [vm(framed1[0], framed[1], lanes)] + [vm(*framed1)] * 4
-        + [vm(3, count2, framed1[1], lanes), vm(8, 128), dma((27,)), dma((6,))],
+        + [vm(3, count2, framed1[1], lanes), dma((27,))],
         compiler_params=params(),
     )(f, a, b, low, high, y_low, y_high, c_low, c_high)
     state0 = results[:6]
@@ -548,31 +566,32 @@
 
     low2 = along_x(to_up, 1)
     high2 = along_x(to_down, -1)
-    span = framed1[0] - 2 * (FRAME // 2 - FINE_X)
-    up2, down2 = pl.pallas_call(
+    far_rows = 3 * (count2 + 2 * COARSE_X)
+    far_rows += -far_rows % 8
+    near_rows = far_rows + FINE_X * (count // 2 + 2 * FINE_X)
+    near_rows += -near_rows % 8
+    far, near_up, near_down = pl.pallas_call(
         pack_coarse_kernel,
-        out_shape=[arr(span, 8, lanes)] * 2,
+        out_shape=[arr(far_rows, lanes)] + [arr(near_rows, lanes)] * 2,
         in_specs=[VMEM] * 4,
-        out_specs=[VMEM] * 2,
+        out_specs=[VMEM] * 3,
         compiler_params=params(),
     )(coarse, state1[0], low2, high2)
-    near_low = along_y(up2, 1)
-    near_high = along_y(down2, -1)
-    far_low = along_y(up2, 2)
-    far_high = along_y(down2, -2)
+    near_low = along_y(near_up, 1)
+    near_high = along_y(near_down, -1)
+    far_low = along_y(far, 2)
+    far_high = along_y(far, -2)
 
     framed2 = (count2 + 2 * COARSE_X, depth // 4 + 2 * COARSE_X, lanes)
     out = pl.pallas_call(
         up_kernel,
         out_shape=arr(count, depth, lanes),
-        in_specs=[ANY] * 5 + [VMEM] * 14,
+        in_specs=[VMEM] * 19,
         out_specs=VMEM,
-        scratch_shapes=[vm(*kept)] * 2 + [vm(*framed1)] * 2
-        + [vm(5, span, 8, lanes)] + [vm(*framed2)] * 9
-        + [vm(framed1[0] // 2, framed1[1], lanes), vm(kept[0] // 2, kept[1], lanes)]
-        + [dma((5,))],
+        scratch_shapes=[vm(*framed)] * 2 + [vm(*framed1)] * 2 + [vm(*framed2)] * 9
+        + [vm(framed1[0] // 2, framed1[1], lanes), vm(count // 2 + 2, framed[1], lanes)],
         compiler_params=params(),
-    )(far_low, near_low, up2, near_high, far_high, low2, high2, *state0, *state1)
+    )(far_low, near_low, far, near_high, far_high, low2, high2, *state0, *state1)
     return out[:, None]
 
 

time: 49.2 us -> 45 us (0.915)
  the two profiles are of different devices: /device:TPU:1 before, /device:TPU:0 now
where the time goes in v4:
time: 45 us; the launch traced here: 44.8 us
  starting transfers between devices  17.8 us (40%)
  waiting for transfers between devices  17.2 us (38%)
  Pallas kernels  9.7 us (22%)
    ppermute x8, starting transfers between devices, along_y(): lax.ppermute(array, 'box', [(code[p], code[(p + by) % blocks]) for p in r...  11.9 us
    ppermute x8, waiting for transfers between devices, along_y(): lax.ppermute(array, 'box', [(code[p], code[(p + by) % blocks]) for p in r...  9.04 us
    ppermute x4, waiting for transfers between devices, along_x(): lax.ppermute(array, 'grp', [(i, (i + by) % groups) for i in range(groups)])  8.13 us
    ppermute x4, starting transfers between devices, along_x(): lax.ppermute(array, 'grp', [(i, (i + by) % groups) for i in range(groups)])  5.9 us
    pallas_call x1, Pallas kernels, body(): pl.pallas_call(up_kernel, out_shape=arr(count, depth, lanes), in_specs=[V...  4.16 us
    pallas_call x1, Pallas kernels, body(): pl.pallas_call(down_kernel, out_shape=[arr(*framed)] * 6 + [arr(*framed1)...  3.98 us
    pallas_call x1, Pallas kernels, body(): pl.pallas_call(pack_faces_kernel, out_shape=faces_out, in_specs=[HBM] * 3...  1.47 us
  transfers between devices with their start and end apart: 12, of which 7 were waited for; matrix products, arithmetic and copies ran while one was open for 0% of the time, Pallas kernels for 0%

profile of v4, /device:TPU:0, one launch (start us, length us, event | category | flops | bytes accessed | tf_op | source)
XLA Modules:
  0.0 44.8 jit_solution(9333321292344963609)
XLA Ops:
  0.0 1.5 %shard_map.37 = (f32[19,16,128]{2,1,0:T(8,128)S(1)}, f32[19,16,128]{2,1,0:T(8,128)S(1)}, f32[96,8,128]{2,1,0:T(8,128)S(1)}, f32[96,8,128]{2,1,0:T(8,128)S(1)}) custom-call(f32[32,16,128]{2,1,0:T(8,128)} %bitcast.6, f32[32,16,128]{2,1,0:T(8,128)} %bitcast.8, f32[32,16,128]{2,1,0:T(8,128)} %bitcast.10), custom_call_target="tpu_custom_call" | custom-call | tf_op jit(solution)/shard_map/pallas_call | solution.py:523
  1.5 0.0 copy-start
  1.5 0.5 %collective-permute-start.2 = (f32[96,8,128]{2,1,0:T(8,128)S(1)}, f32[96,8,128]{2,1,0:T(8,128)S(1)}, u32[]{:S(2)}, u32[]{:S(2)}) collective-permute-start(f32[96,8,128]{2,1,0:T(8,128)S(1)} %get-tuple-element.31), channel_id=1, source_target_pairs={{0,1},{1,3},{3,2},{2,6},{6,7},{7,5},{5,4},{4,0},{8,9},{9,11},{11,1... | collective-permute-start | bytes 1179656 | tf_op jit(solution)/shard_map/ppermute | solution.py:512
  2.0 3.7 %collective-permute-start.3 = (f32[96,8,128]{2,1,0:T(8,128)S(1)}, f32[96,8,128]{2,1,0:T(8,128)S(1)}, u32[]{:S(2)}, u32[]{:S(2)}) collective-permute-start(f32[96,8,128]{2,1,0:T(8,128)S(1)} %get-tuple-element.32), channel_id=1, source_target_pairs={{0,4},{1,0},{3,1},{2,3},{6,2},{7,6},{5,7},{4,5},{8,12},{9,8},{11,9... | collective-permute-start | bytes 1179656 | tf_op jit(solution)/shard_map/ppermute | solution.py:512
  5.7 1.8 %collective-permute-start = (f32[19,16,128]{2,1,0:T(8,128)S(1)}, f32[19,16,128]{2,1,0:T(8,128)S(1)}, u32[]{:S(2)}, u32[]{:S(2)}) collective-permute-start(f32[19,16,128]{2,1,0:T(8,128)S(1)} %get-tuple-element.29), channel_id=1, source_target_pairs={{0,8},{8,16},{16,24},{24,0},{1,9},{9,17},{17,25},{25,1},{2,10},{10... | collective-permute-start | bytes 466952 | tf_op jit(solution)/shard_map/ppermute | solution.py:509
  7.4 1.2 %collective-permute-start.1 = (f32[19,16,128]{2,1,0:T(8,128)S(1)}, f32[19,16,128]{2,1,0:T(8,128)S(1)}, u32[]{:S(2)}, u32[]{:S(2)}) collective-permute-start(f32[19,16,128]{2,1,0:T(8,128)S(1)} %get-tuple-element.30), channel_id=1, source_target_pairs={{0,24},{8,0},{16,8},{24,16},{1,25},{9,1},{17,9},{25,17},{2,26},{10... | collective-permute-start | bytes 466952 | tf_op jit(solution)/shard_map/ppermute | solution.py:509
  8.6 4.0 %collective-permute-done.low = f32[19,16,128]{2,1,0:T(8,128)S(1)} collective-permute-done((f32[19,16,128]{2,1,0:T(8,128)S(1)}, f32[19,16,128]{2,1,0:T(8,128)S(1)}, u32[]{:S(2)}, u32[]{:S(2)}) %collective-permute-start) | collective-permute-done | bytes 155680 | tf_op jit(solution)/shard_map/ppermute | solution.py:509
  12.6 1.7 %collective-permute-done.1.high = f32[19,16,128]{2,1,0:T(8,128)S(1)} collective-permute-done((f32[19,16,128]{2,1,0:T(8,128)S(1)}, f32[19,16,128]{2,1,0:T(8,128)S(1)}, u32[]{:S(2)}, u32[]{:S(2)}) %collective-permute-start.1) | collective-permute-done | bytes 155680 | tf_op jit(solution)/shard_map/ppermute | solution.py:509
  14.4 0.1 shard_map.38
  14.4 0.1 collective-permute-start.4
  14.5 2.9 %collective-permute-start.5 = (f32[38,8,128]{2,1,0:T(8,128)S(1)}, f32[38,8,128]{2,1,0:T(8,128)S(1)}, u32[]{:S(2)}, u32[]{:S(2)}) collective-permute-start(f32[38,8,128]{2,1,0:T(8,128)S(1)} %get-tuple-element.34), channel_id=1, source_target_pairs={{0,4},{1,0},{3,1},{2,3},{6,2},{7,6},{5,7},{4,5},{8,12},{9,8},{11,9... | collective-permute-start | bytes 466952 | tf_op jit(solution)/shard_map/ppermute | solution.py:512
  17.4 3.3 %collective-permute-done.4.c_low = f32[38,8,128]{2,1,0:T(8,128)S(1)} collective-permute-done((f32[38,8,128]{2,1,0:T(8,128)S(1)}, f32[38,8,128]{2,1,0:T(8,128)S(1)}, u32[]{:S(2)}, u32[]{:S(2)}) %collective-permute-start.4) | collective-permute-done | bytes 155680 | tf_op jit(solution)/shard_map/ppermute | solution.py:512
  20.8 4.0 %shard_map.39 = (f32[48,32,128]{2,1,0:T(8,128)S(1)}, f32[48,32,128]{2,1,0:T(8,128)S(1)}, f32[48,32,128]{2,1,0:T(8,128)S(1)}, f32[48,32,128]{2,1,0:T(8,128)S(1)},...) custom-call(f32[32,16,128]{2,1,0:T(8,128)S(1)} %bitcast.7, ...), custom_call_target="tpu_custom_call" | custom-call | tf_op jit(solution)/shard_map/pallas_call | solution.py:552
  24.8 1.5 %collective-permute-start.6 = (f32[48,128]{1,0:T(8,128)S(1)}, f32[48,128]{1,0:T(8,128)S(1)}, u32[]{:S(2)}, u32[]{:S(2)}) collective-permute-start(f32[48,128]{1,0:T(8,128)S(1)} %get-tuple-element.37), channel_id=1, source_target_pairs={{0,8},{8,16},{16,24},{24,0},{1,9},{9,17},{17,25},{25,1},{2,10},{10... | collective-permute-start | bytes 73736 | tf_op jit(solution)/shard_map/ppermute | solution.py:509
  26.3 1.5 %collective-permute-start.7 = (f32[48,128]{1,0:T(8,128)S(1)}, f32[48,128]{1,0:T(8,128)S(1)}, u32[]{:S(2)}, u32[]{:S(2)}) collective-permute-start(f32[48,128]{1,0:T(8,128)S(1)} %get-tuple-element.38), channel_id=1, source_target_pairs={{0,24},{8,0},{16,8},{24,16},{1,25},{9,1},{17,9},{25,17},{2,26},{10... | collective-permute-start | bytes 73736 | tf_op jit(solution)/shard_map/ppermute | solution.py:509
  27.7 1.8 %collective-permute-done.6.low = f32[48,128]{1,0:T(8,128)S(1)} collective-permute-done((f32[48,128]{1,0:T(8,128)S(1)}, f32[48,128]{1,0:T(8,128)S(1)}, u32[]{:S(2)}, u32[]{:S(2)}) %collective-permute-start.6) | collective-permute-done | bytes 24608 | tf_op jit(solution)/shard_map/ppermute | solution.py:509
  29.5 0.6 %collective-permute-done.7.high = f32[48,128]{1,0:T(8,128)S(1)} collective-permute-done((f32[48,128]{1,0:T(8,128)S(1)}, f32[48,128]{1,0:T(8,128)S(1)}, u32[]{:S(2)}, u32[]{:S(2)}) %collective-permute-start.7) | collective-permute-done | bytes 24608 | tf_op jit(solution)/shard_map/ppermute | solution.py:509
  30.1 0.1 collective-permute-start.9
  30.2 3.0 %collective-permute-start.10 = (f32[136,128]{1,0:T(8,128)S(1)}, f32[136,128]{1,0:T(8,128)S(1)}, u32[]{:S(2)}, u32[]{:S(2)}) collective-permute-start(f32[136,128]{1,0:T(8,128)S(1)} %get-tuple-element.41), channel_id=1, source_target_pairs={{0,4},{1,0},{3,1},{2,3},{6,2},{7,6},{5,7},{4,5},{8,12},{9,8},{11,9... | collective-permute-start | bytes 208904 | tf_op jit(solution)/shard_map/ppermute | solution.py:512
  33.2 0.0 collective-permute-start.11
  33.2 1.7 %collective-permute-start.8 = (f32[64,128]{1,0:T(8,128)S(1)}, f32[64,128]{1,0:T(8,128)S(1)}, u32[]{:S(2)}, u32[]{:S(2)}) collective-permute-start(f32[64,128]{1,0:T(8,128)S(1)} %get-tuple-element.39.own), channel_id=1, source_target_pairs={{0,3},{1,2},{3,6},{2,7},{6,5},{7,4},{5,0},{4,1},{8,11},{9,10},{11,... | collective-permute-start | bytes 98312 | tf_op jit(solution)/shard_map/ppermute | solution.py:512
  34.9 1.6 %collective-permute-done.11.far_high = f32[64,128]{1,0:T(8,128)S(1)} collective-permute-done((f32[64,128]{1,0:T(8,128)S(1)}, f32[64,128]{1,0:T(8,128)S(1)}, u32[]{:S(2)}, u32[]{:S(2)}) %collective-permute-start.11) | collective-permute-done | bytes 32800 | tf_op jit(solution)/shard_map/ppermute | solution.py:512
  36.5 4.1 %collective-permute-done.8.far_low = f32[64,128]{1,0:T(8,128)S(1)} collective-permute-done((f32[64,128]{1,0:T(8,128)S(1)}, f32[64,128]{1,0:T(8,128)S(1)}, u32[]{:S(2)}, u32[]{:S(2)}) %collective-permute-start.8) | collective-permute-done | bytes 32800 | tf_op jit(solution)/shard_map/ppermute | solution.py:512
  40.7 4.2 %shard_map.41 = f32[32,16,128]{2,1,0:T(8,128)} custom-call(f32[64,128]{1,0:T(8,128)S(1)} %collective-permute-done.8.far_low, f32[136,128]{1,0:T(8,128)S(1)} %collective-permute-done.9.near_low, f32[64,128]{1,0:T(8,128)S(1)} %get-tuple-element.39.own, f32[136,128]{1,0:T(8,128)S(1)} %collective-permute-done.10.near_high, ...), custom_call_target="tpu_custom_call" | custom-call | tf_op jit(solution)/shard_map/pallas_call | solution.py:586
  (11 shorter events, 0.0 us)
Async XLA Ops:
  0.0 20.7 %copy-start.1 = (f32[32,1,16,128]{3,2,1,0:T(8,128)S(1)}, f32[32,1,16,128]{3,2,1,0:T(8,128)}, u32[]{:S(2)}) copy-start(f32[32,1,16,128]{3,2,1,0:T(8,128)} %param.4) | copy-start | bytes 786436
  0.0 20.8 %copy-start.2 = (f32[32,1,16,128]{3,2,1,0:T(8,128)S(1)}, f32[32,1,16,128]{3,2,1,0:T(8,128)}, u32[]{:S(2)}) copy-start(f32[32,1,16,128]{3,2,1,0:T(8,128)} %param.5) | copy-start | bytes 786436
  1.5 19.3 %copy-start = (f32[32,1,16,128]{3,2,1,0:T(8,128)S(1)}, f32[32,1,16,128]{3,2,1,0:T(8,128)}, u32[]{:S(2)}) copy-start(f32[32,1,16,128]{3,2,1,0:T(8,128)} %param.3) | copy-start | bytes 786436
  1.5 19.2 %collective-permute-start.2 = (f32[96,8,128]{2,1,0:T(8,128)S(1)}, f32[96,8,128]{2,1,0:T(8,128)S(1)}, u32[]{:S(2)}, u32[]{:S(2)}) collective-permute-start(f32[96,8,128]{2,1,0:T(8,128)S(1)} %get-tuple-element.31), channel_id=1, source_target_pairs={{0,1},{1,3},{3,2},{2,6},{6,7},{7,5},{5,4},{4,0},{8,9},{9,11},{11,1... | collective-permute-start | bytes 1179656 | tf_op jit(solution)/shard_map/ppermute | solution.py:512
  2.0 18.7 %collective-permute-start.3 = (f32[96,8,128]{2,1,0:T(8,128)S(1)}, f32[96,8,128]{2,1,0:T(8,128)S(1)}, u32[]{:S(2)}, u32[]{:S(2)}) collective-permute-start(f32[96,8,128]{2,1,0:T(8,128)S(1)} %get-tuple-element.32), channel_id=1, source_target_pairs={{0,4},{1,0},{3,1},{2,3},{6,2},{7,6},{5,7},{4,5},{8,12},{9,8},{11,9... | collective-permute-start | bytes 1179656 | tf_op jit(solution)/shard_map/ppermute | solution.py:512
  5.7 7.0 %collective-permute-start = (f32[19,16,128]{2,1,0:T(8,128)S(1)}, f32[19,16,128]{2,1,0:T(8,128)S(1)}, u32[]{:S(2)}, u32[]{:S(2)}) collective-permute-start(f32[19,16,128]{2,1,0:T(8,128)S(1)} %get-tuple-element.29), channel_id=1, source_target_pairs={{0,8},{8,16},{16,24},{24,0},{1,9},{9,17},{17,25},{25,1},{2,10},{10... | collective-permute-start | bytes 466952 | tf_op jit(solution)/shard_map/ppermute | solution.py:509
  7.4 6.9 %collective-permute-start.1 = (f32[19,16,128]{2,1,0:T(8,128)S(1)}, f32[19,16,128]{2,1,0:T(8,128)S(1)}, u32[]{:S(2)}, u32[]{:S(2)}) collective-permute-start(f32[19,16,128]{2,1,0:T(8,128)S(1)} %get-tuple-element.30), channel_id=1, source_target_pairs={{0,24},{8,0},{16,8},{24,16},{1,25},{9,1},{17,9},{25,17},{2,26},{10... | collective-permute-start | bytes 466952 | tf_op jit(solution)/shard_map/ppermute | solution.py:509
  14.4 6.3 %collective-permute-start.4 = (f32[38,8,128]{2,1,0:T(8,128)S(1)}, f32[38,8,128]{2,1,0:T(8,128)S(1)}, u32[]{:S(2)}, u32[]{:S(2)}) collective-permute-start(f32[38,8,128]{2,1,0:T(8,128)S(1)} %get-tuple-element.33), channel_id=1, source_target_pairs={{0,1},{1,3},{3,2},{2,6},{6,7},{7,5},{5,4},{4,0},{8,9},{9,11},{11,1... | collective-permute-start | bytes 466952 | tf_op jit(solution)/shard_map/ppermute | solution.py:512
  14.5 6.2 %collective-permute-start.5 = (f32[38,8,128]{2,1,0:T(8,128)S(1)}, f32[38,8,128]{2,1,0:T(8,128)S(1)}, u32[]{:S(2)}, u32[]{:S(2)}) collective-permute-start(f32[38,8,128]{2,1,0:T(8,128)S(1)} %get-tuple-element.34), channel_id=1, source_target_pairs={{0,4},{1,0},{3,1},{2,3},{6,2},{7,6},{5,7},{4,5},{8,12},{9,8},{11,9... | collective-permute-start | bytes 466952 | tf_op jit(solution)/shard_map/ppermute | solution.py:512
  24.8 4.8 %collective-permute-start.6 = (f32[48,128]{1,0:T(8,128)S(1)}, f32[48,128]{1,0:T(8,128)S(1)}, u32[]{:S(2)}, u32[]{:S(2)}) collective-permute-start(f32[48,128]{1,0:T(8,128)S(1)} %get-tuple-element.37), channel_id=1, source_target_pairs={{0,8},{8,16},{16,24},{24,0},{1,9},{9,17},{17,25},{25,1},{2,10},{10... | collective-permute-start | bytes 73736 | tf_op jit(solution)/shard_map/ppermute | solution.py:509
  26.3 3.8 %collective-permute-start.7 = (f32[48,128]{1,0:T(8,128)S(1)}, f32[48,128]{1,0:T(8,128)S(1)}, u32[]{:S(2)}, u32[]{:S(2)}) collective-permute-start(f32[48,128]{1,0:T(8,128)S(1)} %get-tuple-element.38), channel_id=1, source_target_pairs={{0,24},{8,0},{16,8},{24,16},{1,25},{9,1},{17,9},{25,17},{2,26},{10... | collective-permute-start | bytes 73736 | tf_op jit(solution)/shard_map/ppermute | solution.py:509
  30.1 10.5 %collective-permute-start.9 = (f32[136,128]{1,0:T(8,128)S(1)}, f32[136,128]{1,0:T(8,128)S(1)}, u32[]{:S(2)}, u32[]{:S(2)}) collective-permute-start(f32[136,128]{1,0:T(8,128)S(1)} %get-tuple-element.40), channel_id=1, source_target_pairs={{0,1},{1,3},{3,2},{2,6},{6,7},{7,5},{5,4},{4,0},{8,9},{9,11},{11,1... | collective-permute-start | bytes 208904 | tf_op jit(solution)/shard_map/ppermute | solution.py:512
  30.2 10.4 %collective-permute-start.10 = (f32[136,128]{1,0:T(8,128)S(1)}, f32[136,128]{1,0:T(8,128)S(1)}, u32[]{:S(2)}, u32[]{:S(2)}) collective-permute-start(f32[136,128]{1,0:T(8,128)S(1)} %get-tuple-element.41), channel_id=1, source_target_pairs={{0,4},{1,0},{3,1},{2,3},{6,2},{7,6},{5,7},{4,5},{8,12},{9,8},{11,9... | collective-permute-start | bytes 208904 | tf_op jit(solution)/shard_map/ppermute | solution.py:512
  33.2 3.3 %collective-permute-start.11 = (f32[64,128]{1,0:T(8,128)S(1)}, f32[64,128]{1,0:T(8,128)S(1)}, u32[]{:S(2)}, u32[]{:S(2)}) collective-permute-start(f32[64,128]{1,0:T(8,128)S(1)} %get-tuple-element.39.own), channel_id=1, source_target_pairs={{0,5},{1,4},{3,0},{2,1},{6,3},{7,2},{5,6},{4,7},{8,13},{9,12},{11,... | collective-permute-start | bytes 98312 | tf_op jit(solution)/shard_map/ppermute | solution.py:512
  33.2 7.4 %collective-permute-start.8 = (f32[64,128]{1,0:T(8,128)S(1)}, f32[64,128]{1,0:T(8,128)S(1)}, u32[]{:S(2)}, u32[]{:S(2)}) collective-permute-start(f32[64,128]{1,0:T(8,128)S(1)} %get-tuple-element.39.own), channel_id=1, source_target_pairs={{0,3},{1,2},{3,6},{2,7},{6,5},{7,4},{5,0},{4,1},{8,11},{9,10},{11,... | collective-permute-start | bytes 98312 | tf_op jit(solution)/shard_map/ppermute | solution.py:512

commit v5 on v4

--- a/solution.py
+++ b/solution.py
@@ -131,103 +131,153 @@
     ref[at] = jnp.zeros_like(ref[at])
 
 
-def pack_faces_kernel(f, a, b, x_up, x_down, y_up, y_down, sems):
+WIDES = (WIDE_F, WIDE_F, WIDE_B)
+
+
+def face_pieces(count):
+    pieces = []
+    at = 0
+    for k, wide in enumerate(WIDES):
+        for x in range(count):
+            pieces.append((k, x, wide, at))
+            at += wide
+    return pieces, at + -at % 8
+
+
+def corner_pieces():
+    pieces = []
+    at = 0
+    for side in range(2):
+        start = 0
+        for k, wide in enumerate(WIDES):
+            for layer in range(wide):
+                distance = layer + 1 if side else wide - layer
+                layers = min(wide, wide + 2 - distance)
+                pieces.append((side, k, start + layer, layers, at))
+                at += layers
+            start += wide
+    return pieces, at + -at % 8
+
+
+def pack_faces_kernel(f, a, b, F, A, B, x_up, x_down, y_up, y_down, sems):
     count, depth = f.shape[:2]
-    pairs = []
+    own = (pl.ds(FRAME, count), pl.ds(FRAME, depth))
+    frames = (F, A, B)
+    copies = run_copies([(src, dst.at[own]) for src, dst in zip((f, a, b), frames)], sems)
+    pieces, _ = face_pieces(count)
     row = 0
-    for k, (ref, wide) in enumerate(((f, WIDE_F), (a, WIDE_F), (b, WIDE_B))):
-        pairs.append((ref.at[pl.ds(count - wide, wide)], x_up.at[pl.ds(row, wide)]))
-        pairs.append((ref.at[pl.ds(0, wide)], x_down.at[pl.ds(row, wide)]))
-        pairs.append((ref.at[:, pl.ds(depth - FRAME, FRAME)], y_up.at[pl.ds(k * count, count)]))
-        pairs.append((ref.at[:, pl.ds(0, FRAME)], y_down.at[pl.ds(k * count, count)]))
+    for k, (ref, wide) in enumerate(zip(frames, WIDES)):
+        copies[k].wait()
+        for layer in range(wide):
+            x_up[row + layer] = ref[FRAME + count - wide + layer, FRAME:FRAME + depth]
+            x_down[row + layer] = ref[FRAME + layer, FRAME:FRAME + depth]
         row += wide
-    wait_copies(run_copies(pairs, sems))
-
-
-def pack_corners_kernel(low, high, up, down, sems):
-    rows, depth = low.shape[:2]
-    pairs = []
-    for k, ref in enumerate((low, high)):
-        pairs.append((ref.at[:, pl.ds(depth - FRAME, FRAME)], up.at[pl.ds(k * rows, rows)]))
-        pairs.append((ref.at[:, pl.ds(0, FRAME)], down.at[pl.ds(k * rows, rows)]))
-    wait_copies(run_copies(pairs, sems))
-
-
-def down_kernel(
-    f, a, b, low, high, y_low, y_high, c_low, c_high,
-    U, F, IN, FX, FY, FZ,
-    out_v1, out_f1, out_inv1, out_fx1, out_fy1, out_fz1,
-    out_coarse, to_up, to_down,
-    A, B, DG, V, T, A1, B1, D1, W1, T1, sems,
-):
-    count = f.shape[0]
-    depth = f.shape[1]
-    own_y = pl.ds(FRAME, depth)
-    low_y = pl.ds(0, FRAME)
-    high_y = pl.ds(FRAME + depth, FRAME)
-    own_x = pl.ds(FRAME, count)
-    x_rows = low.shape[0]
-    pairs = []
-    got = 0
-    for k, (ref, wide, dst) in enumerate(((f, WIDE_F, F), (a, WIDE_F, A), (b, WIDE_B, B))):
-        layers = pl.ds(got, wide)
-        layers_too = pl.ds(x_rows + got, wide)
-        low_x = pl.ds(FRAME - wide, wide)
-        high_x = pl.ds(FRAME + count, wide)
-        block = pl.ds(k * count, count)
-        pairs += [
-            (ref, dst.at[own_x, own_y]),
-            (low.at[layers], dst.at[low_x, own_y]),
-            (high.at[layers], dst.at[high_x, own_y]),
-            (y_low.at[block], dst.at[own_x, low_y]),
-            (y_high.at[block], dst.at[own_x, high_y]),
-            (c_low.at[layers], dst.at[low_x, low_y]),
-            (c_low.at[layers_too], dst.at[high_x, low_y]),
-            (c_high.at[layers], dst.at[low_x, high_y]),
-            (c_high.at[layers_too], dst.at[high_x, high_y]),
-        ]
-        got += wide
-    wait_copies(run_copies(pairs, sems))
-
-    group = lax.axis_index("grp")
-    position = box_position()
-    for edge, x, y in (
-        (group == 0, slice(0, FRAME), slice(None)),
-        (group == lax.axis_size("grp") - 1, slice(FRAME + count, None), slice(None)),
-        (position == 0, slice(None), slice(0, FRAME)),
-        (position == lax.axis_size("box") - 1, slice(None), slice(FRAME + depth, None)),
-    ):
-
-        @pl.when(edge)
-        def _(x=x, y=y):
-            for ref in (F, A, B):
-                zero(ref, x, y)
-
+        for at_k, x, layers, at in pieces:
+            if at_k == k:
+                y_up[at:at + layers] = ref[FRAME + x, FRAME + depth - layers:FRAME + depth]
+                y_down[at:at + layers] = ref[FRAME + x, FRAME:FRAME + layers]
+
+
+def pack_corners_kernel(low, high, up, down):
+    depth = low.shape[1]
+    for side, _, row, layers, at in corner_pieces()[0]:
+        ref = (low, high)[side]
+        up[at:at + layers] = ref[row, depth - layers:depth]
+        down[at:at + layers] = ref[row, 0:layers]
+
+
+def down_rows(F, A, B, FX, FY, FZ, DG, IN, V, U, T):
     faces = (FX, FY, FZ)
-    end = count + 2 * FRAME
-
-    FX[1] = 0.5 * (B[1] + B[2])
 
     def coef_row(i):
         fx, fy, fz, dg, inv = coefficients(A[i], B[i], B[i - 1], B[i + 1], 1, 1.0)
         return [(FX, i, fx), (FY, i, fy), (FZ, i, fz), (DG, i, dg), (IN, i, inv), (V, i, inv * F[i])]
 
-    rows_loop(2, end - 2, 11, coef_row)
-
     def sweep_row(i):
         return [(U, i, relaxed(i, V, F, IN, faces, 1))]
 
-    rows_loop(3, end - 3, 14, sweep_row)
     def residual(i):
         here, off = off_sum(i, U, faces, 1)
         return F[i] - DG[i] * here + off
 
-    half_rows = (depth + 2 * FRAME) // 2
-
     def restrict_row(j):
         return [(T, j, residual(2 * j) + residual(2 * j + 1))]
 
-    rows_loop(2, end // 2 - 2, 5, restrict_row)
+    return coef_row, sweep_row, restrict_row
+
+
+def down_inner_kernel(y_low, y_high, F_in, A_in, B_in, F, A, B, FX, FY, FZ, DG, IN, V, U, T):
+    end = F.shape[0]
+    depth = F.shape[1] - 2 * FRAME
+    count = end - 2 * FRAME
+    frames = (F, A, B)
+    for k, x, layers, at in face_pieces(count)[0]:
+        frames[k][FRAME + x, FRAME - layers:FRAME] = y_low[at:at + layers]
+        frames[k][FRAME + x, FRAME + depth:FRAME + depth + layers] = y_high[at:at + layers]
+    zero_y_edges(frames, depth)
+    coef_row, sweep_row, restrict_row = down_rows(F, A, B, FX, FY, FZ, DG, IN, V, U, T)
+    rows_loop(FRAME + 1, end - FRAME - 1, 10, coef_row)
+    rows_loop(FRAME + 2, end - FRAME - 2, 14, sweep_row)
+    rows_loop(FRAME // 2 + 2, (end - FRAME) // 2 - 2, 6, restrict_row)
+
+
+def zero_y_edges(frames, depth):
+    position = box_position()
+    for edge, y in (
+        (position == 0, slice(0, FRAME)),
+        (position == lax.axis_size("box") - 1, slice(FRAME + depth, FRAME + depth + FRAME)),
+    ):
+
+        @pl.when(edge)
+        def _(y=y):
+            for ref in frames:
+                zero(ref, slice(None), y)
+
+
+def down_kernel(
+    low, high, c_low, c_high,
+    F_in, A_in, B_in, FX_in, FY_in, FZ_in, DG_in, IN_in, V_in, U_in, T_in,
+    F, A, B, FX, FY, FZ, DG, IN, V, U, T,
+    out_v1, out_f1, out_inv1, out_fx1, out_fy1, out_fz1,
+    out_coarse, to_up, to_down,
+    A1, B1, D1, W1, T1,
+):
+    count = F.shape[0] - 2 * FRAME
+    depth = F.shape[1] - 2 * FRAME
+    frames = (F, A, B)
+    start = 0
+    for k, wide in enumerate(WIDES):
+        for layer in range(wide):
+            frames[k][FRAME - wide + layer, FRAME:FRAME + depth] = low[start + layer]
+            frames[k][FRAME + count + layer, FRAME:FRAME + depth] = high[start + layer]
+        start += wide
+    starts = (0, WIDE_F, 2 * WIDE_F)
+    for side, k, row, layers, at in corner_pieces()[0]:
+        x = row - starts[k] + (FRAME + count if side else FRAME - WIDES[k])
+        frames[k][x, FRAME - layers:FRAME] = c_low[at:at + layers]
+        frames[k][x, FRAME + depth:FRAME + depth + layers] = c_high[at:at + layers]
+    zero_y_edges(frames, depth)
+    group = lax.axis_index("grp")
+    for edge, x in (
+        (group == 0, slice(0, FRAME)),
+        (group == lax.axis_size("grp") - 1, slice(FRAME + count, FRAME + count + FRAME)),
+    ):
+
+        @pl.when(edge)
+        def _(x=x):
+            for ref in frames:
+                zero(ref, x)
+
+    end = count + 2 * FRAME
+    coef_row, sweep_row, restrict_row = down_rows(F, A, B, FX, FY, FZ, DG, IN, V, U, T)
+
+    FX[1] = 0.5 * (B[1] + B[2])
+    for margin, fn in ((2, coef_row), (3, sweep_row)):
+        rows_loop(margin, FRAME + margin - 1, 7, fn)
+        rows_loop(end - FRAME - margin + 1, end - margin, 7, fn)
+    rows_loop(2, FRAME // 2 + 2, 4, restrict_row)
+    rows_loop((end - FRAME) // 2 - 2, end // 2 - 2, 4, restrict_row)
+    half_rows = (depth + 2 * FRAME) // 2
 
     def level1_source(j):
         return [(out_f1, j, 0.125 * pair_sum_z(strided_pair(T, j, half_rows), 1))]
@@ -519,13 +569,15 @@
 
     dma = pltpu.SemaphoreType.DMA
     x_rows = 2 * WIDE_F + WIDE_B
-    faces_out = [arr(x_rows, depth, lanes)] * 2 + [arr(3 * count, FRAME, lanes)] * 2
-    x_up, x_down, y_up, y_down = pl.pallas_call(
+    framed = (count + 2 * FRAME, depth + 2 * FRAME, lanes)
+    y_rows = face_pieces(count)[1]
+    c_rows = corner_pieces()[1]
+    *frames, x_up, x_down, y_up, y_down = pl.pallas_call(
         pack_faces_kernel,
-        out_shape=faces_out,
+        out_shape=[arr(*framed)] * 3 + [arr(x_rows, depth, lanes)] * 2 + [arr(y_rows, lanes)] * 2,
         in_specs=[HBM] * 3,
-        out_specs=[VMEM] * 4,
-        scratch_shapes=[dma((12,))],
+        out_specs=[VMEM] * 7,
+        scratch_shapes=[dma((3,))],
         compiler_params=params(),
     )(*[pltpu.with_memory_space_constraint(t, pltpu.HBM) for t in (f, a, b)])
     low = along_x(x_up, 1)
@@ -535,34 +587,41 @@
 
     c_up, c_down = pl.pallas_call(
         pack_corners_kernel,
-        out_shape=[arr(2 * x_rows, FRAME, lanes)] * 2,
-        in_specs=[ANY] * 2,
+        out_shape=[arr(c_rows, lanes)] * 2,
+        in_specs=[VMEM] * 2,
         out_specs=[VMEM] * 2,
-        scratch_shapes=[dma((4,))],
         compiler_params=params(),
     )(low, high)
     c_low = along_y(c_up, 1)
     c_high = along_y(c_down, -1)
 
-    framed = (count + 2 * FRAME, depth + 2 * FRAME, lanes)
     framed1 = (framed[0] // 2, framed[1] // 2, lanes)
+    level0 = [arr(*framed)] * 10 + [arr(framed1[0], framed[1], lanes)]
+    level0 = pl.pallas_call(
+        down_inner_kernel,
+        out_shape=level0,
+        in_specs=[VMEM] * 5,
+        out_specs=[VMEM] * 11,
+        input_output_aliases={2 + k: k for k in range(3)},
+        compiler_params=params(),
+    )(y_low, y_high, *frames)
     count2 = count // 4
     x2_rows = 3 * COARSE_X + FINE_X * depth // 2
     x2_rows += -x2_rows % 8
     results = pl.pallas_call(
         down_kernel,
-        out_shape=[arr(*framed)] * 6 + [arr(*framed1)] * 6
+        out_shape=[arr(*t.shape) for t in level0] + [arr(*framed1)] * 6
         + [arr(3 * count2, lanes)] + [arr(x2_rows, lanes)] * 2,
-        in_specs=[ANY] * 9,
-        out_specs=[VMEM] * 15,
-        scratch_shapes=[vm(*framed)] * 4
-        + [vm(framed1[0], framed[1], lanes)] + [vm(*framed1)] * 4
-        + [vm(3, count2, framed1[1], lanes), dma((27,))],
+        in_specs=[VMEM] * 15,
+        out_specs=[VMEM] * 20,
+        input_output_aliases={4 + k: k for k in range(11)},
+        scratch_shapes=[vm(*framed1)] * 4 + [vm(3, count2, framed1[1], lanes)],
         compiler_params=params(),
-    )(f, a, b, low, high, y_low, y_high, c_low, c_high)
-    state0 = results[:6]
-    state1 = results[6:12]
-    coarse, to_up, to_down = results[12:]
+    )(low, high, c_low, c_high, *level0)
+    F, _, _, FX, FY, FZ, _, IN, _, U, _ = results[:11]
+    state0 = (U, F, IN, FX, FY, FZ)
+    state1 = results[11:17]
+    coarse, to_up, to_down = results[17:]
 
     low2 = along_x(to_up, 1)
     high2 = along_x(to_down, -1)

time: 45 us -> 41.1 us (0.913)
  waiting for transfers between devices: 17.2 us -> 14.2 us
  Pallas kernels: 9.7 us -> 8.79 us
    ppermute x8, waiting for transfers between devices: 9.04 us -> 6.02 us  [along_y(): lax.ppermute(array, 'box', [(code[p], code[(p + by) % blocks]) for p in r...]
    pallas_call x3 -> x4, Pallas kernels: 5.51 us -> 4.6 us  [the longest x1 1.91 us: body(): pl.pallas_call(down_kernel, out_shape=[arr(*t.shape) for t in level0] + [...]
  transfers between devices with their start and end apart: 12 -> 12, of which waited for: 7 -> 7; matrix products, arithmetic and copies ran while one was open for 0% -> 0% of each run, Pallas kernels for 0% -> 4%
where the time goes in v5:
time: 41.1 us; the launch traced here: 40.9 us
  starting transfers between devices  17.9 us (44%)
  waiting for transfers between devices  14.2 us (35%)
  Pallas kernels  8.79 us (21%)
    ppermute x8, starting transfers between devices, along_y(): lax.ppermute(array, 'box', [(code[p], code[(p + by) % blocks]) for p in r...  12 us
    ppermute x4, waiting for transfers between devices, along_x(): lax.ppermute(array, 'grp', [(i, (i + by) % groups) for i in range(groups)])  8.13 us
    ppermute x8, waiting for transfers between devices, along_y(): lax.ppermute(array, 'box', [(code[p], code[(p + by) % blocks]) for p in r...  6.02 us
    ppermute x4, starting transfers between devices, along_x(): lax.ppermute(array, 'grp', [(i, (i + by) % groups) for i in range(groups)])  5.9 us
    pallas_call x1, Pallas kernels, body(): pl.pallas_call(up_kernel, out_shape=arr(count, depth, lanes), in_specs=[V...  4.16 us
    pallas_call x1, Pallas kernels, body(): pl.pallas_call(down_kernel, out_shape=[arr(*t.shape) for t in level0] + [...  1.91 us
    pallas_call x1, Pallas kernels, body(): pl.pallas_call(down_inner_kernel, out_shape=level0, in_specs=[VMEM] * 5,...  1.5 us
    pallas_call x1, Pallas kernels, body(): pl.pallas_call(pack_faces_kernel, out_shape=[arr(*framed)] * 3 + [arr(x_r...  1.16 us
  transfers between devices with their start and end apart: 12, of which 7 were waited for; matrix products, arithmetic and copies ran while one was open for 0% of the time, Pallas kernels for 4%

profile of v5, /device:TPU:0, one launch (start us, length us, event | category | flops | bytes accessed | tf_op | source)
XLA Modules:
  0.0 40.9 jit_solution(3422408101935456463)
XLA Ops:
  0.0 1.2 %shard_map.37 = (f32[48,32,128]{2,1,0:T(8,128)S(1)}, f32[48,32,128]{2,1,0:T(8,128)S(1)}, f32[48,32,128]{2,1,0:T(8,128)S(1)}, f32[19,16,128]{2,1,0:T(8,128)S(1)},...) custom-call(f32[32,16,128]{2,1,0:T(8,128)} %bitcast.6, f32[32,16,128]{2,1,0:T(8,128)} %bitcast.7, ...), custom_call_target="tpu_custom_call" | custom-call | tf_op jit(solution)/shard_map/pallas_call | solution.py:575
  1.2 0.5 %collective-permute-start.4 = (f32[608,128]{1,0:T(8,128)S(1)}, f32[608,128]{1,0:T(8,128)S(1)}, u32[]{:S(2)}, u32[]{:S(2)}) collective-permute-start(f32[608,128]{1,0:T(8,128)S(1)} %get-tuple-element.47), channel_id=1, source_target_pairs={{0,1},{1,3},{3,2},{2,6},{6,7},{7,5},{5,4},{4,0},{8,9},{9,11},{11,1... | collective-permute-start | bytes 933896 | tf_op jit(solution)/shard_map/ppermute | solution.py:562
  1.7 3.7 %collective-permute-start.5 = (f32[608,128]{1,0:T(8,128)S(1)}, f32[608,128]{1,0:T(8,128)S(1)}, u32[]{:S(2)}, u32[]{:S(2)}) collective-permute-start(f32[608,128]{1,0:T(8,128)S(1)} %get-tuple-element.48), channel_id=1, source_target_pairs={{0,4},{1,0},{3,1},{2,3},{6,2},{7,6},{5,7},{4,5},{8,12},{9,8},{11,9... | collective-permute-start | bytes 933896 | tf_op jit(solution)/shard_map/ppermute | solution.py:562
  5.3 1.8 %collective-permute-start = (f32[19,16,128]{2,1,0:T(8,128)S(1)}, f32[19,16,128]{2,1,0:T(8,128)S(1)}, u32[]{:S(2)}, u32[]{:S(2)}) collective-permute-start(f32[19,16,128]{2,1,0:T(8,128)S(1)} %get-tuple-element.43), channel_id=1, source_target_pairs={{0,8},{8,16},{16,24},{24,0},{1,9},{9,17},{17,25},{25,1},{2,10},{10... | collective-permute-start | bytes 466952 | tf_op jit(solution)/shard_map/ppermute | solution.py:559
  7.1 1.2 %collective-permute-start.1 = (f32[19,16,128]{2,1,0:T(8,128)S(1)}, f32[19,16,128]{2,1,0:T(8,128)S(1)}, u32[]{:S(2)}, u32[]{:S(2)}) collective-permute-start(f32[19,16,128]{2,1,0:T(8,128)S(1)} %get-tuple-element.44), channel_id=1, source_target_pairs={{0,24},{8,0},{16,8},{24,16},{1,25},{9,1},{17,9},{25,17},{2,26},{10... | collective-permute-start | bytes 466952 | tf_op jit(solution)/shard_map/ppermute | solution.py:559
  8.3 4.0 %collective-permute-done.low = f32[19,16,128]{2,1,0:T(8,128)S(1)} collective-permute-done((f32[19,16,128]{2,1,0:T(8,128)S(1)}, f32[19,16,128]{2,1,0:T(8,128)S(1)}, u32[]{:S(2)}, u32[]{:S(2)}) %collective-permute-start) | collective-permute-done | bytes 155680 | tf_op jit(solution)/shard_map/ppermute | solution.py:559
  12.3 1.7 %collective-permute-done.1.high = f32[19,16,128]{2,1,0:T(8,128)S(1)} collective-permute-done((f32[19,16,128]{2,1,0:T(8,128)S(1)}, f32[19,16,128]{2,1,0:T(8,128)S(1)}, u32[]{:S(2)}, u32[]{:S(2)}) %collective-permute-start.1) | collective-permute-done | bytes 155680 | tf_op jit(solution)/shard_map/ppermute | solution.py:559
  14.1 0.1 collective-permute-start.2
  14.1 2.9 %collective-permute-start.3 = (f32[176,128]{1,0:T(8,128)S(1)}, f32[176,128]{1,0:T(8,128)S(1)}, u32[]{:S(2)}, u32[]{:S(2)}) collective-permute-start(f32[176,128]{1,0:T(8,128)S(1)} %get-tuple-element.46), channel_id=1, source_target_pairs={{0,4},{1,0},{3,1},{2,3},{6,2},{7,6},{5,7},{4,5},{8,12},{9,8},{11,9... | collective-permute-start | bytes 270344 | tf_op jit(solution)/shard_map/ppermute | solution.py:562
  17.1 1.5 %shard_map.39 = (f32[48,32,128]{2,1,0:T(8,128)S(1)}, f32[48,32,128]{2,1,0:T(8,128)S(1)}, f32[48,32,128]{2,1,0:T(8,128)S(1)}, f32[48,32,128]{2,1,0:T(8,128)S(1)},...) custom-call(f32[608,128]{1,0:T(8,128)S(1)} %collective-permute-done., ...), custom_call_target="tpu_custom_call", output_to_operand_aliasing={{0}: (2, {}), {1}: (3, {}), {2}: (4, {})} | custom-call | tf_op jit(solution)/shard_map/pallas_call | solution.py:600
  18.6 1.0 %collective-permute-done.2.c_low = f32[176,128]{1,0:T(8,128)S(1)} collective-permute-done((f32[176,128]{1,0:T(8,128)S(1)}, f32[176,128]{1,0:T(8,128)S(1)}, u32[]{:S(2)}, u32[]{:S(2)}) %collective-permute-start.2) | collective-permute-done | bytes 90144 | tf_op jit(solution)/shard_map/ppermute | solution.py:562
  19.6 0.0 collective-permute-done.3.c_high
  19.6 1.9 %shard_map.40 = (f32[48,32,128]{2,1,0:T(8,128)S(1)}, f32[48,32,128]{2,1,0:T(8,128)S(1)}, f32[48,32,128]{2,1,0:T(8,128)S(1)}, f32[48,32,128]{2,1,0:T(8,128)S(1)},...) custom-call(f32[19,16,128]{2,1,0:T(8,128)S(1)} %collective-permute-d, ...), custom_call_target="tpu_custom_call", output_to_operand_aliasing={{0}: (4, {}), {1}: (5, {}), {2}: (6, {}), {3}: (7, {}), {4}... | custom-call | tf_op jit(solution)/shard_map/pallas_call | solution.py:611
  21.5 1.5 %collective-permute-start.6 = (f32[48,128]{1,0:T(8,128)S(1)}, f32[48,128]{1,0:T(8,128)S(1)}, u32[]{:S(2)}, u32[]{:S(2)}) collective-permute-start(f32[48,128]{1,0:T(8,128)S(1)} %get-tuple-element.65), channel_id=1, source_target_pairs={{0,8},{8,16},{16,24},{24,0},{1,9},{9,17},{17,25},{25,1},{2,10},{10... | collective-permute-start | bytes 73736 | tf_op jit(solution)/shard_map/ppermute | solution.py:559
  23.0 1.5 %collective-permute-start.7 = (f32[48,128]{1,0:T(8,128)S(1)}, f32[48,128]{1,0:T(8,128)S(1)}, u32[]{:S(2)}, u32[]{:S(2)}) collective-permute-start(f32[48,128]{1,0:T(8,128)S(1)} %get-tuple-element.66), channel_id=1, source_target_pairs={{0,24},{8,0},{16,8},{24,16},{1,25},{9,1},{17,9},{25,17},{2,26},{10... | collective-permute-start | bytes 73736 | tf_op jit(solution)/shard_map/ppermute | solution.py:559
  24.5 1.8 %collective-permute-done.6.low = f32[48,128]{1,0:T(8,128)S(1)} collective-permute-done((f32[48,128]{1,0:T(8,128)S(1)}, f32[48,128]{1,0:T(8,128)S(1)}, u32[]{:S(2)}, u32[]{:S(2)}) %collective-permute-start.6) | collective-permute-done | bytes 24608 | tf_op jit(solution)/shard_map/ppermute | solution.py:559
  26.3 0.6 %collective-permute-done.7.high = f32[48,128]{1,0:T(8,128)S(1)} collective-permute-done((f32[48,128]{1,0:T(8,128)S(1)}, f32[48,128]{1,0:T(8,128)S(1)}, u32[]{:S(2)}, u32[]{:S(2)}) %collective-permute-start.7) | collective-permute-done | bytes 24608 | tf_op jit(solution)/shard_map/ppermute | solution.py:559
  26.8 0.1 collective-permute-start.9
  26.9 3.1 %collective-permute-start.10 = (f32[136,128]{1,0:T(8,128)S(1)}, f32[136,128]{1,0:T(8,128)S(1)}, u32[]{:S(2)}, u32[]{:S(2)}) collective-permute-start(f32[136,128]{1,0:T(8,128)S(1)} %get-tuple-element.69), channel_id=1, source_target_pairs={{0,4},{1,0},{3,1},{2,3},{6,2},{7,6},{5,7},{4,5},{8,12},{9,8},{11,9... | collective-permute-start | bytes 208904 | tf_op jit(solution)/shard_map/ppermute | solution.py:562
  30.0 0.0 collective-permute-start.11
  30.0 1.7 %collective-permute-start.8 = (f32[64,128]{1,0:T(8,128)S(1)}, f32[64,128]{1,0:T(8,128)S(1)}, u32[]{:S(2)}, u32[]{:S(2)}) collective-permute-start(f32[64,128]{1,0:T(8,128)S(1)} %get-tuple-element.67.own), channel_id=1, source_target_pairs={{0,3},{1,2},{3,6},{2,7},{6,5},{7,4},{5,0},{4,1},{8,11},{9,10},{11,... | collective-permute-start | bytes 98312 | tf_op jit(solution)/shard_map/ppermute | solution.py:562
  31.8 1.9 %collective-permute-done.11.far_high = f32[64,128]{1,0:T(8,128)S(1)} collective-permute-done((f32[64,128]{1,0:T(8,128)S(1)}, f32[64,128]{1,0:T(8,128)S(1)}, u32[]{:S(2)}, u32[]{:S(2)}) %collective-permute-start.11) | collective-permute-done | bytes 32800 | tf_op jit(solution)/shard_map/ppermute | solution.py:562
  33.7 3.1 %collective-permute-done.8.far_low = f32[64,128]{1,0:T(8,128)S(1)} collective-permute-done((f32[64,128]{1,0:T(8,128)S(1)}, f32[64,128]{1,0:T(8,128)S(1)}, u32[]{:S(2)}, u32[]{:S(2)}) %collective-permute-start.8) | collective-permute-done | bytes 32800 | tf_op jit(solution)/shard_map/ppermute | solution.py:562
  36.8 4.2 %shard_map.42 = f32[32,16,128]{2,1,0:T(8,128)} custom-call(f32[64,128]{1,0:T(8,128)S(1)} %collective-permute-done.8.far_low, f32[136,128]{1,0:T(8,128)S(1)} %collective-permute-done.9.near_low, f32[64,128]{1,0:T(8,128)S(1)} %get-tuple-element.67.own, f32[136,128]{1,0:T(8,128)S(1)} %collective-permute-done.10.near_high, ...), custom_call_target="tpu_custom_call" | custom-call | tf_op jit(solution)/shard_map/pallas_call | solution.py:645
  (6 shorter events, 0.1 us)
Async XLA Ops:
  1.2 15.9 %collective-permute-start.4 = (f32[608,128]{1,0:T(8,128)S(1)}, f32[608,128]{1,0:T(8,128)S(1)}, u32[]{:S(2)}, u32[]{:S(2)}) collective-permute-start(f32[608,128]{1,0:T(8,128)S(1)} %get-tuple-element.47), channel_id=1, source_target_pairs={{0,1},{1,3},{3,2},{2,6},{6,7},{7,5},{5,4},{4,0},{8,9},{9,11},{11,1... | collective-permute-start | bytes 933896 | tf_op jit(solution)/shard_map/ppermute | solution.py:562
  1.7 15.4 %collective-permute-start.5 = (f32[608,128]{1,0:T(8,128)S(1)}, f32[608,128]{1,0:T(8,128)S(1)}, u32[]{:S(2)}, u32[]{:S(2)}) collective-permute-start(f32[608,128]{1,0:T(8,128)S(1)} %get-tuple-element.48), channel_id=1, source_target_pairs={{0,4},{1,0},{3,1},{2,3},{6,2},{7,6},{5,7},{4,5},{8,12},{9,8},{11,9... | collective-permute-start | bytes 933896 | tf_op jit(solution)/shard_map/ppermute | solution.py:562
  5.3 7.0 %collective-permute-start = (f32[19,16,128]{2,1,0:T(8,128)S(1)}, f32[19,16,128]{2,1,0:T(8,128)S(1)}, u32[]{:S(2)}, u32[]{:S(2)}) collective-permute-start(f32[19,16,128]{2,1,0:T(8,128)S(1)} %get-tuple-element.43), channel_id=1, source_target_pairs={{0,8},{8,16},{16,24},{24,0},{1,9},{9,17},{17,25},{25,1},{2,10},{10... | collective-permute-start | bytes 466952 | tf_op jit(solution)/shard_map/ppermute | solution.py:559
  7.1 6.9 %collective-permute-start.1 = (f32[19,16,128]{2,1,0:T(8,128)S(1)}, f32[19,16,128]{2,1,0:T(8,128)S(1)}, u32[]{:S(2)}, u32[]{:S(2)}) collective-permute-start(f32[19,16,128]{2,1,0:T(8,128)S(1)} %get-tuple-element.44), channel_id=1, source_target_pairs={{0,24},{8,0},{16,8},{24,16},{1,25},{9,1},{17,9},{25,17},{2,26},{10... | collective-permute-start | bytes 466952 | tf_op jit(solution)/shard_map/ppermute | solution.py:559
  14.1 5.5 %collective-permute-start.2 = (f32[176,128]{1,0:T(8,128)S(1)}, f32[176,128]{1,0:T(8,128)S(1)}, u32[]{:S(2)}, u32[]{:S(2)}) collective-permute-start(f32[176,128]{1,0:T(8,128)S(1)} %get-tuple-element.45), channel_id=1, source_target_pairs={{0,1},{1,3},{3,2},{2,6},{6,7},{7,5},{5,4},{4,0},{8,9},{9,11},{11,1... | collective-permute-start | bytes 270344 | tf_op jit(solution)/shard_map/ppermute | solution.py:562
  14.1 5.4 %collective-permute-start.3 = (f32[176,128]{1,0:T(8,128)S(1)}, f32[176,128]{1,0:T(8,128)S(1)}, u32[]{:S(2)}, u32[]{:S(2)}) collective-permute-start(f32[176,128]{1,0:T(8,128)S(1)} %get-tuple-element.46), channel_id=1, source_target_pairs={{0,4},{1,0},{3,1},{2,3},{6,2},{7,6},{5,7},{4,5},{8,12},{9,8},{11,9... | collective-permute-start | bytes 270344 | tf_op jit(solution)/shard_map/ppermute | solution.py:562
  21.5 4.8 %collective-permute-start.6 = (f32[48,128]{1,0:T(8,128)S(1)}, f32[48,128]{1,0:T(8,128)S(1)}, u32[]{:S(2)}, u32[]{:S(2)}) collective-permute-start(f32[48,128]{1,0:T(8,128)S(1)} %get-tuple-element.65), channel_id=1, source_target_pairs={{0,8},{8,16},{16,24},{24,0},{1,9},{9,17},{17,25},{25,1},{2,10},{10... | collective-permute-start | bytes 73736 | tf_op jit(solution)/shard_map/ppermute | solution.py:559
  23.0 3.8 %collective-permute-start.7 = (f32[48,128]{1,0:T(8,128)S(1)}, f32[48,128]{1,0:T(8,128)S(1)}, u32[]{:S(2)}, u32[]{:S(2)}) collective-permute-start(f32[48,128]{1,0:T(8,128)S(1)} %get-tuple-element.66), channel_id=1, source_target_pairs={{0,24},{8,0},{16,8},{24,16},{1,25},{9,1},{17,9},{25,17},{2,26},{10... | collective-permute-start | bytes 73736 | tf_op jit(solution)/shard_map/ppermute | solution.py:559
  26.8 9.9 %collective-permute-start.9 = (f32[136,128]{1,0:T(8,128)S(1)}, f32[136,128]{1,0:T(8,128)S(1)}, u32[]{:S(2)}, u32[]{:S(2)}) collective-permute-start(f32[136,128]{1,0:T(8,128)S(1)} %get-tuple-element.68), channel_id=1, source_target_pairs={{0,1},{1,3},{3,2},{2,6},{6,7},{7,5},{5,4},{4,0},{8,9},{9,11},{11,1... | collective-permute-start | bytes 208904 | tf_op jit(solution)/shard_map/ppermute | solution.py:562
  26.9 9.9 %collective-permute-start.10 = (f32[136,128]{1,0:T(8,128)S(1)}, f32[136,128]{1,0:T(8,128)S(1)}, u32[]{:S(2)}, u32[]{:S(2)}) collective-permute-start(f32[136,128]{1,0:T(8,128)S(1)} %get-tuple-element.69), channel_id=1, source_target_pairs={{0,4},{1,0},{3,1},{2,3},{6,2},{7,6},{5,7},{4,5},{8,12},{9,8},{11,9... | collective-permute-start | bytes 208904 | tf_op jit(solution)/shard_map/ppermute | solution.py:562
  30.0 3.7 %collective-permute-start.11 = (f32[64,128]{1,0:T(8,128)S(1)}, f32[64,128]{1,0:T(8,128)S(1)}, u32[]{:S(2)}, u32[]{:S(2)}) collective-permute-start(f32[64,128]{1,0:T(8,128)S(1)} %get-tuple-element.67.own), channel_id=1, source_target_pairs={{0,5},{1,4},{3,0},{2,1},{6,3},{7,2},{5,6},{4,7},{8,13},{9,12},{11,... | collective-permute-start | bytes 98312 | tf_op jit(solution)/shard_map/ppermute | solution.py:562
  30.0 6.7 %collective-permute-start.8 = (f32[64,128]{1,0:T(8,128)S(1)}, f32[64,128]{1,0:T(8,128)S(1)}, u32[]{:S(2)}, u32[]{:S(2)}) collective-permute-start(f32[64,128]{1,0:T(8,128)S(1)} %get-tuple-element.67.own), channel_id=1, source_target_pairs={{0,3},{1,2},{3,6},{2,7},{6,5},{7,4},{5,0},{4,1},{8,11},{9,10},{11,... | collective-permute-start | bytes 98312 | tf_op jit(solution)/shard_map/ppermute | solution.py:562

commit v6 on v5

v6 whole, which is shorter than its diff:
```python
import jax
import jax.numpy as jnp
from jax import lax
from jax.experimental import pallas as pl
from jax.experimental.pallas import tpu as pltpu
from jax.sharding import PartitionSpec as P

OMEGA = 0.7
FRAME = 8
WIDE_F = 6
WIDE_B = 7
COARSE_PITCH = 24
COARSE_X = 6
FINE_X = 3
LANES = 128
ANY = pl.BlockSpec(memory_space=pl.ANY)
HBM = pl.BlockSpec(memory_space=pltpu.HBM)
VMEM = pl.BlockSpec(memory_space=pltpu.VMEM)
LIMIT = 16 * 1024 * 1024


def params():
    return pltpu.CompilerParams(vmem_limit_bytes=LIMIT)


def gray_position(code, bit_count):
    position = code
    for shift in range(1, bit_count):
        position = position ^ (code >> shift)
    return position


def box_position():
    bit_count = lax.axis_size("box").bit_length() - 1
    return gray_position(lax.axis_index("box"), bit_count)


def even_position():
    return box_position() % 2 == 0


def run_copies(pairs, sems):
    copies = [pltpu.make_async_copy(src, dst, sems.at[at]) for at, (src, dst) in enumerate(pairs)]
    for copy in copies:
        copy.start()
    return copies


def wait_copies(copies):
    for copy in copies:
        copy.wait()


def lane_ids(shape):
    return lax.broadcasted_iota(jnp.int32, shape, 1)


def y_next(row):
    return pltpu.roll(row, row.shape[0] - 1, 0)


def y_prev(row):
    return pltpu.roll(row, 1, 0)


def z_next(row, dist):
    return pltpu.roll(row, LANES - dist, 1)


def z_prev(row, dist):
    return pltpu.roll(row, dist, 1)


def coefficients(alpha, beta, beta_prev, beta_next, dist, scale):
    half = 0.5 * scale
    lane = lane_ids(beta.shape)
    inside = lane < LANES - dist
    up_z = jnp.where(inside, z_next(beta, dist), 0.0)
    down_z = jnp.where(lane >= dist, z_prev(beta, dist), 0.0)
    up_y = y_next(beta)
    face_x = half * (beta + beta_next)
    face_y = half * (beta + up_y)
    face_z = jnp.where(inside, half * (beta + up_z), 0.0)
    total = (beta_prev + beta_next) + (up_y + y_prev(beta)) + (up_z + down_z)
    diagonal = alpha + half * (6.0 * beta + total)
    inverse = jnp.where(alpha > 0.0, OMEGA / diagonal, 0.0)
    return face_x, face_y, face_z, diagonal, inverse


def off_sum(at, v, faces, dist):
    face_x, face_y, face_z = faces
    here = v[at]
    fy = face_y[at]
    fz = face_z[at]
    along_x = face_x[at] * v[at + 1] + face_x[at - 1] * v[at - 1]
    along_y = fy * y_next(here) + y_prev(fy * here)
    along_z = fz * z_next(here, dist) + z_prev(fz * here, dist)
    return here, along_x + along_y + along_z


def relaxed(at, v, f, inverse, faces, dist):
    here, off = off_sum(at, v, faces, dist)
    return (1.0 - OMEGA) * here + inverse[at] * (f[at] + off)


def rows_loop(low, high, step, fn):
    trips = (high - low) // step

    def run(rows):
        stores = [item for row in rows for item in fn(row)]
        for ref, at, value in stores:
            ref[at] = value

    def trip(t, carry):
        base = low + t * step
        run([base + k for k in range(step)])
        return carry

    lax.fori_loop(0, trips, trip, 0)
    rest = list(range(low + trips * step, high))
    if rest:
        run(rest)


def pair_sum_z(row, dist):
    lane = lane_ids(row.shape)
    first = (lane // dist) % 2 == 0
    return row + jnp.where(first, z_next(row, dist), z_prev(row, dist))


def strided_pair(ref, at, count):
    return ref[at, pl.ds(0, count, stride=2), :] + ref[at, pl.ds(1, count, stride=2), :]


def zero(ref, *at):
    ref[at] = jnp.zeros_like(ref[at])


WIDES = (WIDE_F, WIDE_F, WIDE_B)


def face_pieces(count):
    pieces = []
    at = 0
    for k, wide in enumerate(WIDES):
        for x in range(count):
            pieces.append((k, x, wide, at))
            at += wide
    return pieces, at + -at % 8


def corner_pieces():
    pieces = []
    at = 0
    for side in range(2):
        start = 0
        for k, wide in enumerate(WIDES):
            for layer in range(wide):
                distance = layer + 1 if side else wide - layer
                layers = min(wide, wide + 2 - distance)
                pieces.append((side, k, start + layer, layers, at))
                at += layers
            start += wide
    return pieces, at + -at % 8


def pack_faces_kernel(f, a, b, F, A, B, x_up, x_down, y_up, y_down, sems):
    count, depth = f.shape[:2]
    own = (pl.ds(FRAME, count), pl.ds(FRAME, depth))
    frames = (F, A, B)
    copies = run_copies([(src, dst.at[own]) for src, dst in zip((f, a, b), frames)], sems)
    pieces, _ = face_pieces(count)
    row = 0
    for k, (ref, wide) in enumerate(zip(frames, WIDES)):
        copies[k].wait()
        for layer in range(wide):
            x_up[row + layer] = ref[FRAME + count - wide + layer, FRAME:FRAME + depth]
            x_down[row + layer] = ref[FRAME + layer, FRAME:FRAME + depth]
        row += wide
        for at_k, x, layers, at in pieces:
            if at_k == k:
                y_up[at:at + layers] = ref[FRAME + x, FRAME + depth - layers:FRAME + depth]
                y_down[at:at + layers] = ref[FRAME + x, FRAME:FRAME + layers]


def pack_corners_kernel(low, high, to_even, to_odd):
    depth = low.shape[1]
    even = even_position()
    for side, _, row, layers, at in corner_pieces()[0]:
        ref = (low, high)[side]
        up = ref[row, depth - layers:depth]
        down = ref[row, 0:layers]
        to_even[at:at + layers] = jnp.where(even, up, down)
        to_odd[at:at + layers] = jnp.where(even, down, up)


def down_rows(F, A, B, FX, FY, FZ, DG, IN, V, U, T, F1, A1, B1, FX1, FY1, FZ1, D1, IN1, W1, coarse):
    faces = (FX, FY, FZ)
    half_rows = F1.shape[1]
    count2 = coarse.shape[0] // 3
    first1 = FRAME // 2
    own2 = FRAME // 4
    depth2 = half_rows // 2 - 2 * own2
    lane = lane_ids((1, LANES))

    def coef_row(i):
        fx, fy, fz, dg, inv = coefficients(A[i], B[i], B[i - 1], B[i + 1], 1, 1.0)
        return [(FX, i, fx), (FY, i, fy), (FZ, i, fz), (DG, i, dg), (IN, i, inv), (V, i, inv * F[i])]

    def sweep_row(i):
        return [(U, i, relaxed(i, V, F, IN, faces, 1))]

    def residual(i):
        here, off = off_sum(i, U, faces, 1)
        return F[i] - DG[i] * here + off

    def restrict_row(j):
        return [(T, j, residual(2 * j) + residual(2 * j + 1))]

    def level1_source(j):
        return [(F1, j, 0.125 * pair_sum_z(strided_pair(T, j, half_rows), 1))]

    def level1_coef(j):
        stores = []
        for src, dst in ((A, A1), (B, B1)):
            both = strided_pair(src, 2 * j, half_rows) + strided_pair(src, 2 * j + 1, half_rows)
            stores.append((dst, j, 0.125 * pair_sum_z(both, 1)))
        return stores

    def coef_row1(i):
        fx, fy, fz, dg, inv = coefficients(A1[i], B1[i], B1[i - 1], B1[i + 1], 2, 0.25)
        return [(FX1, i, fx), (FY1, i, fy), (FZ1, i, fz), (D1, i, dg), (IN1, i, inv), (W1, i, inv * F1[i])]

    def coarse_pack(k, ref, at, x):
        rows = half_rows // 2
        both = ref[at, pl.ds(0, rows, stride=2), :] + ref[at, pl.ds(1, rows, stride=2), :]
        value = 0.125 * pair_sum_z(both, 2)
        packed = jnp.zeros((1, LANES), jnp.float32)
        for y in range(depth2):
            packed = packed + jnp.where(lane % depth2 == y, value[own2 + y:own2 + y + 1], 0.0)
        return (coarse, pl.ds(k * count2 + x, 1), packed)

    return coef_row, sweep_row, restrict_row, level1_source, level1_coef, coef_row1, coarse_pack


def down_inner_kernel(y_low, y_high, F_in, A_in, B_in, *refs):
    *refs, T1 = refs
    F, A, B = frames = refs[:3]
    A1, B1 = refs[12:14]
    end = F.shape[0]
    depth = F.shape[1] - 2 * FRAME
    count = end - 2 * FRAME
    for k, x, layers, at in face_pieces(count)[0]:
        frames[k][FRAME + x, FRAME - layers:FRAME] = y_low[at:at + layers]
        frames[k][FRAME + x, FRAME + depth:FRAME + depth + layers] = y_high[at:at + layers]
    zero_y_edges(frames, depth)
    coef_row, sweep_row, restrict_row, level1_source, level1_coef, coef_row1, coarse_pack = down_rows(*refs)
    first1 = FRAME // 2
    end1 = end // 2
    rows_loop(FRAME + 1, end - FRAME - 1, 10, coef_row)
    rows_loop(FRAME + 2, end - FRAME - 2, 14, sweep_row)
    rows_loop(first1 + 2, end1 - first1 - 2, 6, restrict_row)
    rows_loop(first1 + 2, end1 - first1 - 2, 12, level1_source)
    rows_loop(first1, end1 - first1, 8, level1_coef)
    rows_loop(first1 + 2, end1 - first1 - 2, 12, coef_row1)
    count2 = count // 4

    def coarse_sum(x):
        i = first1 + 2 * x
        return [(T1, x, A1[i] + A1[i + 1]), (T1, count2 + x, B1[i] + B1[i + 1])]

    rows_loop(0, count2, 8, coarse_sum)

    def coarse_rows(x):
        return [coarse_pack(1, T1, x, x), coarse_pack(2, T1, count2 + x, x)]

    rows_loop(0, count2, 8, coarse_rows)


def zero_y_edges(frames, depth):
    position = box_position()
    for edge, y in (
        (position == 0, slice(0, FRAME)),
        (position == lax.axis_size("box") - 1, slice(FRAME + depth, FRAME + depth + FRAME)),
    ):

        @pl.when(edge)
        def _(y=y):
            for ref in frames:
                zero(ref, slice(None), y)


def down_kernel(low, high, c_even, c_odd, *refs):
    refs = refs[21:]
    *refs, V1, to_up, to_down, T1 = refs
    F, A, B = frames = refs[:3]
    FX = refs[3]
    F1, A1, B1, FX1, FY1, FZ1, D1, IN1, W1, coarse = refs[11:]
    count = F.shape[0] - 2 * FRAME
    depth = F.shape[1] - 2 * FRAME
    even = even_position()
    start = 0
    for k, wide in enumerate(WIDES):
        for layer in range(wide):
            frames[k][FRAME - wide + layer, FRAME:FRAME + depth] = low[start + layer]
            frames[k][FRAME + count + layer, FRAME:FRAME + depth] = high[start + layer]
        start += wide
    starts = (0, WIDE_F, 2 * WIDE_F)
    for side, k, row, layers, at in corner_pieces()[0]:
        x = row - starts[k] + (FRAME + count if side else FRAME - WIDES[k])
        near_even = c_even[at:at + layers]
        near_odd = c_odd[at:at + layers]
        frames[k][x, FRAME - layers:FRAME] = jnp.where(even, near_odd, near_even)
        frames[k][x, FRAME + depth:FRAME + depth + layers] = jnp.where(even, near_even, near_odd)
    zero_y_edges(frames, depth)
    group = lax.axis_index("grp")
    for edge, x in (
        (group == 0, slice(0, FRAME)),
        (group == lax.axis_size("grp") - 1, slice(FRAME + count, FRAME + count + FRAME)),
    ):

        @pl.when(edge)
        def _(x=x):
            for ref in frames:
                zero(ref, x)

    end = count + 2 * FRAME
    coef_row, sweep_row, restrict_row, level1_source, level1_coef, coef_row1, coarse_pack = down_rows(*refs)
    first1 = FRAME // 2
    end1 = end // 2
    FX[1] = 0.5 * (B[1] + B[2])
    for margin, fn in ((2, coef_row), (3, sweep_row)):
        rows_loop(margin, FRAME + margin - 1, 7, fn)
        rows_loop(end - FRAME - margin + 1, end - margin, 7, fn)
    for fn in (restrict_row, level1_source):
        rows_loop(2, first1 + 2, 4, fn)
        rows_loop(end1 - first1 - 2, end1 - 2, 4, fn)
    rows_loop(1, first1, 3, level1_coef)
    rows_loop(end1 - first1, end1 - 1, 3, level1_coef)
    FX1[1] = 0.125 * (B1[1] + B1[2])
    rows_loop(2, first1 + 2, 4, coef_row1)
    rows_loop(end1 - first1 - 2, end1 - 2, 4, coef_row1)

    faces1 = (FX1, FY1, FZ1)

    def sweep_row1(i):
        return [(V1, i, relaxed(i, W1, F1, IN1, faces1, 2))]

    rows_loop(3, end1 - 3, 18, sweep_row1)

    def residual1(i):
        here, off = off_sum(i, V1, faces1, 2)
        return F1[i] - D1[i] * here + off

    count1 = count // 2
    count2 = count // 4

    def coarse_row(x):
        i = first1 + 2 * x
        return [(T1, x, residual1(i) + residual1(i + 1))]

    rows_loop(0, count2, 8, coarse_row)

    def coarse_source(x):
        return [coarse_pack(0, T1, x, x)]

    rows_loop(0, count2, 8, coarse_source)

    own1 = slice(first1, first1 + depth // 2)
    for k in range(3):
        rows = slice(k * COARSE_X, (k + 1) * COARSE_X)
        to_up[rows] = coarse[(k + 1) * count2 - COARSE_X:(k + 1) * count2]
        to_down[rows] = coarse[k * count2:k * count2 + COARSE_X]
    for k in range(FINE_X):
        rows = slice(3 * COARSE_X + k * depth // 2, 3 * COARSE_X + (k + 1) * depth // 2)
        to_up[rows] = V1[first1 + count1 - FINE_X + k, own1]
        to_down[rows] = V1[first1 + k, own1]


def pack_coarse_kernel(coarse, v1, low, high, far, to_even, to_odd):
    count2 = coarse.shape[0] // 3
    first1 = FRAME // 2
    depth1 = v1.shape[1] - FRAME
    count1 = 2 * count2
    for k in range(3):
        row = k * COARSE_PITCH
        part = slice(k * COARSE_X, (k + 1) * COARSE_X)
        far[row:row + COARSE_X] = low[part]
        far[row + COARSE_X:row + COARSE_X + count2] = coarse[k * count2:(k + 1) * count2]
        far[row + COARSE_X + count2:row + 2 * COARSE_X + count2] = high[part]
    rows = far.shape[0]
    to_even[0:rows] = far[...]
    to_odd[0:rows] = far[...]
    even = even_position()
    tiles = [low[3 * COARSE_X + k * depth1:3 * COARSE_X + (k + 1) * depth1] for k in range(FINE_X)]
    tiles += [v1[first1 + k, first1:first1 + depth1] for k in range(count1)]
    tiles += [high[3 * COARSE_X + k * depth1:3 * COARSE_X + (k + 1) * depth1] for k in range(FINE_X)]
    for k, tile in enumerate(tiles):
        part = slice(rows + k * FINE_X, rows + (k + 1) * FINE_X)
        up = tile[depth1 - FINE_X:]
        down = tile[:FINE_X]
        to_even[part] = jnp.where(even, up, down)
        to_odd[part] = jnp.where(even, down, up)


def coarse_solve(source, alpha, beta):
    shape = beta[0].shape
    lane = lane_ids(shape)
    first = lane % 4 == 0
    last = lane % 4 == 3
    inside = lane < LANES - 4
    nothing = jnp.zeros(shape, jnp.float32)

    def next_x(v):
        return pltpu.roll(v, shape[0] - 1, 0)

    def prev_x(v):
        return pltpu.roll(v, 1, 0)

    def next_y(vs):
        over = [pltpu.roll(v, 3, 1) for v in vs[1:]] + [nothing]
        return [jnp.where(last, o, pltpu.roll(v, LANES - 1, 1)) for o, v in zip(over, vs)]

    def prev_y(vs):
        over = [nothing] + [pltpu.roll(v, LANES - 3, 1) for v in vs[:-1]]
        return [jnp.where(first, o, pltpu.roll(v, 1, 1)) for o, v in zip(over, vs)]

    half = 0.5 * 0.0625
    coefs = []
    for a, b, b_next, b_prev in zip(alpha, beta, next_y(beta), prev_y(beta)):
        up_x = next_x(b)
        up_z = jnp.where(inside, z_next(b, 4), 0.0)
        down_z = jnp.where(lane >= 4, z_prev(b, 4), 0.0)
        total = (prev_x(b) + up_x) + (b_next + b_prev) + (up_z + down_z)
        diagonal = a + half * (6.0 * b + total)
        inverse = jnp.where(a > 0.0, OMEGA / diagonal, 0.0)
        face_z = jnp.where(inside, half * (b + up_z), 0.0)
        coefs.append((half * (b + up_x), half * (b + b_next), face_z, inverse))
    field = [c[3] * f for c, f in zip(coefs, source)]
    for _ in range(3):
        flux = prev_y([c[1] * v for c, v in zip(coefs, field)])
        new = []
        for (fx, fy, fz, inverse), v, v_next, back, f in zip(coefs, field, next_y(field), flux, source):
            off = fx * next_x(v) + prev_x(fx * v)
            off = off + (fy * v_next + back)
            off = off + (fz * z_next(v, 4) + z_prev(fz * v, 4))
            new.append((1.0 - OMEGA) * v + inverse * (f + off))
        field = new
    return field


def up_kernel(
    near_even, near_odd, far_even, far_odd, own, low, high,
    in_v, F, IN, FX, FY, FZ,
    in_v1, F1, IN1, FX1, FY1, FZ1,
    out,
    V, U, V1, U1, C2, P0, result, sems,
):
    group = lax.axis_index("grp")
    position = box_position()
    even = position % 2 == 0
    last_group = lax.axis_size("grp") - 1
    last_block = lax.axis_size("box") - 1
    count, depth = result.shape[:2]

    row2 = lax.broadcasted_iota(jnp.int32, (COARSE_PITCH, LANES), 0) - COARSE_X + group * (count // 4)
    in_x = (row2 >= 0) & (row2 < (last_group + 1) * (count // 4))
    arrays = []
    for k in range(3):
        rows = pl.ds(k * COARSE_PITCH, COARSE_PITCH)
        ne, no, fe, fo = near_even[rows], near_odd[rows], far_even[rows], far_odd[rows]
        blocks = (
            jnp.where(even, fo, fe), jnp.where(even, no, ne), own[rows],
            jnp.where(even, ne, no), jnp.where(even, fe, fo),
        )
        column = []
        for at, value in enumerate(blocks):
            place = position + (at - 2)
            column.append(jnp.where(in_x & ((place >= 0) & (place <= last_block)), value, 0.0))
        arrays.append(column)
    field2 = coarse_solve(*arrays)
    for at in range(3):
        C2[at] = field2[1 + at]

    first1 = FRAME // 2
    depth1 = depth // 2
    span1 = V1.shape[0]
    rows1 = V1.shape[1]
    own_rows = pl.ds(first1, depth1)

    def own_row(x):
        i = first1 + x
        return [(V1, (i, own_rows), in_v1[i, own_rows])]

    rows_loop(0, span1 - 2 * first1, 16, own_row)
    for k in range(FINE_X):
        tile = pl.ds(3 * COARSE_X + k * depth1, depth1)
        V1[first1 - FINE_X + k, own_rows] = low[tile]
        V1[span1 - first1 + k, own_rows] = high[tile]

    rim = own.shape[0]

    def rim_row(x):
        i = x + first1 - FINE_X
        part = pl.ds(rim + FINE_X * x, FINE_X)
        ne, no = near_even[part], near_odd[part]
        near_low = jnp.where(even, no, ne)
        near_high = jnp.where(even, ne, no)
        return [
            (V1, (i, slice(first1 - FINE_X, first1)), jnp.where(position > 0, near_low, 0.0)),
            (
                V1,
                (i, slice(first1 + depth1, first1 + depth1 + FINE_X)),
                jnp.where(position < last_block, near_high, 0.0),
            ),
        ]

    rows_loop(0, span1 - 2 * (first1 - FINE_X), 22, rim_row)
    for edge, rows in ((group == 0, slice(0, first1)), (group == last_group, slice(span1 - first1, span1))):

        @pl.when(edge)
        def _(rows=rows):
            zero(V1, rows)

    sub = lax.broadcasted_iota(jnp.int32, (rows1, LANES), 0)
    lane = lane_ids((rows1, LANES))
    block = (sub + 4) // 8
    mine = lane % 4 == (sub // 2 + 2) % 4
    last_of_four = lane % 4 == 3

    def corrected_row(x):
        row = pl.ds(x + COARSE_X - first1 // 2, 1)
        t = jnp.broadcast_to(C2[0, row], (rows1, LANES))
        for at in range(1, 3):
            t = jnp.where(block == at, jnp.broadcast_to(C2[at, row], (rows1, LANES)), t)
        t = jnp.where(mine, t, 0.0)
        t = t + z_prev(t, 1)
        t = t + z_prev(t, 2)
        t = jnp.where(last_of_four, t, 0.0)
        t = t + z_next(t, 1)
        t = t + z_next(t, 2)
        return [(V1, 2 * x + k, V1[2 * x + k] + t) for k in range(2)]

    rows_loop(0, span1 // 2, 12, corrected_row)
    faces1 = (FX1, FY1, FZ1)

    def sweep_a1(i):
        return [(U1, i, relaxed(i, V1, F1, IN1, faces1, 2))]

    rows_loop(2, span1 - 2, 10, sweep_a1)

    def sweep_b1(i):
        return [(V1, i, relaxed(i, U1, F1, IN1, faces1, 2))]

    rows_loop(3, span1 - 3, 18, sweep_b1)

    span = V.shape[0]
    start = FRAME - 2

    def widen(x):
        row = V1[x + start // 2]
        return [(P0, (x, pl.ds(k, rows1, stride=2)), row) for k in range(2)]

    rows_loop(0, (span - 2 * start) // 2, 18, widen)

    def corrected0(x):
        add = P0[x]
        i = start + 2 * x
        return [(V, i + k, in_v[i + k] + add) for k in range(2)]

    rows_loop(0, (span - 2 * start) // 2, 9, corrected0)
    faces = (FX, FY, FZ)

    def sweep_a(i):
        return [(U, i, relaxed(i, V, F, IN, faces, 1))]

    rows_loop(start + 1, span - start - 1, 17, sweep_a)

    def sweep_b(i):
        rows = pl.ds(FRAME, depth)
        here = U[i, rows]
        fz = FZ[i, rows]
        along_x = FX[i, rows] * U[i + 1, rows] + FX[i - 1, rows] * U[i - 1, rows]
        before = pl.ds(FRAME - 1, depth)
        along_y = FY[i, rows] * U[i, pl.ds(FRAME + 1, depth)] + FY[i, before] * U[i, before]
        along_z = fz * z_next(here, 1) + z_prev(fz * here, 1)
        off = along_x + along_y + along_z
        return [(result, i - FRAME, (1.0 - OMEGA) * here + IN[i, rows] * (F[i, rows] + off))]

    chunk = count // 4
    copies = []
    for k in range(4):
        rows_loop(FRAME + k * chunk, FRAME + (k + 1) * chunk, chunk, sweep_b)
        rows = pl.ds(k * chunk, chunk)
        copies.append(pltpu.make_async_copy(result.at[rows], out.at[rows], sems.at[k]))
        copies[-1].start()
    wait_copies(copies)


def body(source, alpha, beta):
    f = source[:, 0]
    a = alpha[:, 0]
    b = beta[:, 0]
    count, depth, lanes = f.shape
    groups = lax.axis_size("grp")
    blocks = lax.axis_size("box")
    code = [p ^ (p >> 1) for p in range(blocks)]

    def along_x(array, by):
        return lax.ppermute(array, "grp", [(i, (i + by) % groups) for i in range(groups)])

    def along_y(array, by):
        return lax.ppermute(array, "box", [(code[p], code[(p + by) % blocks]) for p in range(blocks)])

    def from_partner(array, even_by):
        return lax.ppermute(
            array,
            "box",
            [(code[(p + (even_by if p % 2 == 0 else -even_by)) % blocks], code[p]) for p in range(blocks)],
        )

    def arr(*shape):
        return jax.ShapeDtypeStruct(shape, jnp.float32)

    def vm(*shape):
        return pltpu.VMEM(shape, jnp.float32)

    dma = pltpu.SemaphoreType.DMA
    x_rows = 2 * WIDE_F + WIDE_B
    framed = (count + 2 * FRAME, depth + 2 * FRAME, lanes)
    y_rows = face_pieces(count)[1]
    c_rows = corner_pieces()[1]
    *frames, x_up, x_down, y_up, y_down = pl.pallas_call(
        pack_faces_kernel,
        out_shape=[arr(*framed)] * 3 + [arr(x_rows, depth, lanes)] * 2 + [arr(y_rows, lanes)] * 2,
        in_specs=[HBM] * 3,
        out_specs=[VMEM] * 7,
        scratch_shapes=[dma((3,))],
        compiler_params=params(),
    )(*[pltpu.with_memory_space_constraint(t, pltpu.HBM) for t in (f, a, b)])
    low = along_x(x_up, 1)
    high = along_x(x_down, -1)
    y_low = along_y(y_up, 1)
    y_high = along_y(y_down, -1)

    c_even, c_odd = pl.pallas_call(
        pack_corners_kernel,
        out_shape=[arr(c_rows, lanes)] * 2,
        in_specs=[VMEM] * 2,
        out_specs=[VMEM] * 2,
        compiler_params=params(),
    )(low, high)
    c_even = from_partner(c_even, 1)
    c_odd = from_partner(c_odd, -1)

    framed1 = (framed[0] // 2, framed[1] // 2, lanes)
    count2 = count // 4
    passed = [arr(*framed)] * 10 + [arr(framed1[0], framed[1], lanes)] + [arr(*framed1)] * 9 + [arr(3 * count2, lanes)]
    passed = pl.pallas_call(
        down_inner_kernel,
        out_shape=passed,
        in_specs=[VMEM] * 5,
        out_specs=[VMEM] * 21,
        input_output_aliases={2 + k: k for k in range(3)},
        scratch_shapes=[vm(2 * count2, framed1[1], lanes)],
        compiler_params=params(),
    )(y_low, y_high, *frames)
    x2_rows = 3 * COARSE_X + FINE_X * depth // 2
    x2_rows += -x2_rows % 8
    results = pl.pallas_call(
        down_kernel,
        out_shape=[arr(*t.shape) for t in passed] + [arr(*framed1)] + [arr(x2_rows, lanes)] * 2,
        in_specs=[VMEM] * 25,
        out_specs=[VMEM] * 24,
        input_output_aliases={4 + k: k for k in range(21)},
        scratch_shapes=[vm(count2, framed1[1], lanes)],
        compiler_params=params(),
    )(low, high, c_even, c_odd, *passed)
    F, _, _, FX, FY, FZ, _, IN, _, U, _, F1, _, _, FX1, FY1, FZ1, _, IN1, _, coarse, V1, to_up, to_down = results

    low2 = along_x(to_up, 1)
    high2 = along_x(to_down, -1)
    far_rows = 3 * COARSE_PITCH
    near_rows = far_rows + FINE_X * (count // 2 + 2 * FINE_X)
    near_rows += -near_rows % 8
    far, to_even, to_odd = pl.pallas_call(
        pack_coarse_kernel,
        out_shape=[arr(far_rows, lanes)] + [arr(near_rows, lanes)] * 2,
        in_specs=[VMEM] * 4,
        out_specs=[VMEM] * 3,
        compiler_params=params(),
    )(coarse, V1, low2, high2)
    near_even = from_partner(to_even, 1)
    near_odd = from_partner(to_odd, -1)
    far_even = from_partner(far, 2)
    far_odd = from_partner(far, -2)

    out = pl.pallas_call(
        up_kernel,
        out_shape=arr(count, depth, lanes),
        in_specs=[VMEM] * 19,
        out_specs=HBM,
        scratch_shapes=[vm(*framed)] * 2 + [vm(*framed1)] * 2
        + [vm(3, COARSE_PITCH, lanes), vm(count // 2 + 2, framed[1], lanes), vm(count, depth, lanes), dma((4,))],
        compiler_params=params(),
    )(
        near_even, near_odd, far_even, far_odd, far, low2, high2,
        U, F, IN, FX, FY, FZ, V1, F1, IN1, FX1, FY1, FZ1,
    )
    return out[:, None]


def solution(mesh):
    spec = P("grp", "box", None, None)
    return jax.shard_map(body, mesh=mesh, in_specs=(spec,) * 3, out_specs=spec, check_vma=False)
```

time: 41.1 us -> 37 us (0.900)
  waiting for transfers between devices: 14.2 us -> 10.7 us
  Pallas kernels: 8.79 us -> 7.48 us
  starting transfers between devices: 17.9 us -> 18.6 us
    ppermute x0 -> x6, starting transfers between devices: none -> 8.52 us  [from_partner(): lax.ppermute(array, 'box', [(code[(p + (even_by if p % 2 == 0 else -even_...]
    ppermute x8 -> x2, starting transfers between devices: 12 us -> 4.17 us  [along_y(): lax.ppermute(array, 'box', [(code[p], code[(p + by) % blocks]) for p in r...]
    ppermute x8 -> x2, waiting for transfers between devices: 6.02 us -> 0.01 us  [along_y(): lax.ppermute(array, 'box', [(code[p], code[(p + by) % blocks]) for p in r...]
    ppermute x0 -> x6, waiting for transfers between devices: none -> 2.59 us  [from_partner(): lax.ppermute(array, 'box', [(code[(p + (even_by if p % 2 == 0 else -even_...]
    pallas_call x1, Pallas kernels: 4.16 us -> 2.83 us  [body(): pl.pallas_call(up_kernel, out_shape=arr(count, depth, lanes), in_specs=[V...]
  transfers between devices with their start and end apart: 12 -> 12, of which waited for: 7 -> 6; matrix products, arithmetic and copies ran while one was open for 0% -> 0% of each run, Pallas kernels for 4% -> 6%
where the time goes in v6:
time: 37 us; the launch traced here: 36.9 us
  starting transfers between devices  18.6 us (50%)
  waiting for transfers between devices  10.7 us (29%)
  Pallas kernels  7.48 us (20%)
    ppermute x6, starting transfers between devices, from_partner(): lax.ppermute(array, 'box', [(code[(p + (even_by if p % 2 == 0 else -even_...  8.52 us
    ppermute x4, waiting for transfers between devices, along_x(): lax.ppermute(array, 'grp', [(i, (i + by) % groups) for i in range(groups)])  8.13 us
    ppermute x4, starting transfers between devices, along_x(): lax.ppermute(array, 'grp', [(i, (i + by) % groups) for i in range(groups)])  5.9 us
    ppermute x2, starting transfers between devices, along_y(): lax.ppermute(array, 'box', [(code[p], code[(p + by) % blocks]) for p in r...  4.17 us
    pallas_call x1, Pallas kernels, body(): pl.pallas_call(up_kernel, out_shape=arr(count, depth, lanes), in_specs=[V...  2.83 us
    ppermute x6, waiting for transfers between devices, from_partner(): lax.ppermute(array, 'box', [(code[(p + (even_by if p % 2 == 0 else -even_...  2.59 us
    pallas_call x1, Pallas kernels, body(): pl.pallas_call(down_inner_kernel, out_shape=passed, in_specs=[VMEM] * 5,...  2.08 us
    pallas_call x1, Pallas kernels, body(): pl.pallas_call(down_kernel, out_shape=[arr(*t.shape) for t in passed] + [...  1.35 us
  transfers between devices with their start and end apart: 12, of which 6 were waited for; matrix products, arithmetic and copies ran while one was open for 0% of the time, Pallas kernels for 6%

profile of v6, /device:TPU:0, one launch (start us, length us, event | category | flops | bytes accessed | tf_op | source)
XLA Modules:
  0.0 36.9 jit_solution(3044667466575433866)
XLA Ops:
  0.0 1.2 %shard_map.37 = (f32[48,32,128]{2,1,0:T(8,128)S(1)}, f32[48,32,128]{2,1,0:T(8,128)S(1)}, f32[48,32,128]{2,1,0:T(8,128)S(1)}, f32[19,16,128]{2,1,0:T(8,128)S(1)},...) custom-call(f32[32,16,128]{2,1,0:T(8,128)} %bitcast.6, f32[32,16,128]{2,1,0:T(8,128)} %bitcast.7, ...), custom_call_target="tpu_custom_call" | custom-call | tf_op jit(solution)/shard_map/pallas_call | solution.py:633
  1.2 0.5 %collective-permute-start.4 = (f32[608,128]{1,0:T(8,128)S(1)}, f32[608,128]{1,0:T(8,128)S(1)}, u32[]{:S(2)}, u32[]{:S(2)}) collective-permute-start(f32[608,128]{1,0:T(8,128)S(1)} %get-tuple-element.57), channel_id=1, source_target_pairs={{0,1},{1,3},{3,2},{2,6},{6,7},{7,5},{5,4},{4,0},{8,9},{9,11},{11,1... | collective-permute-start | bytes 933896 | tf_op jit(solution)/shard_map/ppermute | solution.py:613
  1.7 3.7 %collective-permute-start.5 = (f32[608,128]{1,0:T(8,128)S(1)}, f32[608,128]{1,0:T(8,128)S(1)}, u32[]{:S(2)}, u32[]{:S(2)}) collective-permute-start(f32[608,128]{1,0:T(8,128)S(1)} %get-tuple-element.58), channel_id=1, source_target_pairs={{0,4},{1,0},{3,1},{2,3},{6,2},{7,6},{5,7},{4,5},{8,12},{9,8},{11,9... | collective-permute-start | bytes 933896 | tf_op jit(solution)/shard_map/ppermute | solution.py:613
  5.3 1.8 %collective-permute-start = (f32[19,16,128]{2,1,0:T(8,128)S(1)}, f32[19,16,128]{2,1,0:T(8,128)S(1)}, u32[]{:S(2)}, u32[]{:S(2)}) collective-permute-start(f32[19,16,128]{2,1,0:T(8,128)S(1)} %get-tuple-element.53), channel_id=1, source_target_pairs={{0,8},{8,16},{16,24},{24,0},{1,9},{9,17},{17,25},{25,1},{2,10},{10... | collective-permute-start | bytes 466952 | tf_op jit(solution)/shard_map/ppermute | solution.py:610
  7.1 1.2 %collective-permute-start.1 = (f32[19,16,128]{2,1,0:T(8,128)S(1)}, f32[19,16,128]{2,1,0:T(8,128)S(1)}, u32[]{:S(2)}, u32[]{:S(2)}) collective-permute-start(f32[19,16,128]{2,1,0:T(8,128)S(1)} %get-tuple-element.54), channel_id=1, source_target_pairs={{0,24},{8,0},{16,8},{24,16},{1,25},{9,1},{17,9},{25,17},{2,26},{10... | collective-permute-start | bytes 466952 | tf_op jit(solution)/shard_map/ppermute | solution.py:610
  8.3 4.0 %collective-permute-done.low = f32[19,16,128]{2,1,0:T(8,128)S(1)} collective-permute-done((f32[19,16,128]{2,1,0:T(8,128)S(1)}, f32[19,16,128]{2,1,0:T(8,128)S(1)}, u32[]{:S(2)}, u32[]{:S(2)}) %collective-permute-start) | collective-permute-done | bytes 155680 | tf_op jit(solution)/shard_map/ppermute | solution.py:610
  12.3 1.7 %collective-permute-done.1.high = f32[19,16,128]{2,1,0:T(8,128)S(1)} collective-permute-done((f32[19,16,128]{2,1,0:T(8,128)S(1)}, f32[19,16,128]{2,1,0:T(8,128)S(1)}, u32[]{:S(2)}, u32[]{:S(2)}) %collective-permute-start.1) | collective-permute-done | bytes 155680 | tf_op jit(solution)/shard_map/ppermute | solution.py:610
  14.1 0.1 collective-permute-start.2
  14.2 2.8 %collective-permute-start.3 = (f32[176,128]{1,0:T(8,128)S(1)}, f32[176,128]{1,0:T(8,128)S(1)}, u32[]{:S(2)}, u32[]{:S(2)}) collective-permute-start(f32[176,128]{1,0:T(8,128)S(1)} %get-tuple-element.56), channel_id=1, source_target_pairs={{4,0},{3,1},{1,3},{6,2},{2,6},{5,7},{7,5},{0,4},{12,8},{11,9},{9,1... | collective-permute-start | bytes 270344 | tf_op jit(solution)/shard_map/ppermute | solution.py:616
  17.0 0.0 collective-permute-done.4.y_low
  17.0 0.0 collective-permute-done.5.y_high
  17.0 2.1 %shard_map.39 = (f32[48,32,128]{2,1,0:T(8,128)S(1)}, f32[48,32,128]{2,1,0:T(8,128)S(1)}, f32[48,32,128]{2,1,0:T(8,128)S(1)}, f32[48,32,128]{2,1,0:T(8,128)S(1)},...) custom-call(f32[608,128]{1,0:T(8,128)S(1)} %collective-permute-done., ...), custom_call_target="tpu_custom_call", output_to_operand_aliasing={{0}: (2, {}), {1}: (3, {}), {2}: (4, {})} | custom-call | tf_op jit(solution)/shard_map/pallas_call | solution.py:659
  19.1 0.0 collective-permute-done.2.c_even
  19.1 0.6 %collective-permute-done.3.c_odd = f32[176,128]{1,0:T(8,128)S(1)} collective-permute-done((f32[176,128]{1,0:T(8,128)S(1)}, f32[176,128]{1,0:T(8,128)S(1)}, u32[]{:S(2)}, u32[]{:S(2)}) %collective-permute-start.3) | collective-permute-done | bytes 90144 | tf_op jit(solution)/shard_map/ppermute | solution.py:616
  19.6 1.3 %shard_map.40 = (f32[48,32,128]{2,1,0:T(8,128)S(1)}, f32[48,32,128]{2,1,0:T(8,128)S(1)}, f32[48,32,128]{2,1,0:T(8,128)S(1)}, f32[48,32,128]{2,1,0:T(8,128)S(1)},...) custom-call(f32[19,16,128]{2,1,0:T(8,128)S(1)} %collective-permute-d, ...), custom_call_target="tpu_custom_call", output_to_operand_aliasing={{0}: (4, {}), {1}: (5, {}), {2}: (6, {}), {3}: (7, {}), {4}... | custom-call | tf_op jit(solution)/shard_map/pallas_call | solution.py:670
  21.0 1.5 %collective-permute-start.6 = (f32[48,128]{1,0:T(8,128)S(1)}, f32[48,128]{1,0:T(8,128)S(1)}, u32[]{:S(2)}, u32[]{:S(2)}) collective-permute-start(f32[48,128]{1,0:T(8,128)S(1)} %get-tuple-element.85), channel_id=1, source_target_pairs={{0,8},{8,16},{16,24},{24,0},{1,9},{9,17},{17,25},{25,1},{2,10},{10... | collective-permute-start | bytes 73736 | tf_op jit(solution)/shard_map/ppermute | solution.py:610
  22.5 1.5 %collective-permute-start.7 = (f32[48,128]{1,0:T(8,128)S(1)}, f32[48,128]{1,0:T(8,128)S(1)}, u32[]{:S(2)}, u32[]{:S(2)}) collective-permute-start(f32[48,128]{1,0:T(8,128)S(1)} %get-tuple-element.86), channel_id=1, source_target_pairs={{0,24},{8,0},{16,8},{24,16},{1,25},{9,1},{17,9},{25,17},{2,26},{10... | collective-permute-start | bytes 73736 | tf_op jit(solution)/shard_map/ppermute | solution.py:610
  24.0 1.8 %collective-permute-done.6.low = f32[48,128]{1,0:T(8,128)S(1)} collective-permute-done((f32[48,128]{1,0:T(8,128)S(1)}, f32[48,128]{1,0:T(8,128)S(1)}, u32[]{:S(2)}, u32[]{:S(2)}) %collective-permute-start.6) | collective-permute-done | bytes 24608 | tf_op jit(solution)/shard_map/ppermute | solution.py:610
  25.8 0.6 %collective-permute-done.7.high = f32[48,128]{1,0:T(8,128)S(1)} collective-permute-done((f32[48,128]{1,0:T(8,128)S(1)}, f32[48,128]{1,0:T(8,128)S(1)}, u32[]{:S(2)}, u32[]{:S(2)}) %collective-permute-start.7) | collective-permute-done | bytes 24608 | tf_op jit(solution)/shard_map/ppermute | solution.py:610
  26.4 0.1 collective-permute-start.8
  26.5 2.9 %collective-permute-start.9 = (f32[144,128]{1,0:T(8,128)S(1)}, f32[144,128]{1,0:T(8,128)S(1)}, u32[]{:S(2)}, u32[]{:S(2)}) collective-permute-start(f32[144,128]{1,0:T(8,128)S(1)} %get-tuple-element.88), channel_id=1, source_target_pairs={{4,0},{3,1},{1,3},{6,2},{2,6},{5,7},{7,5},{0,4},{12,8},{11,9},{9,1... | collective-permute-start | bytes 221192 | tf_op jit(solution)/shard_map/ppermute | solution.py:616
  29.4 2.6 %collective-permute-start.10 = (f32[72,128]{1,0:T(8,128)S(1)}, f32[72,128]{1,0:T(8,128)S(1)}, u32[]{:S(2)}, u32[]{:S(2)}) collective-permute-start(f32[72,128]{1,0:T(8,128)S(1)} %get-tuple-element.89.own), channel_id=1, source_target_pairs={{3,0},{4,1},{6,3},{1,2},{5,6},{2,7},{0,5},{7,4},{11,8},{12,9},{14,... | collective-permute-start | bytes 110600 | tf_op jit(solution)/shard_map/ppermute | solution.py:616
  32.0 2.0 %collective-permute-done.11.far_odd = f32[72,128]{1,0:T(8,128)S(1)} collective-permute-done((f32[72,128]{1,0:T(8,128)S(1)}, f32[72,128]{1,0:T(8,128)S(1)}, u32[]{:S(2)}, u32[]{:S(2)}) %collective-permute-start.11) | collective-permute-done | bytes 36896 | tf_op jit(solution)/shard_map/ppermute | solution.py:616
  34.0 2.8 %shard_map.42 = f32[32,16,128]{2,1,0:T(8,128)} custom-call(f32[144,128]{1,0:T(8,128)S(1)} %collective-permute-done.8.near_even, f32[144,128]{1,0:T(8,128)S(1)} %collective-permute-done.9.near_odd, f32[72,128]{1,0:T(8,128)S(1)} %collective-permute-done.10.far_even, f32[72,128]{1,0:T(8,128)S(1)} %collective-permute-done.11.far_odd, ...), custom_call_target="tpu_custom_call" | custom-call | tf_op jit(solution)/shard_map/pallas_call | solution.py:698
  (6 shorter events, 0.1 us)
Async XLA Ops:
  1.2 15.8 %collective-permute-start.4 = (f32[608,128]{1,0:T(8,128)S(1)}, f32[608,128]{1,0:T(8,128)S(1)}, u32[]{:S(2)}, u32[]{:S(2)}) collective-permute-start(f32[608,128]{1,0:T(8,128)S(1)} %get-tuple-element.57), channel_id=1, source_target_pairs={{0,1},{1,3},{3,2},{2,6},{6,7},{7,5},{5,4},{4,0},{8,9},{9,11},{11,1... | collective-permute-start | bytes 933896 | tf_op jit(solution)/shard_map/ppermute | solution.py:613
  1.7 15.3 %collective-permute-start.5 = (f32[608,128]{1,0:T(8,128)S(1)}, f32[608,128]{1,0:T(8,128)S(1)}, u32[]{:S(2)}, u32[]{:S(2)}) collective-permute-start(f32[608,128]{1,0:T(8,128)S(1)} %get-tuple-element.58), channel_id=1, source_target_pairs={{0,4},{1,0},{3,1},{2,3},{6,2},{7,6},{5,7},{4,5},{8,12},{9,8},{11,9... | collective-permute-start | bytes 933896 | tf_op jit(solution)/shard_map/ppermute | solution.py:613
  5.3 7.0 %collective-permute-start = (f32[19,16,128]{2,1,0:T(8,128)S(1)}, f32[19,16,128]{2,1,0:T(8,128)S(1)}, u32[]{:S(2)}, u32[]{:S(2)}) collective-permute-start(f32[19,16,128]{2,1,0:T(8,128)S(1)} %get-tuple-element.53), channel_id=1, source_target_pairs={{0,8},{8,16},{16,24},{24,0},{1,9},{9,17},{17,25},{25,1},{2,10},{10... | collective-permute-start | bytes 466952 | tf_op jit(solution)/shard_map/ppermute | solution.py:610
  7.1 6.9 %collective-permute-start.1 = (f32[19,16,128]{2,1,0:T(8,128)S(1)}, f32[19,16,128]{2,1,0:T(8,128)S(1)}, u32[]{:S(2)}, u32[]{:S(2)}) collective-permute-start(f32[19,16,128]{2,1,0:T(8,128)S(1)} %get-tuple-element.54), channel_id=1, source_target_pairs={{0,24},{8,0},{16,8},{24,16},{1,25},{9,1},{17,9},{25,17},{2,26},{10... | collective-permute-start | bytes 466952 | tf_op jit(solution)/shard_map/ppermute | solution.py:610
  14.1 5.0 %collective-permute-start.2 = (f32[176,128]{1,0:T(8,128)S(1)}, f32[176,128]{1,0:T(8,128)S(1)}, u32[]{:S(2)}, u32[]{:S(2)}) collective-permute-start(f32[176,128]{1,0:T(8,128)S(1)} %get-tuple-element.55), channel_id=1, source_target_pairs={{1,0},{0,1},{2,3},{3,2},{7,6},{6,7},{4,5},{5,4},{9,8},{8,9},{10,11... | collective-permute-start | bytes 270344 | tf_op jit(solution)/shard_map/ppermute | solution.py:616
  14.2 5.5 %collective-permute-start.3 = (f32[176,128]{1,0:T(8,128)S(1)}, f32[176,128]{1,0:T(8,128)S(1)}, u32[]{:S(2)}, u32[]{:S(2)}) collective-permute-start(f32[176,128]{1,0:T(8,128)S(1)} %get-tuple-element.56), channel_id=1, source_target_pairs={{4,0},{3,1},{1,3},{6,2},{2,6},{5,7},{7,5},{0,4},{12,8},{11,9},{9,1... | collective-permute-start | bytes 270344 | tf_op jit(solution)/shard_map/ppermute | solution.py:616
  21.0 4.8 %collective-permute-start.6 = (f32[48,128]{1,0:T(8,128)S(1)}, f32[48,128]{1,0:T(8,128)S(1)}, u32[]{:S(2)}, u32[]{:S(2)}) collective-permute-start(f32[48,128]{1,0:T(8,128)S(1)} %get-tuple-element.85), channel_id=1, source_target_pairs={{0,8},{8,16},{16,24},{24,0},{1,9},{9,17},{17,25},{25,1},{2,10},{10... | collective-permute-start | bytes 73736 | tf_op jit(solution)/shard_map/ppermute | solution.py:610
  22.5 3.8 %collective-permute-start.7 = (f32[48,128]{1,0:T(8,128)S(1)}, f32[48,128]{1,0:T(8,128)S(1)}, u32[]{:S(2)}, u32[]{:S(2)}) collective-permute-start(f32[48,128]{1,0:T(8,128)S(1)} %get-tuple-element.86), channel_id=1, source_target_pairs={{0,24},{8,0},{16,8},{24,16},{1,25},{9,1},{17,9},{25,17},{2,26},{10... | collective-permute-start | bytes 73736 | tf_op jit(solution)/shard_map/ppermute | solution.py:610
  26.4 7.7 %collective-permute-start.8 = (f32[144,128]{1,0:T(8,128)S(1)}, f32[144,128]{1,0:T(8,128)S(1)}, u32[]{:S(2)}, u32[]{:S(2)}) collective-permute-start(f32[144,128]{1,0:T(8,128)S(1)} %get-tuple-element.87), channel_id=1, source_target_pairs={{1,0},{0,1},{2,3},{3,2},{7,6},{6,7},{4,5},{5,4},{9,8},{8,9},{10,11... | collective-permute-start | bytes 221192 | tf_op jit(solution)/shard_map/ppermute | solution.py:616
  26.5 7.6 %collective-permute-start.9 = (f32[144,128]{1,0:T(8,128)S(1)}, f32[144,128]{1,0:T(8,128)S(1)}, u32[]{:S(2)}, u32[]{:S(2)}) collective-permute-start(f32[144,128]{1,0:T(8,128)S(1)} %get-tuple-element.88), channel_id=1, source_target_pairs={{4,0},{3,1},{1,3},{6,2},{2,6},{5,7},{7,5},{0,4},{12,8},{11,9},{9,1... | collective-permute-start | bytes 221192 | tf_op jit(solution)/shard_map/ppermute | solution.py:616
  29.4 4.7 %collective-permute-start.11 = (f32[72,128]{1,0:T(8,128)S(1)}, f32[72,128]{1,0:T(8,128)S(1)}, u32[]{:S(2)}, u32[]{:S(2)}) collective-permute-start(f32[72,128]{1,0:T(8,128)S(1)} %get-tuple-element.89.own), channel_id=1, source_target_pairs={{5,0},{2,1},{0,3},{7,2},{3,6},{4,7},{6,5},{1,4},{13,8},{10,9},{8,1... | collective-permute-start | bytes 110600 | tf_op jit(solution)/shard_map/ppermute | solution.py:616
  29.4 4.7 %collective-permute-start.10 = (f32[72,128]{1,0:T(8,128)S(1)}, f32[72,128]{1,0:T(8,128)S(1)}, u32[]{:S(2)}, u32[]{:S(2)}) collective-permute-start(f32[72,128]{1,0:T(8,128)S(1)} %get-tuple-element.89.own), channel_id=1, source_target_pairs={{3,0},{4,1},{6,3},{1,2},{5,6},{2,7},{0,5},{7,4},{11,8},{12,9},{14,... | collective-permute-start | bytes 110600 | tf_op jit(solution)/shard_map/ppermute | solution.py:616

commit v7 on v6

--- a/solution.py
+++ b/solution.py
@@ -37,6 +37,14 @@
 
 def even_position():
     return box_position() % 2 == 0
+
+
+def even_group():
+    return lax.axis_index("grp") % 2 == 0
+
+
+def below_above(even, from_even, from_odd):
+    return jnp.where(even, from_odd, from_even), jnp.where(even, from_even, from_odd)
 
 
 def run_copies(pairs, sems):
@@ -164,34 +172,38 @@
     return pieces, at + -at % 8
 
 
-def pack_faces_kernel(f, a, b, F, A, B, x_up, x_down, y_up, y_down, sems):
+def pack_faces_kernel(f, a, b, F, A, B, x_even, x_odd, y_even, y_odd, sems):
     count, depth = f.shape[:2]
     own = (pl.ds(FRAME, count), pl.ds(FRAME, depth))
     frames = (F, A, B)
     copies = run_copies([(src, dst.at[own]) for src, dst in zip((f, a, b), frames)], sems)
     pieces, _ = face_pieces(count)
+    even = even_position()
+    even_x = even_group()
     row = 0
     for k, (ref, wide) in enumerate(zip(frames, WIDES)):
         copies[k].wait()
         for layer in range(wide):
-            x_up[row + layer] = ref[FRAME + count - wide + layer, FRAME:FRAME + depth]
-            x_down[row + layer] = ref[FRAME + layer, FRAME:FRAME + depth]
+            up = ref[FRAME + count - wide + layer, FRAME:FRAME + depth]
+            down = ref[FRAME + layer, FRAME:FRAME + depth]
+            x_odd[row + layer], x_even[row + layer] = below_above(even_x, up, down)
         row += wide
         for at_k, x, layers, at in pieces:
             if at_k == k:
-                y_up[at:at + layers] = ref[FRAME + x, FRAME + depth - layers:FRAME + depth]
-                y_down[at:at + layers] = ref[FRAME + x, FRAME:FRAME + layers]
-
-
-def pack_corners_kernel(low, high, to_even, to_odd):
-    depth = low.shape[1]
+                up = ref[FRAME + x, FRAME + depth - layers:FRAME + depth]
+                down = ref[FRAME + x, FRAME:FRAME + layers]
+                y_odd[at:at + layers], y_even[at:at + layers] = below_above(even, up, down)
+
+
+def pack_corners_kernel(x_even, x_odd, to_even, to_odd):
+    depth = x_even.shape[1]
     even = even_position()
+    even_x = even_group()
     for side, _, row, layers, at in corner_pieces()[0]:
-        ref = (low, high)[side]
-        up = ref[row, depth - layers:depth]
-        down = ref[row, 0:layers]
-        to_even[at:at + layers] = jnp.where(even, up, down)
-        to_odd[at:at + layers] = jnp.where(even, down, up)
+        up_rows = slice(depth - layers, depth)
+        up = below_above(even_x, x_even[row, up_rows], x_odd[row, up_rows])[side]
+        down = below_above(even_x, x_even[row, 0:layers], x_odd[row, 0:layers])[side]
+        to_odd[at:at + layers], to_even[at:at + layers] = below_above(even, up, down)
 
 
 def down_rows(F, A, B, FX, FY, FZ, DG, IN, V, U, T, F1, A1, B1, FX1, FY1, FZ1, D1, IN1, W1, coarse):
@@ -243,16 +255,18 @@
     return coef_row, sweep_row, restrict_row, level1_source, level1_coef, coef_row1, coarse_pack
 
 
-def down_inner_kernel(y_low, y_high, F_in, A_in, B_in, *refs):
+def down_inner_kernel(y_even, y_odd, F_in, A_in, B_in, *refs):
     *refs, T1 = refs
     F, A, B = frames = refs[:3]
     A1, B1 = refs[12:14]
     end = F.shape[0]
     depth = F.shape[1] - 2 * FRAME
     count = end - 2 * FRAME
+    even = even_position()
     for k, x, layers, at in face_pieces(count)[0]:
-        frames[k][FRAME + x, FRAME - layers:FRAME] = y_low[at:at + layers]
-        frames[k][FRAME + x, FRAME + depth:FRAME + depth + layers] = y_high[at:at + layers]
+        below, above = below_above(even, y_even[at:at + layers], y_odd[at:at + layers])
+        frames[k][FRAME + x, FRAME - layers:FRAME] = below
+        frames[k][FRAME + x, FRAME + depth:FRAME + depth + layers] = above
     zero_y_edges(frames, depth)
     coef_row, sweep_row, restrict_row, level1_source, level1_coef, coef_row1, coarse_pack = down_rows(*refs)
     first1 = FRAME // 2
@@ -290,28 +304,29 @@
                 zero(ref, slice(None), y)
 
 
-def down_kernel(low, high, c_even, c_odd, *refs):
+def down_kernel(x_even, x_odd, c_even, c_odd, *refs):
     refs = refs[21:]
-    *refs, V1, to_up, to_down, T1 = refs
+    *refs, V1, to_even, to_odd, T1 = refs
     F, A, B = frames = refs[:3]
     FX = refs[3]
     F1, A1, B1, FX1, FY1, FZ1, D1, IN1, W1, coarse = refs[11:]
     count = F.shape[0] - 2 * FRAME
     depth = F.shape[1] - 2 * FRAME
     even = even_position()
+    even_x = even_group()
     start = 0
     for k, wide in enumerate(WIDES):
         for layer in range(wide):
-            frames[k][FRAME - wide + layer, FRAME:FRAME + depth] = low[start + layer]
-            frames[k][FRAME + count + layer, FRAME:FRAME + depth] = high[start + layer]
+            below, above = below_above(even_x, x_even[start + layer], x_odd[start + layer])
+            frames[k][FRAME - wide + layer, FRAME:FRAME + depth] = below
+            frames[k][FRAME + count + layer, FRAME:FRAME + depth] = above
         start += wide
     starts = (0, WIDE_F, 2 * WIDE_F)
     for side, k, row, layers, at in corner_pieces()[0]:
         x = row - starts[k] + (FRAME + count if side else FRAME - WIDES[k])
-        near_even = c_even[at:at + layers]
-        near_odd = c_odd[at:at + layers]
-        frames[k][x, FRAME - layers:FRAME] = jnp.where(even, near_odd, near_even)
-        frames[k][x, FRAME + depth:FRAME + depth + layers] = jnp.where(even, near_even, near_odd)
+        below, above = below_above(even, c_even[at:at + layers], c_odd[at:at + layers])
+        frames[k][x, FRAME - layers:FRAME] = below
+        frames[k][x, FRAME + depth:FRAME + depth + layers] = above
     zero_y_edges(frames, depth)
     group = lax.axis_index("grp")
     for edge, x in (
@@ -369,15 +384,18 @@
     own1 = slice(first1, first1 + depth // 2)
     for k in range(3):
         rows = slice(k * COARSE_X, (k + 1) * COARSE_X)
-        to_up[rows] = coarse[(k + 1) * count2 - COARSE_X:(k + 1) * count2]
-        to_down[rows] = coarse[k * count2:k * count2 + COARSE_X]
+        up = coarse[(k + 1) * count2 - COARSE_X:(k + 1) * count2]
+        down = coarse[k * count2:k * count2 + COARSE_X]
+        to_odd[rows], to_even[rows] = below_above(even_x, up, down)
     for k in range(FINE_X):
         rows = slice(3 * COARSE_X + k * depth // 2, 3 * COARSE_X + (k + 1) * depth // 2)
-        to_up[rows] = V1[first1 + count1 - FINE_X + k, own1]
-        to_down[rows] = V1[first1 + k, own1]
-
-
-def pack_coarse_kernel(coarse, v1, low, high, far, to_even, to_odd):
+        up = V1[first1 + count1 - FINE_X + k, own1]
+        down = V1[first1 + k, own1]
+        to_odd[rows], to_even[rows] = below_above(even_x, up, down)
+
+
+def pack_coarse_kernel(coarse, v1, x_even, x_odd, far, to_even, to_odd, low, high):
+    low[...], high[...] = below_above(even_group(), x_even[...], x_odd[...])
     count2 = coarse.shape[0] // 3
     first1 = FRAME // 2
     depth1 = v1.shape[1] - FRAME
@@ -399,8 +417,7 @@
         part = slice(rows + k * FINE_X, rows + (k + 1) * FINE_X)
         up = tile[depth1 - FINE_X:]
         down = tile[:FINE_X]
-        to_even[part] = jnp.where(even, up, down)
-        to_odd[part] = jnp.where(even, down, up)
+        to_odd[part], to_even[part] = below_above(even, up, down)
 
 
 def coarse_solve(source, alpha, beta):
@@ -450,7 +467,7 @@
 
 
 def up_kernel(
-    near_even, near_odd, far_even, far_odd, own, low, high,
+    near_even, near_odd, far_even, far_odd, own, x_even, x_odd,
     in_v, F, IN, FX, FY, FZ,
     in_v1, F1, IN1, FX1, FY1, FZ1,
     out,
@@ -469,10 +486,9 @@
     for k in range(3):
         rows = pl.ds(k * COARSE_PITCH, COARSE_PITCH)
         ne, no, fe, fo = near_even[rows], near_odd[rows], far_even[rows], far_odd[rows]
-        blocks = (
-            jnp.where(even, fo, fe), jnp.where(even, no, ne), own[rows],
-            jnp.where(even, ne, no), jnp.where(even, fe, fo),
-        )
+        near_low, near_high = below_above(even, ne, no)
+        far_low, far_high = below_above(even, fe, fo)
+        blocks = (far_low, near_low, own[rows], near_high, far_high)
         column = []
         for at, value in enumerate(blocks):
             place = position + (at - 2)
@@ -495,17 +511,16 @@
     rows_loop(0, span1 - 2 * first1, 16, own_row)
     for k in range(FINE_X):
         tile = pl.ds(3 * COARSE_X + k * depth1, depth1)
-        V1[first1 - FINE_X + k, own_rows] = low[tile]
-        V1[span1 - first1 + k, own_rows] = high[tile]
+        below, above = below_above(even_group(), x_even[tile], x_odd[tile])
+        V1[first1 - FINE_X + k, own_rows] = below
+        V1[span1 - first1 + k, own_rows] = above
 
     rim = own.shape[0]
 
     def rim_row(x):
         i = x + first1 - FINE_X
         part = pl.ds(rim + FINE_X * x, FINE_X)
-        ne, no = near_even[part], near_odd[part]
-        near_low = jnp.where(even, no, ne)
-        near_high = jnp.where(even, ne, no)
+        near_low, near_high = below_above(even, near_even[part], near_odd[part])
         return [
             (V1, (i, slice(first1 - FINE_X, first1)), jnp.where(position > 0, near_low, 0.0)),
             (
@@ -606,18 +621,38 @@
     blocks = lax.axis_size("box")
     code = [p ^ (p >> 1) for p in range(blocks)]
 
-    def along_x(array, by):
-        return lax.ppermute(array, "grp", [(i, (i + by) % groups) for i in range(groups)])
-
-    def along_y(array, by):
-        return lax.ppermute(array, "box", [(code[p], code[(p + by) % blocks]) for p in range(blocks)])
-
-    def from_partner(array, even_by):
-        return lax.ppermute(
-            array,
-            "box",
-            [(code[(p + (even_by if p % 2 == 0 else -even_by)) % blocks], code[p]) for p in range(blocks)],
-        )
+    def moved(array, target):
+        def index(g, p):
+            return g * blocks + code[p]
+
+        pairs = [(index(g, p), index(*target(g, p))) for g in range(groups) for p in range(blocks)]
+        return lax.ppermute(array, ("grp", "box"), pairs)
+
+    def odd_partner(at, size):
+        other = at + 1 if at % 2 else at - 1
+        return other if 0 <= other < size else None
+
+    def x_even(g, p):
+        return g ^ 1, p
+
+    def x_odd(g, p):
+        other = odd_partner(g, groups)
+        return (g, p ^ 1) if other is None else (other, p)
+
+    def y_even(g, p):
+        return g, p ^ 1
+
+    def y_odd(g, p):
+        other = odd_partner(p, blocks)
+        return (g ^ (groups // 2), p) if other is None else (g, other)
+
+    def far_even(g, p):
+        other = p + 2 if p % 2 else p - 2
+        return g, other if 0 <= other < blocks else p ^ 1
+
+    def far_odd(g, p):
+        other = p - 2 if p % 2 else p + 2
+        return g, other if 0 <= other < blocks else p ^ 1
 
     def arr(*shape):
         return jax.ShapeDtypeStruct(shape, jnp.float32)
@@ -630,7 +665,7 @@
     framed = (count + 2 * FRAME, depth + 2 * FRAME, lanes)
     y_rows = face_pieces(count)[1]
     c_rows = corner_pieces()[1]
-    *frames, x_up, x_down, y_up, y_down = pl.pallas_call(
+    *frames, to_x_even, to_x_odd, to_y_even, to_y_odd = pl.pallas_call(
         pack_faces_kernel,
         out_shape=[arr(*framed)] * 3 + [arr(x_rows, depth, lanes)] * 2 + [arr(y_rows, lanes)] * 2,
         in_specs=[HBM] * 3,
@@ -638,20 +673,17 @@
         scratch_shapes=[dma((3,))],
         compiler_params=params(),
     )(*[pltpu.with_memory_space_constraint(t, pltpu.HBM) for t in (f, a, b)])
-    low = along_x(x_up, 1)
-    high = along_x(x_down, -1)
-    y_low = along_y(y_up, 1)
-    y_high = along_y(y_down, -1)
-
-    c_even, c_odd = pl.pallas_call(
+    x_halo = moved(to_x_even, x_even), moved(to_x_odd, x_odd)
+    y_halo = moved(to_y_even, y_even), moved(to_y_odd, y_odd)
+
+    to_even, to_odd = pl.pallas_call(
         pack_corners_kernel,
         out_shape=[arr(c_rows, lanes)] * 2,
         in_specs=[VMEM] * 2,
         out_specs=[VMEM] * 2,
         compiler_params=params(),
-    )(low, high)
-    c_even = from_partner(c_even, 1)
-    c_odd = from_partner(c_odd, -1)
+    )(*x_halo)
+    corners = moved(to_even, y_even), moved(to_odd, y_odd)
 
     framed1 = (framed[0] // 2, framed[1] // 2, lanes)
     count2 = count // 4
@@ -664,7 +696,7 @@
         input_output_aliases={2 + k: k for k in range(3)},
         scratch_shapes=[vm(2 * count2, framed1[1], lanes)],
         compiler_params=params(),
-    )(y_low, y_high, *frames)
+    )(*y_halo, *frames)
     x2_rows = 3 * COARSE_X + FINE_X * depth // 2
     x2_rows += -x2_rows % 8
     results = pl.pallas_call(
@@ -675,11 +707,10 @@
         input_output_aliases={4 + k: k for k in range(21)},
         scratch_shapes=[vm(count2, framed1[1], lanes)],
         compiler_params=params(),
-    )(low, high, c_even, c_odd, *passed)
-    F, _, _, FX, FY, FZ, _, IN, _, U, _, F1, _, _, FX1, FY1, FZ1, _, IN1, _, coarse, V1, to_up, to_down = results
-
-    low2 = along_x(to_up, 1)
-    high2 = along_x(to_down, -1)
+    )(*x_halo, *corners, *passed)
+    F, _, _, FX, FY, FZ, _, IN, _, U, _, F1, _, _, FX1, FY1, FZ1, _, IN1, _, coarse, V1, to_even, to_odd = results
+
+    x_halo = moved(to_even, x_even), moved(to_odd, x_odd)
     far_rows = 3 * COARSE_PITCH
     near_rows = far_rows + FINE_X * (count // 2 + 2 * FINE_X)
     near_rows += -near_rows % 8
@@ -688,12 +719,11 @@
         out_shape=[arr(far_rows, lanes)] + [arr(near_rows, lanes)] * 2,
         in_specs=[VMEM] * 4,
         out_specs=[VMEM] * 3,
+        scratch_shapes=[vm(x2_rows, lanes)] * 2,
         compiler_params=params(),
-    )(coarse, V1, low2, high2)
-    near_even = from_partner(to_even, 1)
-    near_odd = from_partner(to_odd, -1)
-    far_even = from_partner(far, 2)
-    far_odd = from_partner(far, -2)
+    )(coarse, V1, *x_halo)
+    near = moved(to_even, y_even), moved(to_odd, y_odd)
+    distant = moved(far, far_even), moved(far, far_odd)
 
     out = pl.pallas_call(
         up_kernel,
@@ -704,7 +734,7 @@
         + [vm(3, COARSE_PITCH, lanes), vm(count // 2 + 2, framed[1], lanes), vm(count, depth, lanes), dma((4,))],
         compiler_params=params(),
     )(
-        near_even, near_odd, far_even, far_odd, far, low2, high2,
+        *near, *distant, far, *x_halo,
         U, F, IN, FX, FY, FZ, V1, F1, IN1, FX1, FY1, FZ1,
     )
     return out[:, None]

time: 37 us -> 35.3 us (0.954)
  the two profiles are of different devices: /device:TPU:0 before, /device:TPU:11 now
where the time goes in v7:
time: 35.3 us; the launch traced here: 35.2 us
  starting transfers between devices  15.2 us (43%)
  waiting for transfers between devices  12.6 us (36%)
  Pallas kernels  7.35 us (21%)
    ppermute x12, starting transfers between devices, moved(): return lax.ppermute(array, ('grp', 'box'), pairs)  15.2 us
    ppermute x12, waiting for transfers between devices, moved(): return lax.ppermute(array, ('grp', 'box'), pairs)  12.6 us
    pallas_call x1, Pallas kernels, body(): pl.pallas_call(up_kernel, out_shape=arr(count, depth, lanes), in_specs=[V...  2.83 us
    pallas_call x1, Pallas kernels, body(): pl.pallas_call(down_inner_kernel, out_shape=passed, in_specs=[VMEM] * 5,...  2.01 us
    pallas_call x1, Pallas kernels, body(): pl.pallas_call(down_kernel, out_shape=[arr(*t.shape) for t in passed] + [...  1.26 us
    pallas_call x1, Pallas kernels, body(): pl.pallas_call(pack_faces_kernel, out_shape=[arr(*framed)] * 3 + [arr(x_r...  1.16 us
  transfers between devices with their start and end apart: 12, of which 7 were waited for; matrix products, arithmetic and copies ran while one was open for 0% of the time, Pallas kernels for 6%

profile of v7, /device:TPU:11, one launch (start us, length us, event | category | flops | bytes accessed | tf_op | source)
XLA Modules:
  0.0 35.2 jit_solution(5297428650480546157)
XLA Ops:
  0.0 1.2 %shard_map.37 = (f32[48,32,128]{2,1,0:T(8,128)S(1)}, f32[48,32,128]{2,1,0:T(8,128)S(1)}, f32[48,32,128]{2,1,0:T(8,128)S(1)}, f32[19,16,128]{2,1,0:T(8,128)S(1)},...) custom-call(f32[32,16,128]{2,1,0:T(8,128)} %bitcast.6, f32[32,16,128]{2,1,0:T(8,128)} %bitcast.7, ...), custom_call_target="tpu_custom_call" | custom-call | tf_op jit(solution)/shard_map/pallas_call | solution.py:668
  1.2 0.7 %collective-permute-start.4 = (f32[608,128]{1,0:T(8,128)S(1)}, f32[608,128]{1,0:T(8,128)S(1)}, u32[]{:S(2)}, u32[]{:S(2)}) collective-permute-start(f32[608,128]{1,0:T(8,128)S(1)} %get-tuple-element.57), channel_id=1, source_target_pairs={{0,1},{1,0},{3,2},{2,3},{6,7},{7,6},{5,4},{4,5},{8,9},{9,8},{11,10... | collective-permute-start | bytes 933896 | tf_op jit(solution)/shard_map/ppermute | solution.py:629
  1.9 0.2 collective-permute-start.5
  2.1 0.1 collective-permute-start
  2.2 2.3 %collective-permute-start.1 = (f32[19,16,128]{2,1,0:T(8,128)S(1)}, f32[19,16,128]{2,1,0:T(8,128)S(1)}, u32[]{:S(2)}, u32[]{:S(2)}) collective-permute-start(f32[19,16,128]{2,1,0:T(8,128)S(1)} %get-tuple-element.54), channel_id=1, source_target_pairs={{0,1},{1,0},{3,2},{2,3},{6,7},{7,6},{5,4},{4,5},{8,16},{9,17},{11,... | collective-permute-start | bytes 466952 | tf_op jit(solution)/shard_map/ppermute | solution.py:629
  4.5 2.0 %collective-permute-done.x_even = f32[19,16,128]{2,1,0:T(8,128)S(1)} collective-permute-done((f32[19,16,128]{2,1,0:T(8,128)S(1)}, f32[19,16,128]{2,1,0:T(8,128)S(1)}, u32[]{:S(2)}, u32[]{:S(2)}) %collective-permute-start) | collective-permute-done | bytes 155680 | tf_op jit(solution)/shard_map/ppermute | solution.py:629
  6.5 2.9 %collective-permute-done.1.x_odd = f32[19,16,128]{2,1,0:T(8,128)S(1)} collective-permute-done((f32[19,16,128]{2,1,0:T(8,128)S(1)}, f32[19,16,128]{2,1,0:T(8,128)S(1)}, u32[]{:S(2)}, u32[]{:S(2)}) %collective-permute-start.1) | collective-permute-done | bytes 155680 | tf_op jit(solution)/shard_map/ppermute | solution.py:629
  9.4 0.1 shard_map.38
  9.4 3.5 %collective-permute-start.2 = (f32[176,128]{1,0:T(8,128)S(1)}, f32[176,128]{1,0:T(8,128)S(1)}, u32[]{:S(2)}, u32[]{:S(2)}) collective-permute-start(f32[176,128]{1,0:T(8,128)S(1)} %get-tuple-element.55), channel_id=1, source_target_pairs={{0,1},{1,0},{3,2},{2,3},{6,7},{7,6},{5,4},{4,5},{8,9},{9,8},{11,10... | collective-permute-start | bytes 270344 | tf_op jit(solution)/shard_map/ppermute | solution.py:629
  12.9 0.8 %collective-permute-start.3 = (f32[176,128]{1,0:T(8,128)S(1)}, f32[176,128]{1,0:T(8,128)S(1)}, u32[]{:S(2)}, u32[]{:S(2)}) collective-permute-start(f32[176,128]{1,0:T(8,128)S(1)} %get-tuple-element.56), channel_id=1, source_target_pairs={{0,16},{1,3},{3,1},{2,6},{6,2},{7,5},{5,7},{4,20},{8,24},{9,11},{1... | collective-permute-start | bytes 270344 | tf_op jit(solution)/shard_map/ppermute | solution.py:629
  13.7 0.0 collective-permute-done.5.y_odd
  13.7 2.0 %shard_map.39 = (f32[48,32,128]{2,1,0:T(8,128)S(1)}, f32[48,32,128]{2,1,0:T(8,128)S(1)}, f32[48,32,128]{2,1,0:T(8,128)S(1)}, f32[48,32,128]{2,1,0:T(8,128)S(1)},...) custom-call(f32[608,128]{1,0:T(8,128)S(1)} %collective-permute-done., ...), custom_call_target="tpu_custom_call", output_to_operand_aliasing={{0}: (2, {}), {1}: (3, {}), {2}: (4, {})} | custom-call | tf_op jit(solution)/shard_map/pallas_call | solution.py:691
  15.8 0.0 collective-permute-done.2.c_even
  15.8 0.6 %collective-permute-done.3.c_odd = f32[176,128]{1,0:T(8,128)S(1)} collective-permute-done((f32[176,128]{1,0:T(8,128)S(1)}, f32[176,128]{1,0:T(8,128)S(1)}, u32[]{:S(2)}, u32[]{:S(2)}) %collective-permute-start.3) | collective-permute-done | bytes 90144 | tf_op jit(solution)/shard_map/ppermute | solution.py:629
  16.3 1.3 %shard_map.40 = (f32[48,32,128]{2,1,0:T(8,128)S(1)}, f32[48,32,128]{2,1,0:T(8,128)S(1)}, f32[48,32,128]{2,1,0:T(8,128)S(1)}, f32[48,32,128]{2,1,0:T(8,128)S(1)},...) custom-call(f32[19,16,128]{2,1,0:T(8,128)S(1)} %collective-permute-d, ...), custom_call_target="tpu_custom_call", output_to_operand_aliasing={{0}: (4, {}), {1}: (5, {}), {2}: (6, {}), {3}: (7, {}), {4}... | custom-call | tf_op jit(solution)/shard_map/pallas_call | solution.py:702
  17.6 0.1 collective-permute-start.6
  17.7 0.8 %collective-permute-start.7 = (f32[48,128]{1,0:T(8,128)S(1)}, f32[48,128]{1,0:T(8,128)S(1)}, u32[]{:S(2)}, u32[]{:S(2)}) collective-permute-start(f32[48,128]{1,0:T(8,128)S(1)} %get-tuple-element.86), channel_id=1, source_target_pairs={{0,1},{1,0},{3,2},{2,3},{6,7},{7,6},{5,4},{4,5},{8,16},{9,17},{11,... | collective-permute-start | bytes 73736 | tf_op jit(solution)/shard_map/ppermute | solution.py:629
  18.4 1.9 %collective-permute-done.6.x_even = f32[48,128]{1,0:T(8,128)S(1)} collective-permute-done((f32[48,128]{1,0:T(8,128)S(1)}, f32[48,128]{1,0:T(8,128)S(1)}, u32[]{:S(2)}, u32[]{:S(2)}) %collective-permute-start.6) | collective-permute-done | bytes 24608 | tf_op jit(solution)/shard_map/ppermute | solution.py:629
  20.3 1.0 %collective-permute-done.7.x_odd = f32[48,128]{1,0:T(8,128)S(1)} collective-permute-done((f32[48,128]{1,0:T(8,128)S(1)}, f32[48,128]{1,0:T(8,128)S(1)}, u32[]{:S(2)}, u32[]{:S(2)}) %collective-permute-start.7) | collective-permute-done | bytes 24608 | tf_op jit(solution)/shard_map/ppermute | solution.py:629
  21.3 4.1 %collective-permute-start.8 = (f32[144,128]{1,0:T(8,128)S(1)}, f32[144,128]{1,0:T(8,128)S(1)}, u32[]{:S(2)}, u32[]{:S(2)}) collective-permute-start(f32[144,128]{1,0:T(8,128)S(1)} %get-tuple-element.87), channel_id=1, source_target_pairs={{0,1},{1,0},{3,2},{2,3},{6,7},{7,6},{5,4},{4,5},{8,9},{9,8},{11,10... | collective-permute-start | bytes 221192 | tf_op jit(solution)/shard_map/ppermute | solution.py:629
  25.4 2.6 %collective-permute-start.11 = (f32[72,128]{1,0:T(8,128)S(1)}, f32[72,128]{1,0:T(8,128)S(1)}, u32[]{:S(2)}, u32[]{:S(2)}) collective-permute-start(f32[72,128]{1,0:T(8,128)S(1)} %get-tuple-element.89.own), channel_id=1, source_target_pairs={{0,3},{1,0},{3,6},{2,1},{6,5},{7,2},{5,4},{4,7},{8,11},{9,8},{11,1... | collective-permute-start | bytes 110600 | tf_op jit(solution)/shard_map/ppermute | solution.py:629
  28.1 1.2 %collective-permute-done.11.far_odd = f32[72,128]{1,0:T(8,128)S(1)} collective-permute-done((f32[72,128]{1,0:T(8,128)S(1)}, f32[72,128]{1,0:T(8,128)S(1)}, u32[]{:S(2)}, u32[]{:S(2)}) %collective-permute-start.11) | collective-permute-done | bytes 36896 | tf_op jit(solution)/shard_map/ppermute | solution.py:629
  29.3 3.1 %collective-permute-done.10.far_even = f32[72,128]{1,0:T(8,128)S(1)} collective-permute-done((f32[72,128]{1,0:T(8,128)S(1)}, f32[72,128]{1,0:T(8,128)S(1)}, u32[]{:S(2)}, u32[]{:S(2)}) %collective-permute-start.10) | collective-permute-done | bytes 36896 | tf_op jit(solution)/shard_map/ppermute | solution.py:629
  32.3 2.8 %shard_map.42 = f32[32,16,128]{2,1,0:T(8,128)} custom-call(f32[144,128]{1,0:T(8,128)S(1)} %collective-permute-done.8.near_even, f32[144,128]{1,0:T(8,128)S(1)} %collective-permute-done.9.near_odd, f32[72,128]{1,0:T(8,128)S(1)} %collective-permute-done.10.far_even, f32[72,128]{1,0:T(8,128)S(1)} %collective-permute-done.11.far_odd, ...), custom_call_target="tpu_custom_call" | custom-call | tf_op jit(solution)/shard_map/pallas_call | solution.py:728
  (6 shorter events, 0.0 us)
Async XLA Ops:
  1.2 12.6 %collective-permute-start.4 = (f32[608,128]{1,0:T(8,128)S(1)}, f32[608,128]{1,0:T(8,128)S(1)}, u32[]{:S(2)}, u32[]{:S(2)}) collective-permute-start(f32[608,128]{1,0:T(8,128)S(1)} %get-tuple-element.57), channel_id=1, source_target_pairs={{0,1},{1,0},{3,2},{2,3},{6,7},{7,6},{5,4},{4,5},{8,9},{9,8},{11,10... | collective-permute-start | bytes 933896 | tf_op jit(solution)/shard_map/ppermute | solution.py:629
  1.9 11.8 %collective-permute-start.5 = (f32[608,128]{1,0:T(8,128)S(1)}, f32[608,128]{1,0:T(8,128)S(1)}, u32[]{:S(2)}, u32[]{:S(2)}) collective-permute-start(f32[608,128]{1,0:T(8,128)S(1)} %get-tuple-element.58), channel_id=1, source_target_pairs={{0,16},{1,3},{3,1},{2,6},{6,2},{7,5},{5,7},{4,20},{8,24},{9,11},{1... | collective-permute-start | bytes 933896 | tf_op jit(solution)/shard_map/ppermute | solution.py:629
  2.1 4.4 %collective-permute-start = (f32[19,16,128]{2,1,0:T(8,128)S(1)}, f32[19,16,128]{2,1,0:T(8,128)S(1)}, u32[]{:S(2)}, u32[]{:S(2)}) collective-permute-start(f32[19,16,128]{2,1,0:T(8,128)S(1)} %get-tuple-element.53), channel_id=1, source_target_pairs={{0,8},{1,9},{3,11},{2,10},{6,14},{7,15},{5,13},{4,12},{8,0},{9,1},... | collective-permute-start | bytes 466952 | tf_op jit(solution)/shard_map/ppermute | solution.py:629
  2.2 7.2 %collective-permute-start.1 = (f32[19,16,128]{2,1,0:T(8,128)S(1)}, f32[19,16,128]{2,1,0:T(8,128)S(1)}, u32[]{:S(2)}, u32[]{:S(2)}) collective-permute-start(f32[19,16,128]{2,1,0:T(8,128)S(1)} %get-tuple-element.54), channel_id=1, source_target_pairs={{0,1},{1,0},{3,2},{2,3},{6,7},{7,6},{5,4},{4,5},{8,16},{9,17},{11,... | collective-permute-start | bytes 466952 | tf_op jit(solution)/shard_map/ppermute | solution.py:629
  9.4 6.3 %collective-permute-start.2 = (f32[176,128]{1,0:T(8,128)S(1)}, f32[176,128]{1,0:T(8,128)S(1)}, u32[]{:S(2)}, u32[]{:S(2)}) collective-permute-start(f32[176,128]{1,0:T(8,128)S(1)} %get-tuple-element.55), channel_id=1, source_target_pairs={{0,1},{1,0},{3,2},{2,3},{6,7},{7,6},{5,4},{4,5},{8,9},{9,8},{11,10... | collective-permute-start | bytes 270344 | tf_op jit(solution)/shard_map/ppermute | solution.py:629
  12.9 3.4 %collective-permute-start.3 = (f32[176,128]{1,0:T(8,128)S(1)}, f32[176,128]{1,0:T(8,128)S(1)}, u32[]{:S(2)}, u32[]{:S(2)}) collective-permute-start(f32[176,128]{1,0:T(8,128)S(1)} %get-tuple-element.56), channel_id=1, source_target_pairs={{0,16},{1,3},{3,1},{2,6},{6,2},{7,5},{5,7},{4,20},{8,24},{9,11},{1... | collective-permute-start | bytes 270344 | tf_op jit(solution)/shard_map/ppermute | solution.py:629
  17.6 2.7 %collective-permute-start.6 = (f32[48,128]{1,0:T(8,128)S(1)}, f32[48,128]{1,0:T(8,128)S(1)}, u32[]{:S(2)}, u32[]{:S(2)}) collective-permute-start(f32[48,128]{1,0:T(8,128)S(1)} %get-tuple-element.85), channel_id=1, source_target_pairs={{0,8},{1,9},{3,11},{2,10},{6,14},{7,15},{5,13},{4,12},{8,0},{9,1},... | collective-permute-start | bytes 73736 | tf_op jit(solution)/shard_map/ppermute | solution.py:629
  17.7 3.6 %collective-permute-start.7 = (f32[48,128]{1,0:T(8,128)S(1)}, f32[48,128]{1,0:T(8,128)S(1)}, u32[]{:S(2)}, u32[]{:S(2)}) collective-permute-start(f32[48,128]{1,0:T(8,128)S(1)} %get-tuple-element.86), channel_id=1, source_target_pairs={{0,1},{1,0},{3,2},{2,3},{6,7},{7,6},{5,4},{4,5},{8,16},{9,17},{11,... | collective-permute-start | bytes 73736 | tf_op jit(solution)/shard_map/ppermute | solution.py:629
  21.3 11.0 %collective-permute-start.8 = (f32[144,128]{1,0:T(8,128)S(1)}, f32[144,128]{1,0:T(8,128)S(1)}, u32[]{:S(2)}, u32[]{:S(2)}) collective-permute-start(f32[144,128]{1,0:T(8,128)S(1)} %get-tuple-element.87), channel_id=1, source_target_pairs={{0,1},{1,0},{3,2},{2,3},{6,7},{7,6},{5,4},{4,5},{8,9},{9,8},{11,10... | collective-permute-start | bytes 221192 | tf_op jit(solution)/shard_map/ppermute | solution.py:629
  25.4 6.9 %collective-permute-start.9 = (f32[144,128]{1,0:T(8,128)S(1)}, f32[144,128]{1,0:T(8,128)S(1)}, u32[]{:S(2)}, u32[]{:S(2)}) collective-permute-start(f32[144,128]{1,0:T(8,128)S(1)} %get-tuple-element.88), channel_id=1, source_target_pairs={{0,16},{1,3},{3,1},{2,6},{6,2},{7,5},{5,7},{4,20},{8,24},{9,11},{1... | collective-permute-start | bytes 221192 | tf_op jit(solution)/shard_map/ppermute | solution.py:629
  25.4 3.8 %collective-permute-start.11 = (f32[72,128]{1,0:T(8,128)S(1)}, f32[72,128]{1,0:T(8,128)S(1)}, u32[]{:S(2)}, u32[]{:S(2)}) collective-permute-start(f32[72,128]{1,0:T(8,128)S(1)} %get-tuple-element.89.own), channel_id=1, source_target_pairs={{0,3},{1,0},{3,6},{2,1},{6,5},{7,2},{5,4},{4,7},{8,11},{9,8},{11,1... | collective-permute-start | bytes 110600 | tf_op jit(solution)/shard_map/ppermute | solution.py:629
  28.0 4.3 %collective-permute-start.10 = (f32[72,128]{1,0:T(8,128)S(1)}, f32[72,128]{1,0:T(8,128)S(1)}, u32[]{:S(2)}, u32[]{:S(2)}) collective-permute-start(f32[72,128]{1,0:T(8,128)S(1)} %get-tuple-element.89.own), channel_id=1, source_target_pairs={{0,1},{1,2},{3,0},{2,7},{6,3},{7,4},{5,6},{4,5},{8,9},{9,10},{11,8... | collective-permute-start | bytes 110600 | tf_op jit(solution)/shard_map/ppermute | solution.py:629

commit v8 on v7

--- a/solution.py
+++ b/solution.py
@@ -124,7 +124,11 @@
         run([base + k for k in range(step)])
         return carry
 
-    lax.fori_loop(0, trips, trip, 0)
+    if trips <= 4:
+        for t in range(trips):
+            run([low + t * step + k for k in range(step)])
+    else:
+        lax.fori_loop(0, trips, trip, 0)
     rest = list(range(low + trips * step, high))
     if rest:
         run(rest)
@@ -132,8 +136,7 @@
 
 def pair_sum_z(row, dist):
     lane = lane_ids(row.shape)
-    first = (lane // dist) % 2 == 0
-    return row + jnp.where(first, z_next(row, dist), z_prev(row, dist))
+    return row + jnp.take_along_axis(row, lane ^ dist, axis=1)
 
 
 def strided_pair(ref, at, count):
@@ -147,14 +150,20 @@
 WIDES = (WIDE_F, WIDE_F, WIDE_B)
 
 
+FACE_PARTS = ((0, 1), (2,))
+
+
 def face_pieces(count):
     pieces = []
-    at = 0
-    for k, wide in enumerate(WIDES):
-        for x in range(count):
-            pieces.append((k, x, wide, at))
-            at += wide
-    return pieces, at + -at % 8
+    sizes = []
+    for part, arrays in enumerate(FACE_PARTS):
+        at = 0
+        for k in arrays:
+            for x in range(count):
+                pieces.append((k, x, WIDES[k], part, at))
+                at += WIDES[k]
+        sizes.append(at + -at % 8)
+    return pieces, sizes
 
 
 def corner_pieces():
@@ -172,7 +181,10 @@
     return pieces, at + -at % 8
 
 
-def pack_faces_kernel(f, a, b, F, A, B, x_even, x_odd, y_even, y_odd, sems):
+def pack_faces_kernel(f, a, b, F, A, B, x_even, x_odd, *rest):
+    *y_faces, sems = rest
+    y_even = y_faces[:len(FACE_PARTS)]
+    y_odd = y_faces[len(FACE_PARTS):]
     count, depth = f.shape[:2]
     own = (pl.ds(FRAME, count), pl.ds(FRAME, depth))
     frames = (F, A, B)
@@ -188,11 +200,12 @@
             down = ref[FRAME + layer, FRAME:FRAME + depth]
             x_odd[row + layer], x_even[row + layer] = below_above(even_x, up, down)
         row += wide
-        for at_k, x, layers, at in pieces:
+        for at_k, x, layers, part, at in pieces:
             if at_k == k:
                 up = ref[FRAME + x, FRAME + depth - layers:FRAME + depth]
                 down = ref[FRAME + x, FRAME:FRAME + layers]
-                y_odd[at:at + layers], y_even[at:at + layers] = below_above(even, up, down)
+                rows = slice(at, at + layers)
+                y_odd[part][rows], y_even[part][rows] = below_above(even, up, down)
 
 
 def pack_corners_kernel(x_even, x_odd, to_even, to_odd):
@@ -255,16 +268,19 @@
     return coef_row, sweep_row, restrict_row, level1_source, level1_coef, coef_row1, coarse_pack
 
 
-def down_inner_kernel(y_even, y_odd, F_in, A_in, B_in, *refs):
-    *refs, T1 = refs
+def down_inner_kernel(*refs):
+    y_even = refs[:len(FACE_PARTS)]
+    y_odd = refs[len(FACE_PARTS):2 * len(FACE_PARTS)]
+    *refs, T1 = refs[2 * len(FACE_PARTS) + 3:]
     F, A, B = frames = refs[:3]
     A1, B1 = refs[12:14]
     end = F.shape[0]
     depth = F.shape[1] - 2 * FRAME
     count = end - 2 * FRAME
     even = even_position()
-    for k, x, layers, at in face_pieces(count)[0]:
-        below, above = below_above(even, y_even[at:at + layers], y_odd[at:at + layers])
+    for k, x, layers, part, at in face_pieces(count)[0]:
+        rows = slice(at, at + layers)
+        below, above = below_above(even, y_even[part][rows], y_odd[part][rows])
         frames[k][FRAME + x, FRAME - layers:FRAME] = below
         frames[k][FRAME + x, FRAME + depth:FRAME + depth + layers] = above
     zero_y_edges(frames, depth)
@@ -540,20 +556,14 @@
     sub = lax.broadcasted_iota(jnp.int32, (rows1, LANES), 0)
     lane = lane_ids((rows1, LANES))
     block = (sub + 4) // 8
-    mine = lane % 4 == (sub // 2 + 2) % 4
-    last_of_four = lane % 4 == 3
+    spread = lane - lane % 4 + (sub // 2 + 2) % 4
 
     def corrected_row(x):
         row = pl.ds(x + COARSE_X - first1 // 2, 1)
         t = jnp.broadcast_to(C2[0, row], (rows1, LANES))
         for at in range(1, 3):
             t = jnp.where(block == at, jnp.broadcast_to(C2[at, row], (rows1, LANES)), t)
-        t = jnp.where(mine, t, 0.0)
-        t = t + z_prev(t, 1)
-        t = t + z_prev(t, 2)
-        t = jnp.where(last_of_four, t, 0.0)
-        t = t + z_next(t, 1)
-        t = t + z_next(t, 2)
+        t = jnp.take_along_axis(t, spread, axis=1)
         return [(V1, 2 * x + k, V1[2 * x + k] + t) for k in range(2)]
 
     rows_loop(0, span1 // 2, 12, corrected_row)
@@ -592,15 +602,7 @@
     rows_loop(start + 1, span - start - 1, 17, sweep_a)
 
     def sweep_b(i):
-        rows = pl.ds(FRAME, depth)
-        here = U[i, rows]
-        fz = FZ[i, rows]
-        along_x = FX[i, rows] * U[i + 1, rows] + FX[i - 1, rows] * U[i - 1, rows]
-        before = pl.ds(FRAME - 1, depth)
-        along_y = FY[i, rows] * U[i, pl.ds(FRAME + 1, depth)] + FY[i, before] * U[i, before]
-        along_z = fz * z_next(here, 1) + z_prev(fz * here, 1)
-        off = along_x + along_y + along_z
-        return [(result, i - FRAME, (1.0 - OMEGA) * here + IN[i, rows] * (F[i, rows] + off))]
+        return [(result, i - FRAME, relaxed(i, U, F, IN, faces, 1)[FRAME:FRAME + depth])]
 
     chunk = count // 4
     copies = []
@@ -663,18 +665,19 @@
     dma = pltpu.SemaphoreType.DMA
     x_rows = 2 * WIDE_F + WIDE_B
     framed = (count + 2 * FRAME, depth + 2 * FRAME, lanes)
-    y_rows = face_pieces(count)[1]
+    y_parts = [arr(rows, lanes) for rows in face_pieces(count)[1]]
+    parts = len(y_parts)
     c_rows = corner_pieces()[1]
-    *frames, to_x_even, to_x_odd, to_y_even, to_y_odd = pl.pallas_call(
+    frame_f, frame_a, frame_b, to_x_even, to_x_odd, *to_y = pl.pallas_call(
         pack_faces_kernel,
-        out_shape=[arr(*framed)] * 3 + [arr(x_rows, depth, lanes)] * 2 + [arr(y_rows, lanes)] * 2,
+        out_shape=[arr(*framed)] * 3 + [arr(x_rows, depth, lanes)] * 2 + y_parts * 2,
         in_specs=[HBM] * 3,
-        out_specs=[VMEM] * 7,
+        out_specs=[VMEM] * (5 + 2 * parts),
         scratch_shapes=[dma((3,))],
         compiler_params=params(),
     )(*[pltpu.with_memory_space_constraint(t, pltpu.HBM) for t in (f, a, b)])
     x_halo = moved(to_x_even, x_even), moved(to_x_odd, x_odd)
-    y_halo = moved(to_y_even, y_even), moved(to_y_odd, y_odd)
+    y_halo = [moved(t, y_even) for t in to_y[:parts]] + [moved(t, y_odd) for t in to_y[parts:]]
 
     to_even, to_odd = pl.pallas_call(
         pack_corners_kernel,
@@ -691,12 +694,12 @@
     passed = pl.pallas_call(
         down_inner_kernel,
         out_shape=passed,
-        in_specs=[VMEM] * 5,
+        in_specs=[VMEM] * (2 * parts + 3),
         out_specs=[VMEM] * 21,
-        input_output_aliases={2 + k: k for k in range(3)},
+        input_output_aliases={2 * parts + k: k for k in range(3)},
         scratch_shapes=[vm(2 * count2, framed1[1], lanes)],
         compiler_params=params(),
-    )(*y_halo, *frames)
+    )(*y_halo, frame_f, frame_a, frame_b)
     x2_rows = 3 * COARSE_X + FINE_X * depth // 2
     x2_rows += -x2_rows % 8
     results = pl.pallas_call(

time: 35.3 us -> 34.1 us (0.966)
  Pallas kernels: 7.35 us -> 6.26 us
  starting transfers between devices: 15.2 us -> 14.7 us
    pallas_call x1, Pallas kernels: 2.01 us -> 1.45 us  [body(): pl.pallas_call(down_inner_kernel, out_shape=passed, in_specs=[VMEM] * (2...]
    pallas_call x1, Pallas kernels: 2.83 us -> 2.32 us  [body(): pl.pallas_call(up_kernel, out_shape=arr(count, depth, lanes), in_specs=[V...]
    ppermute x12 -> x14, starting transfers between devices: 15.2 us -> 14.7 us  [moved(): return lax.ppermute(array, ('grp', 'box'), pairs)]
    ppermute x12 -> x14, waiting for transfers between devices: 12.6 us -> 12.7 us  [moved(): return lax.ppermute(array, ('grp', 'box'), pairs)]
  transfers between devices with their start and end apart: 12 -> 14, of which waited for: 7 -> 7; matrix products, arithmetic and copies ran while one was open for 0% -> 0% of each run, Pallas kernels for 6% -> 4%
where the time goes in v8:
time: 34.1 us; the launch traced here: 33.7 us
  starting transfers between devices  14.7 us (43%)
  waiting for transfers between devices  12.7 us (37%)
  Pallas kernels  6.26 us (18%)
    ppermute x14, starting transfers between devices, moved(): return lax.ppermute(array, ('grp', 'box'), pairs)  14.7 us
    ppermute x14, waiting for transfers between devices, moved(): return lax.ppermute(array, ('grp', 'box'), pairs)  12.7 us
    pallas_call x1, Pallas kernels, body(): pl.pallas_call(up_kernel, out_shape=arr(count, depth, lanes), in_specs=[V...  2.32 us
    pallas_call x1, Pallas kernels, body(): pl.pallas_call(down_inner_kernel, out_shape=passed, in_specs=[VMEM] * (2...  1.45 us
    pallas_call x1, Pallas kernels, body(): pl.pallas_call(down_kernel, out_shape=[arr(*t.shape) for t in passed] + [...  1.24 us
    pallas_call x1, Pallas kernels, body(): pl.pallas_call(pack_faces_kernel, out_shape=[arr(*framed)] * 3 + [arr(x_r...  1.16 us
  transfers between devices with their start and end apart: 14, of which 7 were waited for; matrix products, arithmetic and copies ran while one was open for 0% of the time, Pallas kernels for 4%

profile of v8, /device:TPU:11, one launch (start us, length us, event | category | flops | bytes accessed | tf_op | source)
XLA Modules:
  0.0 33.7 jit_solution(1337638872750251315)
XLA Ops:
  0.0 1.2 %shard_map.37 = (f32[48,32,128]{2,1,0:T(8,128)S(1)}, f32[48,32,128]{2,1,0:T(8,128)S(1)}, f32[48,32,128]{2,1,0:T(8,128)S(1)}, f32[19,16,128]{2,1,0:T(8,128)S(1)},...) custom-call(f32[32,16,128]{2,1,0:T(8,128)} %bitcast.6, ...), custom_call_target="tpu_custom_call" | custom-call | tf_op jit(solution)/shard_map/pallas_call | solution.py:671
  1.2 0.3 collective-permute-start
  1.5 2.2 %collective-permute-start.1 = (f32[19,16,128]{2,1,0:T(8,128)S(1)}, f32[19,16,128]{2,1,0:T(8,128)S(1)}, u32[]{:S(2)}, u32[]{:S(2)}) collective-permute-start(f32[19,16,128]{2,1,0:T(8,128)S(1)} %get-tuple-element.56), channel_id=1, source_target_pairs={{0,1},{1,0},{3,2},{2,3},{6,7},{7,6},{5,4},{4,5},{8,16},{9,17},{11,... | collective-permute-start | bytes 466952 | tf_op jit(solution)/shard_map/ppermute | solution.py:631
  3.7 1.2 %collective-permute-start.5 = (f32[224,128]{1,0:T(8,128)S(1)}, f32[224,128]{1,0:T(8,128)S(1)}, u32[]{:S(2)}, u32[]{:S(2)}) collective-permute-start(f32[224,128]{1,0:T(8,128)S(1)} %get-tuple-element.60), channel_id=1, source_target_pairs={{0,1},{1,0},{3,2},{2,3},{6,7},{7,6},{5,4},{4,5},{8,9},{9,8},{11,10... | collective-permute-start | bytes 344072 | tf_op jit(solution)/shard_map/ppermute | solution.py:631
  4.9 0.0 collective-permute-start.4
  4.9 0.2 collective-permute-start.6
  5.1 1.1 %collective-permute-done.x_even = f32[19,16,128]{2,1,0:T(8,128)S(1)} collective-permute-done((f32[19,16,128]{2,1,0:T(8,128)S(1)}, f32[19,16,128]{2,1,0:T(8,128)S(1)}, u32[]{:S(2)}, u32[]{:S(2)}) %collective-permute-start) | collective-permute-done | bytes 155680 | tf_op jit(solution)/shard_map/ppermute | solution.py:631
  6.1 0.2 collective-permute-start.7
  6.4 4.1 %collective-permute-done.1.x_odd = f32[19,16,128]{2,1,0:T(8,128)S(1)} collective-permute-done((f32[19,16,128]{2,1,0:T(8,128)S(1)}, f32[19,16,128]{2,1,0:T(8,128)S(1)}, u32[]{:S(2)}, u32[]{:S(2)}) %collective-permute-start.1) | collective-permute-done | bytes 155680 | tf_op jit(solution)/shard_map/ppermute | solution.py:631
  10.4 0.1 shard_map.38
  10.5 1.6 %collective-permute-start.2 = (f32[176,128]{1,0:T(8,128)S(1)}, f32[176,128]{1,0:T(8,128)S(1)}, u32[]{:S(2)}, u32[]{:S(2)}) collective-permute-start(f32[176,128]{1,0:T(8,128)S(1)} %get-tuple-element.57), channel_id=1, source_target_pairs={{0,1},{1,0},{3,2},{2,3},{6,7},{7,6},{5,4},{4,5},{8,9},{9,8},{11,10... | collective-permute-start | bytes 270344 | tf_op jit(solution)/shard_map/ppermute | solution.py:631
  12.1 0.3 collective-permute-start.3
  12.4 1.4 %shard_map.39 = (f32[48,32,128]{2,1,0:T(8,128)S(1)}, f32[48,32,128]{2,1,0:T(8,128)S(1)}, f32[48,32,128]{2,1,0:T(8,128)S(1)}, f32[48,32,128]{2,1,0:T(8,128)S(1)},...) custom-call(f32[384,128]{1,0:T(8,128)S(1)} %collective-permute-done., ...), custom_call_target="tpu_custom_call", output_to_operand_aliasing={{0}: (4, {}), {1}: (5, {}), {2}: (6, {})} | custom-call | tf_op jit(solution)/shard_map/pallas_call | solution.py:694
  13.8 1.6 %collective-permute-done.3.c_odd = f32[176,128]{1,0:T(8,128)S(1)} collective-permute-done((f32[176,128]{1,0:T(8,128)S(1)}, f32[176,128]{1,0:T(8,128)S(1)}, u32[]{:S(2)}, u32[]{:S(2)}) %collective-permute-start.3) | collective-permute-done | bytes 90144 | tf_op jit(solution)/shard_map/ppermute | solution.py:631
  15.5 1.2 %shard_map.40 = (f32[48,32,128]{2,1,0:T(8,128)S(1)}, f32[48,32,128]{2,1,0:T(8,128)S(1)}, f32[48,32,128]{2,1,0:T(8,128)S(1)}, f32[48,32,128]{2,1,0:T(8,128)S(1)},...) custom-call(f32[19,16,128]{2,1,0:T(8,128)S(1)} %collective-permute-d, ...), custom_call_target="tpu_custom_call", output_to_operand_aliasing={{0}: (4, {}), {1}: (5, {}), {2}: (6, {}), {3}: (7, {}), {4}... | custom-call | tf_op jit(solution)/shard_map/pallas_call | solution.py:705
  16.7 0.1 collective-permute-start.8
  16.8 2.0 %collective-permute-start.9 = (f32[48,128]{1,0:T(8,128)S(1)}, f32[48,128]{1,0:T(8,128)S(1)}, u32[]{:S(2)}, u32[]{:S(2)}) collective-permute-start(f32[48,128]{1,0:T(8,128)S(1)} %get-tuple-element.90), channel_id=1, source_target_pairs={{0,1},{1,0},{3,2},{2,3},{6,7},{7,6},{5,4},{4,5},{8,16},{9,17},{11,... | collective-permute-start | bytes 73736 | tf_op jit(solution)/shard_map/ppermute | solution.py:631
  18.8 0.7 %collective-permute-done.8.x_even = f32[48,128]{1,0:T(8,128)S(1)} collective-permute-done((f32[48,128]{1,0:T(8,128)S(1)}, f32[48,128]{1,0:T(8,128)S(1)}, u32[]{:S(2)}, u32[]{:S(2)}) %collective-permute-start.8) | collective-permute-done | bytes 24608 | tf_op jit(solution)/shard_map/ppermute | solution.py:631
  19.4 1.0 %collective-permute-done.9.x_odd = f32[48,128]{1,0:T(8,128)S(1)} collective-permute-done((f32[48,128]{1,0:T(8,128)S(1)}, f32[48,128]{1,0:T(8,128)S(1)}, u32[]{:S(2)}, u32[]{:S(2)}) %collective-permute-start.9) | collective-permute-done | bytes 24608 | tf_op jit(solution)/shard_map/ppermute | solution.py:631
  20.5 4.0 %collective-permute-start.10 = (f32[144,128]{1,0:T(8,128)S(1)}, f32[144,128]{1,0:T(8,128)S(1)}, u32[]{:S(2)}, u32[]{:S(2)}) collective-permute-start(f32[144,128]{1,0:T(8,128)S(1)} %get-tuple-element.91), channel_id=1, source_target_pairs={{0,1},{1,0},{3,2},{2,3},{6,7},{7,6},{5,4},{4,5},{8,9},{9,8},{11,10... | collective-permute-start | bytes 221192 | tf_op jit(solution)/shard_map/ppermute | solution.py:631
  24.5 2.6 %collective-permute-start.13 = (f32[72,128]{1,0:T(8,128)S(1)}, f32[72,128]{1,0:T(8,128)S(1)}, u32[]{:S(2)}, u32[]{:S(2)}) collective-permute-start(f32[72,128]{1,0:T(8,128)S(1)} %get-tuple-element.93.own), channel_id=1, source_target_pairs={{0,3},{1,0},{3,6},{2,1},{6,5},{7,2},{5,4},{4,7},{8,11},{9,8},{11,1... | collective-permute-start | bytes 110600 | tf_op jit(solution)/shard_map/ppermute | solution.py:631
  27.1 1.2 %collective-permute-done.13.far_odd = f32[72,128]{1,0:T(8,128)S(1)} collective-permute-done((f32[72,128]{1,0:T(8,128)S(1)}, f32[72,128]{1,0:T(8,128)S(1)}, u32[]{:S(2)}, u32[]{:S(2)}) %collective-permute-start.13) | collective-permute-done | bytes 36896 | tf_op jit(solution)/shard_map/ppermute | solution.py:631
  28.3 3.1 %collective-permute-done.12.far_even = f32[72,128]{1,0:T(8,128)S(1)} collective-permute-done((f32[72,128]{1,0:T(8,128)S(1)}, f32[72,128]{1,0:T(8,128)S(1)}, u32[]{:S(2)}, u32[]{:S(2)}) %collective-permute-start.12) | collective-permute-done | bytes 36896 | tf_op jit(solution)/shard_map/ppermute | solution.py:631
  31.4 2.3 %shard_map.42 = f32[32,16,128]{2,1,0:T(8,128)} custom-call(f32[144,128]{1,0:T(8,128)S(1)} %collective-permute-done.10.near_even, f32[144,128]{1,0:T(8,128)S(1)} %collective-permute-done.11.near_odd, f32[72,128]{1,0:T(8,128)S(1)} %collective-permute-done.12.far_even, f32[72,128]{1,0:T(8,128)S(1)} %collective-permute-done.13.far_odd, ...), custom_call_target="tpu_custom_call" | custom-call | tf_op jit(solution)/shard_map/pallas_call | solution.py:731
  (10 shorter events, 0.1 us)
Async XLA Ops:
  1.2 5.0 %collective-permute-start = (f32[19,16,128]{2,1,0:T(8,128)S(1)}, f32[19,16,128]{2,1,0:T(8,128)S(1)}, u32[]{:S(2)}, u32[]{:S(2)}) collective-permute-start(f32[19,16,128]{2,1,0:T(8,128)S(1)} %get-tuple-element.55), channel_id=1, source_target_pairs={{0,8},{1,9},{3,11},{2,10},{6,14},{7,15},{5,13},{4,12},{8,0},{9,1},... | collective-permute-start | bytes 466952 | tf_op jit(solution)/shard_map/ppermute | solution.py:631
  1.5 8.9 %collective-permute-start.1 = (f32[19,16,128]{2,1,0:T(8,128)S(1)}, f32[19,16,128]{2,1,0:T(8,128)S(1)}, u32[]{:S(2)}, u32[]{:S(2)}) collective-permute-start(f32[19,16,128]{2,1,0:T(8,128)S(1)} %get-tuple-element.56), channel_id=1, source_target_pairs={{0,1},{1,0},{3,2},{2,3},{6,7},{7,6},{5,4},{4,5},{8,16},{9,17},{11,... | collective-permute-start | bytes 466952 | tf_op jit(solution)/shard_map/ppermute | solution.py:631
  3.7 8.4 %collective-permute-start.5 = (f32[224,128]{1,0:T(8,128)S(1)}, f32[224,128]{1,0:T(8,128)S(1)}, u32[]{:S(2)}, u32[]{:S(2)}) collective-permute-start(f32[224,128]{1,0:T(8,128)S(1)} %get-tuple-element.60), channel_id=1, source_target_pairs={{0,1},{1,0},{3,2},{2,3},{6,7},{7,6},{5,4},{4,5},{8,9},{9,8},{11,10... | collective-permute-start | bytes 344072 | tf_op jit(solution)/shard_map/ppermute | solution.py:631
  4.9 7.5 %collective-permute-start.4 = (f32[384,128]{1,0:T(8,128)S(1)}, f32[384,128]{1,0:T(8,128)S(1)}, u32[]{:S(2)}, u32[]{:S(2)}) collective-permute-start(f32[384,128]{1,0:T(8,128)S(1)} %get-tuple-element.59), channel_id=1, source_target_pairs={{0,1},{1,0},{3,2},{2,3},{6,7},{7,6},{5,4},{4,5},{8,9},{9,8},{11,10... | collective-permute-start | bytes 589832 | tf_op jit(solution)/shard_map/ppermute | solution.py:631
  4.9 7.5 %collective-permute-start.6 = (f32[384,128]{1,0:T(8,128)S(1)}, f32[384,128]{1,0:T(8,128)S(1)}, u32[]{:S(2)}, u32[]{:S(2)}) collective-permute-start(f32[384,128]{1,0:T(8,128)S(1)} %get-tuple-element.61), channel_id=1, source_target_pairs={{0,16},{1,3},{3,1},{2,6},{6,2},{7,5},{5,7},{4,20},{8,24},{9,11},{1... | collective-permute-start | bytes 589832 | tf_op jit(solution)/shard_map/ppermute | solution.py:631
  6.1 6.2 %collective-permute-start.7 = (f32[224,128]{1,0:T(8,128)S(1)}, f32[224,128]{1,0:T(8,128)S(1)}, u32[]{:S(2)}, u32[]{:S(2)}) collective-permute-start(f32[224,128]{1,0:T(8,128)S(1)} %get-tuple-element.62), channel_id=1, source_target_pairs={{0,16},{1,3},{3,1},{2,6},{6,2},{7,5},{5,7},{4,20},{8,24},{9,11},{1... | collective-permute-start | bytes 344072 | tf_op jit(solution)/shard_map/ppermute | solution.py:631
  10.5 3.4 %collective-permute-start.2 = (f32[176,128]{1,0:T(8,128)S(1)}, f32[176,128]{1,0:T(8,128)S(1)}, u32[]{:S(2)}, u32[]{:S(2)}) collective-permute-start(f32[176,128]{1,0:T(8,128)S(1)} %get-tuple-element.57), channel_id=1, source_target_pairs={{0,1},{1,0},{3,2},{2,3},{6,7},{7,6},{5,4},{4,5},{8,9},{9,8},{11,10... | collective-permute-start | bytes 270344 | tf_op jit(solution)/shard_map/ppermute | solution.py:631
  12.1 3.4 %collective-permute-start.3 = (f32[176,128]{1,0:T(8,128)S(1)}, f32[176,128]{1,0:T(8,128)S(1)}, u32[]{:S(2)}, u32[]{:S(2)}) collective-permute-start(f32[176,128]{1,0:T(8,128)S(1)} %get-tuple-element.58), channel_id=1, source_target_pairs={{0,16},{1,3},{3,1},{2,6},{6,2},{7,5},{5,7},{4,20},{8,24},{9,11},{1... | collective-permute-start | bytes 270344 | tf_op jit(solution)/shard_map/ppermute | solution.py:631
  16.7 2.7 %collective-permute-start.8 = (f32[48,128]{1,0:T(8,128)S(1)}, f32[48,128]{1,0:T(8,128)S(1)}, u32[]{:S(2)}, u32[]{:S(2)}) collective-permute-start(f32[48,128]{1,0:T(8,128)S(1)} %get-tuple-element.89), channel_id=1, source_target_pairs={{0,8},{1,9},{3,11},{2,10},{6,14},{7,15},{5,13},{4,12},{8,0},{9,1},... | collective-permute-start | bytes 73736 | tf_op jit(solution)/shard_map/ppermute | solution.py:631
  16.8 3.6 %collective-permute-start.9 = (f32[48,128]{1,0:T(8,128)S(1)}, f32[48,128]{1,0:T(8,128)S(1)}, u32[]{:S(2)}, u32[]{:S(2)}) collective-permute-start(f32[48,128]{1,0:T(8,128)S(1)} %get-tuple-element.90), channel_id=1, source_target_pairs={{0,1},{1,0},{3,2},{2,3},{6,7},{7,6},{5,4},{4,5},{8,16},{9,17},{11,... | collective-permute-start | bytes 73736 | tf_op jit(solution)/shard_map/ppermute | solution.py:631
  20.5 10.9 %collective-permute-start.10 = (f32[144,128]{1,0:T(8,128)S(1)}, f32[144,128]{1,0:T(8,128)S(1)}, u32[]{:S(2)}, u32[]{:S(2)}) collective-permute-start(f32[144,128]{1,0:T(8,128)S(1)} %get-tuple-element.91), channel_id=1, source_target_pairs={{0,1},{1,0},{3,2},{2,3},{6,7},{7,6},{5,4},{4,5},{8,9},{9,8},{11,10... | collective-permute-start | bytes 221192 | tf_op jit(solution)/shard_map/ppermute | solution.py:631
  24.5 6.9 %collective-permute-start.11 = (f32[144,128]{1,0:T(8,128)S(1)}, f32[144,128]{1,0:T(8,128)S(1)}, u32[]{:S(2)}, u32[]{:S(2)}) collective-permute-start(f32[144,128]{1,0:T(8,128)S(1)} %get-tuple-element.92), channel_id=1, source_target_pairs={{0,16},{1,3},{3,1},{2,6},{6,2},{7,5},{5,7},{4,20},{8,24},{9,11},{1... | collective-permute-start | bytes 221192 | tf_op jit(solution)/shard_map/ppermute | solution.py:631
  24.5 3.8 %collective-permute-start.13 = (f32[72,128]{1,0:T(8,128)S(1)}, f32[72,128]{1,0:T(8,128)S(1)}, u32[]{:S(2)}, u32[]{:S(2)}) collective-permute-start(f32[72,128]{1,0:T(8,128)S(1)} %get-tuple-element.93.own), channel_id=1, source_target_pairs={{0,3},{1,0},{3,6},{2,1},{6,5},{7,2},{5,4},{4,7},{8,11},{9,8},{11,1... | collective-permute-start | bytes 110600 | tf_op jit(solution)/shard_map/ppermute | solution.py:631
  27.1 4.3 %collective-permute-start.12 = (f32[72,128]{1,0:T(8,128)S(1)}, f32[72,128]{1,0:T(8,128)S(1)}, u32[]{:S(2)}, u32[]{:S(2)}) collective-permute-start(f32[72,128]{1,0:T(8,128)S(1)} %get-tuple-element.93.own), channel_id=1, source_target_pairs={{0,1},{1,2},{3,0},{2,7},{6,3},{7,4},{5,6},{4,5},{8,9},{9,10},{11,8... | collective-permute-start | bytes 110600 | tf_op jit(solution)/shard_map/ppermute | solution.py:631

commit v9 on v8

--- a/solution.py
+++ b/solution.py
@@ -10,6 +10,7 @@
 WIDE_F = 6
 WIDE_B = 7
 COARSE_PITCH = 24
+FAR_X = 4
 COARSE_X = 6
 FINE_X = 3
 LANES = 128
@@ -419,12 +420,14 @@
     for k in range(3):
         row = k * COARSE_PITCH
         part = slice(k * COARSE_X, (k + 1) * COARSE_X)
-        far[row:row + COARSE_X] = low[part]
-        far[row + COARSE_X:row + COARSE_X + count2] = coarse[k * count2:(k + 1) * count2]
-        far[row + COARSE_X + count2:row + 2 * COARSE_X + count2] = high[part]
-    rows = far.shape[0]
-    to_even[0:rows] = far[...]
-    to_odd[0:rows] = far[...]
+        to_even[row:row + COARSE_X] = low[part]
+        to_even[row + COARSE_X:row + COARSE_X + count2] = coarse[k * count2:(k + 1) * count2]
+        to_even[row + COARSE_X + count2:row + 2 * COARSE_X + count2] = high[part]
+        size = count2 + 2 * FAR_X
+        first = row + COARSE_X - FAR_X
+        far[k * size:(k + 1) * size] = to_even[first:first + size]
+    rows = 3 * COARSE_PITCH
+    to_odd[0:rows] = to_even[0:rows]
     even = even_position()
     tiles = [low[3 * COARSE_X + k * depth1:3 * COARSE_X + (k + 1) * depth1] for k in range(FINE_X)]
     tiles += [v1[first1 + k, first1:first1 + depth1] for k in range(count1)]
@@ -487,7 +490,7 @@
     in_v, F, IN, FX, FY, FZ,
     in_v1, F1, IN1, FX1, FY1, FZ1,
     out,
-    V, U, V1, U1, C2, P0, result, sems,
+    V, U, V1, U1, C2, P0, R2, result, sems,
 ):
     group = lax.axis_index("grp")
     position = box_position()
@@ -501,10 +504,13 @@
     arrays = []
     for k in range(3):
         rows = pl.ds(k * COARSE_PITCH, COARSE_PITCH)
-        ne, no, fe, fo = near_even[rows], near_odd[rows], far_even[rows], far_odd[rows]
-        near_low, near_high = below_above(even, ne, no)
-        far_low, far_high = below_above(even, fe, fo)
-        blocks = (far_low, near_low, own[rows], near_high, far_high)
+        near_low, near_high = below_above(even, near_even[rows], near_odd[rows])
+        size = count // 4 + 2 * FAR_X
+        far_rows = pl.ds(k * size, size)
+        for at, value in enumerate(below_above(even, far_even[far_rows], far_odd[far_rows])):
+            R2[at, k] = jnp.zeros((COARSE_PITCH, LANES), jnp.float32)
+            R2[at, k, COARSE_X - FAR_X:COARSE_X - FAR_X + size] = value
+        blocks = (R2[0, k], near_low, own[rows], near_high, R2[1, k])
         column = []
         for at, value in enumerate(blocks):
             place = position + (at - 2)
@@ -531,7 +537,7 @@
         V1[first1 - FINE_X + k, own_rows] = below
         V1[span1 - first1 + k, own_rows] = above
 
-    rim = own.shape[0]
+    rim = 3 * COARSE_PITCH
 
     def rim_row(x):
         i = x + first1 - FINE_X
@@ -714,8 +720,8 @@
     F, _, _, FX, FY, FZ, _, IN, _, U, _, F1, _, _, FX1, FY1, FZ1, _, IN1, _, coarse, V1, to_even, to_odd = results
 
     x_halo = moved(to_even, x_even), moved(to_odd, x_odd)
-    far_rows = 3 * COARSE_PITCH
-    near_rows = far_rows + FINE_X * (count // 2 + 2 * FINE_X)
+    far_rows = 3 * (count2 + 2 * FAR_X)
+    near_rows = 3 * COARSE_PITCH + FINE_X * (count // 2 + 2 * FINE_X)
     near_rows += -near_rows % 8
     far, to_even, to_odd = pl.pallas_call(
         pack_coarse_kernel,
@@ -734,10 +740,11 @@
         in_specs=[VMEM] * 19,
         out_specs=HBM,
         scratch_shapes=[vm(*framed)] * 2 + [vm(*framed1)] * 2
-        + [vm(3, COARSE_PITCH, lanes), vm(count // 2 + 2, framed[1], lanes), vm(count, depth, lanes), dma((4,))],
+        + [vm(3, COARSE_PITCH, lanes), vm(count // 2 + 2, framed[1], lanes),
+           vm(2, 3, COARSE_PITCH, lanes), vm(count, depth, lanes), dma((4,))],
         compiler_params=params(),
     )(
-        *near, *distant, far, *x_halo,
+        *near, *distant, to_even, *x_halo,
         U, F, IN, FX, FY, FZ, V1, F1, IN1, FX1, FY1, FZ1,
     )
     return out[:, None]

time: 34.1 us -> 33.8 us (level)
  waiting for transfers between devices: 12.7 us -> 11.4 us
  starting transfers between devices: 14.7 us -> 15.8 us
    ppermute x14, waiting for transfers between devices: 12.7 us -> 11.4 us  [moved(): return lax.ppermute(array, ('grp', 'box'), pairs)]
    ppermute x14, starting transfers between devices: 14.7 us -> 15.8 us  [moved(): return lax.ppermute(array, ('grp', 'box'), pairs)]
where the time goes in v9:
time: 33.8 us; the launch traced here: 33.5 us
  starting transfers between devices  15.8 us (47%)
  waiting for transfers between devices  11.4 us (34%)
  Pallas kernels  6.23 us (18%)
    ppermute x14, starting transfers between devices, moved(): return lax.ppermute(array, ('grp', 'box'), pairs)  15.8 us
    ppermute x14, waiting for transfers between devices, moved(): return lax.ppermute(array, ('grp', 'box'), pairs)  11.4 us
    pallas_call x1, Pallas kernels, body(): pl.pallas_call(up_kernel, out_shape=arr(count, depth, lanes), in_specs=[V...  2.32 us
    pallas_call x1, Pallas kernels, body(): pl.pallas_call(down_inner_kernel, out_shape=passed, in_specs=[VMEM] * (2...  1.43 us
    pallas_call x1, Pallas kernels, body(): pl.pallas_call(down_kernel, out_shape=[arr(*t.shape) for t in passed] + [...  1.23 us
    pallas_call x1, Pallas kernels, body(): pl.pallas_call(pack_faces_kernel, out_shape=[arr(*framed)] * 3 + [arr(x_r...  1.16 us
  transfers between devices with their start and end apart: 14, of which 7 were waited for; matrix products, arithmetic and copies ran while one was open for 0% of the time, Pallas kernels for 4%

profile of v9, /device:TPU:11, one launch (start us, length us, event | category | flops | bytes accessed | tf_op | source)
XLA Modules:
  0.0 33.5 jit_solution(8862389363489164238)
XLA Ops:
  0.0 1.2 %shard_map.37 = (f32[48,32,128]{2,1,0:T(8,128)S(1)}, f32[48,32,128]{2,1,0:T(8,128)S(1)}, f32[48,32,128]{2,1,0:T(8,128)S(1)}, f32[19,16,128]{2,1,0:T(8,128)S(1)},...) custom-call(f32[32,16,128]{2,1,0:T(8,128)} %bitcast.6, ...), custom_call_target="tpu_custom_call" | custom-call | tf_op jit(solution)/shard_map/pallas_call | solution.py:677
  1.2 0.3 collective-permute-start
  1.5 2.2 %collective-permute-start.1 = (f32[19,16,128]{2,1,0:T(8,128)S(1)}, f32[19,16,128]{2,1,0:T(8,128)S(1)}, u32[]{:S(2)}, u32[]{:S(2)}) collective-permute-start(f32[19,16,128]{2,1,0:T(8,128)S(1)} %get-tuple-element.56), channel_id=1, source_target_pairs={{0,1},{1,0},{3,2},{2,3},{6,7},{7,6},{5,4},{4,5},{8,16},{9,17},{11,... | collective-permute-start | bytes 466952 | tf_op jit(solution)/shard_map/ppermute | solution.py:637
  3.7 1.2 %collective-permute-start.5 = (f32[224,128]{1,0:T(8,128)S(1)}, f32[224,128]{1,0:T(8,128)S(1)}, u32[]{:S(2)}, u32[]{:S(2)}) collective-permute-start(f32[224,128]{1,0:T(8,128)S(1)} %get-tuple-element.60), channel_id=1, source_target_pairs={{0,1},{1,0},{3,2},{2,3},{6,7},{7,6},{5,4},{4,5},{8,9},{9,8},{11,10... | collective-permute-start | bytes 344072 | tf_op jit(solution)/shard_map/ppermute | solution.py:637
  4.9 0.2 collective-permute-start.6
  5.1 1.1 %collective-permute-done.x_even = f32[19,16,128]{2,1,0:T(8,128)S(1)} collective-permute-done((f32[19,16,128]{2,1,0:T(8,128)S(1)}, f32[19,16,128]{2,1,0:T(8,128)S(1)}, u32[]{:S(2)}, u32[]{:S(2)}) %collective-permute-start) | collective-permute-done | bytes 155680 | tf_op jit(solution)/shard_map/ppermute | solution.py:637
  6.1 0.2 collective-permute-start.7
  6.4 4.1 %collective-permute-done.1.x_odd = f32[19,16,128]{2,1,0:T(8,128)S(1)} collective-permute-done((f32[19,16,128]{2,1,0:T(8,128)S(1)}, f32[19,16,128]{2,1,0:T(8,128)S(1)}, u32[]{:S(2)}, u32[]{:S(2)}) %collective-permute-start.1) | collective-permute-done | bytes 155680 | tf_op jit(solution)/shard_map/ppermute | solution.py:637
  10.5 1.6 %collective-permute-start.2 = (f32[176,128]{1,0:T(8,128)S(1)}, f32[176,128]{1,0:T(8,128)S(1)}, u32[]{:S(2)}, u32[]{:S(2)}) collective-permute-start(f32[176,128]{1,0:T(8,128)S(1)} %get-tuple-element.57), channel_id=1, source_target_pairs={{0,1},{1,0},{3,2},{2,3},{6,7},{7,6},{5,4},{4,5},{8,9},{9,8},{11,10... | collective-permute-start | bytes 270344 | tf_op jit(solution)/shard_map/ppermute | solution.py:637
  12.1 0.3 collective-permute-start.3
  12.4 1.4 %shard_map.39 = (f32[48,32,128]{2,1,0:T(8,128)S(1)}, f32[48,32,128]{2,1,0:T(8,128)S(1)}, f32[48,32,128]{2,1,0:T(8,128)S(1)}, f32[48,32,128]{2,1,0:T(8,128)S(1)},...) custom-call(f32[384,128]{1,0:T(8,128)S(1)} %collective-permute-done., ...), custom_call_target="tpu_custom_call", output_to_operand_aliasing={{0}: (4, {}), {1}: (5, {}), {2}: (6, {})} | custom-call | tf_op jit(solution)/shard_map/pallas_call | solution.py:700
  13.8 1.6 %collective-permute-done.3.c_odd = f32[176,128]{1,0:T(8,128)S(1)} collective-permute-done((f32[176,128]{1,0:T(8,128)S(1)}, f32[176,128]{1,0:T(8,128)S(1)}, u32[]{:S(2)}, u32[]{:S(2)}) %collective-permute-start.3) | collective-permute-done | bytes 90144 | tf_op jit(solution)/shard_map/ppermute | solution.py:637
  15.5 1.2 %shard_map.40 = (f32[48,32,128]{2,1,0:T(8,128)S(1)}, f32[48,32,128]{2,1,0:T(8,128)S(1)}, f32[48,32,128]{2,1,0:T(8,128)S(1)}, f32[48,32,128]{2,1,0:T(8,128)S(1)},...) custom-call(f32[19,16,128]{2,1,0:T(8,128)S(1)} %collective-permute-d, ...), custom_call_target="tpu_custom_call", output_to_operand_aliasing={{0}: (4, {}), {1}: (5, {}), {2}: (6, {}), {3}: (7, {}), {4}... | custom-call | tf_op jit(solution)/shard_map/pallas_call | solution.py:711
  16.7 0.1 collective-permute-start.8
  16.8 2.0 %collective-permute-start.9 = (f32[48,128]{1,0:T(8,128)S(1)}, f32[48,128]{1,0:T(8,128)S(1)}, u32[]{:S(2)}, u32[]{:S(2)}) collective-permute-start(f32[48,128]{1,0:T(8,128)S(1)} %get-tuple-element.90), channel_id=1, source_target_pairs={{0,1},{1,0},{3,2},{2,3},{6,7},{7,6},{5,4},{4,5},{8,16},{9,17},{11,... | collective-permute-start | bytes 73736 | tf_op jit(solution)/shard_map/ppermute | solution.py:637
  18.8 0.7 %collective-permute-done.8.x_even = f32[48,128]{1,0:T(8,128)S(1)} collective-permute-done((f32[48,128]{1,0:T(8,128)S(1)}, f32[48,128]{1,0:T(8,128)S(1)}, u32[]{:S(2)}, u32[]{:S(2)}) %collective-permute-start.8) | collective-permute-done | bytes 24608 | tf_op jit(solution)/shard_map/ppermute | solution.py:637
  19.4 1.0 %collective-permute-done.9.x_odd = f32[48,128]{1,0:T(8,128)S(1)} collective-permute-done((f32[48,128]{1,0:T(8,128)S(1)}, f32[48,128]{1,0:T(8,128)S(1)}, u32[]{:S(2)}, u32[]{:S(2)}) %collective-permute-start.9) | collective-permute-done | bytes 24608 | tf_op jit(solution)/shard_map/ppermute | solution.py:637
  20.5 0.9 %collective-permute-start.11 = (f32[144,128]{1,0:T(8,128)S(1)}, f32[144,128]{1,0:T(8,128)S(1)}, u32[]{:S(2)}, u32[]{:S(2)}) collective-permute-start(f32[144,128]{1,0:T(8,128)S(1)} %get-tuple-element.92), channel_id=1, source_target_pairs={{0,16},{1,3},{3,1},{2,6},{6,2},{7,5},{5,7},{4,20},{8,24},{9,11},{1... | collective-permute-start | bytes 221192 | tf_op jit(solution)/shard_map/ppermute | solution.py:637
  21.3 5.1 %collective-permute-start.10 = (f32[144,128]{1,0:T(8,128)S(1)}, f32[144,128]{1,0:T(8,128)S(1)}, u32[]{:S(2)}, u32[]{:S(2)}) collective-permute-start(f32[144,128]{1,0:T(8,128)S(1)} %get-tuple-element.91.own), channel_id=1, source_target_pairs={{0,1},{1,0},{3,2},{2,3},{6,7},{7,6},{5,4},{4,5},{8,9},{9,8},{11,10... | collective-permute-start | bytes 221192 | tf_op jit(solution)/shard_map/ppermute | solution.py:637
  26.4 0.6 %collective-permute-start.13 = (f32[48,128]{1,0:T(8,128)S(1)}, f32[48,128]{1,0:T(8,128)S(1)}, u32[]{:S(2)}, u32[]{:S(2)}) collective-permute-start(f32[48,128]{1,0:T(8,128)S(1)} %get-tuple-element.93), channel_id=1, source_target_pairs={{0,3},{1,0},{3,6},{2,1},{6,5},{7,2},{5,4},{4,7},{8,11},{9,8},{11,1... | collective-permute-start | bytes 73736 | tf_op jit(solution)/shard_map/ppermute | solution.py:637
  27.0 1.2 %collective-permute-start.12 = (f32[48,128]{1,0:T(8,128)S(1)}, f32[48,128]{1,0:T(8,128)S(1)}, u32[]{:S(2)}, u32[]{:S(2)}) collective-permute-start(f32[48,128]{1,0:T(8,128)S(1)} %get-tuple-element.93), channel_id=1, source_target_pairs={{0,1},{1,2},{3,0},{2,7},{6,3},{7,4},{5,6},{4,5},{8,9},{9,10},{11,8... | collective-permute-start | bytes 73736 | tf_op jit(solution)/shard_map/ppermute | solution.py:637
  28.1 1.8 %collective-permute-done.13.far_odd = f32[48,128]{1,0:T(8,128)S(1)} collective-permute-done((f32[48,128]{1,0:T(8,128)S(1)}, f32[48,128]{1,0:T(8,128)S(1)}, u32[]{:S(2)}, u32[]{:S(2)}) %collective-permute-start.13) | collective-permute-done | bytes 24608 | tf_op jit(solution)/shard_map/ppermute | solution.py:637
  29.9 1.2 %collective-permute-done.12.far_even = f32[48,128]{1,0:T(8,128)S(1)} collective-permute-done((f32[48,128]{1,0:T(8,128)S(1)}, f32[48,128]{1,0:T(8,128)S(1)}, u32[]{:S(2)}, u32[]{:S(2)}) %collective-permute-start.12) | collective-permute-done | bytes 24608 | tf_op jit(solution)/shard_map/ppermute | solution.py:637
  31.1 2.3 %shard_map.42 = f32[32,16,128]{2,1,0:T(8,128)} custom-call(f32[144,128]{1,0:T(8,128)S(1)} %collective-permute-done.10.near_even, f32[144,128]{1,0:T(8,128)S(1)} %collective-permute-done.11.near_odd, f32[48,128]{1,0:T(8,128)S(1)} %collective-permute-done.12.far_even, f32[48,128]{1,0:T(8,128)S(1)} %collective-permute-done.13.far_odd, ...), custom_call_target="tpu_custom_call" | custom-call | tf_op jit(solution)/shard_map/pallas_call | solution.py:737
  (10 shorter events, 0.1 us)
Async XLA Ops:
  1.2 5.0 %collective-permute-start = (f32[19,16,128]{2,1,0:T(8,128)S(1)}, f32[19,16,128]{2,1,0:T(8,128)S(1)}, u32[]{:S(2)}, u32[]{:S(2)}) collective-permute-start(f32[19,16,128]{2,1,0:T(8,128)S(1)} %get-tuple-element.55), channel_id=1, source_target_pairs={{0,8},{1,9},{3,11},{2,10},{6,14},{7,15},{5,13},{4,12},{8,0},{9,1},... | collective-permute-start | bytes 466952 | tf_op jit(solution)/shard_map/ppermute | solution.py:637
  1.5 8.9 %collective-permute-start.1 = (f32[19,16,128]{2,1,0:T(8,128)S(1)}, f32[19,16,128]{2,1,0:T(8,128)S(1)}, u32[]{:S(2)}, u32[]{:S(2)}) collective-permute-start(f32[19,16,128]{2,1,0:T(8,128)S(1)} %get-tuple-element.56), channel_id=1, source_target_pairs={{0,1},{1,0},{3,2},{2,3},{6,7},{7,6},{5,4},{4,5},{8,16},{9,17},{11,... | collective-permute-start | bytes 466952 | tf_op jit(solution)/shard_map/ppermute | solution.py:637
  3.7 8.4 %collective-permute-start.5 = (f32[224,128]{1,0:T(8,128)S(1)}, f32[224,128]{1,0:T(8,128)S(1)}, u32[]{:S(2)}, u32[]{:S(2)}) collective-permute-start(f32[224,128]{1,0:T(8,128)S(1)} %get-tuple-element.60), channel_id=1, source_target_pairs={{0,1},{1,0},{3,2},{2,3},{6,7},{7,6},{5,4},{4,5},{8,9},{9,8},{11,10... | collective-permute-start | bytes 344072 | tf_op jit(solution)/shard_map/ppermute | solution.py:637
  4.9 7.5 %collective-permute-start.4 = (f32[384,128]{1,0:T(8,128)S(1)}, f32[384,128]{1,0:T(8,128)S(1)}, u32[]{:S(2)}, u32[]{:S(2)}) collective-permute-start(f32[384,128]{1,0:T(8,128)S(1)} %get-tuple-element.59), channel_id=1, source_target_pairs={{0,1},{1,0},{3,2},{2,3},{6,7},{7,6},{5,4},{4,5},{8,9},{9,8},{11,10... | collective-permute-start | bytes 589832 | tf_op jit(solution)/shard_map/ppermute | solution.py:637
  4.9 7.5 %collective-permute-start.6 = (f32[384,128]{1,0:T(8,128)S(1)}, f32[384,128]{1,0:T(8,128)S(1)}, u32[]{:S(2)}, u32[]{:S(2)}) collective-permute-start(f32[384,128]{1,0:T(8,128)S(1)} %get-tuple-element.61), channel_id=1, source_target_pairs={{0,16},{1,3},{3,1},{2,6},{6,2},{7,5},{5,7},{4,20},{8,24},{9,11},{1... | collective-permute-start | bytes 589832 | tf_op jit(solution)/shard_map/ppermute | solution.py:637
  6.1 6.2 %collective-permute-start.7 = (f32[224,128]{1,0:T(8,128)S(1)}, f32[224,128]{1,0:T(8,128)S(1)}, u32[]{:S(2)}, u32[]{:S(2)}) collective-permute-start(f32[224,128]{1,0:T(8,128)S(1)} %get-tuple-element.62), channel_id=1, source_target_pairs={{0,16},{1,3},{3,1},{2,6},{6,2},{7,5},{5,7},{4,20},{8,24},{9,11},{1... | collective-permute-start | bytes 344072 | tf_op jit(solution)/shard_map/ppermute | solution.py:637
  10.5 3.3 %collective-permute-start.2 = (f32[176,128]{1,0:T(8,128)S(1)}, f32[176,128]{1,0:T(8,128)S(1)}, u32[]{:S(2)}, u32[]{:S(2)}) collective-permute-start(f32[176,128]{1,0:T(8,128)S(1)} %get-tuple-element.57), channel_id=1, source_target_pairs={{0,1},{1,0},{3,2},{2,3},{6,7},{7,6},{5,4},{4,5},{8,9},{9,8},{11,10... | collective-permute-start | bytes 270344 | tf_op jit(solution)/shard_map/ppermute | solution.py:637
  12.1 3.4 %collective-permute-start.3 = (f32[176,128]{1,0:T(8,128)S(1)}, f32[176,128]{1,0:T(8,128)S(1)}, u32[]{:S(2)}, u32[]{:S(2)}) collective-permute-start(f32[176,128]{1,0:T(8,128)S(1)} %get-tuple-element.58), channel_id=1, source_target_pairs={{0,16},{1,3},{3,1},{2,6},{6,2},{7,5},{5,7},{4,20},{8,24},{9,11},{1... | collective-permute-start | bytes 270344 | tf_op jit(solution)/shard_map/ppermute | solution.py:637
  16.7 2.7 %collective-permute-start.8 = (f32[48,128]{1,0:T(8,128)S(1)}, f32[48,128]{1,0:T(8,128)S(1)}, u32[]{:S(2)}, u32[]{:S(2)}) collective-permute-start(f32[48,128]{1,0:T(8,128)S(1)} %get-tuple-element.89), channel_id=1, source_target_pairs={{0,8},{1,9},{3,11},{2,10},{6,14},{7,15},{5,13},{4,12},{8,0},{9,1},... | collective-permute-start | bytes 73736 | tf_op jit(solution)/shard_map/ppermute | solution.py:637
  16.8 3.6 %collective-permute-start.9 = (f32[48,128]{1,0:T(8,128)S(1)}, f32[48,128]{1,0:T(8,128)S(1)}, u32[]{:S(2)}, u32[]{:S(2)}) collective-permute-start(f32[48,128]{1,0:T(8,128)S(1)} %get-tuple-element.90), channel_id=1, source_target_pairs={{0,1},{1,0},{3,2},{2,3},{6,7},{7,6},{5,4},{4,5},{8,16},{9,17},{11,... | collective-permute-start | bytes 73736 | tf_op jit(solution)/shard_map/ppermute | solution.py:637
  20.5 10.7 %collective-permute-start.11 = (f32[144,128]{1,0:T(8,128)S(1)}, f32[144,128]{1,0:T(8,128)S(1)}, u32[]{:S(2)}, u32[]{:S(2)}) collective-permute-start(f32[144,128]{1,0:T(8,128)S(1)} %get-tuple-element.92), channel_id=1, source_target_pairs={{0,16},{1,3},{3,1},{2,6},{6,2},{7,5},{5,7},{4,20},{8,24},{9,11},{1... | collective-permute-start | bytes 221192 | tf_op jit(solution)/shard_map/ppermute | solution.py:637
  21.3 9.8 %collective-permute-start.10 = (f32[144,128]{1,0:T(8,128)S(1)}, f32[144,128]{1,0:T(8,128)S(1)}, u32[]{:S(2)}, u32[]{:S(2)}) collective-permute-start(f32[144,128]{1,0:T(8,128)S(1)} %get-tuple-element.91.own), channel_id=1, source_target_pairs={{0,1},{1,0},{3,2},{2,3},{6,7},{7,6},{5,4},{4,5},{8,9},{9,8},{11,10... | collective-permute-start | bytes 221192 | tf_op jit(solution)/shard_map/ppermute | solution.py:637
  26.4 3.5 %collective-permute-start.13 = (f32[48,128]{1,0:T(8,128)S(1)}, f32[48,128]{1,0:T(8,128)S(1)}, u32[]{:S(2)}, u32[]{:S(2)}) collective-permute-start(f32[48,128]{1,0:T(8,128)S(1)} %get-tuple-element.93), channel_id=1, source_target_pairs={{0,3},{1,0},{3,6},{2,1},{6,5},{7,2},{5,4},{4,7},{8,11},{9,8},{11,1... | collective-permute-start | bytes 73736 | tf_op jit(solution)/shard_map/ppermute | solution.py:637
  27.0 4.2 %collective-permute-start.12 = (f32[48,128]{1,0:T(8,128)S(1)}, f32[48,128]{1,0:T(8,128)S(1)}, u32[]{:S(2)}, u32[]{:S(2)}) collective-permute-start(f32[48,128]{1,0:T(8,128)S(1)} %get-tuple-element.93), channel_id=1, source_target_pairs={{0,1},{1,2},{3,0},{2,7},{6,3},{7,4},{5,6},{4,5},{8,9},{9,10},{11,8... | collective-permute-start | bytes 73736 | tf_op jit(solution)/shard_map/ppermute | solution.py:637

commit v10 on v9

--- a/solution.py
+++ b/solution.py
@@ -1,3 +1,5 @@
+import functools
+
 import jax
 import jax.numpy as jnp
 from jax import lax
@@ -151,7 +153,7 @@
 WIDES = (WIDE_F, WIDE_F, WIDE_B)
 
 
-FACE_PARTS = ((0, 1), (2,))
+FACE_PARTS = ((0,), (1, 2))
 
 
 def face_pieces(count):
@@ -167,18 +169,39 @@
     return pieces, sizes
 
 
+EDGE = 2
+
+
+def x_layout(depth):
+    whole = {}
+    for k, wide in enumerate(WIDES):
+        for distance in range(1, wide):
+            whole[k, distance] = len(whole) * depth
+    edges = len(whole) * depth
+    swept = edges + 2 * EDGE * len(WIDES)
+    rows = swept + depth - 2 * EDGE
+    return whole, edges, swept, rows + -rows % 8
+
+
+def x_rows(depth, k, distance, n, upper):
+    whole, edges, _, _ = x_layout(depth)
+    if (k, distance) in whole:
+        start = whole[k, distance] + (depth - n if upper else 0)
+    else:
+        assert n == EDGE
+        start = edges + 2 * EDGE * k + (EDGE if upper else 0)
+    return slice(start, start + n)
+
+
 def corner_pieces():
     pieces = []
     at = 0
     for side in range(2):
-        start = 0
         for k, wide in enumerate(WIDES):
-            for layer in range(wide):
-                distance = layer + 1 if side else wide - layer
+            for distance in range(1, wide + 1):
                 layers = min(wide, wide + 2 - distance)
-                pieces.append((side, k, start + layer, layers, at))
+                pieces.append((side, k, distance, layers, at))
                 at += layers
-            start += wide
     return pieces, at + -at % 8
 
 
@@ -193,31 +216,44 @@
     pieces, _ = face_pieces(count)
     even = even_position()
     even_x = even_group()
-    row = 0
+    whole, _, swept, _ = x_layout(depth)
+
+    def send_x(rows, up, down):
+        x_odd[rows], x_even[rows] = below_above(even_x, up, down)
+
     for k, (ref, wide) in enumerate(zip(frames, WIDES)):
         copies[k].wait()
-        for layer in range(wide):
-            up = ref[FRAME + count - wide + layer, FRAME:FRAME + depth]
-            down = ref[FRAME + layer, FRAME:FRAME + depth]
-            x_odd[row + layer], x_even[row + layer] = below_above(even_x, up, down)
-        row += wide
+        for distance in range(1, wide + 1):
+            ends = (FRAME + count - distance, FRAME + distance - 1)
+            if distance < wide:
+                start = whole[k, distance]
+                send_x(slice(start, start + depth), *(ref[x, FRAME:FRAME + depth] for x in ends))
+            else:
+                for upper, y in ((False, FRAME), (True, FRAME + depth - EDGE)):
+                    send_x(x_rows(depth, k, distance, EDGE, upper), *(ref[x, y:y + EDGE] for x in ends))
         for at_k, x, layers, part, at in pieces:
             if at_k == k:
                 up = ref[FRAME + x, FRAME + depth - layers:FRAME + depth]
                 down = ref[FRAME + x, FRAME:FRAME + layers]
                 rows = slice(at, at + layers)
                 y_odd[part][rows], y_even[part][rows] = below_above(even, up, down)
-
-
-def pack_corners_kernel(x_even, x_odd, to_even, to_odd):
-    depth = x_even.shape[1]
+    first_sweep = []
+    for x in (FRAME + count - WIDE_F, FRAME + WIDE_F - 1):
+        rows = slice(FRAME, FRAME + depth)
+        inverse = coefficients(A[x, rows], B[x, rows], B[x - 1, rows], B[x + 1, rows], 1, 1.0)[-1]
+        first_sweep.append((inverse * F[x, rows])[EDGE:depth - EDGE])
+    send_x(slice(swept, swept + depth - 2 * EDGE), *first_sweep)
+
+
+def pack_corners_kernel(depth, x_even, x_odd, to_even, to_odd):
     even = even_position()
     even_x = even_group()
-    for side, _, row, layers, at in corner_pieces()[0]:
-        up_rows = slice(depth - layers, depth)
-        up = below_above(even_x, x_even[row, up_rows], x_odd[row, up_rows])[side]
-        down = below_above(even_x, x_even[row, 0:layers], x_odd[row, 0:layers])[side]
-        to_odd[at:at + layers], to_even[at:at + layers] = below_above(even, up, down)
+    for side, k, distance, n, at in corner_pieces()[0]:
+        up, down = (
+            below_above(even_x, x_even[rows], x_odd[rows])[side]
+            for rows in (x_rows(depth, k, distance, n, upper) for upper in (True, False))
+        )
+        to_odd[at:at + n], to_even[at:at + n] = below_above(even, up, down)
 
 
 def down_rows(F, A, B, FX, FY, FZ, DG, IN, V, U, T, F1, A1, B1, FX1, FY1, FZ1, D1, IN1, W1, coarse):
@@ -331,16 +367,23 @@
     depth = F.shape[1] - 2 * FRAME
     even = even_position()
     even_x = even_group()
-    start = 0
+    whole, _, swept, _ = x_layout(depth)
     for k, wide in enumerate(WIDES):
-        for layer in range(wide):
-            below, above = below_above(even_x, x_even[start + layer], x_odd[start + layer])
-            frames[k][FRAME - wide + layer, FRAME:FRAME + depth] = below
-            frames[k][FRAME + count + layer, FRAME:FRAME + depth] = above
-        start += wide
-    starts = (0, WIDE_F, 2 * WIDE_F)
-    for side, k, row, layers, at in corner_pieces()[0]:
-        x = row - starts[k] + (FRAME + count if side else FRAME - WIDES[k])
+        for distance in range(1, wide + 1):
+            ends = (FRAME - distance, FRAME + count + distance - 1)
+            if distance < wide:
+                parts = [(slice(whole[k, distance], whole[k, distance] + depth), FRAME)]
+            else:
+                parts = [
+                    (x_rows(depth, k, distance, EDGE, False), FRAME),
+                    (x_rows(depth, k, distance, EDGE, True), FRAME + depth - EDGE),
+                ]
+            for rows, y in parts:
+                size = rows.stop - rows.start
+                for x, value in zip(ends, below_above(even_x, x_even[rows], x_odd[rows])):
+                    frames[k][x, y:y + size] = value
+    for side, k, distance, layers, at in corner_pieces()[0]:
+        x = FRAME + count + distance - 1 if side else FRAME - distance
         below, above = below_above(even, c_even[at:at + layers], c_odd[at:at + layers])
         frames[k][x, FRAME - layers:FRAME] = below
         frames[k][x, FRAME + depth:FRAME + depth + layers] = above
@@ -361,9 +404,16 @@
     first1 = FRAME // 2
     end1 = end // 2
     FX[1] = 0.5 * (B[1] + B[2])
+    V = refs[8]
+    rows = slice(swept, swept + depth - 2 * EDGE)
+    below, above = below_above(even_x, x_even[rows], x_odd[rows])
     for margin, fn in ((2, coef_row), (3, sweep_row)):
         rows_loop(margin, FRAME + margin - 1, 7, fn)
         rows_loop(end - FRAME - margin + 1, end - margin, 7, fn)
+        if fn is coef_row:
+            middle = slice(FRAME + EDGE, FRAME + depth - EDGE)
+            V[FRAME - WIDE_F, middle] = jnp.where(group > 0, below, 0.0)
+            V[FRAME + count + WIDE_F - 1, middle] = jnp.where(group < lax.axis_size("grp") - 1, above, 0.0)
     for fn in (restrict_row, level1_source):
         rows_loop(2, first1 + 2, 4, fn)
         rows_loop(end1 - first1 - 2, end1 - 2, 4, fn)
@@ -669,14 +719,13 @@
         return pltpu.VMEM(shape, jnp.float32)
 
     dma = pltpu.SemaphoreType.DMA
-    x_rows = 2 * WIDE_F + WIDE_B
     framed = (count + 2 * FRAME, depth + 2 * FRAME, lanes)
     y_parts = [arr(rows, lanes) for rows in face_pieces(count)[1]]
     parts = len(y_parts)
     c_rows = corner_pieces()[1]
     frame_f, frame_a, frame_b, to_x_even, to_x_odd, *to_y = pl.pallas_call(
         pack_faces_kernel,
-        out_shape=[arr(*framed)] * 3 + [arr(x_rows, depth, lanes)] * 2 + y_parts * 2,
+        out_shape=[arr(*framed)] * 3 + [arr(x_layout(depth)[-1], lanes)] * 2 + y_parts * 2,
         in_specs=[HBM] * 3,
         out_specs=[VMEM] * (5 + 2 * parts),
         scratch_shapes=[dma((3,))],
@@ -686,7 +735,7 @@
     y_halo = [moved(t, y_even) for t in to_y[:parts]] + [moved(t, y_odd) for t in to_y[parts:]]
 
     to_even, to_odd = pl.pallas_call(
-        pack_corners_kernel,
+        functools.partial(pack_corners_kernel, depth),
         out_shape=[arr(c_rows, lanes)] * 2,
         in_specs=[VMEM] * 2,
         out_specs=[VMEM] * 2,

time: 33.8 us -> 33.7 us (level)
  waiting for transfers between devices: 11.4 us -> 9.13 us
  starting transfers between devices: 15.8 us -> 17.5 us
    ppermute x14, waiting for transfers between devices: 11.4 us -> 9.13 us  [moved(): return lax.ppermute(array, ('grp', 'box'), pairs)]
    ppermute x14, starting transfers between devices: 15.8 us -> 17.5 us  [moved(): return lax.ppermute(array, ('grp', 'box'), pairs)]
  transfers between devices with their start and end apart: 14 -> 14, of which waited for: 7 -> 6; matrix products, arithmetic and copies ran while one was open for 0% -> 0% of each run, Pallas kernels for 4% -> 5%
where the time goes in v10:
time: 33.7 us; the launch traced here: 33 us
  starting transfers between devices  17.5 us (52%)
  waiting for transfers between devices  9.13 us (27%)
  Pallas kernels  6.33 us (19%)
    ppermute x14, starting transfers between devices, moved(): return lax.ppermute(array, ('grp', 'box'), pairs)  17.5 us
    ppermute x14, waiting for transfers between devices, moved(): return lax.ppermute(array, ('grp', 'box'), pairs)  9.13 us
    pallas_call x1, Pallas kernels, body(): pl.pallas_call(up_kernel, out_shape=arr(count, depth, lanes), in_specs=[V...  2.34 us
    pallas_call x1, Pallas kernels, body(): pl.pallas_call(down_inner_kernel, out_shape=passed, in_specs=[VMEM] * (2...  1.44 us
    pallas_call x1, Pallas kernels, body(): pl.pallas_call(down_kernel, out_shape=[arr(*t.shape) for t in passed] + [...  1.24 us
    pallas_call x1, Pallas kernels, body(): pl.pallas_call(pack_faces_kernel, out_shape=[arr(*framed)] * 3 + [arr(x_l...  1.23 us
  transfers between devices with their start and end apart: 14, of which 6 were waited for; matrix products, arithmetic and copies ran while one was open for 0% of the time, Pallas kernels for 5%

profile of v10, /device:TPU:11, one launch (start us, length us, event | category | flops | bytes accessed | tf_op | source)
XLA Modules:
  0.0 33.0 jit_solution(1104493340490994327)
XLA Ops:
  0.0 1.2 %shard_map.37 = (f32[48,32,128]{2,1,0:T(8,128)S(1)}, f32[48,32,128]{2,1,0:T(8,128)S(1)}, f32[48,32,128]{2,1,0:T(8,128)S(1)}, f32[280,128]{1,0:T(8,128)S(1)}, f32...) custom-call(f32[32,16,128]{2,1,0:T(8,128)} %bitcast.6, ...), custom_call_target="tpu_custom_call" | custom-call | tf_op jit(solution)/shard_map/pallas_call | solution.py:726
  1.2 0.3 collective-permute-start
  1.6 2.2 %collective-permute-start.1 = (f32[280,128]{1,0:T(8,128)S(1)}, f32[280,128]{1,0:T(8,128)S(1)}, u32[]{:S(2)}, u32[]{:S(2)}) collective-permute-start(f32[280,128]{1,0:T(8,128)S(1)} %get-tuple-element.56), channel_id=1, source_target_pairs={{0,1},{1,0},{3,2},{2,3},{6,7},{7,6},{5,4},{4,5},{8,16},{9,17},{11,... | collective-permute-start | bytes 430088 | tf_op jit(solution)/shard_map/ppermute | solution.py:687
  3.7 1.2 %collective-permute-start.5 = (f32[416,128]{1,0:T(8,128)S(1)}, f32[416,128]{1,0:T(8,128)S(1)}, u32[]{:S(2)}, u32[]{:S(2)}) collective-permute-start(f32[416,128]{1,0:T(8,128)S(1)} %get-tuple-element.60), channel_id=1, source_target_pairs={{0,1},{1,0},{3,2},{2,3},{6,7},{7,6},{5,4},{4,5},{8,9},{9,8},{11,10... | collective-permute-start | bytes 638984 | tf_op jit(solution)/shard_map/ppermute | solution.py:687
  5.0 0.2 collective-permute-start.7
  5.1 2.4 %collective-permute-start.4 = (f32[192,128]{1,0:T(8,128)S(1)}, f32[192,128]{1,0:T(8,128)S(1)}, u32[]{:S(2)}, u32[]{:S(2)}) collective-permute-start(f32[192,128]{1,0:T(8,128)S(1)} %get-tuple-element.59), channel_id=1, source_target_pairs={{0,1},{1,0},{3,2},{2,3},{6,7},{7,6},{5,4},{4,5},{8,9},{9,8},{11,10... | collective-permute-start | bytes 294920 | tf_op jit(solution)/shard_map/ppermute | solution.py:687
  7.6 0.0 collective-permute-done.x_even
  7.6 2.4 %collective-permute-done.1.x_odd = f32[280,128]{1,0:T(8,128)S(1)} collective-permute-done((f32[280,128]{1,0:T(8,128)S(1)}, f32[280,128]{1,0:T(8,128)S(1)}, u32[]{:S(2)}, u32[]{:S(2)}) %collective-permute-start.1) | collective-permute-done | bytes 143392 | tf_op jit(solution)/shard_map/ppermute | solution.py:687
  10.0 1.6 %collective-permute-start.2 = (f32[176,128]{1,0:T(8,128)S(1)}, f32[176,128]{1,0:T(8,128)S(1)}, u32[]{:S(2)}, u32[]{:S(2)}) collective-permute-start(f32[176,128]{1,0:T(8,128)S(1)} %get-tuple-element.57), channel_id=1, source_target_pairs={{0,1},{1,0},{3,2},{2,3},{6,7},{7,6},{5,4},{4,5},{8,9},{9,8},{11,10... | collective-permute-start | bytes 270344 | tf_op jit(solution)/shard_map/ppermute | solution.py:687
  11.6 0.3 collective-permute-start.3
  11.9 1.4 %shard_map.39 = (f32[48,32,128]{2,1,0:T(8,128)S(1)}, f32[48,32,128]{2,1,0:T(8,128)S(1)}, f32[48,32,128]{2,1,0:T(8,128)S(1)}, f32[48,32,128]{2,1,0:T(8,128)S(1)},...) custom-call(f32[192,128]{1,0:T(8,128)S(1)} %collective-permute-done., ...), custom_call_target="tpu_custom_call", output_to_operand_aliasing={{0}: (4, {}), {1}: (5, {}), {2}: (6, {})} | custom-call | tf_op jit(solution)/shard_map/pallas_call | solution.py:749
  13.4 1.9 %collective-permute-done.3.c_odd = f32[176,128]{1,0:T(8,128)S(1)} collective-permute-done((f32[176,128]{1,0:T(8,128)S(1)}, f32[176,128]{1,0:T(8,128)S(1)}, u32[]{:S(2)}, u32[]{:S(2)}) %collective-permute-start.3) | collective-permute-done | bytes 90144 | tf_op jit(solution)/shard_map/ppermute | solution.py:687
  15.3 1.2 %shard_map.40 = (f32[48,32,128]{2,1,0:T(8,128)S(1)}, f32[48,32,128]{2,1,0:T(8,128)S(1)}, f32[48,32,128]{2,1,0:T(8,128)S(1)}, f32[48,32,128]{2,1,0:T(8,128)S(1)},...) custom-call(f32[280,128]{1,0:T(8,128)S(1)} %collective-permute-done., ...), custom_call_target="tpu_custom_call", output_to_operand_aliasing={{0}: (4, {}), {1}: (5, {}), {2}: (6, {}), {3}: (7, {}), {4}... | custom-call | tf_op jit(solution)/shard_map/pallas_call | solution.py:760
  16.5 0.1 collective-permute-start.8
  16.6 1.8 %collective-permute-start.9 = (f32[48,128]{1,0:T(8,128)S(1)}, f32[48,128]{1,0:T(8,128)S(1)}, u32[]{:S(2)}, u32[]{:S(2)}) collective-permute-start(f32[48,128]{1,0:T(8,128)S(1)} %get-tuple-element.90), channel_id=1, source_target_pairs={{0,1},{1,0},{3,2},{2,3},{6,7},{7,6},{5,4},{4,5},{8,16},{9,17},{11,... | collective-permute-start | bytes 73736 | tf_op jit(solution)/shard_map/ppermute | solution.py:687
  18.5 0.8 %collective-permute-done.8.x_even = f32[48,128]{1,0:T(8,128)S(1)} collective-permute-done((f32[48,128]{1,0:T(8,128)S(1)}, f32[48,128]{1,0:T(8,128)S(1)}, u32[]{:S(2)}, u32[]{:S(2)}) %collective-permute-start.8) | collective-permute-done | bytes 24608 | tf_op jit(solution)/shard_map/ppermute | solution.py:687
  19.3 1.0 %collective-permute-done.9.x_odd = f32[48,128]{1,0:T(8,128)S(1)} collective-permute-done((f32[48,128]{1,0:T(8,128)S(1)}, f32[48,128]{1,0:T(8,128)S(1)}, u32[]{:S(2)}, u32[]{:S(2)}) %collective-permute-start.9) | collective-permute-done | bytes 24608 | tf_op jit(solution)/shard_map/ppermute | solution.py:687
  20.3 0.6 %collective-permute-start.11 = (f32[144,128]{1,0:T(8,128)S(1)}, f32[144,128]{1,0:T(8,128)S(1)}, u32[]{:S(2)}, u32[]{:S(2)}) collective-permute-start(f32[144,128]{1,0:T(8,128)S(1)} %get-tuple-element.92), channel_id=1, source_target_pairs={{0,16},{1,3},{3,1},{2,6},{6,2},{7,5},{5,7},{4,20},{8,24},{9,11},{1... | collective-permute-start | bytes 221192 | tf_op jit(solution)/shard_map/ppermute | solution.py:687
  20.9 5.1 %collective-permute-start.10 = (f32[144,128]{1,0:T(8,128)S(1)}, f32[144,128]{1,0:T(8,128)S(1)}, u32[]{:S(2)}, u32[]{:S(2)}) collective-permute-start(f32[144,128]{1,0:T(8,128)S(1)} %get-tuple-element.91.own), channel_id=1, source_target_pairs={{0,1},{1,0},{3,2},{2,3},{6,7},{7,6},{5,4},{4,5},{8,9},{9,8},{11,10... | collective-permute-start | bytes 221192 | tf_op jit(solution)/shard_map/ppermute | solution.py:687
  25.9 0.6 %collective-permute-start.13 = (f32[48,128]{1,0:T(8,128)S(1)}, f32[48,128]{1,0:T(8,128)S(1)}, u32[]{:S(2)}, u32[]{:S(2)}) collective-permute-start(f32[48,128]{1,0:T(8,128)S(1)} %get-tuple-element.93), channel_id=1, source_target_pairs={{0,3},{1,0},{3,6},{2,1},{6,5},{7,2},{5,4},{4,7},{8,11},{9,8},{11,1... | collective-permute-start | bytes 73736 | tf_op jit(solution)/shard_map/ppermute | solution.py:687
  26.5 1.2 %collective-permute-start.12 = (f32[48,128]{1,0:T(8,128)S(1)}, f32[48,128]{1,0:T(8,128)S(1)}, u32[]{:S(2)}, u32[]{:S(2)}) collective-permute-start(f32[48,128]{1,0:T(8,128)S(1)} %get-tuple-element.93), channel_id=1, source_target_pairs={{0,1},{1,2},{3,0},{2,7},{6,3},{7,4},{5,6},{4,5},{8,9},{9,10},{11,8... | collective-permute-start | bytes 73736 | tf_op jit(solution)/shard_map/ppermute | solution.py:687
  27.7 1.8 %collective-permute-done.13.far_odd = f32[48,128]{1,0:T(8,128)S(1)} collective-permute-done((f32[48,128]{1,0:T(8,128)S(1)}, f32[48,128]{1,0:T(8,128)S(1)}, u32[]{:S(2)}, u32[]{:S(2)}) %collective-permute-start.13) | collective-permute-done | bytes 24608 | tf_op jit(solution)/shard_map/ppermute | solution.py:687
  29.5 1.2 %collective-permute-done.12.far_even = f32[48,128]{1,0:T(8,128)S(1)} collective-permute-done((f32[48,128]{1,0:T(8,128)S(1)}, f32[48,128]{1,0:T(8,128)S(1)}, u32[]{:S(2)}, u32[]{:S(2)}) %collective-permute-start.12) | collective-permute-done | bytes 24608 | tf_op jit(solution)/shard_map/ppermute | solution.py:687
  30.7 2.3 %shard_map.42 = f32[32,16,128]{2,1,0:T(8,128)} custom-call(f32[144,128]{1,0:T(8,128)S(1)} %collective-permute-done.10.near_even, f32[144,128]{1,0:T(8,128)S(1)} %collective-permute-done.11.near_odd, f32[48,128]{1,0:T(8,128)S(1)} %collective-permute-done.12.far_even, f32[48,128]{1,0:T(8,128)S(1)} %collective-permute-done.13.far_odd, ...), custom_call_target="tpu_custom_call" | custom-call | tf_op jit(solution)/shard_map/pallas_call | solution.py:786
  (10 shorter events, 0.1 us)
Async XLA Ops:
  1.2 6.3 %collective-permute-start = (f32[280,128]{1,0:T(8,128)S(1)}, f32[280,128]{1,0:T(8,128)S(1)}, u32[]{:S(2)}, u32[]{:S(2)}) collective-permute-start(f32[280,128]{1,0:T(8,128)S(1)} %get-tuple-element.55), channel_id=1, source_target_pairs={{0,8},{1,9},{3,11},{2,10},{6,14},{7,15},{5,13},{4,12},{8,0},{9,1},... | collective-permute-start | bytes 430088 | tf_op jit(solution)/shard_map/ppermute | solution.py:687
  1.6 8.4 %collective-permute-start.1 = (f32[280,128]{1,0:T(8,128)S(1)}, f32[280,128]{1,0:T(8,128)S(1)}, u32[]{:S(2)}, u32[]{:S(2)}) collective-permute-start(f32[280,128]{1,0:T(8,128)S(1)} %get-tuple-element.56), channel_id=1, source_target_pairs={{0,1},{1,0},{3,2},{2,3},{6,7},{7,6},{5,4},{4,5},{8,16},{9,17},{11,... | collective-permute-start | bytes 430088 | tf_op jit(solution)/shard_map/ppermute | solution.py:687
  3.7 8.2 %collective-permute-start.5 = (f32[416,128]{1,0:T(8,128)S(1)}, f32[416,128]{1,0:T(8,128)S(1)}, u32[]{:S(2)}, u32[]{:S(2)}) collective-permute-start(f32[416,128]{1,0:T(8,128)S(1)} %get-tuple-element.60), channel_id=1, source_target_pairs={{0,1},{1,0},{3,2},{2,3},{6,7},{7,6},{5,4},{4,5},{8,9},{9,8},{11,10... | collective-permute-start | bytes 638984 | tf_op jit(solution)/shard_map/ppermute | solution.py:687
  5.0 7.0 %collective-permute-start.7 = (f32[416,128]{1,0:T(8,128)S(1)}, f32[416,128]{1,0:T(8,128)S(1)}, u32[]{:S(2)}, u32[]{:S(2)}) collective-permute-start(f32[416,128]{1,0:T(8,128)S(1)} %get-tuple-element.62), channel_id=1, source_target_pairs={{0,16},{1,3},{3,1},{2,6},{6,2},{7,5},{5,7},{4,20},{8,24},{9,11},{1... | collective-permute-start | bytes 638984 | tf_op jit(solution)/shard_map/ppermute | solution.py:687
  5.1 6.5 %collective-permute-start.4 = (f32[192,128]{1,0:T(8,128)S(1)}, f32[192,128]{1,0:T(8,128)S(1)}, u32[]{:S(2)}, u32[]{:S(2)}) collective-permute-start(f32[192,128]{1,0:T(8,128)S(1)} %get-tuple-element.59), channel_id=1, source_target_pairs={{0,1},{1,0},{3,2},{2,3},{6,7},{7,6},{5,4},{4,5},{8,9},{9,8},{11,10... | collective-permute-start | bytes 294920 | tf_op jit(solution)/shard_map/ppermute | solution.py:687
  7.6 4.4 %collective-permute-start.6 = (f32[192,128]{1,0:T(8,128)S(1)}, f32[192,128]{1,0:T(8,128)S(1)}, u32[]{:S(2)}, u32[]{:S(2)}) collective-permute-start(f32[192,128]{1,0:T(8,128)S(1)} %get-tuple-element.61), channel_id=1, source_target_pairs={{0,16},{1,3},{3,1},{2,6},{6,2},{7,5},{5,7},{4,20},{8,24},{9,11},{1... | collective-permute-start | bytes 294920 | tf_op jit(solution)/shard_map/ppermute | solution.py:687
  10.0 3.4 %collective-permute-start.2 = (f32[176,128]{1,0:T(8,128)S(1)}, f32[176,128]{1,0:T(8,128)S(1)}, u32[]{:S(2)}, u32[]{:S(2)}) collective-permute-start(f32[176,128]{1,0:T(8,128)S(1)} %get-tuple-element.57), channel_id=1, source_target_pairs={{0,1},{1,0},{3,2},{2,3},{6,7},{7,6},{5,4},{4,5},{8,9},{9,8},{11,10... | collective-permute-start | bytes 270344 | tf_op jit(solution)/shard_map/ppermute | solution.py:687
  11.6 3.7 %collective-permute-start.3 = (f32[176,128]{1,0:T(8,128)S(1)}, f32[176,128]{1,0:T(8,128)S(1)}, u32[]{:S(2)}, u32[]{:S(2)}) collective-permute-start(f32[176,128]{1,0:T(8,128)S(1)} %get-tuple-element.58), channel_id=1, source_target_pairs={{0,16},{1,3},{3,1},{2,6},{6,2},{7,5},{5,7},{4,20},{8,24},{9,11},{1... | collective-permute-start | bytes 270344 | tf_op jit(solution)/shard_map/ppermute | solution.py:687
  16.5 2.7 %collective-permute-start.8 = (f32[48,128]{1,0:T(8,128)S(1)}, f32[48,128]{1,0:T(8,128)S(1)}, u32[]{:S(2)}, u32[]{:S(2)}) collective-permute-start(f32[48,128]{1,0:T(8,128)S(1)} %get-tuple-element.89), channel_id=1, source_target_pairs={{0,8},{1,9},{3,11},{2,10},{6,14},{7,15},{5,13},{4,12},{8,0},{9,1},... | collective-permute-start | bytes 73736 | tf_op jit(solution)/shard_map/ppermute | solution.py:687
  16.6 3.6 %collective-permute-start.9 = (f32[48,128]{1,0:T(8,128)S(1)}, f32[48,128]{1,0:T(8,128)S(1)}, u32[]{:S(2)}, u32[]{:S(2)}) collective-permute-start(f32[48,128]{1,0:T(8,128)S(1)} %get-tuple-element.90), channel_id=1, source_target_pairs={{0,1},{1,0},{3,2},{2,3},{6,7},{7,6},{5,4},{4,5},{8,16},{9,17},{11,... | collective-permute-start | bytes 73736 | tf_op jit(solution)/shard_map/ppermute | solution.py:687
  20.3 10.4 %collective-permute-start.11 = (f32[144,128]{1,0:T(8,128)S(1)}, f32[144,128]{1,0:T(8,128)S(1)}, u32[]{:S(2)}, u32[]{:S(2)}) collective-permute-start(f32[144,128]{1,0:T(8,128)S(1)} %get-tuple-element.92), channel_id=1, source_target_pairs={{0,16},{1,3},{3,1},{2,6},{6,2},{7,5},{5,7},{4,20},{8,24},{9,11},{1... | collective-permute-start | bytes 221192 | tf_op jit(solution)/shard_map/ppermute | solution.py:687
  20.9 9.8 %collective-permute-start.10 = (f32[144,128]{1,0:T(8,128)S(1)}, f32[144,128]{1,0:T(8,128)S(1)}, u32[]{:S(2)}, u32[]{:S(2)}) collective-permute-start(f32[144,128]{1,0:T(8,128)S(1)} %get-tuple-element.91.own), channel_id=1, source_target_pairs={{0,1},{1,0},{3,2},{2,3},{6,7},{7,6},{5,4},{4,5},{8,9},{9,8},{11,10... | collective-permute-start | bytes 221192 | tf_op jit(solution)/shard_map/ppermute | solution.py:687
  25.9 3.5 %collective-permute-start.13 = (f32[48,128]{1,0:T(8,128)S(1)}, f32[48,128]{1,0:T(8,128)S(1)}, u32[]{:S(2)}, u32[]{:S(2)}) collective-permute-start(f32[48,128]{1,0:T(8,128)S(1)} %get-tuple-element.93), channel_id=1, source_target_pairs={{0,3},{1,0},{3,6},{2,1},{6,5},{7,2},{5,4},{4,7},{8,11},{9,8},{11,1... | collective-permute-start | bytes 73736 | tf_op jit(solution)/shard_map/ppermute | solution.py:687
  26.5 4.2 %collective-permute-start.12 = (f32[48,128]{1,0:T(8,128)S(1)}, f32[48,128]{1,0:T(8,128)S(1)}, u32[]{:S(2)}, u32[]{:S(2)}) collective-permute-start(f32[48,128]{1,0:T(8,128)S(1)} %get-tuple-element.93), channel_id=1, source_target_pairs={{0,1},{1,2},{3,0},{2,7},{6,3},{7,4},{5,6},{4,5},{8,9},{9,10},{11,8... | collective-permute-start | bytes 73736 | tf_op jit(solution)/shard_map/ppermute | solution.py:687

commit v11 on v10

--- a/solution.py
+++ b/solution.py
@@ -715,6 +715,9 @@
     def arr(*shape):
         return jax.ShapeDtypeStruct(shape, jnp.float32)
 
+    def in_vmem(array):
+        return pltpu.VMEM(array.shape, jnp.float32)
+
     def vm(*shape):
         return pltpu.VMEM(shape, jnp.float32)
 
@@ -725,7 +728,7 @@
     c_rows = corner_pieces()[1]
     frame_f, frame_a, frame_b, to_x_even, to_x_odd, *to_y = pl.pallas_call(
         pack_faces_kernel,
-        out_shape=[arr(*framed)] * 3 + [arr(x_layout(depth)[-1], lanes)] * 2 + y_parts * 2,
+        out_shape=[in_vmem(arr(*framed))] * 3 + [arr(x_layout(depth)[-1], lanes)] * 2 + y_parts * 2,
         in_specs=[HBM] * 3,
         out_specs=[VMEM] * (5 + 2 * parts),
         scratch_shapes=[dma((3,))],
@@ -748,7 +751,7 @@
     passed = [arr(*framed)] * 10 + [arr(framed1[0], framed[1], lanes)] + [arr(*framed1)] * 9 + [arr(3 * count2, lanes)]
     passed = pl.pallas_call(
         down_inner_kernel,
-        out_shape=passed,
+        out_shape=[in_vmem(t) for t in passed],
         in_specs=[VMEM] * (2 * parts + 3),
         out_specs=[VMEM] * 21,
         input_output_aliases={2 * parts + k: k for k in range(3)},
@@ -759,7 +762,7 @@
     x2_rows += -x2_rows % 8
     results = pl.pallas_call(
         down_kernel,
-        out_shape=[arr(*t.shape) for t in passed] + [arr(*framed1)] + [arr(x2_rows, lanes)] * 2,
+        out_shape=[in_vmem(t) for t in passed] + [arr(*framed1)] + [arr(x2_rows, lanes)] * 2,
         in_specs=[VMEM] * 25,
         out_specs=[VMEM] * 24,
         input_output_aliases={4 + k: k for k in range(21)},

time: 33.7 us -> 33.7 us (level)
  no operation moved by 1% of the time
where the time goes in v11:
time: 33.7 us; the launch traced here: 33 us
  starting transfers between devices  17.5 us (52%)
  waiting for transfers between devices  9.13 us (27%)
  Pallas kernels  6.33 us (19%)
    ppermute x14, starting transfers between devices, moved(): return lax.ppermute(array, ('grp', 'box'), pairs)  17.5 us
    ppermute x14, waiting for transfers between devices, moved(): return lax.ppermute(array, ('grp', 'box'), pairs)  9.13 us
    pallas_call x1, Pallas kernels, body(): pl.pallas_call(up_kernel, out_shape=arr(count, depth, lanes), in_specs=[V...  2.34 us
    pallas_call x1, Pallas kernels, body(): pl.pallas_call(down_inner_kernel, out_shape=[in_vmem(t) for t in passed],...  1.44 us
    pallas_call x1, Pallas kernels, body(): pl.pallas_call(down_kernel, out_shape=[in_vmem(t) for t in passed] + [arr...  1.24 us
    pallas_call x1, Pallas kernels, body(): pl.pallas_call(pack_faces_kernel, out_shape=[in_vmem(arr(*framed))] * 3 +...  1.23 us
  transfers between devices with their start and end apart: 14, of which 6 were waited for; matrix products, arithmetic and copies ran while one was open for 0% of the time, Pallas kernels for 5%

profile of v11, /device:TPU:11, one launch (start us, length us, event | category | flops | bytes accessed | tf_op | source)
XLA Modules:
  0.0 33.0 jit_solution(1104493340490994327)
XLA Ops:
  0.0 1.2 %shard_map.37 = (f32[48,32,128]{2,1,0:T(8,128)S(1)}, f32[48,32,128]{2,1,0:T(8,128)S(1)}, f32[48,32,128]{2,1,0:T(8,128)S(1)}, f32[280,128]{1,0:T(8,128)S(1)}, f32...) custom-call(f32[32,16,128]{2,1,0:T(8,128)} %bitcast.6, ...), custom_call_target="tpu_custom_call" | custom-call | tf_op jit(solution)/shard_map/pallas_call | solution.py:729
  1.2 0.3 collective-permute-start
  1.6 2.2 %collective-permute-start.1 = (f32[280,128]{1,0:T(8,128)S(1)}, f32[280,128]{1,0:T(8,128)S(1)}, u32[]{:S(2)}, u32[]{:S(2)}) collective-permute-start(f32[280,128]{1,0:T(8,128)S(1)} %get-tuple-element.56), channel_id=1, source_target_pairs={{0,1},{1,0},{3,2},{2,3},{6,7},{7,6},{5,4},{4,5},{8,16},{9,17},{11,... | collective-permute-start | bytes 430088 | tf_op jit(solution)/shard_map/ppermute | solution.py:687
  3.7 1.2 %collective-permute-start.5 = (f32[416,128]{1,0:T(8,128)S(1)}, f32[416,128]{1,0:T(8,128)S(1)}, u32[]{:S(2)}, u32[]{:S(2)}) collective-permute-start(f32[416,128]{1,0:T(8,128)S(1)} %get-tuple-element.60), channel_id=1, source_target_pairs={{0,1},{1,0},{3,2},{2,3},{6,7},{7,6},{5,4},{4,5},{8,9},{9,8},{11,10... | collective-permute-start | bytes 638984 | tf_op jit(solution)/shard_map/ppermute | solution.py:687
  5.0 0.2 collective-permute-start.7
  5.1 2.4 %collective-permute-start.4 = (f32[192,128]{1,0:T(8,128)S(1)}, f32[192,128]{1,0:T(8,128)S(1)}, u32[]{:S(2)}, u32[]{:S(2)}) collective-permute-start(f32[192,128]{1,0:T(8,128)S(1)} %get-tuple-element.59), channel_id=1, source_target_pairs={{0,1},{1,0},{3,2},{2,3},{6,7},{7,6},{5,4},{4,5},{8,9},{9,8},{11,10... | collective-permute-start | bytes 294920 | tf_op jit(solution)/shard_map/ppermute | solution.py:687
  7.6 0.0 collective-permute-done.x_even
  7.6 2.4 %collective-permute-done.1.x_odd = f32[280,128]{1,0:T(8,128)S(1)} collective-permute-done((f32[280,128]{1,0:T(8,128)S(1)}, f32[280,128]{1,0:T(8,128)S(1)}, u32[]{:S(2)}, u32[]{:S(2)}) %collective-permute-start.1) | collective-permute-done | bytes 143392 | tf_op jit(solution)/shard_map/ppermute | solution.py:687
  10.0 1.6 %collective-permute-start.2 = (f32[176,128]{1,0:T(8,128)S(1)}, f32[176,128]{1,0:T(8,128)S(1)}, u32[]{:S(2)}, u32[]{:S(2)}) collective-permute-start(f32[176,128]{1,0:T(8,128)S(1)} %get-tuple-element.57), channel_id=1, source_target_pairs={{0,1},{1,0},{3,2},{2,3},{6,7},{7,6},{5,4},{4,5},{8,9},{9,8},{11,10... | collective-permute-start | bytes 270344 | tf_op jit(solution)/shard_map/ppermute | solution.py:687
  11.6 0.3 collective-permute-start.3
  11.9 1.4 %shard_map.39 = (f32[48,32,128]{2,1,0:T(8,128)S(1)}, f32[48,32,128]{2,1,0:T(8,128)S(1)}, f32[48,32,128]{2,1,0:T(8,128)S(1)}, f32[48,32,128]{2,1,0:T(8,128)S(1)},...) custom-call(f32[192,128]{1,0:T(8,128)S(1)} %collective-permute-done., ...), custom_call_target="tpu_custom_call", output_to_operand_aliasing={{0}: (4, {}), {1}: (5, {}), {2}: (6, {})} | custom-call | tf_op jit(solution)/shard_map/pallas_call | solution.py:752
  13.4 1.9 %collective-permute-done.3.c_odd = f32[176,128]{1,0:T(8,128)S(1)} collective-permute-done((f32[176,128]{1,0:T(8,128)S(1)}, f32[176,128]{1,0:T(8,128)S(1)}, u32[]{:S(2)}, u32[]{:S(2)}) %collective-permute-start.3) | collective-permute-done | bytes 90144 | tf_op jit(solution)/shard_map/ppermute | solution.py:687
  15.3 1.2 %shard_map.40 = (f32[48,32,128]{2,1,0:T(8,128)S(1)}, f32[48,32,128]{2,1,0:T(8,128)S(1)}, f32[48,32,128]{2,1,0:T(8,128)S(1)}, f32[48,32,128]{2,1,0:T(8,128)S(1)},...) custom-call(f32[280,128]{1,0:T(8,128)S(1)} %collective-permute-done., ...), custom_call_target="tpu_custom_call", output_to_operand_aliasing={{0}: (4, {}), {1}: (5, {}), {2}: (6, {}), {3}: (7, {}), {4}... | custom-call | tf_op jit(solution)/shard_map/pallas_call | solution.py:763
  16.5 0.1 collective-permute-start.8
  16.6 1.8 %collective-permute-start.9 = (f32[48,128]{1,0:T(8,128)S(1)}, f32[48,128]{1,0:T(8,128)S(1)}, u32[]{:S(2)}, u32[]{:S(2)}) collective-permute-start(f32[48,128]{1,0:T(8,128)S(1)} %get-tuple-element.90), channel_id=1, source_target_pairs={{0,1},{1,0},{3,2},{2,3},{6,7},{7,6},{5,4},{4,5},{8,16},{9,17},{11,... | collective-permute-start | bytes 73736 | tf_op jit(solution)/shard_map/ppermute | solution.py:687
  18.5 0.8 %collective-permute-done.8.x_even = f32[48,128]{1,0:T(8,128)S(1)} collective-permute-done((f32[48,128]{1,0:T(8,128)S(1)}, f32[48,128]{1,0:T(8,128)S(1)}, u32[]{:S(2)}, u32[]{:S(2)}) %collective-permute-start.8) | collective-permute-done | bytes 24608 | tf_op jit(solution)/shard_map/ppermute | solution.py:687
  19.3 1.0 %collective-permute-done.9.x_odd = f32[48,128]{1,0:T(8,128)S(1)} collective-permute-done((f32[48,128]{1,0:T(8,128)S(1)}, f32[48,128]{1,0:T(8,128)S(1)}, u32[]{:S(2)}, u32[]{:S(2)}) %collective-permute-start.9) | collective-permute-done | bytes 24608 | tf_op jit(solution)/shard_map/ppermute | solution.py:687
  20.3 0.6 %collective-permute-start.11 = (f32[144,128]{1,0:T(8,128)S(1)}, f32[144,128]{1,0:T(8,128)S(1)}, u32[]{:S(2)}, u32[]{:S(2)}) collective-permute-start(f32[144,128]{1,0:T(8,128)S(1)} %get-tuple-element.92), channel_id=1, source_target_pairs={{0,16},{1,3},{3,1},{2,6},{6,2},{7,5},{5,7},{4,20},{8,24},{9,11},{1... | collective-permute-start | bytes 221192 | tf_op jit(solution)/shard_map/ppermute | solution.py:687
  20.9 5.1 %collective-permute-start.10 = (f32[144,128]{1,0:T(8,128)S(1)}, f32[144,128]{1,0:T(8,128)S(1)}, u32[]{:S(2)}, u32[]{:S(2)}) collective-permute-start(f32[144,128]{1,0:T(8,128)S(1)} %get-tuple-element.91.own), channel_id=1, source_target_pairs={{0,1},{1,0},{3,2},{2,3},{6,7},{7,6},{5,4},{4,5},{8,9},{9,8},{11,10... | collective-permute-start | bytes 221192 | tf_op jit(solution)/shard_map/ppermute | solution.py:687
  25.9 0.6 %collective-permute-start.13 = (f32[48,128]{1,0:T(8,128)S(1)}, f32[48,128]{1,0:T(8,128)S(1)}, u32[]{:S(2)}, u32[]{:S(2)}) collective-permute-start(f32[48,128]{1,0:T(8,128)S(1)} %get-tuple-element.93), channel_id=1, source_target_pairs={{0,3},{1,0},{3,6},{2,1},{6,5},{7,2},{5,4},{4,7},{8,11},{9,8},{11,1... | collective-permute-start | bytes 73736 | tf_op jit(solution)/shard_map/ppermute | solution.py:687
  26.5 1.2 %collective-permute-start.12 = (f32[48,128]{1,0:T(8,128)S(1)}, f32[48,128]{1,0:T(8,128)S(1)}, u32[]{:S(2)}, u32[]{:S(2)}) collective-permute-start(f32[48,128]{1,0:T(8,128)S(1)} %get-tuple-element.93), channel_id=1, source_target_pairs={{0,1},{1,2},{3,0},{2,7},{6,3},{7,4},{5,6},{4,5},{8,9},{9,10},{11,8... | collective-permute-start | bytes 73736 | tf_op jit(solution)/shard_map/ppermute | solution.py:687
  27.7 1.8 %collective-permute-done.13.far_odd = f32[48,128]{1,0:T(8,128)S(1)} collective-permute-done((f32[48,128]{1,0:T(8,128)S(1)}, f32[48,128]{1,0:T(8,128)S(1)}, u32[]{:S(2)}, u32[]{:S(2)}) %collective-permute-start.13) | collective-permute-done | bytes 24608 | tf_op jit(solution)/shard_map/ppermute | solution.py:687
  29.5 1.2 %collective-permute-done.12.far_even = f32[48,128]{1,0:T(8,128)S(1)} collective-permute-done((f32[48,128]{1,0:T(8,128)S(1)}, f32[48,128]{1,0:T(8,128)S(1)}, u32[]{:S(2)}, u32[]{:S(2)}) %collective-permute-start.12) | collective-permute-done | bytes 24608 | tf_op jit(solution)/shard_map/ppermute | solution.py:687
  30.7 2.3 %shard_map.42 = f32[32,16,128]{2,1,0:T(8,128)} custom-call(f32[144,128]{1,0:T(8,128)S(1)} %collective-permute-done.10.near_even, f32[144,128]{1,0:T(8,128)S(1)} %collective-permute-done.11.near_odd, f32[48,128]{1,0:T(8,128)S(1)} %collective-permute-done.12.far_even, f32[48,128]{1,0:T(8,128)S(1)} %collective-permute-done.13.far_odd, ...), custom_call_target="tpu_custom_call" | custom-call | tf_op jit(solution)/shard_map/pallas_call | solution.py:789
  (10 shorter events, 0.1 us)
Async XLA Ops:
  1.2 6.3 %collective-permute-start = (f32[280,128]{1,0:T(8,128)S(1)}, f32[280,128]{1,0:T(8,128)S(1)}, u32[]{:S(2)}, u32[]{:S(2)}) collective-permute-start(f32[280,128]{1,0:T(8,128)S(1)} %get-tuple-element.55), channel_id=1, source_target_pairs={{0,8},{1,9},{3,11},{2,10},{6,14},{7,15},{5,13},{4,12},{8,0},{9,1},... | collective-permute-start | bytes 430088 | tf_op jit(solution)/shard_map/ppermute | solution.py:687
  1.6 8.4 %collective-permute-start.1 = (f32[280,128]{1,0:T(8,128)S(1)}, f32[280,128]{1,0:T(8,128)S(1)}, u32[]{:S(2)}, u32[]{:S(2)}) collective-permute-start(f32[280,128]{1,0:T(8,128)S(1)} %get-tuple-element.56), channel_id=1, source_target_pairs={{0,1},{1,0},{3,2},{2,3},{6,7},{7,6},{5,4},{4,5},{8,16},{9,17},{11,... | collective-permute-start | bytes 430088 | tf_op jit(solution)/shard_map/ppermute | solution.py:687
  3.7 8.2 %collective-permute-start.5 = (f32[416,128]{1,0:T(8,128)S(1)}, f32[416,128]{1,0:T(8,128)S(1)}, u32[]{:S(2)}, u32[]{:S(2)}) collective-permute-start(f32[416,128]{1,0:T(8,128)S(1)} %get-tuple-element.60), channel_id=1, source_target_pairs={{0,1},{1,0},{3,2},{2,3},{6,7},{7,6},{5,4},{4,5},{8,9},{9,8},{11,10... | collective-permute-start | bytes 638984 | tf_op jit(solution)/shard_map/ppermute | solution.py:687
  5.0 7.0 %collective-permute-start.7 = (f32[416,128]{1,0:T(8,128)S(1)}, f32[416,128]{1,0:T(8,128)S(1)}, u32[]{:S(2)}, u32[]{:S(2)}) collective-permute-start(f32[416,128]{1,0:T(8,128)S(1)} %get-tuple-element.62), channel_id=1, source_target_pairs={{0,16},{1,3},{3,1},{2,6},{6,2},{7,5},{5,7},{4,20},{8,24},{9,11},{1... | collective-permute-start | bytes 638984 | tf_op jit(solution)/shard_map/ppermute | solution.py:687
  5.1 6.5 %collective-permute-start.4 = (f32[192,128]{1,0:T(8,128)S(1)}, f32[192,128]{1,0:T(8,128)S(1)}, u32[]{:S(2)}, u32[]{:S(2)}) collective-permute-start(f32[192,128]{1,0:T(8,128)S(1)} %get-tuple-element.59), channel_id=1, source_target_pairs={{0,1},{1,0},{3,2},{2,3},{6,7},{7,6},{5,4},{4,5},{8,9},{9,8},{11,10... | collective-permute-start | bytes 294920 | tf_op jit(solution)/shard_map/ppermute | solution.py:687
  7.6 4.4 %collective-permute-start.6 = (f32[192,128]{1,0:T(8,128)S(1)}, f32[192,128]{1,0:T(8,128)S(1)}, u32[]{:S(2)}, u32[]{:S(2)}) collective-permute-start(f32[192,128]{1,0:T(8,128)S(1)} %get-tuple-element.61), channel_id=1, source_target_pairs={{0,16},{1,3},{3,1},{2,6},{6,2},{7,5},{5,7},{4,20},{8,24},{9,11},{1... | collective-permute-start | bytes 294920 | tf_op jit(solution)/shard_map/ppermute | solution.py:687
  10.0 3.4 %collective-permute-start.2 = (f32[176,128]{1,0:T(8,128)S(1)}, f32[176,128]{1,0:T(8,128)S(1)}, u32[]{:S(2)}, u32[]{:S(2)}) collective-permute-start(f32[176,128]{1,0:T(8,128)S(1)} %get-tuple-element.57), channel_id=1, source_target_pairs={{0,1},{1,0},{3,2},{2,3},{6,7},{7,6},{5,4},{4,5},{8,9},{9,8},{11,10... | collective-permute-start | bytes 270344 | tf_op jit(solution)/shard_map/ppermute | solution.py:687
  11.6 3.7 %collective-permute-start.3 = (f32[176,128]{1,0:T(8,128)S(1)}, f32[176,128]{1,0:T(8,128)S(1)}, u32[]{:S(2)}, u32[]{:S(2)}) collective-permute-start(f32[176,128]{1,0:T(8,128)S(1)} %get-tuple-element.58), channel_id=1, source_target_pairs={{0,16},{1,3},{3,1},{2,6},{6,2},{7,5},{5,7},{4,20},{8,24},{9,11},{1... | collective-permute-start | bytes 270344 | tf_op jit(solution)/shard_map/ppermute | solution.py:687
  16.5 2.7 %collective-permute-start.8 = (f32[48,128]{1,0:T(8,128)S(1)}, f32[48,128]{1,0:T(8,128)S(1)}, u32[]{:S(2)}, u32[]{:S(2)}) collective-permute-start(f32[48,128]{1,0:T(8,128)S(1)} %get-tuple-element.89), channel_id=1, source_target_pairs={{0,8},{1,9},{3,11},{2,10},{6,14},{7,15},{5,13},{4,12},{8,0},{9,1},... | collective-permute-start | bytes 73736 | tf_op jit(solution)/shard_map/ppermute | solution.py:687
  16.6 3.6 %collective-permute-start.9 = (f32[48,128]{1,0:T(8,128)S(1)}, f32[48,128]{1,0:T(8,128)S(1)}, u32[]{:S(2)}, u32[]{:S(2)}) collective-permute-start(f32[48,128]{1,0:T(8,128)S(1)} %get-tuple-element.90), channel_id=1, source_target_pairs={{0,1},{1,0},{3,2},{2,3},{6,7},{7,6},{5,4},{4,5},{8,16},{9,17},{11,... | collective-permute-start | bytes 73736 | tf_op jit(solution)/shard_map/ppermute | solution.py:687
  20.3 10.4 %collective-permute-start.11 = (f32[144,128]{1,0:T(8,128)S(1)}, f32[144,128]{1,0:T(8,128)S(1)}, u32[]{:S(2)}, u32[]{:S(2)}) collective-permute-start(f32[144,128]{1,0:T(8,128)S(1)} %get-tuple-element.92), channel_id=1, source_target_pairs={{0,16},{1,3},{3,1},{2,6},{6,2},{7,5},{5,7},{4,20},{8,24},{9,11},{1... | collective-permute-start | bytes 221192 | tf_op jit(solution)/shard_map/ppermute | solution.py:687
  20.9 9.8 %collective-permute-start.10 = (f32[144,128]{1,0:T(8,128)S(1)}, f32[144,128]{1,0:T(8,128)S(1)}, u32[]{:S(2)}, u32[]{:S(2)}) collective-permute-start(f32[144,128]{1,0:T(8,128)S(1)} %get-tuple-element.91.own), channel_id=1, source_target_pairs={{0,1},{1,0},{3,2},{2,3},{6,7},{7,6},{5,4},{4,5},{8,9},{9,8},{11,10... | collective-permute-start | bytes 221192 | tf_op jit(solution)/shard_map/ppermute | solution.py:687
  25.9 3.5 %collective-permute-start.13 = (f32[48,128]{1,0:T(8,128)S(1)}, f32[48,128]{1,0:T(8,128)S(1)}, u32[]{:S(2)}, u32[]{:S(2)}) collective-permute-start(f32[48,128]{1,0:T(8,128)S(1)} %get-tuple-element.93), channel_id=1, source_target_pairs={{0,3},{1,0},{3,6},{2,1},{6,5},{7,2},{5,4},{4,7},{8,11},{9,8},{11,1... | collective-permute-start | bytes 73736 | tf_op jit(solution)/shard_map/ppermute | solution.py:687
  26.5 4.2 %collective-permute-start.12 = (f32[48,128]{1,0:T(8,128)S(1)}, f32[48,128]{1,0:T(8,128)S(1)}, u32[]{:S(2)}, u32[]{:S(2)}) collective-permute-start(f32[48,128]{1,0:T(8,128)S(1)} %get-tuple-element.93), channel_id=1, source_target_pairs={{0,1},{1,2},{3,0},{2,7},{6,3},{7,4},{5,6},{4,5},{8,9},{9,10},{11,8... | collective-permute-start | bytes 73736 | tf_op jit(solution)/shard_map/ppermute | solution.py:687

commit v12 on v11

--- a/solution.py
+++ b/solution.py
@@ -660,9 +660,9 @@
     def sweep_b(i):
         return [(result, i - FRAME, relaxed(i, U, F, IN, faces, 1)[FRAME:FRAME + depth])]
 
-    chunk = count // 4
+    chunk = count // 8
     copies = []
-    for k in range(4):
+    for k in range(8):
         rows_loop(FRAME + k * chunk, FRAME + (k + 1) * chunk, chunk, sweep_b)
         rows = pl.ds(k * chunk, chunk)
         copies.append(pltpu.make_async_copy(result.at[rows], out.at[rows], sems.at[k]))
@@ -793,7 +793,7 @@
         out_specs=HBM,
         scratch_shapes=[vm(*framed)] * 2 + [vm(*framed1)] * 2
         + [vm(3, COARSE_PITCH, lanes), vm(count // 2 + 2, framed[1], lanes),
-           vm(2, 3, COARSE_PITCH, lanes), vm(count, depth, lanes), dma((4,))],
+           vm(2, 3, COARSE_PITCH, lanes), vm(count, depth, lanes), dma((8,))],
         compiler_params=params(),
     )(
         *near, *distant, to_even, *x_halo,

time: 33.7 us -> 33.7 us (level)
  no operation moved by 1% of the time
where the time goes in v12:
time: 33.7 us; the launch traced here: 33 us
  starting transfers between devices  17.5 us (52%)
  waiting for transfers between devices  9.13 us (27%)
  Pallas kernels  6.35 us (19%)
    ppermute x14, starting transfers between devices, moved(): return lax.ppermute(array, ('grp', 'box'), pairs)  17.5 us
    ppermute x14, waiting for transfers between devices, moved(): return lax.ppermute(array, ('grp', 'box'), pairs)  9.13 us
    pallas_call x1, Pallas kernels, body(): pl.pallas_call(up_kernel, out_shape=arr(count, depth, lanes), in_specs=[V...  2.36 us
    pallas_call x1, Pallas kernels, body(): pl.pallas_call(down_inner_kernel, out_shape=[in_vmem(t) for t in passed],...  1.44 us
    pallas_call x1, Pallas kernels, body(): pl.pallas_call(down_kernel, out_shape=[in_vmem(t) for t in passed] + [arr...  1.24 us
    pallas_call x1, Pallas kernels, body(): pl.pallas_call(pack_faces_kernel, out_shape=[in_vmem(arr(*framed))] * 3 +...  1.23 us
  transfers between devices with their start and end apart: 14, of which 6 were waited for; matrix products, arithmetic and copies ran while one was open for 0% of the time, Pallas kernels for 5%

profile of v12, /device:TPU:11, one launch (start us, length us, event | category | flops | bytes accessed | tf_op | source)
XLA Modules:
  0.0 33.0 jit_solution(15933203606955045184)
XLA Ops:
  0.0 1.2 %shard_map.37 = (f32[48,32,128]{2,1,0:T(8,128)S(1)}, f32[48,32,128]{2,1,0:T(8,128)S(1)}, f32[48,32,128]{2,1,0:T(8,128)S(1)}, f32[280,128]{1,0:T(8,128)S(1)}, f32...) custom-call(f32[32,16,128]{2,1,0:T(8,128)} %bitcast.6, ...), custom_call_target="tpu_custom_call" | custom-call | tf_op jit(solution)/shard_map/pallas_call | solution.py:729
  1.2 0.3 collective-permute-start
  1.6 2.2 %collective-permute-start.1 = (f32[280,128]{1,0:T(8,128)S(1)}, f32[280,128]{1,0:T(8,128)S(1)}, u32[]{:S(2)}, u32[]{:S(2)}) collective-permute-start(f32[280,128]{1,0:T(8,128)S(1)} %get-tuple-element.56), channel_id=1, source_target_pairs={{0,1},{1,0},{3,2},{2,3},{6,7},{7,6},{5,4},{4,5},{8,16},{9,17},{11,... | collective-permute-start | bytes 430088 | tf_op jit(solution)/shard_map/ppermute | solution.py:687
  3.7 1.2 %collective-permute-start.5 = (f32[416,128]{1,0:T(8,128)S(1)}, f32[416,128]{1,0:T(8,128)S(1)}, u32[]{:S(2)}, u32[]{:S(2)}) collective-permute-start(f32[416,128]{1,0:T(8,128)S(1)} %get-tuple-element.60), channel_id=1, source_target_pairs={{0,1},{1,0},{3,2},{2,3},{6,7},{7,6},{5,4},{4,5},{8,9},{9,8},{11,10... | collective-permute-start | bytes 638984 | tf_op jit(solution)/shard_map/ppermute | solution.py:687
  5.0 0.2 collective-permute-start.7
  5.1 2.4 %collective-permute-start.4 = (f32[192,128]{1,0:T(8,128)S(1)}, f32[192,128]{1,0:T(8,128)S(1)}, u32[]{:S(2)}, u32[]{:S(2)}) collective-permute-start(f32[192,128]{1,0:T(8,128)S(1)} %get-tuple-element.59), channel_id=1, source_target_pairs={{0,1},{1,0},{3,2},{2,3},{6,7},{7,6},{5,4},{4,5},{8,9},{9,8},{11,10... | collective-permute-start | bytes 294920 | tf_op jit(solution)/shard_map/ppermute | solution.py:687
  7.6 0.0 collective-permute-done.x_even
  7.6 2.4 %collective-permute-done.1.x_odd = f32[280,128]{1,0:T(8,128)S(1)} collective-permute-done((f32[280,128]{1,0:T(8,128)S(1)}, f32[280,128]{1,0:T(8,128)S(1)}, u32[]{:S(2)}, u32[]{:S(2)}) %collective-permute-start.1) | collective-permute-done | bytes 143392 | tf_op jit(solution)/shard_map/ppermute | solution.py:687
  10.0 1.6 %collective-permute-start.2 = (f32[176,128]{1,0:T(8,128)S(1)}, f32[176,128]{1,0:T(8,128)S(1)}, u32[]{:S(2)}, u32[]{:S(2)}) collective-permute-start(f32[176,128]{1,0:T(8,128)S(1)} %get-tuple-element.57), channel_id=1, source_target_pairs={{0,1},{1,0},{3,2},{2,3},{6,7},{7,6},{5,4},{4,5},{8,9},{9,8},{11,10... | collective-permute-start | bytes 270344 | tf_op jit(solution)/shard_map/ppermute | solution.py:687
  11.6 0.3 collective-permute-start.3
  11.9 1.4 %shard_map.39 = (f32[48,32,128]{2,1,0:T(8,128)S(1)}, f32[48,32,128]{2,1,0:T(8,128)S(1)}, f32[48,32,128]{2,1,0:T(8,128)S(1)}, f32[48,32,128]{2,1,0:T(8,128)S(1)},...) custom-call(f32[192,128]{1,0:T(8,128)S(1)} %collective-permute-done., ...), custom_call_target="tpu_custom_call", output_to_operand_aliasing={{0}: (4, {}), {1}: (5, {}), {2}: (6, {})} | custom-call | tf_op jit(solution)/shard_map/pallas_call | solution.py:752
  13.4 1.9 %collective-permute-done.3.c_odd = f32[176,128]{1,0:T(8,128)S(1)} collective-permute-done((f32[176,128]{1,0:T(8,128)S(1)}, f32[176,128]{1,0:T(8,128)S(1)}, u32[]{:S(2)}, u32[]{:S(2)}) %collective-permute-start.3) | collective-permute-done | bytes 90144 | tf_op jit(solution)/shard_map/ppermute | solution.py:687
  15.3 1.2 %shard_map.40 = (f32[48,32,128]{2,1,0:T(8,128)S(1)}, f32[48,32,128]{2,1,0:T(8,128)S(1)}, f32[48,32,128]{2,1,0:T(8,128)S(1)}, f32[48,32,128]{2,1,0:T(8,128)S(1)},...) custom-call(f32[280,128]{1,0:T(8,128)S(1)} %collective-permute-done., ...), custom_call_target="tpu_custom_call", output_to_operand_aliasing={{0}: (4, {}), {1}: (5, {}), {2}: (6, {}), {3}: (7, {}), {4}... | custom-call | tf_op jit(solution)/shard_map/pallas_call | solution.py:763
  16.5 0.1 collective-permute-start.8
  16.6 1.8 %collective-permute-start.9 = (f32[48,128]{1,0:T(8,128)S(1)}, f32[48,128]{1,0:T(8,128)S(1)}, u32[]{:S(2)}, u32[]{:S(2)}) collective-permute-start(f32[48,128]{1,0:T(8,128)S(1)} %get-tuple-element.90), channel_id=1, source_target_pairs={{0,1},{1,0},{3,2},{2,3},{6,7},{7,6},{5,4},{4,5},{8,16},{9,17},{11,... | collective-permute-start | bytes 73736 | tf_op jit(solution)/shard_map/ppermute | solution.py:687
  18.5 0.8 %collective-permute-done.8.x_even = f32[48,128]{1,0:T(8,128)S(1)} collective-permute-done((f32[48,128]{1,0:T(8,128)S(1)}, f32[48,128]{1,0:T(8,128)S(1)}, u32[]{:S(2)}, u32[]{:S(2)}) %collective-permute-start.8) | collective-permute-done | bytes 24608 | tf_op jit(solution)/shard_map/ppermute | solution.py:687
  19.3 1.0 %collective-permute-done.9.x_odd = f32[48,128]{1,0:T(8,128)S(1)} collective-permute-done((f32[48,128]{1,0:T(8,128)S(1)}, f32[48,128]{1,0:T(8,128)S(1)}, u32[]{:S(2)}, u32[]{:S(2)}) %collective-permute-start.9) | collective-permute-done | bytes 24608 | tf_op jit(solution)/shard_map/ppermute | solution.py:687
  20.3 0.6 %collective-permute-start.11 = (f32[144,128]{1,0:T(8,128)S(1)}, f32[144,128]{1,0:T(8,128)S(1)}, u32[]{:S(2)}, u32[]{:S(2)}) collective-permute-start(f32[144,128]{1,0:T(8,128)S(1)} %get-tuple-element.92), channel_id=1, source_target_pairs={{0,16},{1,3},{3,1},{2,6},{6,2},{7,5},{5,7},{4,20},{8,24},{9,11},{1... | collective-permute-start | bytes 221192 | tf_op jit(solution)/shard_map/ppermute | solution.py:687
  20.9 5.1 %collective-permute-start.10 = (f32[144,128]{1,0:T(8,128)S(1)}, f32[144,128]{1,0:T(8,128)S(1)}, u32[]{:S(2)}, u32[]{:S(2)}) collective-permute-start(f32[144,128]{1,0:T(8,128)S(1)} %get-tuple-element.91.own), channel_id=1, source_target_pairs={{0,1},{1,0},{3,2},{2,3},{6,7},{7,6},{5,4},{4,5},{8,9},{9,8},{11,10... | collective-permute-start | bytes 221192 | tf_op jit(solution)/shard_map/ppermute | solution.py:687
  25.9 0.6 %collective-permute-start.13 = (f32[48,128]{1,0:T(8,128)S(1)}, f32[48,128]{1,0:T(8,128)S(1)}, u32[]{:S(2)}, u32[]{:S(2)}) collective-permute-start(f32[48,128]{1,0:T(8,128)S(1)} %get-tuple-element.93), channel_id=1, source_target_pairs={{0,3},{1,0},{3,6},{2,1},{6,5},{7,2},{5,4},{4,7},{8,11},{9,8},{11,1... | collective-permute-start | bytes 73736 | tf_op jit(solution)/shard_map/ppermute | solution.py:687
  26.5 1.2 %collective-permute-start.12 = (f32[48,128]{1,0:T(8,128)S(1)}, f32[48,128]{1,0:T(8,128)S(1)}, u32[]{:S(2)}, u32[]{:S(2)}) collective-permute-start(f32[48,128]{1,0:T(8,128)S(1)} %get-tuple-element.93), channel_id=1, source_target_pairs={{0,1},{1,2},{3,0},{2,7},{6,3},{7,4},{5,6},{4,5},{8,9},{9,10},{11,8... | collective-permute-start | bytes 73736 | tf_op jit(solution)/shard_map/ppermute | solution.py:687
  27.7 1.8 %collective-permute-done.13.far_odd = f32[48,128]{1,0:T(8,128)S(1)} collective-permute-done((f32[48,128]{1,0:T(8,128)S(1)}, f32[48,128]{1,0:T(8,128)S(1)}, u32[]{:S(2)}, u32[]{:S(2)}) %collective-permute-start.13) | collective-permute-done | bytes 24608 | tf_op jit(solution)/shard_map/ppermute | solution.py:687
  29.5 1.2 %collective-permute-done.12.far_even = f32[48,128]{1,0:T(8,128)S(1)} collective-permute-done((f32[48,128]{1,0:T(8,128)S(1)}, f32[48,128]{1,0:T(8,128)S(1)}, u32[]{:S(2)}, u32[]{:S(2)}) %collective-permute-start.12) | collective-permute-done | bytes 24608 | tf_op jit(solution)/shard_map/ppermute | solution.py:687
  30.7 2.4 %shard_map.42 = f32[32,16,128]{2,1,0:T(8,128)} custom-call(f32[144,128]{1,0:T(8,128)S(1)} %collective-permute-done.10.near_even, f32[144,128]{1,0:T(8,128)S(1)} %collective-permute-done.11.near_odd, f32[48,128]{1,0:T(8,128)S(1)} %collective-permute-done.12.far_even, f32[48,128]{1,0:T(8,128)S(1)} %collective-permute-done.13.far_odd, ...), custom_call_target="tpu_custom_call" | custom-call | tf_op jit(solution)/shard_map/pallas_call | solution.py:789
  (10 shorter events, 0.1 us)
Async XLA Ops:
  1.2 6.3 %collective-permute-start = (f32[280,128]{1,0:T(8,128)S(1)}, f32[280,128]{1,0:T(8,128)S(1)}, u32[]{:S(2)}, u32[]{:S(2)}) collective-permute-start(f32[280,128]{1,0:T(8,128)S(1)} %get-tuple-element.55), channel_id=1, source_target_pairs={{0,8},{1,9},{3,11},{2,10},{6,14},{7,15},{5,13},{4,12},{8,0},{9,1},... | collective-permute-start | bytes 430088 | tf_op jit(solution)/shard_map/ppermute | solution.py:687
  1.6 8.4 %collective-permute-start.1 = (f32[280,128]{1,0:T(8,128)S(1)}, f32[280,128]{1,0:T(8,128)S(1)}, u32[]{:S(2)}, u32[]{:S(2)}) collective-permute-start(f32[280,128]{1,0:T(8,128)S(1)} %get-tuple-element.56), channel_id=1, source_target_pairs={{0,1},{1,0},{3,2},{2,3},{6,7},{7,6},{5,4},{4,5},{8,16},{9,17},{11,... | collective-permute-start | bytes 430088 | tf_op jit(solution)/shard_map/ppermute | solution.py:687
  3.7 8.2 %collective-permute-start.5 = (f32[416,128]{1,0:T(8,128)S(1)}, f32[416,128]{1,0:T(8,128)S(1)}, u32[]{:S(2)}, u32[]{:S(2)}) collective-permute-start(f32[416,128]{1,0:T(8,128)S(1)} %get-tuple-element.60), channel_id=1, source_target_pairs={{0,1},{1,0},{3,2},{2,3},{6,7},{7,6},{5,4},{4,5},{8,9},{9,8},{11,10... | collective-permute-start | bytes 638984 | tf_op jit(solution)/shard_map/ppermute | solution.py:687
  5.0 7.0 %collective-permute-start.7 = (f32[416,128]{1,0:T(8,128)S(1)}, f32[416,128]{1,0:T(8,128)S(1)}, u32[]{:S(2)}, u32[]{:S(2)}) collective-permute-start(f32[416,128]{1,0:T(8,128)S(1)} %get-tuple-element.62), channel_id=1, source_target_pairs={{0,16},{1,3},{3,1},{2,6},{6,2},{7,5},{5,7},{4,20},{8,24},{9,11},{1... | collective-permute-start | bytes 638984 | tf_op jit(solution)/shard_map/ppermute | solution.py:687
  5.1 6.5 %collective-permute-start.4 = (f32[192,128]{1,0:T(8,128)S(1)}, f32[192,128]{1,0:T(8,128)S(1)}, u32[]{:S(2)}, u32[]{:S(2)}) collective-permute-start(f32[192,128]{1,0:T(8,128)S(1)} %get-tuple-element.59), channel_id=1, source_target_pairs={{0,1},{1,0},{3,2},{2,3},{6,7},{7,6},{5,4},{4,5},{8,9},{9,8},{11,10... | collective-permute-start | bytes 294920 | tf_op jit(solution)/shard_map/ppermute | solution.py:687
  7.6 4.4 %collective-permute-start.6 = (f32[192,128]{1,0:T(8,128)S(1)}, f32[192,128]{1,0:T(8,128)S(1)}, u32[]{:S(2)}, u32[]{:S(2)}) collective-permute-start(f32[192,128]{1,0:T(8,128)S(1)} %get-tuple-element.61), channel_id=1, source_target_pairs={{0,16},{1,3},{3,1},{2,6},{6,2},{7,5},{5,7},{4,20},{8,24},{9,11},{1... | collective-permute-start | bytes 294920 | tf_op jit(solution)/shard_map/ppermute | solution.py:687
  10.0 3.4 %collective-permute-start.2 = (f32[176,128]{1,0:T(8,128)S(1)}, f32[176,128]{1,0:T(8,128)S(1)}, u32[]{:S(2)}, u32[]{:S(2)}) collective-permute-start(f32[176,128]{1,0:T(8,128)S(1)} %get-tuple-element.57), channel_id=1, source_target_pairs={{0,1},{1,0},{3,2},{2,3},{6,7},{7,6},{5,4},{4,5},{8,9},{9,8},{11,10... | collective-permute-start | bytes 270344 | tf_op jit(solution)/shard_map/ppermute | solution.py:687
  11.6 3.7 %collective-permute-start.3 = (f32[176,128]{1,0:T(8,128)S(1)}, f32[176,128]{1,0:T(8,128)S(1)}, u32[]{:S(2)}, u32[]{:S(2)}) collective-permute-start(f32[176,128]{1,0:T(8,128)S(1)} %get-tuple-element.58), channel_id=1, source_target_pairs={{0,16},{1,3},{3,1},{2,6},{6,2},{7,5},{5,7},{4,20},{8,24},{9,11},{1... | collective-permute-start | bytes 270344 | tf_op jit(solution)/shard_map/ppermute | solution.py:687
  16.5 2.7 %collective-permute-start.8 = (f32[48,128]{1,0:T(8,128)S(1)}, f32[48,128]{1,0:T(8,128)S(1)}, u32[]{:S(2)}, u32[]{:S(2)}) collective-permute-start(f32[48,128]{1,0:T(8,128)S(1)} %get-tuple-element.89), channel_id=1, source_target_pairs={{0,8},{1,9},{3,11},{2,10},{6,14},{7,15},{5,13},{4,12},{8,0},{9,1},... | collective-permute-start | bytes 73736 | tf_op jit(solution)/shard_map/ppermute | solution.py:687
  16.6 3.6 %collective-permute-start.9 = (f32[48,128]{1,0:T(8,128)S(1)}, f32[48,128]{1,0:T(8,128)S(1)}, u32[]{:S(2)}, u32[]{:S(2)}) collective-permute-start(f32[48,128]{1,0:T(8,128)S(1)} %get-tuple-element.90), channel_id=1, source_target_pairs={{0,1},{1,0},{3,2},{2,3},{6,7},{7,6},{5,4},{4,5},{8,16},{9,17},{11,... | collective-permute-start | bytes 73736 | tf_op jit(solution)/shard_map/ppermute | solution.py:687
  20.3 10.4 %collective-permute-start.11 = (f32[144,128]{1,0:T(8,128)S(1)}, f32[144,128]{1,0:T(8,128)S(1)}, u32[]{:S(2)}, u32[]{:S(2)}) collective-permute-start(f32[144,128]{1,0:T(8,128)S(1)} %get-tuple-element.92), channel_id=1, source_target_pairs={{0,16},{1,3},{3,1},{2,6},{6,2},{7,5},{5,7},{4,20},{8,24},{9,11},{1... | collective-permute-start | bytes 221192 | tf_op jit(solution)/shard_map/ppermute | solution.py:687
  20.9 9.8 %collective-permute-start.10 = (f32[144,128]{1,0:T(8,128)S(1)}, f32[144,128]{1,0:T(8,128)S(1)}, u32[]{:S(2)}, u32[]{:S(2)}) collective-permute-start(f32[144,128]{1,0:T(8,128)S(1)} %get-tuple-element.91.own), channel_id=1, source_target_pairs={{0,1},{1,0},{3,2},{2,3},{6,7},{7,6},{5,4},{4,5},{8,9},{9,8},{11,10... | collective-permute-start | bytes 221192 | tf_op jit(solution)/shard_map/ppermute | solution.py:687
  25.9 3.5 %collective-permute-start.13 = (f32[48,128]{1,0:T(8,128)S(1)}, f32[48,128]{1,0:T(8,128)S(1)}, u32[]{:S(2)}, u32[]{:S(2)}) collective-permute-start(f32[48,128]{1,0:T(8,128)S(1)} %get-tuple-element.93), channel_id=1, source_target_pairs={{0,3},{1,0},{3,6},{2,1},{6,5},{7,2},{5,4},{4,7},{8,11},{9,8},{11,1... | collective-permute-start | bytes 73736 | tf_op jit(solution)/shard_map/ppermute | solution.py:687
  26.5 4.2 %collective-permute-start.12 = (f32[48,128]{1,0:T(8,128)S(1)}, f32[48,128]{1,0:T(8,128)S(1)}, u32[]{:S(2)}, u32[]{:S(2)}) collective-permute-start(f32[48,128]{1,0:T(8,128)S(1)} %get-tuple-element.93), channel_id=1, source_target_pairs={{0,1},{1,2},{3,0},{2,7},{6,3},{7,4},{5,6},{4,5},{8,9},{9,10},{11,8... | collective-permute-start | bytes 73736 | tf_op jit(solution)/shard_map/ppermute | solution.py:687
